TPU v7x, 256 devices: a whole 4x4x8 slice. The times are simulated.
256 devices in a mesh: dp: 32 (over z, x), tensor: 8 (over y, core).
Axes of the slice: x: 4, y: 4, z: 8, core: 2. Of those that a mesh axis runs over, the one named last changes fastest.
Arguments:
- queries: bfloat16 [16384, 4096], P('dp', 'tensor'), may hold values from -5 to 5
- new_keys: bfloat16 [16384, 1024], P('dp', 'tensor'), may hold values from -5 to 5
- new_values: bfloat16 [16384, 1024], P('dp', 'tensor'), may hold values from -5 to 5
- hidden: bfloat16 [16384, 8192], P('dp', 'tensor'), may hold values from -6 to 6
- row_counts: int32 [32, 32], P('dp'), may hold values from 1 to 64, 512 in all within a row
- pack_of: int32 [32, 32], P('dp'), may hold values from 0 to 31, each once within a row
- cache_keys: bfloat16 [32, 32, 128, 1024], P('dp', None, None, 'tensor'), may hold values from -5 to 5
- cache_values: bfloat16 [32, 32, 128, 1024], P('dp', None, None, 'tensor'), may hold values from -5 to 5
- prefix_lengths: int32 [32, 32], P('dp'), may hold values from 32 to 128
- out_weight: bfloat16 [4096, 8192], P('tensor'), may hold values from -0.09375 to 0.09375
- norm_gain: float32 [8192], P('tensor'), may hold values from 0.1 to 1.9
Outputs:
- residual_out: bfloat16 [16384, 8192], P('dp', 'tensor')
- normed: bfloat16 [16384, 8192], P('dp', 'tensor')
Inputs may be any that keep to these rules, and one draw needn't show every extreme that they name: Each row of row_counts sums to 512; its largest count is exactly 64. Each row of pack_of names every pack once.
All inputs are finite; a program needn't handle non-finite values.
Results may differ from a plain program's by a relative error of at most 0.011.
Values may be sent and summed in bfloat16 or wider, within the bound.
No kernel may reach another device: no remote copies, remote signals or barrier semaphores. Data moves between devices by JAX's collectives and lax.ppermute only.
A program may use at most 64 MiB of HBM per device.

v0:
```python
import math

import jax
import jax.numpy as jnp
from jax import lax
from jax.sharding import PartitionSpec as P

D = 8192
HEADS = 32
KV_HEADS = 8
HD = 128
MOST = 64


def slot_plan(counts, packs, total_rows, slot_most):
    roll_count = counts.shape[0]
    starts = jnp.cumsum(counts) - counts
    pack_ids = lax.broadcasted_iota(jnp.int32, (roll_count, roll_count), 1)
    hits = (packs[:, None] == pack_ids).astype(jnp.int32)
    first_row = jnp.sum(starts[:, None] * hits, axis=0)
    pack_rows = jnp.sum(counts[:, None] * hits, axis=0)
    offsets = jnp.arange(slot_most, dtype=jnp.int32)
    index = jnp.minimum(first_row[:, None] + offsets[None, :], total_rows - 1)
    valid = offsets[None, :] < pack_rows[:, None]
    return (index, valid)


def row_lookup(counts, packs, total_rows, slot_most):
    roll_count = counts.shape[0]
    starts = jnp.cumsum(counts) - counts
    ends = starts + counts
    row_ids = jnp.arange(total_rows, dtype=jnp.int32)
    rollout = jnp.sum((ends[None, :] <= row_ids[:, None]).astype(jnp.int32), axis=1)
    hit = rollout[:, None] == jnp.arange(roll_count, dtype=jnp.int32)[None, :]
    start_row = jnp.sum(jnp.where(hit, starts[None, :], 0), axis=1)
    pack_row = jnp.sum(jnp.where(hit, packs[None, :], 0), axis=1)
    return pack_row * slot_most + row_ids - start_row


def attend(
    query_flat, key_flat, value_flat, key_cache, value_cache, live_lengths, kv_local, group_size
):
    slot_count = query_flat.shape[0]
    slot_most = query_flat.shape[1]
    prefix_len = key_cache.shape[1]
    query_slots = query_flat.reshape(slot_count, slot_most, kv_local, group_size, HD)
    key_slots = key_flat.reshape(slot_count, slot_most, kv_local, HD)
    value_slots = value_flat.reshape(slot_count, slot_most, kv_local, HD)
    cache_k = key_cache.reshape(slot_count, prefix_len, kv_local, HD)
    cache_v = value_cache.reshape(slot_count, prefix_len, kv_local, HD)
    score_scale = 1.0 / math.sqrt(HD)
    cached = (
        jnp.einsum("bmkgh,bpkh->bkgmp", query_slots, cache_k, preferred_element_type=jnp.float32)
        * score_scale
    )
    fresh_scores = (
        jnp.einsum("bmkgh,bnkh->bkgmn", query_slots, key_slots, preferred_element_type=jnp.float32)
        * score_scale
    )
    positions = jnp.arange(prefix_len, dtype=jnp.int32)
    cached = jnp.where(
        positions[None, None, None, None, :] < live_lengths[:, None, None, None, None],
        cached,
        -1e30,
    )
    slot_order = jnp.arange(slot_most, dtype=jnp.int32)
    fresh_scores = jnp.where(slot_order[None, :] <= slot_order[:, None], fresh_scores, -1e30)
    scores = jnp.concatenate([cached, fresh_scores], axis=-1)
    row_top = jnp.max(scores, axis=-1, keepdims=True)
    lifted = jnp.exp(scores - row_top)
    weights = (lifted / jnp.sum(lifted, axis=-1, keepdims=True)).astype(jnp.bfloat16)
    all_values = jnp.concatenate([cache_v, value_slots], axis=1)
    mixed = jnp.einsum("bkgmn,bnkh->bmkgh", weights, all_values, preferred_element_type=jnp.float32)
    return mixed.astype(jnp.bfloat16).reshape(slot_count, slot_most, -1)


def on_device(
    queries,
    new_keys,
    new_values,
    hidden,
    row_counts,
    pack_of,
    cache_keys,
    cache_values,
    prefix_lengths,
    out_weight,
    norm_gain,
):
    total_rows = queries.shape[0]
    q_width = queries.shape[1]
    k_width = new_keys.shape[1]
    kv_local = k_width // HD
    group_size = HEADS // KV_HEADS
    slot_most = MOST
    counts = row_counts[0]
    packs = pack_of[0]
    index, valid = slot_plan(counts, packs, total_rows, slot_most)
    keep = valid[:, :, None]

    def take_rows(source):
        return jnp.where(keep, source[index], jnp.zeros((), source.dtype))

    query_slots = take_rows(queries)
    key_slots = take_rows(new_keys)
    value_slots = take_rows(new_values)
    payload = jnp.concatenate([query_slots, key_slots, value_slots], axis=2)
    arrived = lax.all_to_all(payload, "dp", split_axis=0, concat_axis=0, tiled=True)
    got_query = arrived[:, :, :q_width]
    got_key = arrived[:, :, q_width : q_width + k_width]
    got_value = arrived[:, :, q_width + k_width :]
    result = attend(
        got_query,
        got_key,
        got_value,
        cache_keys[0],
        cache_values[0],
        prefix_lengths[0],
        kv_local,
        group_size,
    )
    attended_slots = lax.all_to_all(result, "dp", split_axis=0, concat_axis=0, tiled=True)
    flat_slots = attended_slots.reshape(-1, q_width)
    attended = flat_slots[row_lookup(counts, packs, total_rows, slot_most)]
    partial_value = jnp.dot(attended, out_weight, preferred_element_type=jnp.float32)
    delta = lax.psum_scatter(
        partial_value.astype(jnp.bfloat16), "tensor", scatter_dimension=1, tiled=True
    ).astype(jnp.float32)
    summed = hidden.astype(jnp.float32) + delta
    residual_out = summed.astype(jnp.bfloat16)
    squares = lax.psum(jnp.sum(summed * summed, axis=1), "tensor")
    mean_square = squares / D
    normed = (summed * lax.rsqrt(mean_square + 1e-06)[:, None] * norm_gain[None, :]).astype(
        jnp.bfloat16
    )
    return (residual_out, normed)


def solution(mesh):
    return jax.shard_map(
        on_device,
        mesh=mesh,
        in_specs=(
            P("dp", "tensor"),
            P("dp", "tensor"),
            P("dp", "tensor"),
            P("dp", "tensor"),
            P("dp", None),
            P("dp", None),
            P("dp", None, None, "tensor"),
            P("dp", None, None, "tensor"),
            P("dp", None),
            P("tensor", None),
            P("tensor"),
        ),
        out_specs=(P("dp", "tensor"), P("dp", "tensor")),
        check_vma=False,
    )
```

profile of v0, /device:TPU:2, one launch (start us, length us, event | category | flops | bytes accessed | tf_op | source)
XLA Modules:
  0.0 286.7 jit_solution(206235643374108034)
XLA Ops:
  7.2 0.8 copy.18
  8.1 0.1 reduce.5
  8.2 0.7 bitcast_subtract_fusion.1
  8.9 0.8 select_reduce_fusion.3
  9.9 6.6 %gather_fusion.2 = bf16[2048,128]{1,0:T(8,128)(2,1)S(1)} fusion(bf16[512,128]{1,0:T(8,128)(2,1)} %param.13, s32[2048]{0:T(1024)S(1)} %broadcast_clamp_fusion), kind=kCustom, calls=%fused_computation.2 | custom fusion | bytes 1056768 | tf_op jit(solution)/shard_map/gather | solution.py:102
  16.5 6.2 %gather_fusion.1 = bf16[2048,128]{1,0:T(8,128)(2,1)S(1)} fusion(bf16[512,128]{1,0:T(8,128)(2,1)S(1)} %copy-done.2, s32[2048]{0:T(1024)S(1)} %broadcast_clamp_fusion), kind=kCustom, calls=%fused_computation.1 | custom fusion | bytes 1056768 | tf_op jit(solution)/shard_map/gather | solution.py:102
  22.7 9.2 %gather_fusion = bf16[2048,512]{1,0:T(8,128)(2,1)} fusion(bf16[512,512]{1,0:T(8,128)(2,1)S(1)} %copy-done.1, s32[2048]{0:T(1024)S(1)} %broadcast_clamp_fusion), kind=kCustom, calls=%fused_computation | custom fusion | bytes 4202496 | tf_op jit(solution)/shard_map/gather | solution.py:102
  31.8 1.8 broadcast_select_fusion
  33.6 0.5 broadcast_select_fusion.2
  34.1 2.0 pad_maximum_fusion
  36.1 11.8 %all-to-all-start = ((bf16[32,64,768]{2,1,0:T(8,128)(2,1)}), bf16[32,64,768]{2,1,0:T(8,128)(2,1)}, u32[]{:S(2)}, u32[]{:S(2)}) async-start(bf16[32,64,768]{2,1,0:T(8,128)(2,1)} %pad_maximum_fusion), calls=%async_computation | async-start | bytes 6291456 | tf_op jit(solution)/shard_map/all_to_all | solution.py:108
  48.0 71.2 %all-to-all-done = bf16[32,64,768]{2,1,0:T(8,128)(2,1)} async-done(((bf16[32,64,768]{2,1,0:T(8,128)(2,1)}), bf16[32,64,768]{2,1,0:T(8,128)(2,1)}, u32[]{:S(2)}, u32[]{:S(2)}) %all-to-all-start) | async-done | bytes 3145760 | tf_op jit(solution)/shard_map/all_to_all | solution.py:108
  119.2 2.3 fusion.10
  121.5 1.0 fusion.7
  122.5 1.2 fusion.23
  123.8 3.2 %fusion.25 = (f32[32,4,64]{2,1,0:T(4,128)S(1)}, f32[32,1,4,64,64]{4,3,2,0,1:T(8,128)S(1)}) fusion(bf16[32,64,768]{2,1,0:T(8,128)(2,1)} %all-to-all-done, pred[64,64]{1,0:T(8,128)(4,1)S(1)} %iota_compare_fusion.2), kind=kOutput, calls=%fused_computation.61 | convolution fusion | flops 135782400 | bytes 4755456 | tf_op jit(solution)/shard_map/bmkgh,bnkh->bkgmn/dot_general | solution.py:57
  127.0 2.8 fusion.3
  129.8 1.1 slice_bitcast_fusion.3
  130.9 3.8 %convert_bitcast_fusion = bf16[32,64,1,4,128]{4,1,3,0,2:T(8,128)(2,1)S(1)} fusion(f32[32,4,64,64]{3,2,1,0:T(8,128)S(1)} %bitcast.85, f32[32,4,64,128]{3,2,1,0:T(8,128)S(1)} %fusion.7, f32[32,4,64]{2,1,0:T(4,128)S(1)} %fusion.3, f32[32,4,64]{2,1,0:T(4,128)S(1)} %reduce_max.22, bf16[32,64,1,128]{3,1,0,2:T(8,128)(2,1)S(1)} %slice_bitcast_fusion.3, ...), kind=kOutput, calls=%fused_computation.25 | convolution fusion | flops 413138944 | bytes 10027008 | tf_op jit(solution)/shard_map/bkgmn,bnkh->bmkgh/dot_general | solution.py:73
  134.6 2.0 copy.21
  136.6 2.2 reshape.250
  138.9 7.3 %all-to-all-start.1 = ((bf16[32,64,512]{2,1,0:T(8,128)(2,1)}), bf16[32,64,512]{2,1,0:T(8,128)(2,1)S(1)}, u32[]{:S(2)}, u32[]{:S(2)}) async-start(bf16[32,64,512]{2,1,0:T(8,128)(2,1)} %reshape.250), calls=%async_computation.1 | async-start | bytes 4194304 | tf_op jit(solution)/shard_map/all_to_all | solution.py:122
  146.2 0.2 reduce-scatter.2.cloned.1.call-start
  146.4 0.1 convert_reduce_fusion
  146.5 0.1 select_reduce_fusion.1
  146.7 48.5 %all-to-all-done.1 = bf16[32,64,512]{2,1,0:T(8,128)(2,1)S(1)} async-done(((bf16[32,64,512]{2,1,0:T(8,128)(2,1)}), bf16[32,64,512]{2,1,0:T(8,128)(2,1)S(1)}, u32[]{:S(2)}, u32[]{:S(2)}) %all-to-all-start.1) | async-done | bytes 2097184 | tf_op jit(solution)/shard_map/all_to_all | solution.py:122
  195.2 2.6 gather_fusion.3
  197.8 11.3 %convolution_convert_fusion = bf16[512,8192]{1,0:T(8,128)(2,1)} fusion(bf16[512,512]{1,0:T(8,128)(2,1)} %gather_fusion.3, bf16[512,8192]{1,0:T(8,128)(2,1)} %param.20), kind=kOutput, calls=%fused_computation.4 | convolution fusion | flops 4299161600 | bytes 17301504 | tf_op jit(solution)/shard_map/dot_general | solution.py:125
  209.1 53.3 %reduce-scatter.2.cloned.1.call-done = bf16[512,1024]{1,0:T(8,128)(2,1)} async-done(((bf16[512,8192]{1,0:T(8,128)(2,1)}), bf16[512,1024]{1,0:T(8,128)(2,1)}) %reduce-scatter.2.cloned.1.call-update) | async-done | bytes 1048592 | tf_op jit(solution)/shard_map/reduce_scatter | solution.py:126
  262.4 1.6 multiply_reduce_fusion
  264.1 12.9 %psum.7 = f32[512]{0:T(512)S(1)} all-reduce(f32[512]{0:T(512)S(1)} %multiply_reduce_fusion), channel_id=1, replica_groups=mesh['dp'=32,'tensor'=8] {'tensor'}, use_global_device_ids=true, to_apply=%region_11.12 | all-reduce | flops 512 | bytes 4096 | tf_op jit(solution)/shard_map/psum | solution.py:131
  276.9 3.0 %multiply_convert_fusion = (bf16[512,1024]{1,0:T(8,128)(2,1)}, bf16[512,1024]{1,0:T(8,128)(2,1)}) fusion(bf16[512,1024]{1,0:T(8,128)(2,1)} %reduce-scatter.2.cloned.1.call-done, bf16[512,1024]{1,0:T(8,128)(2,1)S(1)} %copy-done.3, f32[1024]{0:T(1024)S(1)} %copy-done.4, f32[512]{0:T(512)S(1)} %add_rsqrt_fusion), kind=kLoop, calls=%fused_computation.22 | loop fusion | flops 3670016 | bytes 4200448 | tf_op jit(solution)/shard_map/convert_element_type | solution.py:133
  (32 shorter events, 0.5 us)
Async XLA Ops:
  7.2 112.1 %copy-start = (bf16[1,32,128,128]{3,2,1,0:T(8,128)(2,1)S(1)}, bf16[1,32,128,128]{3,2,1,0:T(8,128)(2,1)}, u32[]{:S(2)}) copy-start(bf16[1,32,128,128]{3,2,1,0:T(8,128)(2,1)} %param.17) | copy-start | bytes 3145732
  7.2 9.3 %copy-start.2 = (bf16[512,128]{1,0:T(8,128)(2,1)S(1)}, bf16[512,128]{1,0:T(8,128)(2,1)}, u32[]{:S(2)}) copy-start(bf16[512,128]{1,0:T(8,128)(2,1)} %param.12) | copy-start | bytes 393220
  9.9 12.8 %copy-start.1 = (bf16[512,512]{1,0:T(8,128)(2,1)S(1)}, bf16[512,512]{1,0:T(8,128)(2,1)}, u32[]{:S(2)}) copy-start(bf16[512,512]{1,0:T(8,128)(2,1)} %param.11) | copy-start | bytes 1572868
  36.1 11.8 %copy-start.7 = (s32[1,32]{1,0:T(1,128)S(1)}, s32[1,32]{1,0:T(1,128)}, u32[]{:S(2)}) copy-start(s32[1,32]{1,0:T(1,128)} %param.19) | copy-start | bytes 388
  36.1 83.1 %all-to-all-start = ((bf16[32,64,768]{2,1,0:T(8,128)(2,1)}), bf16[32,64,768]{2,1,0:T(8,128)(2,1)}, u32[]{:S(2)}, u32[]{:S(2)}) async-start(bf16[32,64,768]{2,1,0:T(8,128)(2,1)} %pad_maximum_fusion), calls=%async_computation | async-start | bytes 6291456 | tf_op jit(solution)/shard_map/all_to_all | solution.py:108
  127.0 3.9 %copy-start.8 = (bf16[1,32,128,128]{3,2,1,0:T(8,128)(2,1)S(1)}, bf16[1,32,128,128]{3,2,1,0:T(8,128)(2,1)}, u32[]{:S(2)}) copy-start(bf16[1,32,128,128]{3,2,1,0:T(8,128)(2,1)} %param.18) | copy-start | bytes 3145732
  136.6 9.9 %copy-start.6 = (s32[1,32]{1,0:T(1,128)S(1)}, s32[1,32]{1,0:T(1,128)}, u32[]{:S(2)}) copy-start(s32[1,32]{1,0:T(1,128)} %param.15) | copy-start | bytes 388
  136.6 9.9 %copy-start.5 = (s32[1,32]{1,0:T(1,128)S(1)}, s32[1,32]{1,0:T(1,128)}, u32[]{:S(2)}) copy-start(s32[1,32]{1,0:T(1,128)} %param.16) | copy-start | bytes 388
  138.9 56.3 %all-to-all-start.1 = ((bf16[32,64,512]{2,1,0:T(8,128)(2,1)}), bf16[32,64,512]{2,1,0:T(8,128)(2,1)S(1)}, u32[]{:S(2)}, u32[]{:S(2)}) async-start(bf16[32,64,512]{2,1,0:T(8,128)(2,1)} %reshape.250), calls=%async_computation.1 | async-start | bytes 4194304 | tf_op jit(solution)/shard_map/all_to_all | solution.py:122
  146.2 116.2 %reduce-scatter.2.cloned.1.call-start = ((), (), s32[]{:S(2)}) async-start(), calls=%async_computation.3 | async-start | bytes 9437184 | tf_op jit(solution)/shard_map/reduce_scatter | solution.py:126
  209.1 53.3 %copy-start.3 = (bf16[512,1024]{1,0:T(8,128)(2,1)S(1)}, bf16[512,1024]{1,0:T(8,128)(2,1)}, u32[]{:S(2)}) copy-start(bf16[512,1024]{1,0:T(8,128)(2,1)} %param.14) | copy-start | bytes 3145732
  209.1 67.8 %copy-start.4 = (f32[1024]{0:T(1024)S(1)}, f32[1024]{0:T(1024)}, u32[]{:S(2)}) copy-start(f32[1024]{0:T(1024)} %param.21) | copy-start | bytes 12292
Sparse Core Ops, SparseCore 0:
  209.3 53.1 reduce-scatter.1
where the time goes:
time: 288 us; the launch traced here: 287 us
  waiting for transfers between devices  173 us (60%)
  local copies, waits for them, and re-layouts  30.8 us (11%)
  matrix products  20.6 us (7%)
  starting transfers between devices  19.4 us (7%)
  other arithmetic  15.9 us (6%)
  between operations  14.3 us (5%)
  blocking collectives  12.9 us (4%)
    all_to_all x1, waiting for transfers between devices, on_device(): lax.all_to_all(payload, 'dp', split_axis=0, concat_axis=0, tiled=True)  71.2 us
    reduce_scatter x1, waiting for transfers between devices, on_device(): lax.psum_scatter(partial_value.astype(jnp.bfloat16), 'tensor', scatter_di...  53.3 us
    all_to_all x1, waiting for transfers between devices, on_device(): lax.all_to_all(result, 'dp', split_axis=0, concat_axis=0, tiled=True)  48.5 us
    gather x3, local copies, waits for them, and re-layouts, take_rows(): return jnp.where(keep, source[index], jnp.zeros((), source.dtype))  21.9 us
    psum x1, blocking collectives, on_device(): squares = lax.psum(jnp.sum(summed * summed, axis=1), 'tensor')  12.9 us
    all_to_all x1, starting transfers between devices, on_device(): lax.all_to_all(payload, 'dp', split_axis=0, concat_axis=0, tiled=True)  11.8 us
    dot_general x1, matrix products, on_device(): jnp.dot(attended, out_weight, preferred_element_type=jnp.float32)  11.3 us
    all_to_all x1, starting transfers between devices, on_device(): lax.all_to_all(result, 'dp', split_axis=0, concat_axis=0, tiled=True)  7.33 us
  transfers between devices with their start and end apart: 3, of which 3 were waited for; matrix products, arithmetic and copies ran while one was open for 0% of the time, Pallas kernels for 0%

commit v1 on v0

v1 whole, which is shorter than its diff:
```python
import math

import jax
import jax.numpy as jnp
from jax import lax
from jax.experimental import pallas as pl
from jax.experimental.pallas import tpu as pltpu
from jax.sharding import PartitionSpec as P

D = 8192
HEADS = 32
KV_HEADS = 8
HD = 128
MOST = 64
GROUP = HEADS // KV_HEADS
BLOCK = 32
FRESH = 128
PAIRS = 48
UNROLL = 8
LOW = -1e30
DEAD = 8192.0
SCALE = 1.0 / math.sqrt(HD)


def pair_plan(counts, packs):
    roll = counts.shape[0]
    ids = jnp.arange(roll, dtype=jnp.int32)
    before = ids[None, :] < ids[:, None]
    starts = jnp.sum(jnp.where(before, counts[None, :], 0), axis=1)
    ends = starts + counts
    first = starts // BLOCK
    spans = (ends - 1) // BLOCK - first + 1
    offsets = jnp.sum(jnp.where(before, spans[None, :], 0), axis=1)
    slot = jnp.arange(PAIRS, dtype=jnp.int32)[:, None]
    hit = (slot >= offsets[None, :]) & (slot < (offsets + spans)[None, :])

    def pick(values):
        return jnp.sum(jnp.where(hit, values, 0), axis=1)

    block = pick(first[None, :] + slot - offsets[None, :])
    plan = jnp.stack(
        [block, pick(packs[None, :]), pick(starts[None, :]), pick(ends[None, :])]
    ).astype(jnp.int32)
    rows = jnp.arange(512, dtype=jnp.int32)[:, None]
    row_start = jnp.max(jnp.where(starts[None, :] <= rows, starts[None, :], 0), axis=1)
    return plan, jnp.broadcast_to(row_start[:, None], (512, HD))


def stack_heads(ref, base):
    return [ref[pl.ds(base, BLOCK), h * HD : (h + 1) * HD] for h in range(GROUP)]


def block_rows(base):
    sub = lax.broadcasted_iota(jnp.int32, (GROUP * BLOCK, HD), 0)
    return base + jnp.bitwise_and(sub, BLOCK - 1)


def score_kernel(plan, q, k, fresh_k, fresh_v, row_start, weights, fresh_out, scores):
    ones = jnp.ones((16, HD), jnp.bfloat16)
    nt = (((1,), (1,)), ((), ()))

    def group(step, carry):
        for u in range(UNROLL):
            i = step * UNROLL + u
            block = plan[0, i]
            base = pl.multiple_of(block * BLOCK, BLOCK)
            left = jnp.concatenate(stack_heads(q, base) + [ones], axis=0)
            both = lax.dot_general(left, k[plan[1, i]], nt, preferred_element_type=jnp.float32)
            live = both[GROUP * BLOCK : GROUP * BLOCK + 1] < 32.0 * DEAD
            found = jnp.where(live, both[: GROUP * BLOCK] * SCALE, LOW)
            rows = block_rows(base)
            mine = (rows >= plan[2, i]) & (rows < plan[3, i])
            scores[block] = jnp.where(mine, found, scores[block])
        return carry

    lax.fori_loop(0, PAIRS // UNROLL, group, 0)

    def finish(block, carry):
        base = pl.multiple_of(block * BLOCK, BLOCK)
        left = jnp.concatenate(stack_heads(q, base), axis=0)
        window = pl.ds(base, FRESH)
        fresh = lax.dot_general(left, fresh_k[window, :], nt, preferred_element_type=jnp.float32)
        key = base - (FRESH - BLOCK) + lax.broadcasted_iota(jnp.int32, fresh.shape, 1)
        start = jnp.concatenate([row_start[pl.ds(base, BLOCK), :]] * GROUP, axis=0)
        fresh = jnp.where((key <= block_rows(base)) & (key >= start), fresh * SCALE, LOW)
        cached = scores[block]
        top = jnp.max(jnp.maximum(cached, fresh), axis=1, keepdims=True)
        lift_c = jnp.exp(cached - top)
        lift_f = jnp.exp(fresh - top)
        total = jnp.sum(lift_c + lift_f, axis=1, keepdims=True)
        share = 1.0 / total
        weights[block] = (lift_c * share).astype(jnp.bfloat16)
        fresh_out[block] = jnp.dot(
            (lift_f * share).astype(jnp.bfloat16),
            fresh_v[window, :],
            preferred_element_type=jnp.float32,
        )
        return carry

    lax.fori_loop(0, 512 // BLOCK, finish, 0, unroll=4)


def mix_kernel(plan, weights, v, fresh_out, out, mixed):
    def group(step, carry):
        for u in range(UNROLL):
            i = step * UNROLL + u
            block = plan[0, i]
            rows = block_rows(block * BLOCK)
            mine = (rows >= plan[2, i]) & (rows < plan[3, i])
            found = jnp.dot(weights[block], v[plan[1, i]], preferred_element_type=jnp.float32)
            mixed[block] = jnp.where(mine, found, mixed[block])
        return carry

    lax.fori_loop(0, PAIRS // UNROLL, group, 0)
    for block in range(512 // BLOCK):
        total = (mixed[block] + fresh_out[block]).astype(jnp.bfloat16)
        for h in range(GROUP):
            out[block * BLOCK : (block + 1) * BLOCK, h * HD : (h + 1) * HD] = total[
                h * BLOCK : (h + 1) * BLOCK
            ]


def call(kernel, inputs, out_shape, scratch, flops):
    return pl.pallas_call(
        kernel,
        out_shape=out_shape,
        grid_spec=pltpu.PrefetchScalarGridSpec(
            num_scalar_prefetch=1,
            grid=(),
            in_specs=[pl.BlockSpec(memory_space=pltpu.VMEM)] * inputs,
            out_specs=jax.tree.map(lambda _: pl.BlockSpec(memory_space=pltpu.VMEM), out_shape),
            scratch_shapes=[scratch],
        ),
        compiler_params=pltpu.CompilerParams(vmem_limit_bytes=24 * 1024 * 1024),
        cost_estimate=pl.CostEstimate(flops=flops, bytes_accessed=4 << 20, transcendentals=0),
    )


def on_device(
    queries,
    new_keys,
    new_values,
    hidden,
    row_counts,
    pack_of,
    cache_keys,
    cache_values,
    prefix_lengths,
    out_weight,
    norm_gain,
):
    count = lax.axis_size("tensor")
    me = lax.axis_index("tensor")
    core = jnp.bitwise_and(me, 1)
    place = lax.shift_right_logical(me, 1)
    f32 = jnp.float32
    bf16 = jnp.bfloat16

    def send(value, step):
        return lax.ppermute(value, "tensor", [(t, (t + 2 * step) % count) for t in range(count)])

    def swap(value):
        return lax.ppermute(value, "tensor", [(t, t ^ 1) for t in range(count)])

    position = lax.broadcasted_iota(jnp.int32, cache_keys.shape[1:], 1)
    marked = jnp.where(
        position < prefix_lengths[0][:, None, None], cache_keys[0], jnp.asarray(DEAD, bf16)
    )
    got_keys = lax.all_to_all(marked, "dp", split_axis=0, concat_axis=0, tiled=True)
    got_values = lax.all_to_all(cache_values[0], "dp", split_axis=0, concat_axis=0, tiled=True)

    order = [jnp.bitwise_and(place + ahead, 3) for ahead in (2, 1, 3, 0)]

    def columns(parity):
        return [
            lax.dynamic_slice_in_dim(out_weight, (2 * spot + parity) * 1024, 1024, 1)
            for spot in order
        ]

    theirs = swap(jnp.concatenate(columns(1 - core), axis=1))
    mats = [
        jnp.concatenate([mine, theirs[:, i * 1024 : (i + 1) * 1024]], axis=0)
        for i, mine in enumerate(columns(core))
    ]

    plan, row_start = pair_plan(row_counts[0], pack_of[0])
    front = ((FRESH - BLOCK, 0), (0, 0))
    blocks = 512 // BLOCK
    area = (blocks, GROUP * BLOCK, HD)
    weights, fresh_out = call(
        score_kernel,
        5,
        (jax.ShapeDtypeStruct(area, bf16), jax.ShapeDtypeStruct(area, f32)),
        pltpu.VMEM(area, f32),
        1 << 30,
    )(plan, queries, got_keys, jnp.pad(new_keys, front), jnp.pad(new_values, front), row_start)
    attended = call(
        mix_kernel,
        3,
        jax.ShapeDtypeStruct(queries.shape, bf16),
        pltpu.VMEM(area, f32),
        1 << 29,
    )(plan, weights, got_values, fresh_out)

    both = jnp.concatenate([attended, swap(attended)], axis=1)
    half_a, half_b = both[:256], both[256:]

    def part(rows, i):
        return jnp.dot(rows, mats[i], preferred_element_type=f32)

    far_a = send(part(half_a, 0).astype(bf16), -1)
    far_b = send(part(half_b, 0).astype(bf16), 1)
    near_up_a = send(part(half_a, 1).astype(bf16), 1)
    near_down_b = send(part(half_b, 2).astype(bf16), -1)
    near_down_a = send((part(half_a, 2) + far_a.astype(f32)).astype(bf16), -1)
    near_up_b = send((part(half_b, 1) + far_b.astype(f32)).astype(bf16), 1)
    delta = jnp.concatenate(
        [
            part(half_a, 3) + near_up_a.astype(f32) + near_down_a.astype(f32),
            part(half_b, 3) + near_up_b.astype(f32) + near_down_b.astype(f32),
        ],
        axis=0,
    )
    summed = hidden.astype(f32) + delta
    residual_out = summed.astype(bf16)
    squares = jnp.sum(summed * summed, axis=1)
    squares = squares + swap(squares)
    squares = squares + send(squares, 1) + send(squares, 2) + send(squares, 3)
    mean_square = squares / D
    normed = (summed * lax.rsqrt(mean_square + 1e-06)[:, None] * norm_gain[None, :]).astype(bf16)
    return (residual_out, normed)


def solution(mesh):
    return jax.shard_map(
        on_device,
        mesh=mesh,
        in_specs=(
            P("dp", "tensor"),
            P("dp", "tensor"),
            P("dp", "tensor"),
            P("dp", "tensor"),
            P("dp", None),
            P("dp", None),
            P("dp", None, None, "tensor"),
            P("dp", None, None, "tensor"),
            P("dp", None),
            P("tensor", None),
            P("tensor"),
        ),
        out_specs=(P("dp", "tensor"), P("dp", "tensor")),
        check_vma=False,
    )
```

time: 288 us -> 140 us (0.49)
  waiting for transfers between devices: 173 us -> 75.9 us
  local copies, waits for them, and re-layouts: 30.8 us -> 11.9 us
  matrix products: 20.6 us -> 5.77 us
  between operations: 14.3 us -> 0.99 us
  blocking collectives: 12.9 us -> 0 us
  Pallas kernels: 0 us -> 10.6 us
  other arithmetic: 15.9 us -> 7.4 us
  starting transfers between devices: 19.4 us -> 27.4 us
    all_to_all x2, waiting for transfers between devices: 120 us -> 35.8 us  [the longest x1 19.8 us: on_device(): lax.all_to_all(marked, 'dp', split_axis=0, concat_axis=0, tiled=True)]
    reduce_scatter x1 -> x0, waiting for transfers between devices: 53.3 us -> none  [on_device(): lax.psum_scatter(partial_value.astype(jnp.bfloat16), 'tensor', scatter_di...]
    ppermute x0 -> x12, waiting for transfers between devices: none -> 40 us  [the longest x9 37 us: send(): lax.ppermute(value, 'tensor', [(t, (t + 2 * step) % count) for t in range...]
    gather x4 -> x0, local copies, waits for them, and re-layouts: 24.5 us -> none  [the longest x3 21.9 us: take_rows(): return jnp.where(keep, source[index], jnp.zeros((), source.dtype))]
    dot_general x4 -> x8, matrix products: 20.6 us -> 5.77 us  [part(): return jnp.dot(rows, mats[i], preferred_element_type=f32)]
    psum x1 -> x0, blocking collectives: 12.9 us -> none  [on_device(): squares = lax.psum(jnp.sum(summed * summed, axis=1), 'tensor')]
    pallas_call x0 -> x2, Pallas kernels: none -> 10.6 us  [the longest x1 8.37 us: on_device(): call(score_kernel, 5, (jax.ShapeDtypeStruct(area, bf16), jax.ShapeDtypeSt...]
    ppermute x0 -> x12, starting transfers between devices: none -> 10.2 us  [the longest x9 9.97 us: send(): lax.ppermute(value, 'tensor', [(t, (t + 2 * step) % count) for t in range...]
  transfers between devices with their start and end apart: 3 -> 14, of which waited for: 3 -> 11; matrix products, arithmetic and copies ran while one was open for 0% -> 9% of each run, Pallas kernels for 0% -> 8%
where the time goes in v1:
time: 140 us
  waiting for transfers between devices  75.9 us (54%)
  starting transfers between devices  27.4 us (20%)
  local copies, waits for them, and re-layouts  11.9 us (8%)
  Pallas kernels  10.6 us (8%)
  other arithmetic  7.4 us (5%)
  matrix products  5.77 us (4%)
    ppermute x9, waiting for transfers between devices, send(): lax.ppermute(value, 'tensor', [(t, (t + 2 * step) % count) for t in range...  37 us
    all_to_all x1, waiting for transfers between devices, on_device(): lax.all_to_all(marked, 'dp', split_axis=0, concat_axis=0, tiled=True)  19.8 us
    all_to_all x1, waiting for transfers between devices, on_device(): lax.all_to_all(cache_values[0], 'dp', split_axis=0, concat_axis=0, tiled=...  16.1 us
    all_to_all x1, starting transfers between devices, on_device(): lax.all_to_all(marked, 'dp', split_axis=0, concat_axis=0, tiled=True)  11.6 us
    ppermute x9, starting transfers between devices, send(): lax.ppermute(value, 'tensor', [(t, (t + 2 * step) % count) for t in range...  9.97 us
    pallas_call x1, Pallas kernels, on_device(): call(score_kernel, 5, (jax.ShapeDtypeStruct(area, bf16), jax.ShapeDtypeSt...  8.37 us
    dynamic_slice x1, local copies, waits for them, and re-layouts, columns(): lax.dynamic_slice_in_dim(out_weight, (2 * spot + parity) * 1024, 1024, 1)  6.09 us
    dot_general x8, matrix products, part(): return jnp.dot(rows, mats[i], preferred_element_type=f32)  5.77 us
  transfers between devices with their start and end apart: 14, of which 11 were waited for; matrix products, arithmetic and copies ran while one was open for 9% of the time, Pallas kernels for 8%

profile of v1, /device:TPU:2, one launch (start us, length us, event | category | flops | bytes accessed | tf_op | source)
XLA Modules:
  0.0 139.9 jit_solution(18052365702067514020)
XLA Ops:
  0.6 2.6 %fusion = bf16[32,128,128]{2,1,0:T(8,128)(2,1)} fusion(bf16[1,32,128,128]{3,2,1,0:T(8,128)(2,1)} %param.17, s32[32]{0:T(128)} %bitcast.46), kind=kLoop, calls=%fused_computation.9 | loop fusion | flops 1048576 | bytes 2097280 | tf_op jit(solution)/shard_map/jit(_where)/select_n | solution.py:166
  3.2 11.6 %all-to-all-start = ((bf16[32,128,128]{2,1,0:T(8,128)(2,1)}), bf16[32,128,128]{2,1,0:T(8,128)(2,1)S(1)}, u32[]{:S(2)}, u32[]{:S(2)}) async-start(bf16[32,128,128]{2,1,0:T(8,128)(2,1)} %fusion), calls=%async_computation | async-start | bytes 2097152 | tf_op jit(solution)/shard_map/all_to_all | solution.py:169
  14.9 6.1 %constant_dynamic-slice_fusion.7 = (bf16[512,1024]{1,0:T(8,128)(2,1)}, bf16[512,1024]{1,0:T(8,128)(2,1)}, bf16[512,1024]{1,0:T(8,128)(2,1)S(1)}, bf16[512,1024]{...) fusion(bf16[512,8192]{1,0:T(8,128)(2,1)} %param.20, ...), kind=kLoop, calls=%fused_computation.52 | loop fusion | bytes 16777248 | tf_op jit(solution)/shard_map/dynamic_slice | solution.py:176
  21.0 2.1 %pad_maximum_fusion = bf16[512,4096]{1,0:T(8,128)(2,1)} fusion(bf16[512,1024]{1,0:T(8,128)(2,1)S(1)} %get-tuple-element.12, bf16[512,1024]{1,0:T(8,128)(2,1)S(1)} %get-tuple-element.13, bf16[512,1024]{1,0:T(8,128)(2,1)S(1)} %get-tuple-element.14, bf16[512,1024]{1,0:T(8,128)(2,1)S(1)} %get-tuple-element.15), kind=kLoop, calls=%fused_computation | loop fusion | flops 16777216 | bytes 8388608 | tf_op jit(solution)/shard_map/concatenate | solution.py:180
  23.2 19.8 %all-to-all-done.k = bf16[32,128,128]{2,1,0:T(8,128)(2,1)S(1)} async-done(((bf16[32,128,128]{2,1,0:T(8,128)(2,1)}), bf16[32,128,128]{2,1,0:T(8,128)(2,1)S(1)}, u32[]{:S(2)}, u32[]{:S(2)}) %all-to-all-start) | async-done | bytes 1048608 | tf_op jit(solution)/shard_map/all_to_all | solution.py:169
  42.9 5.6 %all-to-all-start.1 = ((bf16[32,128,128]{2,1,0:T(8,128)(2,1)}), bf16[32,128,128]{2,1,0:T(8,128)(2,1)S(1)}, u32[]{:S(2)}, u32[]{:S(2)}) async-start(bf16[32,128,128]{2,1,0:T(8,128)(2,1)} %bitcast.13), calls=%async_computation.1 | async-start | bytes 2097152 | tf_op jit(solution)/shard_map/all_to_all | solution.py:170
  49.2 1.0 copy-done.2
  50.3 8.4 %shard_map.122 = (bf16[16,128,128]{2,1,0:T(8,128)(2,1)S(1)}, f32[16,128,128]{2,1,0:T(8,128)S(1)}) custom-call(s32[4,48]{1,0:T(4,128)S(1)} %pad_add_fusion.plan, bf16[512,512]{1,0:T(8,128)(2,1)S(1)} %copy-done.2, bf16[32,128,128]{2,1,0:T(8,128)(2,1)S(1)} %all-to-all-done.k, bf16[608,128]{1,0:T(8,128)(2,1)S(1)} %pad.7.fresh_k, ...), custom_call_target="tpu_custom_call" | custom-call | flops 1073741824 | bytes 4194304 | tf_op jit(solution)/shard_map/pallas_call | solution.py:190
  58.6 0.8 copy-done
  59.4 16.1 %all-to-all-done.1.v = bf16[32,128,128]{2,1,0:T(8,128)(2,1)S(1)} async-done(((bf16[32,128,128]{2,1,0:T(8,128)(2,1)}), bf16[32,128,128]{2,1,0:T(8,128)(2,1)S(1)}, u32[]{:S(2)}, u32[]{:S(2)}) %all-to-all-start.1) | async-done | bytes 1048608 | tf_op jit(solution)/shard_map/all_to_all | solution.py:170
  75.5 1.0 copy-done.1
  76.5 2.2 %shard_map.123 = bf16[512,512]{1,0:T(8,128)(2,1)S(1)} custom-call(s32[4,48]{1,0:T(4,128)S(1)} %pad_add_fusion.plan, bf16[16,128,128]{2,1,0:T(8,128)(2,1)S(1)} %copy-done.1, bf16[32,128,128]{2,1,0:T(8,128)(2,1)S(1)} %all-to-all-done.1.v, f32[16,128,128]{2,1,0:T(8,128)S(1)} %get-tuple-element.5.fresh_out), custom_call_target="tpu_custom_call" | custom-call | flops 536870912 | bytes 4194304 | tf_op jit(solution)/shard_map/pallas_call | solution.py:197
  78.9 1.9 %collective-permute-done = bf16[512,512]{1,0:T(8,128)(2,1)S(1)} collective-permute-done((bf16[512,512]{1,0:T(8,128)(2,1)S(1)}, bf16[512,512]{1,0:T(8,128)(2,1)S(1)}, u32[]{:S(2)}, u32[]{:S(2)}) %collective-permute-start) | collective-permute-done | bytes 524320 | tf_op jit(solution)/shard_map/ppermute | solution.py:163
  80.9 2.7 %fusion.26 = (bf16[512,1024]{1,0:T(8,128)(2,1)S(1)}, bf16[512,1024]{1,0:T(8,128)(2,1)S(1)}, bf16[512,1024]{1,0:T(8,128)(2,1)S(1)}, bf16[512,1024]{1,0:T(8,128)(2,1)S(1)}) fusion(bf16[512,4096]{1,0:T(8,128)(2,1)} %collective-permute-done.1), kind=kLoop, calls=%fused_computation.79 | loop fusion | bytes 8388608 | tf_op jit(solution)/shard_map/slice | solution.py:182
  83.7 0.7 fusion.9
  84.4 3.1 %collective-permute-start.3 = (bf16[256,1024]{1,0:T(8,128)(2,1)S(1)}, bf16[256,1024]{1,0:T(8,128)(2,1)S(1)}, u32[]{:S(2)}, u32[]{:S(2)}) collective-permute-start(bf16[256,1024]{1,0:T(8,128)(2,1)S(1)} %fusion.9), channel_id=1, source_target_pairs={{0,6},{1,7},{2,0},{3,1},{4,2},{5,3},{6,4},{7,5},{8,14},{9,15},{10,... | collective-permute-start | bytes 1572872 | tf_op jit(solution)/shard_map/ppermute | solution.py:160
  88.3 0.7 fusion.10
  89.6 9.3 %collective-permute-done.3 = bf16[256,1024]{1,0:T(8,128)(2,1)S(1)} collective-permute-done((bf16[256,1024]{1,0:T(8,128)(2,1)S(1)}, bf16[256,1024]{1,0:T(8,128)(2,1)S(1)}, u32[]{:S(2)}, u32[]{:S(2)}) %collective-permute-start.3) | collective-permute-done | bytes 524320 | tf_op jit(solution)/shard_map/ppermute | solution.py:160
  99.0 0.7 fusion.11
  99.7 3.8 %collective-permute-start.4 = (bf16[256,1024]{1,0:T(8,128)(2,1)S(1)}, bf16[256,1024]{1,0:T(8,128)(2,1)S(1)}, u32[]{:S(2)}, u32[]{:S(2)}) collective-permute-start(bf16[256,1024]{1,0:T(8,128)(2,1)S(1)} %fusion.11), channel_id=1, source_target_pairs={{0,6},{1,7},{2,0},{3,1},{4,2},{5,3},{6,4},{7,5},{8,14},{9,15},{10,... | collective-permute-start | bytes 1572872 | tf_op jit(solution)/shard_map/ppermute | solution.py:160
  103.5 0.7 fusion.8
  104.5 9.9 %collective-permute-done.5 = bf16[256,1024]{1,0:T(8,128)(2,1)S(1)} collective-permute-done((bf16[256,1024]{1,0:T(8,128)(2,1)S(1)}, bf16[256,1024]{1,0:T(8,128)(2,1)S(1)}, u32[]{:S(2)}, u32[]{:S(2)}) %collective-permute-start.5) | collective-permute-done | bytes 524320 | tf_op jit(solution)/shard_map/ppermute | solution.py:160
  114.4 0.7 fusion.12
  115.8 0.8 fusion.2
  116.6 8.7 %collective-permute-done.7 = bf16[256,1024]{1,0:T(8,128)(2,1)S(1)} collective-permute-done((bf16[256,1024]{1,0:T(8,128)(2,1)S(1)}, bf16[256,1024]{1,0:T(8,128)(2,1)S(1)}, u32[]{:S(2)}, u32[]{:S(2)}) %collective-permute-start.7) | collective-permute-done | bytes 524320 | tf_op jit(solution)/shard_map/ppermute | solution.py:160
  125.3 3.9 %collective-permute-done.6 = bf16[256,1024]{1,0:T(8,128)(2,1)S(1)} collective-permute-done((bf16[256,1024]{1,0:T(8,128)(2,1)S(1)}, bf16[256,1024]{1,0:T(8,128)(2,1)S(1)}, u32[]{:S(2)}, u32[]{:S(2)}) %collective-permute-start.6) | collective-permute-done | bytes 524320 | tf_op jit(solution)/shard_map/ppermute | solution.py:160
  129.2 0.7 fusion.1
  130.5 1.1 collective-permute-done.8
  131.6 1.7 %collective-permute-start.11 = (f32[512]{0:T(512)S(1)}, f32[512]{0:T(512)S(1)}, u32[]{:S(2)}, u32[]{:S(2)}) collective-permute-start(f32[512]{0:T(512)S(1)} %add.174), channel_id=1, source_target_pairs={{0,6},{1,7},{2,0},{3,1},{4,2},{5,3},{6,4},{7,5},{8,14},{9,15},{10,... | collective-permute-start | bytes 6152 | tf_op jit(solution)/shard_map/ppermute | solution.py:160
  133.7 3.1 %collective-permute-done.10 = f32[512]{0:T(512)S(1)} collective-permute-done((f32[512]{0:T(512)S(1)}, f32[512]{0:T(512)S(1)}, u32[]{:S(2)}, u32[]{:S(2)}) %collective-permute-start.10) | collective-permute-done | bytes 2080 | tf_op jit(solution)/shard_map/ppermute | solution.py:160
  136.7 1.5 %collective-permute-done.9 = f32[512]{0:T(512)S(1)} collective-permute-done((f32[512]{0:T(512)S(1)}, f32[512]{0:T(512)S(1)}, u32[]{:S(2)}, u32[]{:S(2)}) %collective-permute-start.9) | collective-permute-done | bytes 2080 | tf_op jit(solution)/shard_map/ppermute | solution.py:160
  138.2 1.7 %multiply_convert_fusion = (bf16[512,1024]{1,0:T(8,128)(2,1)}, bf16[512,1024]{1,0:T(8,128)(2,1)}) fusion(f32[1024]{0:T(1024)S(1)} %copy-done.10, f32[512]{0:T(512)S(1)} %add_rsqrt_fusion, f32[256,1024]{1,0:T(8,128)S(1)} %fusion.1, f32[256,1024]{1,0:T(8,128)S(1)} %fusion.2, bf16[512,1024]{1,0:T(8,128)(2,1)S(1)} %copy-done.3), kind=kLoop, calls=%fused_computation.6 | loop fusion | flops 3670016 | bytes 5249024 | tf_op jit(solution)/shard_map/convert_element_type | solution.py:230
  (52 shorter events, 4.2 us)
Async XLA Ops:
  3.2 39.7 %all-to-all-start = ((bf16[32,128,128]{2,1,0:T(8,128)(2,1)}), bf16[32,128,128]{2,1,0:T(8,128)(2,1)S(1)}, u32[]{:S(2)}, u32[]{:S(2)}) async-start(bf16[32,128,128]{2,1,0:T(8,128)(2,1)} %fusion), calls=%async_computation | async-start | bytes 2097152 | tf_op jit(solution)/shard_map/all_to_all | solution.py:169
  23.0 25.4 %copy-start.8 = (bf16[512,128]{1,0:T(8,128)(2,1)S(1)}, bf16[512,128]{1,0:T(8,128)(2,1)}, u32[]{:S(2)}) copy-start(bf16[512,128]{1,0:T(8,128)(2,1)} %param.12) | copy-start | bytes 393220
  23.1 25.5 %copy-start.9 = (bf16[512,128]{1,0:T(8,128)(2,1)S(1)}, bf16[512,128]{1,0:T(8,128)(2,1)}, u32[]{:S(2)}) copy-start(bf16[512,128]{1,0:T(8,128)(2,1)} %param.13) | copy-start | bytes 393220
  23.1 25.5 %copy-start.12 = (s32[1,32]{1,0:T(1,128)S(1)}, s32[1,32]{1,0:T(1,128)}, u32[]{:S(2)}) copy-start(s32[1,32]{1,0:T(1,128)} %param.15) | copy-start | bytes 388
  23.1 25.8 %copy-start.11 = (s32[1,32]{1,0:T(1,128)S(1)}, s32[1,32]{1,0:T(1,128)}, u32[]{:S(2)}) copy-start(s32[1,32]{1,0:T(1,128)} %param.16) | copy-start | bytes 388
  23.1 57.9 %collective-permute-start.1 = (bf16[512,4096]{1,0:T(8,128)(2,1)}, bf16[512,4096]{1,0:T(8,128)(2,1)}, u32[]{:S(2)}, u32[]{:S(2)}) collective-permute-start(bf16[512,4096]{1,0:T(8,128)(2,1)} %pad_maximum_fusion), channel_id=1, source_target_pairs={{0,1},{1,0},{2,3},{3,2},{4,5},{5,4},{6,7},{7,6},{8,9},{9,8},{10,11... | collective-permute-start | bytes 12582920 | tf_op jit(solution)/shard_map/ppermute | solution.py:163
  42.9 32.6 %all-to-all-start.1 = ((bf16[32,128,128]{2,1,0:T(8,128)(2,1)}), bf16[32,128,128]{2,1,0:T(8,128)(2,1)S(1)}, u32[]{:S(2)}, u32[]{:S(2)}) async-start(bf16[32,128,128]{2,1,0:T(8,128)(2,1)} %bitcast.13), calls=%async_computation.1 | async-start | bytes 2097152 | tf_op jit(solution)/shard_map/all_to_all | solution.py:170
  49.2 1.0 copy-start.2
  58.6 0.8 copy-start
  75.5 1.0 copy-start.1
  78.8 2.0 %collective-permute-start = (bf16[512,512]{1,0:T(8,128)(2,1)S(1)}, bf16[512,512]{1,0:T(8,128)(2,1)S(1)}, u32[]{:S(2)}, u32[]{:S(2)}) collective-permute-start(bf16[512,512]{1,0:T(8,128)(2,1)S(1)} %shard_map.123), channel_id=1, source_target_pairs={{0,1},{1,0},{2,3},{3,2},{4,5},{5,4},{6,7},{7,6},{8,9},{9,8},{10,11... | collective-permute-start | bytes 1572872 | tf_op jit(solution)/shard_map/ppermute | solution.py:163
  80.9 2.7 %copy-start.7 = (bf16[512,1024]{1,0:T(8,128)(2,1)S(1)}, bf16[512,1024]{1,0:T(8,128)(2,1)}, u32[]{:S(2)}) copy-start(bf16[512,1024]{1,0:T(8,128)(2,1)} %get-tuple-element.10) | copy-start | bytes 3145732
  83.6 3.8 %copy-start.5 = (bf16[512,1024]{1,0:T(8,128)(2,1)S(1)}, bf16[512,1024]{1,0:T(8,128)(2,1)}, u32[]{:S(2)}) copy-start(bf16[512,1024]{1,0:T(8,128)(2,1)} %get-tuple-element.11) | copy-start | bytes 3145732
  84.4 14.6 %collective-permute-start.3 = (bf16[256,1024]{1,0:T(8,128)(2,1)S(1)}, bf16[256,1024]{1,0:T(8,128)(2,1)S(1)}, u32[]{:S(2)}, u32[]{:S(2)}) collective-permute-start(bf16[256,1024]{1,0:T(8,128)(2,1)S(1)} %fusion.9), channel_id=1, source_target_pairs={{0,6},{1,7},{2,0},{3,1},{4,2},{5,3},{6,4},{7,5},{8,14},{9,15},{10,... | collective-permute-start | bytes 1572872 | tf_op jit(solution)/shard_map/ppermute | solution.py:160
  88.2 27.0 %collective-permute-start.2 = (bf16[256,1024]{1,0:T(8,128)(2,1)S(1)}, bf16[256,1024]{1,0:T(8,128)(2,1)S(1)}, u32[]{:S(2)}, u32[]{:S(2)}) collective-permute-start(bf16[256,1024]{1,0:T(8,128)(2,1)S(1)} %fusion.7), channel_id=1, source_target_pairs={{0,2},{1,3},{2,4},{3,5},{4,6},{5,7},{6,0},{7,1},{8,10},{9,11},{10,... | collective-permute-start | bytes 1572872 | tf_op jit(solution)/shard_map/ppermute | solution.py:160
  88.3 10.7 %copy-start.6 = (bf16[512,1024]{1,0:T(8,128)(2,1)S(1)}, bf16[512,1024]{1,0:T(8,128)(2,1)}, u32[]{:S(2)}) copy-start(bf16[512,1024]{1,0:T(8,128)(2,1)} %get-tuple-element.17) | copy-start | bytes 3145732
  89.0 25.4 %collective-permute-start.5 = (bf16[256,1024]{1,0:T(8,128)(2,1)S(1)}, bf16[256,1024]{1,0:T(8,128)(2,1)S(1)}, u32[]{:S(2)}, u32[]{:S(2)}) collective-permute-start(bf16[256,1024]{1,0:T(8,128)(2,1)S(1)} %fusion.10), channel_id=1, source_target_pairs={{0,2},{1,3},{2,4},{3,5},{4,6},{5,7},{6,0},{7,1},{8,10},{9,11},{10,... | collective-permute-start | bytes 1572872 | tf_op jit(solution)/shard_map/ppermute | solution.py:160
  99.7 16.2 %collective-permute-start.4 = (bf16[256,1024]{1,0:T(8,128)(2,1)S(1)}, bf16[256,1024]{1,0:T(8,128)(2,1)S(1)}, u32[]{:S(2)}, u32[]{:S(2)}) collective-permute-start(bf16[256,1024]{1,0:T(8,128)(2,1)S(1)} %fusion.11), channel_id=1, source_target_pairs={{0,6},{1,7},{2,0},{3,1},{4,2},{5,3},{6,4},{7,5},{8,14},{9,15},{10,... | collective-permute-start | bytes 1572872 | tf_op jit(solution)/shard_map/ppermute | solution.py:160
  104.2 11.7 %copy-start.4 = (bf16[512,1024]{1,0:T(8,128)(2,1)S(1)}, bf16[512,1024]{1,0:T(8,128)(2,1)}, u32[]{:S(2)}) copy-start(bf16[512,1024]{1,0:T(8,128)(2,1)} %get-tuple-element.16) | copy-start | bytes 3145732
  104.2 21.2 %collective-permute-start.7 = (bf16[256,1024]{1,0:T(8,128)(2,1)S(1)}, bf16[256,1024]{1,0:T(8,128)(2,1)S(1)}, u32[]{:S(2)}, u32[]{:S(2)}) collective-permute-start(bf16[256,1024]{1,0:T(8,128)(2,1)S(1)} %fusion.8), channel_id=1, source_target_pairs={{0,6},{1,7},{2,0},{3,1},{4,2},{5,3},{6,4},{7,5},{8,14},{9,15},{10,... | collective-permute-start | bytes 1572872 | tf_op jit(solution)/shard_map/ppermute | solution.py:160
  115.1 14.1 %collective-permute-start.6 = (bf16[256,1024]{1,0:T(8,128)(2,1)S(1)}, bf16[256,1024]{1,0:T(8,128)(2,1)S(1)}, u32[]{:S(2)}, u32[]{:S(2)}) collective-permute-start(bf16[256,1024]{1,0:T(8,128)(2,1)S(1)} %fusion.12), channel_id=1, source_target_pairs={{0,2},{1,3},{2,4},{3,5},{4,6},{5,7},{6,0},{7,1},{8,10},{9,11},{10,... | collective-permute-start | bytes 1572872 | tf_op jit(solution)/shard_map/ppermute | solution.py:160
  116.6 13.4 %copy-start.3 = (bf16[512,1024]{1,0:T(8,128)(2,1)S(1)}, bf16[512,1024]{1,0:T(8,128)(2,1)}, u32[]{:S(2)}) copy-start(bf16[512,1024]{1,0:T(8,128)(2,1)} %param.14) | copy-start | bytes 3145732
  130.0 8.2 %copy-start.10 = (f32[1024]{0:T(1024)S(1)}, f32[1024]{0:T(1024)}, u32[]{:S(2)}) copy-start(f32[1024]{0:T(1024)} %param.21) | copy-start | bytes 12292
  130.4 1.2 collective-permute-start.8
  131.6 5.1 %collective-permute-start.10 = (f32[512]{0:T(512)S(1)}, f32[512]{0:T(512)S(1)}, u32[]{:S(2)}, u32[]{:S(2)}) collective-permute-start(f32[512]{0:T(512)S(1)} %add.174), channel_id=1, source_target_pairs={{0,4},{1,5},{2,6},{3,7},{4,0},{5,1},{6,2},{7,3},{8,12},{9,13},{10,... | collective-permute-start | bytes 6152 | tf_op jit(solution)/shard_map/ppermute | solution.py:160
  131.6 5.1 %collective-permute-start.11 = (f32[512]{0:T(512)S(1)}, f32[512]{0:T(512)S(1)}, u32[]{:S(2)}, u32[]{:S(2)}) collective-permute-start(f32[512]{0:T(512)S(1)} %add.174), channel_id=1, source_target_pairs={{0,6},{1,7},{2,0},{3,1},{4,2},{5,3},{6,4},{7,5},{8,14},{9,15},{10,... | collective-permute-start | bytes 6152 | tf_op jit(solution)/shard_map/ppermute | solution.py:160
  133.4 4.8 %collective-permute-start.9 = (f32[512]{0:T(512)S(1)}, f32[512]{0:T(512)S(1)}, u32[]{:S(2)}, u32[]{:S(2)}) collective-permute-start(f32[512]{0:T(512)S(1)} %add.174), channel_id=1, source_target_pairs={{0,2},{1,3},{2,4},{3,5},{4,6},{5,7},{6,0},{7,1},{8,10},{9,11},{10,... | collective-permute-start | bytes 6152 | tf_op jit(solution)/shard_map/ppermute | solution.py:160

commit v2 on v1

v2 whole, which is shorter than its diff:
```python
import math

import jax
import jax.numpy as jnp
from jax import lax
from jax.experimental import pallas as pl
from jax.experimental.pallas import tpu as pltpu
from jax.sharding import PartitionSpec as P

D = 8192
HEADS = 32
KV_HEADS = 8
HD = 128
MOST = 64
GROUP = HEADS // KV_HEADS
BLOCK = 32
FRESH = 128
PAIRS = 48
CHUNKS = 4
UNROLL = 8
LOW = -1e30
DEAD = 8192.0
SCALE = 1.0 / math.sqrt(HD)
NT = (((1,), (1,)), ((), ()))


def pair_plan(counts, packs):
    roll = counts.shape[0]
    ids = jnp.arange(roll, dtype=jnp.int32)
    before = ids[None, :] < ids[:, None]
    starts = jnp.sum(jnp.where(before, counts[None, :], 0), axis=1)
    ends = starts + counts
    first = starts // BLOCK
    spans = (ends - 1) // BLOCK - first + 1
    offsets = jnp.sum(jnp.where(before, spans[None, :], 0), axis=1)
    slot = jnp.arange(PAIRS, dtype=jnp.int32)[:, None]
    hit = (slot >= offsets[None, :]) & (slot < (offsets + spans)[None, :])

    def pick(values):
        return jnp.sum(jnp.where(hit, values, 0), axis=1)

    block = pick(first[None, :] + slot - offsets[None, :])
    plan = jnp.stack(
        [block, pick(packs[None, :]), pick(starts[None, :]), pick(ends[None, :])]
    ).astype(jnp.int32)
    rows = jnp.arange(512, dtype=jnp.int32)[:, None]
    row_start = jnp.max(jnp.where(starts[None, :] <= rows, starts[None, :], 0), axis=1)
    return plan, jnp.broadcast_to(row_start[:, None], (512, HD))


def stack_heads(ref, base):
    return [ref[pl.ds(base, BLOCK), h * HD : (h + 1) * HD] for h in range(GROUP)]


def payload_kernel(lengths, keys, values, out, held, sems):
    packs, prefix, _ = keys.shape
    tile = packs // CHUNKS

    def copies(c):
        part = pl.ds(c * tile, tile)
        front, back = held.at[part, pl.ds(0, prefix)], held.at[part, pl.ds(prefix, prefix)]
        return (
            pltpu.make_async_copy(keys.at[part], front, sems.at[0, c]),
            pltpu.make_async_copy(values.at[part], back, sems.at[1, c]),
            pltpu.make_async_copy(held.at[part], out.at[part], sems.at[2, c]),
        )

    steps = [copies(c) for c in range(CHUNKS)]
    for step in steps:
        step[0].start()
        step[1].start()
    position = lax.broadcasted_iota(jnp.int32, keys.shape[1:], 0)
    for c, step in enumerate(steps):
        step[0].wait()
        for u in range(tile):
            pack = c * tile + u
            found = held[pack, :prefix].astype(jnp.float32)
            marked = jnp.where(position < lengths[pack], found, DEAD)
            held[pack, :prefix] = marked.astype(jnp.bfloat16)
        step[1].wait()
        step[2].start()
    for step in steps:
        step[2].wait()


def fresh_kernel(q, fresh_k, fresh_v, row_start, mean_out, level_out):
    def body(block, carry):
        base = pl.multiple_of(block * BLOCK, BLOCK)
        left = jnp.concatenate(stack_heads(q, base), axis=0)
        window = pl.ds(base, FRESH)
        found = lax.dot_general(left, fresh_k[window, :], NT, preferred_element_type=jnp.float32)
        key = base - (FRESH - BLOCK) + lax.broadcasted_iota(jnp.int32, found.shape, 1)
        sub = lax.broadcasted_iota(jnp.int32, found.shape, 0)
        row = base + jnp.bitwise_and(sub, BLOCK - 1)
        start = jnp.concatenate([row_start[pl.ds(base, BLOCK), :]] * GROUP, axis=0)
        found = jnp.where((key <= row) & (key >= start), found * SCALE, LOW)
        top = jnp.max(found, axis=1, keepdims=True)
        lifted = jnp.exp(found - top)
        total = jnp.sum(lifted, axis=1, keepdims=True)
        mean_out[block] = jnp.dot(
            (lifted / total).astype(jnp.bfloat16),
            fresh_v[window, :],
            preferred_element_type=jnp.float32,
        )
        level_out[block] = jnp.broadcast_to(top + jnp.log(total), found.shape)
        return carry

    lax.fori_loop(0, 512 // BLOCK, body, 0, unroll=2)


def main_kernel(
    plan, q, cache_hbm, mean_hbm, level_hbm, out_a, out_b, cache, means, levels, scores, weights, mixed, sems
):
    half = cache.shape[1] // 2
    fetch = [
        pltpu.make_async_copy(
            cache_hbm.at[:, pl.ds(i * half, half)], cache.at[:, pl.ds(i * half, half)], sems.at[i]
        )
        for i in range(2)
    ]
    fetch.append(pltpu.make_async_copy(level_hbm, levels, sems.at[2]))
    fetch.append(pltpu.make_async_copy(mean_hbm, means, sems.at[3]))
    for i in (0, 2, 3, 1):
        fetch[i].start()
    ones = jnp.ones((16, HD), jnp.bfloat16)
    prefix = cache.shape[1] // 2

    def own_rows(base, i):
        row = base + lax.broadcasted_iota(jnp.int32, (BLOCK, HD), 0)
        return (row >= plan[2, i]) & (row < plan[3, i])

    def score(step, carry):
        for u in range(UNROLL):
            i = step * UNROLL + u
            block = plan[0, i]
            base = pl.multiple_of(block * BLOCK, BLOCK)
            left = jnp.concatenate(stack_heads(q, base) + [ones], axis=0)
            both = lax.dot_general(
                left, cache[plan[1, i], :prefix], NT, preferred_element_type=jnp.float32
            )
            live = both[GROUP * BLOCK : GROUP * BLOCK + 1] < 32.0 * DEAD
            found = jnp.where(live, both[: GROUP * BLOCK] * SCALE, LOW)
            mine = own_rows(base, i)
            for h in range(GROUP):
                part = pl.ds(h * BLOCK, BLOCK)
                scores[block, part] = jnp.where(
                    mine, found[h * BLOCK : (h + 1) * BLOCK], scores[block, part]
                )
        return carry

    def soften(block, carry):
        cached = scores[block]
        level = levels[block]
        top = jnp.maximum(jnp.max(cached, axis=1, keepdims=True), level)
        lifted = jnp.exp(cached - top)
        fresh = jnp.exp(level - top)
        share = 1.0 / (jnp.sum(lifted, axis=1, keepdims=True) + fresh)
        weights[block] = (lifted * share).astype(jnp.bfloat16)
        mixed[block] = means[block] * (fresh * share)
        return carry

    def mix(step, carry):
        for u in range(UNROLL):
            i = step * UNROLL + u
            block = plan[0, i]
            found = jnp.dot(
                weights[block], cache[plan[1, i], prefix:], preferred_element_type=jnp.float32
            )
            mine = own_rows(block * BLOCK, i)
            for h in range(GROUP):
                part = pl.ds(h * BLOCK, BLOCK)
                mixed[block, part] += jnp.where(mine, found[h * BLOCK : (h + 1) * BLOCK], 0.0)
        return carry

    fetch[0].wait()
    lax.fori_loop(0, PAIRS // UNROLL, score, 0)
    fetch[2].wait()
    fetch[3].wait()
    lax.fori_loop(0, 512 // BLOCK, soften, 0, unroll=8)
    fetch[1].wait()
    lax.fori_loop(0, PAIRS // UNROLL, mix, 0)
    for block in range(512 // BLOCK):
        total = mixed[block].astype(jnp.bfloat16)
        out = out_a if block < 8 else out_b
        base = (block % 8) * BLOCK
        for h in range(GROUP):
            out[base : base + BLOCK, h * HD : (h + 1) * HD] = total[h * BLOCK : (h + 1) * BLOCK]


def whole(count):
    return [pl.BlockSpec(memory_space=pltpu.VMEM)] * count


def in_hbm(*values):
    return [pltpu.with_memory_space_constraint(value, pltpu.HBM) for value in values]


def far(count):
    return [pl.BlockSpec(memory_space=pltpu.HBM)] * count


def anywhere(count):
    return [pl.BlockSpec(memory_space=pl.ANY)] * count


def make_payload(lengths, keys, values):
    packs, prefix, width = keys.shape
    return pl.pallas_call(
        payload_kernel,
        out_shape=jax.ShapeDtypeStruct((packs, 2 * prefix, width), keys.dtype),
        grid_spec=pltpu.PrefetchScalarGridSpec(
            num_scalar_prefetch=1,
            grid=(),
            in_specs=far(2),
            out_specs=far(1)[0],
            scratch_shapes=[
                pltpu.VMEM((packs, 2 * prefix, width), keys.dtype),
                pltpu.SemaphoreType.DMA((3, CHUNKS)),
            ],
        ),
        compiler_params=pltpu.CompilerParams(vmem_limit_bytes=4 << 20),
        cost_estimate=pl.CostEstimate(flops=1 << 20, bytes_accessed=4 << 20, transcendentals=0),
    )(lengths, *in_hbm(keys, values))


def cut_kernel(starts, weight, after, *refs):
    outs, held, sems = refs[:-2], refs[-2], refs[-1]
    fetch, store = [], []
    for out in outs:
        for i in range(out.shape[1] // 512):
            slot = len(fetch)
            start = pl.multiple_of(starts[slot], 512)
            source = weight.at[:, pl.ds(start, 512)]
            target = out.at[:, pl.ds(i * 512, 512)]
            fetch.append(pltpu.make_async_copy(source, held.at[slot], sems.at[0, slot]))
            store.append(pltpu.make_async_copy(held.at[slot], target, sems.at[1, slot]))
    for copy in fetch:
        copy.start()
    for first, second in zip(fetch, store):
        first.wait()
        second.start()
    for copy in store:
        copy.wait()


def cut(starts, weight, widths, after):
    rows = weight.shape[0]
    count = sum(widths) // 512
    return pl.pallas_call(
        cut_kernel,
        out_shape=tuple(jax.ShapeDtypeStruct((rows, width), weight.dtype) for width in widths),
        grid_spec=pltpu.PrefetchScalarGridSpec(
            num_scalar_prefetch=1,
            grid=(),
            in_specs=far(1) + anywhere(1),
            out_specs=tuple(far(len(widths))),
            scratch_shapes=[
                pltpu.VMEM((count, rows, 512), weight.dtype),
                pltpu.SemaphoreType.DMA((2, count)),
            ],
        ),
        compiler_params=pltpu.CompilerParams(vmem_limit_bytes=8 << 20),
        cost_estimate=pl.CostEstimate(flops=0, bytes_accessed=12 << 20, transcendentals=0),
    )(starts, *in_hbm(weight), after)


def attend_fresh(queries, new_keys, new_values, row_start):
    front = ((FRESH - BLOCK, 0), (0, 0))
    area = jax.ShapeDtypeStruct((512 // BLOCK, GROUP * BLOCK, HD), jnp.float32)
    return pl.pallas_call(
        fresh_kernel,
        out_shape=(area, area),
        in_specs=whole(4),
        out_specs=tuple(whole(2)),
        compiler_params=pltpu.CompilerParams(vmem_limit_bytes=5 << 20),
        cost_estimate=pl.CostEstimate(
            flops=1 << 31, bytes_accessed=4 << 20, transcendentals=1 << 18
        ),
    )(queries, jnp.pad(new_keys, front), jnp.pad(new_values, front), row_start)


def attend(plan, queries, cache, fresh_mean, fresh_level):
    area = fresh_mean.shape
    half = jax.ShapeDtypeStruct((256, queries.shape[1]), queries.dtype)
    return pl.pallas_call(
        main_kernel,
        out_shape=(half, half),
        grid_spec=pltpu.PrefetchScalarGridSpec(
            num_scalar_prefetch=1,
            grid=(),
            in_specs=whole(1) + anywhere(3),
            out_specs=tuple(whole(2)),
            scratch_shapes=[
                pltpu.VMEM(cache.shape, cache.dtype),
                pltpu.VMEM(area, jnp.float32),
                pltpu.VMEM(area, jnp.float32),
                pltpu.VMEM(area, jnp.float32),
                pltpu.VMEM(area, jnp.bfloat16),
                pltpu.VMEM(area, jnp.float32),
                pltpu.SemaphoreType.DMA((4,)),
            ],
        ),
        compiler_params=pltpu.CompilerParams(vmem_limit_bytes=10 << 20),
        cost_estimate=pl.CostEstimate(
            flops=1 << 31, bytes_accessed=4 << 20, transcendentals=1 << 18
        ),
    )(plan, queries, cache, fresh_mean, fresh_level)


def attention(counts, packs, queries, marked, values, new_keys, new_values):
    plan, row_start = pair_plan(counts, packs)
    fresh = attend_fresh(queries, new_keys, new_values, row_start)
    cache = jnp.concatenate([marked, values], axis=1)
    return jnp.concatenate(attend(plan, queries, cache, *fresh), axis=0)


def on_device(
    queries,
    new_keys,
    new_values,
    hidden,
    row_counts,
    pack_of,
    cache_keys,
    cache_values,
    prefix_lengths,
    out_weight,
    norm_gain,
):
    count = lax.axis_size("tensor")
    me = lax.axis_index("tensor")
    f32 = jnp.float32
    bf16 = jnp.bfloat16

    def swap(value, mask):
        return lax.ppermute(value, "tensor", [(t, t ^ mask) for t in range(count)])

    def shared(mask):
        to = jnp.bitwise_xor(me, mask)
        first = [to * 1024, jnp.bitwise_xor(to, 6) * 1024]
        second = [to * 1024 + 512, jnp.bitwise_xor(to, 2) * 1024 + 512]
        return first, second

    payload = make_payload(prefix_lengths[0], cache_keys[0], cache_values[0])
    cache = lax.all_to_all(payload, "dp", split_axis=0, concat_axis=0, tiled=True)

    starts = sum([shared(mask)[half] for mask, half in ((2, 0), (6, 1), (3, 0), (7, 1))], [])
    starts = jnp.stack(starts + sum(shared(1), []))
    pieces = cut(starts, out_weight, (1024, 1024, 1024, 1024, 2048), payload)
    starts, pieces = lax.optimization_barrier((jnp.stack(sum(shared(0), [])), pieces))
    arrived = [swap(piece, mask) for piece, mask in zip(pieces, (2, 6, 3, 7, 1))]
    sibling = arrived[4]
    mine = cut(starts, out_weight, (1024, 1024), payload)
    mats = [
        [mine[0], sibling[:, :1024], arrived[0], arrived[2]],
        [mine[1], sibling[:, 1024:], arrived[1], arrived[3]],
    ]

    plan, row_start = pair_plan(row_counts[0], pack_of[0])
    fresh = attend_fresh(queries, new_keys, new_values, row_start)
    plan, mats = lax.optimization_barrier((plan, mats))
    attended = attend(plan, queries, cache, *fresh)

    near = [[swap(rows, mask) for mask in (2, 6)] for rows in attended]
    others = [swap(rows, 1) for rows in attended]
    own = []
    got = []
    sent = []
    for rows, other, close in zip(attended, others, near):
        close, sent = lax.optimization_barrier((close, sent))
        totals = [
            sum(
                jnp.dot(part, mat, preferred_element_type=f32)
                for part, mat in zip((rows, other, arrival, swap(arrival, 1)), mats[half])
            )
            for half, arrival in enumerate(close)
        ]
        own.append([total[:, :512] for total in totals])
        sent = [total[:, 512:].astype(bf16) for total in totals]
        got.append([swap(part, mask) for part, mask in zip(sent, (6, 2))])

    delta = jnp.concatenate(
        [
            jnp.concatenate([a + b.astype(f32) for a, b in zip(*pair)], axis=1)
            for pair in zip(own, got)
        ],
        axis=0,
    )
    summed = hidden.astype(f32) + delta
    residual_out = summed.astype(bf16)
    squares = jnp.sum(summed * summed, axis=1)
    squares = squares + swap(squares, 1)
    squares = squares + swap(squares, 4) + swap(squares, 2) + swap(squares, 6)
    mean_square = squares / D
    normed = (summed * lax.rsqrt(mean_square + 1e-06)[:, None] * norm_gain[None, :]).astype(bf16)
    return (residual_out, normed)


def solution(mesh):
    return jax.shard_map(
        on_device,
        mesh=mesh,
        in_specs=(
            P("dp", "tensor"),
            P("dp", "tensor"),
            P("dp", "tensor"),
            P("dp", "tensor"),
            P("dp", None),
            P("dp", None),
            P("dp", None, None, "tensor"),
            P("dp", None, None, "tensor"),
            P("dp", None),
            P("tensor", None),
            P("tensor"),
        ),
        out_specs=(P("dp", "tensor"), P("dp", "tensor")),
        check_vma=False,
    )
```

time: 140 us -> 126 us (0.900)
  waiting for transfers between devices: 75.9 us -> 51.2 us
  Pallas kernels: 10.6 us -> 21.5 us
  starting transfers between devices: 27.4 us -> 32.5 us
  other arithmetic: 7.4 us -> 2.89 us
  local copies, waits for them, and re-layouts: 11.9 us -> 9.07 us
    all_to_all x2 -> x1, waiting for transfers between devices: 35.8 us -> 0.01 us  [on_device(): lax.all_to_all(payload, 'dp', split_axis=0, concat_axis=0, tiled=True)]
    ppermute x12 -> x23, waiting for transfers between devices: 40 us -> 51.2 us  [swap(): return lax.ppermute(value, 'tensor', [(t, t ^ mask) for t in range(count)])]
    pallas_call x2 -> x5, Pallas kernels: 10.6 us -> 21.5 us  [the longest x1 6.43 us: attend(): pl.pallas_call(main_kernel, out_shape=(half, half), grid_spec=pltpu.Prefe...]
    ppermute x12 -> x23, starting transfers between devices: 10.2 us -> 20.8 us  [swap(): return lax.ppermute(value, 'tensor', [(t, t ^ mask) for t in range(count)])]
    dynamic_slice x1 -> x0, local copies, waits for them, and re-layouts: 6.09 us -> none  [columns(): lax.dynamic_slice_in_dim(out_weight, (2 * spot + parity) * 1024, 1024, 1)]
    all_to_all x2 -> x1, starting transfers between devices: 17.2 us -> 11.7 us  [on_device(): lax.all_to_all(payload, 'dp', split_axis=0, concat_axis=0, tiled=True)]
    unnamed x26 -> x44, local copies, waits for them, and re-layouts: 2.92 us -> 7.15 us
    select_n x1 -> x0, other arithmetic: 2.6 us -> none  [on_device(): jnp.where(position < prefix_lengths[0][:, None, None], cache_keys[0], jnp...]
  transfers between devices with their start and end apart: 14 -> 24, of which waited for: 11 -> 13; matrix products, arithmetic and copies ran while one was open for 9% -> 8% of each run, Pallas kernels for 8% -> 10%
where the time goes in v2:
time: 126 us; the launch traced here: 125 us
  waiting for transfers between devices  51.2 us (41%)
  starting transfers between devices  32.5 us (26%)
  Pallas kernels  21.5 us (17%)
  local copies, waits for them, and re-layouts  9.07 us (7%)
  matrix products  7.08 us (6%)
  other arithmetic  2.89 us (2%)
    ppermute x23, waiting for transfers between devices, swap(): return lax.ppermute(value, 'tensor', [(t, t ^ mask) for t in range(count)])  51.2 us
    ppermute x23, starting transfers between devices, swap(): return lax.ppermute(value, 'tensor', [(t, t ^ mask) for t in range(count)])  20.8 us
    all_to_all x1, starting transfers between devices, on_device(): lax.all_to_all(payload, 'dp', split_axis=0, concat_axis=0, tiled=True)  11.7 us
    unnamed x44, local copies, waits for them, and re-layouts  7.15 us
    dot_general x16, matrix products, on_device(): jnp.dot(part, mat, preferred_element_type=f32)  7.08 us
    pallas_call x1, Pallas kernels, attend(): pl.pallas_call(main_kernel, out_shape=(half, half), grid_spec=pltpu.Prefe...  6.43 us
    pallas_call x1, Pallas kernels, attend_fresh(): pl.pallas_call(fresh_kernel, out_shape=(area, area), in_specs=whole(4), o...  6.16 us
    pallas_call x2, Pallas kernels, cut(): pl.pallas_call(cut_kernel, out_shape=tuple((jax.ShapeDtypeStruct((rows, w...  5.89 us
  transfers between devices with their start and end apart: 24, of which 13 were waited for; matrix products, arithmetic and copies ran while one was open for 8% of the time, Pallas kernels for 10%

profile of v2, /device:TPU:2, one launch (start us, length us, event | category | flops | bytes accessed | tf_op | source)
XLA Modules:
  0.0 125.5 jit_solution(12766582734074785327)
XLA Ops:
  1.3 3.0 %shard_map.122.after = bf16[32,256,128]{2,1,0:T(8,128)(2,1)} custom-call(s32[32]{0:T(128)S(1)} %bitcast.81, bf16[32,128,128]{2,1,0:T(8,128)(2,1)} %bitcast.82, bf16[32,128,128]{2,1,0:T(8,128)(2,1)} %bitcast.83), custom_call_target="tpu_custom_call" | custom-call | flops 1048576 | bytes 4194304 | tf_op jit(solution)/shard_map/pallas_call | solution.py:208
  4.3 11.7 %all-to-all-start = ((bf16[32,256,128]{2,1,0:T(8,128)(2,1)}), bf16[32,256,128]{2,1,0:T(8,128)(2,1)}, u32[]{:S(2)}, u32[]{:S(2)}) async-start(bf16[32,256,128]{2,1,0:T(8,128)(2,1)} %shard_map.122.after), calls=%async_computation | async-start | bytes 4194304 | tf_op jit(solution)/shard_map/all_to_all | solution.py:345
  16.1 3.7 %shard_map.123 = (bf16[512,1024]{1,0:T(8,128)(2,1)S(1)}, bf16[512,1024]{1,0:T(8,128)(2,1)S(1)}, bf16[512,1024]{1,0:T(8,128)(2,1)S(1)}, bf16[512,1024]{1,0:T(8,128)(2,1)S(1)}, bf16[512,2048]{1,0:T(8,128)(2,1)S(1)}) custom-call(s32[12]{0:T(128)S(1)} %stack.91.starts, bf16[512,8192]{1,0:T(8,128)(2,1)} %weight.3, bf16[32,256,128]{2,1,0:T(8,128)(2,1)} %shard_map.122.after), custom_call_target="tpu_custom_call" | custom-call | bytes 12582912 | tf_op jit(solution)/shard_map/pallas_call | solution.py:249
  20.0 1.7 %collective-permute-start.1 = (bf16[512,1024]{1,0:T(8,128)(2,1)S(1)}, bf16[512,1024]{1,0:T(8,128)(2,1)S(1)}, u32[]{:S(2)}, u32[]{:S(2)}) collective-permute-start(bf16[512,1024]{1,0:T(8,128)(2,1)S(1)} %get-tuple-element.40), channel_id=1, source_target_pairs={{0,2},{1,3},{2,0},{3,1},{4,6},{5,7},{6,4},{7,5},{8,10},{9,11},{10,... | collective-permute-start | bytes 3145736 | tf_op jit(solution)/shard_map/ppermute | solution.py:336
  21.8 3.0 %collective-permute-start.3 = (bf16[512,1024]{1,0:T(8,128)(2,1)S(1)}, bf16[512,1024]{1,0:T(8,128)(2,1)S(1)}, u32[]{:S(2)}, u32[]{:S(2)}) collective-permute-start(bf16[512,1024]{1,0:T(8,128)(2,1)S(1)} %get-tuple-element.43), channel_id=1, source_target_pairs={{0,6},{1,7},{2,4},{3,5},{4,2},{5,3},{6,0},{7,1},{8,14},{9,15},{10,... | collective-permute-start | bytes 3145736 | tf_op jit(solution)/shard_map/ppermute | solution.py:336
  24.9 2.2 %shard_map.124 = (bf16[512,1024]{1,0:T(8,128)(2,1)S(1)}, bf16[512,1024]{1,0:T(8,128)(2,1)S(1)}) custom-call(s32[4]{0:T(128)S(1)} %pad_add_fusion.1.starts, bf16[512,8192]{1,0:T(8,128)(2,1)} %weight.3, bf16[32,256,128]{2,1,0:T(8,128)(2,1)} %shard_map.122.after), custom_call_target="tpu_custom_call" | custom-call | bytes 12582912 | tf_op jit(solution)/shard_map/pallas_call | solution.py:249
  27.8 6.2 %shard_map.125 = (f32[16,128,128]{2,1,0:T(8,128)S(1)}, f32[16,128,128]{2,1,0:T(8,128)S(1)}) custom-call(bf16[512,512]{1,0:T(8,128)(2,1)S(1)} %copy-done.1, bf16[608,128]{1,0:T(8,128)(2,1)S(1)} %pad.7.fresh_k, bf16[608,128]{1,0:T(8,128)(2,1)S(1)} %pad.8.fresh_v, s32[512,128]{1,0:T(8,128)S(1)} %broadcast_in_dim.95.row_start), custom_call_target="tpu_custom_call" | custom-call | flops 2147483648 | bytes 4194304 | tf_op jit(solution)/shard_map/pallas_call | solution.py:270
  34.0 1.0 copy-done.2
  35.0 1.0 copy-done.4
  35.9 1.5 %fusion.12 = (bf16[512,1024]{1,0:T(8,128)(2,1)}, bf16[512,1024]{1,0:T(8,128)(2,1)}) fusion(bf16[512,2048]{1,0:T(8,128)(2,1)S(1)} %collective-permute-done), kind=kLoop, calls=%fused_computation.57 | loop fusion | bytes 4194304 | tf_op jit(solution)/shard_map/slice | solution.py:356
  37.5 8.5 %collective-permute-done.1 = bf16[512,1024]{1,0:T(8,128)(2,1)S(1)} collective-permute-done((bf16[512,1024]{1,0:T(8,128)(2,1)S(1)}, bf16[512,1024]{1,0:T(8,128)(2,1)S(1)}, u32[]{:S(2)}, u32[]{:S(2)}) %collective-permute-start.1) | collective-permute-done | bytes 1048608 | tf_op jit(solution)/shard_map/ppermute | solution.py:336
  46.0 21.5 %collective-permute-done.2 = bf16[512,1024]{1,0:T(8,128)(2,1)S(1)} collective-permute-done((bf16[512,1024]{1,0:T(8,128)(2,1)S(1)}, bf16[512,1024]{1,0:T(8,128)(2,1)S(1)}, u32[]{:S(2)}, u32[]{:S(2)}) %collective-permute-start.2) | collective-permute-done | bytes 1048608 | tf_op jit(solution)/shard_map/ppermute | solution.py:336
  67.5 3.0 %collective-permute-done.4 = bf16[512,1024]{1,0:T(8,128)(2,1)S(1)} collective-permute-done((bf16[512,1024]{1,0:T(8,128)(2,1)S(1)}, bf16[512,1024]{1,0:T(8,128)(2,1)S(1)}, u32[]{:S(2)}, u32[]{:S(2)}) %collective-permute-start.4) | collective-permute-done | bytes 1048608 | tf_op jit(solution)/shard_map/ppermute | solution.py:336
  70.5 1.1 copy-done.12
  71.6 1.2 copy-done.3
  72.8 1.2 copy-done.5
  74.0 6.4 %shard_map.126 = (bf16[256,512]{1,0:T(8,128)(2,1)S(1)}, bf16[256,512]{1,0:T(8,128)(2,1)S(1)}) custom-call(s32[4,48]{1,0:T(4,128)S(1)} %pad_add_fusion.plan, bf16[512,512]{1,0:T(8,128)(2,1)S(1)} %copy-done.1, bf16[32,256,128]{2,1,0:T(8,128)(2,1)} %all-to-all-done.cache_hbm, f32[16,128,128]{2,1,0:T(8,128)S(1)} %copy-done.3, f32[16,128,128]{2,1,0:T(8,128)S(1)} %copy-done.5), custom_call_target="tpu_custom_call" | custom-call | flops 2147483648 | bytes 4194304 | tf_op jit(solution)/shard_map/pallas_call | solution.py:285
  80.8 2.7 %collective-permute-start.7 = (bf16[256,512]{1,0:T(8,128)(2,1)S(1)}, bf16[256,512]{1,0:T(8,128)(2,1)S(1)}, u32[]{:S(2)}, u32[]{:S(2)}) collective-permute-start(bf16[256,512]{1,0:T(8,128)(2,1)S(1)} %get-tuple-element.48), channel_id=1, source_target_pairs={{0,6},{1,7},{2,4},{3,5},{4,2},{5,3},{6,0},{7,1},{8,14},{9,15},{10,... | collective-permute-start | bytes 786440 | tf_op jit(solution)/shard_map/ppermute | solution.py:336
  83.5 1.3 %collective-permute-start.13 = (bf16[256,512]{1,0:T(8,128)(2,1)S(1)}, bf16[256,512]{1,0:T(8,128)(2,1)S(1)}, u32[]{:S(2)}, u32[]{:S(2)}) collective-permute-start(bf16[256,512]{1,0:T(8,128)(2,1)S(1)} %get-tuple-element.59), channel_id=1, source_target_pairs={{0,2},{1,3},{2,0},{3,1},{4,6},{5,7},{6,4},{7,5},{8,10},{9,11},{10,... | collective-permute-start | bytes 786440 | tf_op jit(solution)/shard_map/ppermute | solution.py:336
  85.5 4.2 %collective-permute-done.6 = bf16[256,512]{1,0:T(8,128)(2,1)S(1)} collective-permute-done((bf16[256,512]{1,0:T(8,128)(2,1)S(1)}, bf16[256,512]{1,0:T(8,128)(2,1)S(1)}, u32[]{:S(2)}, u32[]{:S(2)}) %collective-permute-start.6) | collective-permute-done | bytes 262176 | tf_op jit(solution)/shard_map/ppermute | solution.py:336
  89.7 1.5 %collective-permute-done.7 = bf16[256,512]{1,0:T(8,128)(2,1)S(1)} collective-permute-done((bf16[256,512]{1,0:T(8,128)(2,1)S(1)}, bf16[256,512]{1,0:T(8,128)(2,1)S(1)}, u32[]{:S(2)}, u32[]{:S(2)}) %collective-permute-start.7) | collective-permute-done | bytes 262176 | tf_op jit(solution)/shard_map/ppermute | solution.py:336
  99.1 2.7 %collective-permute-start.9 = (bf16[256,512]{1,0:T(8,128)(2,1)S(1)}, bf16[256,512]{1,0:T(8,128)(2,1)S(1)}, u32[]{:S(2)}, u32[]{:S(2)}) collective-permute-start(bf16[256,512]{1,0:T(8,128)(2,1)S(1)} %slice.65), channel_id=1, source_target_pairs={{0,6},{1,7},{2,4},{3,5},{4,2},{5,3},{6,0},{7,1},{8,14},{9,15},{10,... | collective-permute-start | bytes 786440 | tf_op jit(solution)/shard_map/ppermute | solution.py:336
  105.7 1.7 %collective-permute-done.11 = bf16[256,512]{1,0:T(8,128)(2,1)S(1)} collective-permute-done((bf16[256,512]{1,0:T(8,128)(2,1)S(1)}, bf16[256,512]{1,0:T(8,128)(2,1)S(1)}, u32[]{:S(2)}, u32[]{:S(2)}) %collective-permute-start.11) | collective-permute-done | bytes 262176 | tf_op jit(solution)/shard_map/ppermute | solution.py:336
  107.5 1.2 collective-permute-done.9
  108.8 3.8 %collective-permute-done.18 = bf16[256,512]{1,0:T(8,128)(2,1)S(1)} collective-permute-done((bf16[256,512]{1,0:T(8,128)(2,1)S(1)}, bf16[256,512]{1,0:T(8,128)(2,1)S(1)}, u32[]{:S(2)}, u32[]{:S(2)}) %collective-permute-start.18) | collective-permute-done | bytes 262176 | tf_op jit(solution)/shard_map/ppermute | solution.py:336
  112.7 1.8 %collective-permute-done.16 = bf16[256,512]{1,0:T(8,128)(2,1)S(1)} collective-permute-done((bf16[256,512]{1,0:T(8,128)(2,1)S(1)}, bf16[256,512]{1,0:T(8,128)(2,1)S(1)}, u32[]{:S(2)}, u32[]{:S(2)}) %collective-permute-start.16) | collective-permute-done | bytes 262176 | tf_op jit(solution)/shard_map/ppermute | solution.py:336
  115.1 1.1 collective-permute-done.19
  116.3 2.4 %collective-permute-start.22 = (f32[512]{0:T(512)S(1)}, f32[512]{0:T(512)S(1)}, u32[]{:S(2)}, u32[]{:S(2)}) collective-permute-start(f32[512]{0:T(512)S(1)} %add.170), channel_id=1, source_target_pairs={{0,6},{1,7},{2,4},{3,5},{4,2},{5,3},{6,0},{7,1},{8,14},{9,15},{10,... | collective-permute-start | bytes 6152 | tf_op jit(solution)/shard_map/ppermute | solution.py:336
  118.7 2.3 %collective-permute-start.20 = (f32[512]{0:T(512)S(1)}, f32[512]{0:T(512)S(1)}, u32[]{:S(2)}, u32[]{:S(2)}) collective-permute-start(f32[512]{0:T(512)S(1)} %add.170), channel_id=1, source_target_pairs={{0,4},{1,5},{2,6},{3,7},{4,0},{5,1},{6,2},{7,3},{8,12},{9,13},{10,... | collective-permute-start | bytes 6152 | tf_op jit(solution)/shard_map/ppermute | solution.py:336
  121.1 1.2 collective-permute-done.21
  122.3 1.5 %collective-permute-done.20 = f32[512]{0:T(512)S(1)} collective-permute-done((f32[512]{0:T(512)S(1)}, f32[512]{0:T(512)S(1)}, u32[]{:S(2)}, u32[]{:S(2)}) %collective-permute-start.20) | collective-permute-done | bytes 2080 | tf_op jit(solution)/shard_map/ppermute | solution.py:336
  123.8 1.7 %multiply_convert_fusion = (bf16[512,1024]{1,0:T(8,128)(2,1)}, bf16[512,1024]{1,0:T(8,128)(2,1)}) fusion(f32[1024]{0:T(1024)S(1)} %copy-done.19, f32[512]{0:T(512)S(1)} %add_rsqrt_fusion, f32[256,512]{1,0:T(8,128)S(1)} %slice_add_fusion, f32[256,512]{1,0:T(8,128)S(1)} %slice_add_fusion.1, f32[256,512]{1,0:T(8,128)S(1)} %slice_add_fusion.2, ...), kind=kLoop, calls=%fused_computation.1 | loop fusion | flops 4718592 | bytes 5249024 | tf_op jit(solution)/shard_map/convert_element_type | solution.py:395
  (107 shorter events, 15.2 us)
Async XLA Ops:
  4.3 67.3 %all-to-all-start = ((bf16[32,256,128]{2,1,0:T(8,128)(2,1)}), bf16[32,256,128]{2,1,0:T(8,128)(2,1)}, u32[]{:S(2)}, u32[]{:S(2)}) async-start(bf16[32,256,128]{2,1,0:T(8,128)(2,1)} %shard_map.122.after), calls=%async_computation | async-start | bytes 4194304 | tf_op jit(solution)/shard_map/all_to_all | solution.py:345
  19.8 7.3 %copy-start.21 = (s32[1,32]{1,0:T(1,128)S(1)}, s32[1,32]{1,0:T(1,128)}, u32[]{:S(2)}) copy-start(s32[1,32]{1,0:T(1,128)} %param.15) | copy-start | bytes 388
  19.8 7.6 %copy-start.20 = (s32[1,32]{1,0:T(1,128)S(1)}, s32[1,32]{1,0:T(1,128)}, u32[]{:S(2)}) copy-start(s32[1,32]{1,0:T(1,128)} %param.16) | copy-start | bytes 388
  19.8 8.0 %copy-start.1 = (bf16[512,512]{1,0:T(8,128)(2,1)S(1)}, bf16[512,512]{1,0:T(8,128)(2,1)}, u32[]{:S(2)}) copy-start(bf16[512,512]{1,0:T(8,128)(2,1)} %q.3) | copy-start | bytes 1572868
  19.9 16.1 %collective-permute-start = (bf16[512,2048]{1,0:T(8,128)(2,1)S(1)}, bf16[512,2048]{1,0:T(8,128)(2,1)S(1)}, u32[]{:S(2)}, u32[]{:S(2)}) collective-permute-start(bf16[512,2048]{1,0:T(8,128)(2,1)S(1)} %get-tuple-element.39), channel_id=1, source_target_pairs={{0,1},{1,0},{2,3},{3,2},{4,5},{5,4},{6,7},{7,6},{8,9},{9,8},{10,11... | collective-permute-start | bytes 6291464 | tf_op jit(solution)/shard_map/ppermute | solution.py:336
  20.0 26.1 %collective-permute-start.1 = (bf16[512,1024]{1,0:T(8,128)(2,1)S(1)}, bf16[512,1024]{1,0:T(8,128)(2,1)S(1)}, u32[]{:S(2)}, u32[]{:S(2)}) collective-permute-start(bf16[512,1024]{1,0:T(8,128)(2,1)S(1)} %get-tuple-element.40), channel_id=1, source_target_pairs={{0,2},{1,3},{2,0},{3,1},{4,6},{5,7},{6,4},{7,5},{8,10},{9,11},{10,... | collective-permute-start | bytes 3145736 | tf_op jit(solution)/shard_map/ppermute | solution.py:336
  21.6 45.9 %collective-permute-start.2 = (bf16[512,1024]{1,0:T(8,128)(2,1)S(1)}, bf16[512,1024]{1,0:T(8,128)(2,1)S(1)}, u32[]{:S(2)}, u32[]{:S(2)}) collective-permute-start(bf16[512,1024]{1,0:T(8,128)(2,1)S(1)} %get-tuple-element.41), channel_id=1, source_target_pairs={{0,3},{1,2},{2,1},{3,0},{4,7},{5,6},{6,5},{7,4},{8,11},{9,10},{10,... | collective-permute-start | bytes 3145736 | tf_op jit(solution)/shard_map/ppermute | solution.py:336
  21.8 45.7 %collective-permute-start.3 = (bf16[512,1024]{1,0:T(8,128)(2,1)S(1)}, bf16[512,1024]{1,0:T(8,128)(2,1)S(1)}, u32[]{:S(2)}, u32[]{:S(2)}) collective-permute-start(bf16[512,1024]{1,0:T(8,128)(2,1)S(1)} %get-tuple-element.43), channel_id=1, source_target_pairs={{0,6},{1,7},{2,4},{3,5},{4,2},{5,3},{6,0},{7,1},{8,14},{9,15},{10,... | collective-permute-start | bytes 3145736 | tf_op jit(solution)/shard_map/ppermute | solution.py:336
  24.9 45.6 %collective-permute-start.4 = (bf16[512,1024]{1,0:T(8,128)(2,1)S(1)}, bf16[512,1024]{1,0:T(8,128)(2,1)S(1)}, u32[]{:S(2)}, u32[]{:S(2)}) collective-permute-start(bf16[512,1024]{1,0:T(8,128)(2,1)S(1)} %get-tuple-element.44), channel_id=1, source_target_pairs={{0,7},{1,6},{2,5},{3,4},{4,3},{5,2},{6,1},{7,0},{8,15},{9,14},{10,... | collective-permute-start | bytes 3145736 | tf_op jit(solution)/shard_map/ppermute | solution.py:336
  46.0 24.5 %copy-start.10 = (bf16[512,1024]{1,0:T(8,128)(2,1)}, bf16[512,1024]{1,0:T(8,128)(2,1)S(1)}, u32[]{:S(2)}) copy-start(bf16[512,1024]{1,0:T(8,128)(2,1)S(1)} %collective-permute-done.1) | copy-start | bytes 3145732
  74.0 17.2 %copy-start.11 = (bf16[512,1024]{1,0:T(8,128)(2,1)S(1)}, bf16[512,1024]{1,0:T(8,128)(2,1)}, u32[]{:S(2)}) copy-start(bf16[512,1024]{1,0:T(8,128)(2,1)} %copy-done.10) | copy-start | bytes 3145732
  80.5 11.2 %copy-start.15 = (bf16[512,1024]{1,0:T(8,128)(2,1)S(1)}, bf16[512,1024]{1,0:T(8,128)(2,1)}, u32[]{:S(2)}) copy-start(bf16[512,1024]{1,0:T(8,128)(2,1)} %copy-done.14) | copy-start | bytes 3145732
  80.5 9.2 %collective-permute-start.6 = (bf16[256,512]{1,0:T(8,128)(2,1)S(1)}, bf16[256,512]{1,0:T(8,128)(2,1)S(1)}, u32[]{:S(2)}, u32[]{:S(2)}) collective-permute-start(bf16[256,512]{1,0:T(8,128)(2,1)S(1)} %get-tuple-element.48), channel_id=1, source_target_pairs={{0,2},{1,3},{2,0},{3,1},{4,6},{5,7},{6,4},{7,5},{8,10},{9,11},{10,... | collective-permute-start | bytes 786440 | tf_op jit(solution)/shard_map/ppermute | solution.py:336
  80.8 10.4 %collective-permute-start.7 = (bf16[256,512]{1,0:T(8,128)(2,1)S(1)}, bf16[256,512]{1,0:T(8,128)(2,1)S(1)}, u32[]{:S(2)}, u32[]{:S(2)}) collective-permute-start(bf16[256,512]{1,0:T(8,128)(2,1)S(1)} %get-tuple-element.48), channel_id=1, source_target_pairs={{0,6},{1,7},{2,4},{3,5},{4,2},{5,3},{6,0},{7,1},{8,14},{9,15},{10,... | collective-permute-start | bytes 786440 | tf_op jit(solution)/shard_map/ppermute | solution.py:336
  83.5 9.4 %copy-start.6 = (bf16[512,1024]{1,0:T(8,128)(2,1)S(1)}, bf16[512,1024]{1,0:T(8,128)(2,1)}, u32[]{:S(2)}) copy-start(bf16[512,1024]{1,0:T(8,128)(2,1)} %get-tuple-element.50) | copy-start | bytes 3145732
  83.5 14.1 %collective-permute-start.13 = (bf16[256,512]{1,0:T(8,128)(2,1)S(1)}, bf16[256,512]{1,0:T(8,128)(2,1)S(1)}, u32[]{:S(2)}, u32[]{:S(2)}) collective-permute-start(bf16[256,512]{1,0:T(8,128)(2,1)S(1)} %get-tuple-element.59), channel_id=1, source_target_pairs={{0,2},{1,3},{2,0},{3,1},{4,6},{5,7},{6,4},{7,5},{8,10},{9,11},{10,... | collective-permute-start | bytes 786440 | tf_op jit(solution)/shard_map/ppermute | solution.py:336
  84.9 12.8 %collective-permute-start.14 = (bf16[256,512]{1,0:T(8,128)(2,1)S(1)}, bf16[256,512]{1,0:T(8,128)(2,1)S(1)}, u32[]{:S(2)}, u32[]{:S(2)}) collective-permute-start(bf16[256,512]{1,0:T(8,128)(2,1)S(1)} %get-tuple-element.59), channel_id=1, source_target_pairs={{0,6},{1,7},{2,4},{3,5},{4,2},{5,3},{6,0},{7,1},{8,14},{9,15},{10,... | collective-permute-start | bytes 786440 | tf_op jit(solution)/shard_map/ppermute | solution.py:336
  85.5 6.6 %collective-permute-start.5 = (bf16[256,512]{1,0:T(8,128)(2,1)S(1)}, bf16[256,512]{1,0:T(8,128)(2,1)S(1)}, u32[]{:S(2)}, u32[]{:S(2)}) collective-permute-start(bf16[256,512]{1,0:T(8,128)(2,1)S(1)} %get-tuple-element.48), channel_id=1, source_target_pairs={{0,1},{1,0},{2,3},{3,2},{4,5},{5,4},{6,7},{7,6},{8,9},{9,8},{10,11... | collective-permute-start | bytes 786440 | tf_op jit(solution)/shard_map/ppermute | solution.py:336
  89.7 4.1 %collective-permute-start.12 = (bf16[256,512]{1,0:T(8,128)(2,1)S(1)}, bf16[256,512]{1,0:T(8,128)(2,1)S(1)}, u32[]{:S(2)}, u32[]{:S(2)}) collective-permute-start(bf16[256,512]{1,0:T(8,128)(2,1)S(1)} %get-tuple-element.59), channel_id=1, source_target_pairs={{0,1},{1,0},{2,3},{3,2},{4,5},{5,4},{6,7},{7,6},{8,9},{9,8},{10,11... | collective-permute-start | bytes 786440 | tf_op jit(solution)/shard_map/ppermute | solution.py:336
  91.2 3.6 %collective-permute-start.8 = (bf16[256,512]{1,0:T(8,128)(2,1)S(1)}, bf16[256,512]{1,0:T(8,128)(2,1)S(1)}, u32[]{:S(2)}, u32[]{:S(2)}) collective-permute-start(bf16[256,512]{1,0:T(8,128)(2,1)S(1)} %collective-permute-done.6), channel_id=1, source_target_pairs={{0,1},{1,0},{2,3},{3,2},{4,5},{5,4},{6,7},{7,6},{8,9},{9,8},{10,11... | collective-permute-start | bytes 786440 | tf_op jit(solution)/shard_map/ppermute | solution.py:336
  92.1 3.9 %collective-permute-start.10 = (bf16[256,512]{1,0:T(8,128)(2,1)S(1)}, bf16[256,512]{1,0:T(8,128)(2,1)S(1)}, u32[]{:S(2)}, u32[]{:S(2)}) collective-permute-start(bf16[256,512]{1,0:T(8,128)(2,1)S(1)} %collective-permute-done.7), channel_id=1, source_target_pairs={{0,1},{1,0},{2,3},{3,2},{4,5},{5,4},{6,7},{7,6},{8,9},{9,8},{10,11... | collective-permute-start | bytes 786440 | tf_op jit(solution)/shard_map/ppermute | solution.py:336
  97.7 4.5 %collective-permute-start.17 = (bf16[256,512]{1,0:T(8,128)(2,1)S(1)}, bf16[256,512]{1,0:T(8,128)(2,1)S(1)}, u32[]{:S(2)}, u32[]{:S(2)}) collective-permute-start(bf16[256,512]{1,0:T(8,128)(2,1)S(1)} %collective-permute-done.14), channel_id=1, source_target_pairs={{0,1},{1,0},{2,3},{3,2},{4,5},{5,4},{6,7},{7,6},{8,9},{9,8},{10,11... | collective-permute-start | bytes 786440 | tf_op jit(solution)/shard_map/ppermute | solution.py:336
  98.2 9.2 %collective-permute-start.11 = (bf16[256,512]{1,0:T(8,128)(2,1)S(1)}, bf16[256,512]{1,0:T(8,128)(2,1)S(1)}, u32[]{:S(2)}, u32[]{:S(2)}) collective-permute-start(bf16[256,512]{1,0:T(8,128)(2,1)S(1)} %slice.64), channel_id=1, source_target_pairs={{0,2},{1,3},{2,0},{3,1},{4,6},{5,7},{6,4},{7,5},{8,10},{9,11},{10,... | collective-permute-start | bytes 786440 | tf_op jit(solution)/shard_map/ppermute | solution.py:336
  99.1 9.6 %collective-permute-start.9 = (bf16[256,512]{1,0:T(8,128)(2,1)S(1)}, bf16[256,512]{1,0:T(8,128)(2,1)S(1)}, u32[]{:S(2)}, u32[]{:S(2)}) collective-permute-start(bf16[256,512]{1,0:T(8,128)(2,1)S(1)} %slice.65), channel_id=1, source_target_pairs={{0,6},{1,7},{2,4},{3,5},{4,2},{5,3},{6,0},{7,1},{8,14},{9,15},{10,... | collective-permute-start | bytes 786440 | tf_op jit(solution)/shard_map/ppermute | solution.py:336
  101.7 2.2 %collective-permute-start.15 = (bf16[256,512]{1,0:T(8,128)(2,1)S(1)}, bf16[256,512]{1,0:T(8,128)(2,1)S(1)}, u32[]{:S(2)}, u32[]{:S(2)}) collective-permute-start(bf16[256,512]{1,0:T(8,128)(2,1)S(1)} %collective-permute-done.13), channel_id=1, source_target_pairs={{0,1},{1,0},{2,3},{3,2},{4,5},{5,4},{6,7},{7,6},{8,9},{9,8},{10,11... | collective-permute-start | bytes 786440 | tf_op jit(solution)/shard_map/ppermute | solution.py:336
  103.1 9.5 %collective-permute-start.18 = (bf16[256,512]{1,0:T(8,128)(2,1)S(1)}, bf16[256,512]{1,0:T(8,128)(2,1)S(1)}, u32[]{:S(2)}, u32[]{:S(2)}) collective-permute-start(bf16[256,512]{1,0:T(8,128)(2,1)S(1)} %slice.62), channel_id=1, source_target_pairs={{0,2},{1,3},{2,0},{3,1},{4,6},{5,7},{6,4},{7,5},{8,10},{9,11},{10,... | collective-permute-start | bytes 786440 | tf_op jit(solution)/shard_map/ppermute | solution.py:336
  104.8 9.7 %collective-permute-start.16 = (bf16[256,512]{1,0:T(8,128)(2,1)S(1)}, bf16[256,512]{1,0:T(8,128)(2,1)S(1)}, u32[]{:S(2)}, u32[]{:S(2)}) collective-permute-start(bf16[256,512]{1,0:T(8,128)(2,1)S(1)} %slice.63), channel_id=1, source_target_pairs={{0,6},{1,7},{2,4},{3,5},{4,2},{5,3},{6,0},{7,1},{8,14},{9,15},{10,... | collective-permute-start | bytes 786440 | tf_op jit(solution)/shard_map/ppermute | solution.py:336
  112.7 11.1 %copy-start.19 = (f32[1024]{0:T(1024)S(1)}, f32[1024]{0:T(1024)}, u32[]{:S(2)}) copy-start(f32[1024]{0:T(1024)} %param.21) | copy-start | bytes 12292
  115.0 1.2 collective-permute-start.19
  116.3 4.8 %collective-permute-start.22 = (f32[512]{0:T(512)S(1)}, f32[512]{0:T(512)S(1)}, u32[]{:S(2)}, u32[]{:S(2)}) collective-permute-start(f32[512]{0:T(512)S(1)} %add.170), channel_id=1, source_target_pairs={{0,6},{1,7},{2,4},{3,5},{4,2},{5,3},{6,0},{7,1},{8,14},{9,15},{10,... | collective-permute-start | bytes 6152 | tf_op jit(solution)/shard_map/ppermute | solution.py:336
  118.7 3.6 %collective-permute-start.21 = (f32[512]{0:T(512)S(1)}, f32[512]{0:T(512)S(1)}, u32[]{:S(2)}, u32[]{:S(2)}) collective-permute-start(f32[512]{0:T(512)S(1)} %add.170), channel_id=1, source_target_pairs={{0,2},{1,3},{2,0},{3,1},{4,6},{5,7},{6,4},{7,5},{8,10},{9,11},{10,... | collective-permute-start | bytes 6152 | tf_op jit(solution)/shard_map/ppermute | solution.py:336
  118.7 5.1 %collective-permute-start.20 = (f32[512]{0:T(512)S(1)}, f32[512]{0:T(512)S(1)}, u32[]{:S(2)}, u32[]{:S(2)}) collective-permute-start(f32[512]{0:T(512)S(1)} %add.170), channel_id=1, source_target_pairs={{0,4},{1,5},{2,6},{3,7},{4,0},{5,1},{6,2},{7,3},{8,12},{9,13},{10,... | collective-permute-start | bytes 6152 | tf_op jit(solution)/shard_map/ppermute | solution.py:336
  (14 other events, 39.0 us)

commit v3 on v2

--- a/solution.py
+++ b/solution.py
@@ -1,3 +1,4 @@
+import functools
 import math
 
 import jax
@@ -17,6 +18,7 @@
 FRESH = 128
 PAIRS = 48
 CHUNKS = 4
+PIECE = 8
 UNROLL = 8
 LOW = -1e30
 DEAD = 8192.0
@@ -40,8 +42,15 @@
         return jnp.sum(jnp.where(hit, values, 0), axis=1)
 
     block = pick(first[None, :] + slot - offsets[None, :])
+    ahead = jnp.sum(jnp.where((block < PIECE) & jnp.any(hit, axis=1), 1, 0))
     plan = jnp.stack(
-        [block, pick(packs[None, :]), pick(starts[None, :]), pick(ends[None, :])]
+        [
+            block,
+            pick(packs[None, :]),
+            pick(starts[None, :]),
+            pick(ends[None, :]),
+            jnp.full((PAIRS,), ahead),
+        ]
     ).astype(jnp.int32)
     rows = jnp.arange(512, dtype=jnp.int32)[:, None]
     row_start = jnp.max(jnp.where(starts[None, :] <= rows, starts[None, :], 0), axis=1)
@@ -75,7 +84,7 @@
         for u in range(tile):
             pack = c * tile + u
             found = held[pack, :prefix].astype(jnp.float32)
-            marked = jnp.where(position < lengths[pack], found, DEAD)
+            marked = jnp.where(position < lengths[0, pack], found, DEAD)
             held[pack, :prefix] = marked.astype(jnp.bfloat16)
         step[1].wait()
         step[2].start()
@@ -109,7 +118,7 @@
 
 
 def main_kernel(
-    plan, q, cache_hbm, mean_hbm, level_hbm, out_a, out_b, cache, means, levels, scores, weights, mixed, sems
+    first, plan, q, cache_hbm, mean_hbm, level_hbm, out, cache, means, levels, scores, weights, mixed, sems
 ):
     half = cache.shape[1] // 2
     fetch = [
@@ -118,12 +127,21 @@
         )
         for i in range(2)
     ]
-    fetch.append(pltpu.make_async_copy(level_hbm, levels, sems.at[2]))
-    fetch.append(pltpu.make_async_copy(mean_hbm, means, sems.at[3]))
+    blocks = pl.ds(first, PIECE)
+    fetch.append(pltpu.make_async_copy(level_hbm.at[blocks], levels, sems.at[2]))
+    fetch.append(pltpu.make_async_copy(mean_hbm.at[blocks], means, sems.at[3]))
     for i in (0, 2, 3, 1):
         fetch[i].start()
     ones = jnp.ones((16, HD), jnp.bfloat16)
-    prefix = cache.shape[1] // 2
+    ahead = plan[4, 0]
+    if first == 0:
+        lower, upper = 0, lax.div(ahead + UNROLL - 1, UNROLL)
+    else:
+        lower, upper = lax.div(ahead, UNROLL), PAIRS // UNROLL
+
+    def place(i):
+        block = plan[0, i] - first
+        return jnp.where((block >= 0) & (block < PIECE), block, PIECE)
 
     def own_rows(base, i):
         row = base + lax.broadcasted_iota(jnp.int32, (BLOCK, HD), 0)
@@ -132,11 +150,11 @@
     def score(step, carry):
         for u in range(UNROLL):
             i = step * UNROLL + u
-            block = plan[0, i]
-            base = pl.multiple_of(block * BLOCK, BLOCK)
+            block = place(i)
+            base = pl.multiple_of(plan[0, i] * BLOCK, BLOCK)
             left = jnp.concatenate(stack_heads(q, base) + [ones], axis=0)
             both = lax.dot_general(
-                left, cache[plan[1, i], :prefix], NT, preferred_element_type=jnp.float32
+                left, cache[plan[1, i], :half], NT, preferred_element_type=jnp.float32
             )
             live = both[GROUP * BLOCK : GROUP * BLOCK + 1] < 32.0 * DEAD
             found = jnp.where(live, both[: GROUP * BLOCK] * SCALE, LOW)
@@ -162,27 +180,26 @@
     def mix(step, carry):
         for u in range(UNROLL):
             i = step * UNROLL + u
-            block = plan[0, i]
+            block = place(i)
             found = jnp.dot(
-                weights[block], cache[plan[1, i], prefix:], preferred_element_type=jnp.float32
+                weights[block], cache[plan[1, i], half:], preferred_element_type=jnp.float32
             )
-            mine = own_rows(block * BLOCK, i)
+            mine = own_rows(plan[0, i] * BLOCK, i)
             for h in range(GROUP):
                 part = pl.ds(h * BLOCK, BLOCK)
                 mixed[block, part] += jnp.where(mine, found[h * BLOCK : (h + 1) * BLOCK], 0.0)
         return carry
 
     fetch[0].wait()
-    lax.fori_loop(0, PAIRS // UNROLL, score, 0)
+    lax.fori_loop(lower, upper, score, 0)
     fetch[2].wait()
     fetch[3].wait()
-    lax.fori_loop(0, 512 // BLOCK, soften, 0, unroll=8)
+    lax.fori_loop(0, PIECE, soften, 0, unroll=PIECE)
     fetch[1].wait()
-    lax.fori_loop(0, PAIRS // UNROLL, mix, 0)
-    for block in range(512 // BLOCK):
+    lax.fori_loop(lower, upper, mix, 0)
+    for block in range(PIECE):
         total = mixed[block].astype(jnp.bfloat16)
-        out = out_a if block < 8 else out_b
-        base = (block % 8) * BLOCK
+        base = block * BLOCK
         for h in range(GROUP):
             out[base : base + BLOCK, h * HD : (h + 1) * HD] = total[h * BLOCK : (h + 1) * BLOCK]
 
@@ -279,39 +296,38 @@
     )(queries, jnp.pad(new_keys, front), jnp.pad(new_values, front), row_start)
 
 
-def attend(plan, queries, cache, fresh_mean, fresh_level):
-    area = fresh_mean.shape
-    half = jax.ShapeDtypeStruct((256, queries.shape[1]), queries.dtype)
+def attend(first, plan, queries, cache, fresh_mean, fresh_level):
+    area = fresh_mean.shape[1:]
     return pl.pallas_call(
-        main_kernel,
-        out_shape=(half, half),
+        functools.partial(main_kernel, first),
+        out_shape=jax.ShapeDtypeStruct((PIECE * BLOCK, queries.shape[1]), queries.dtype),
         grid_spec=pltpu.PrefetchScalarGridSpec(
             num_scalar_prefetch=1,
             grid=(),
             in_specs=whole(1) + anywhere(3),
-            out_specs=tuple(whole(2)),
+            out_specs=whole(1)[0],
             scratch_shapes=[
                 pltpu.VMEM(cache.shape, cache.dtype),
-                pltpu.VMEM(area, jnp.float32),
-                pltpu.VMEM(area, jnp.float32),
-                pltpu.VMEM(area, jnp.float32),
-                pltpu.VMEM(area, jnp.bfloat16),
-                pltpu.VMEM(area, jnp.float32),
+                pltpu.VMEM((PIECE, *area), jnp.float32),
+                pltpu.VMEM((PIECE, *area), jnp.float32),
+                pltpu.VMEM((PIECE + 1, *area), jnp.float32),
+                pltpu.VMEM((PIECE + 1, *area), jnp.bfloat16),
+                pltpu.VMEM((PIECE + 1, *area), jnp.float32),
                 pltpu.SemaphoreType.DMA((4,)),
             ],
         ),
-        compiler_params=pltpu.CompilerParams(vmem_limit_bytes=10 << 20),
+        compiler_params=pltpu.CompilerParams(vmem_limit_bytes=7 << 20),
         cost_estimate=pl.CostEstimate(
             flops=1 << 31, bytes_accessed=4 << 20, transcendentals=1 << 18
         ),
-    )(plan, queries, cache, fresh_mean, fresh_level)
+    )(plan, queries, cache, *in_hbm(fresh_mean, fresh_level))
 
 
 def attention(counts, packs, queries, marked, values, new_keys, new_values):
     plan, row_start = pair_plan(counts, packs)
     fresh = attend_fresh(queries, new_keys, new_values, row_start)
     cache = jnp.concatenate([marked, values], axis=1)
-    return jnp.concatenate(attend(plan, queries, cache, *fresh), axis=0)
+    return jnp.concatenate([attend(i, plan, queries, cache, *fresh) for i in (0, PIECE)], axis=0)
 
 
 def on_device(
@@ -341,39 +357,40 @@
         second = [to * 1024 + 512, jnp.bitwise_xor(to, 2) * 1024 + 512]
         return first, second
 
-    payload = make_payload(prefix_lengths[0], cache_keys[0], cache_values[0])
+    payload = make_payload(prefix_lengths, cache_keys[0], cache_values[0])
     cache = lax.all_to_all(payload, "dp", split_axis=0, concat_axis=0, tiled=True)
 
     starts = sum([shared(mask)[half] for mask, half in ((2, 0), (6, 1), (3, 0), (7, 1))], [])
-    starts = jnp.stack(starts + sum(shared(1), []))
-    pieces = cut(starts, out_weight, (1024, 1024, 1024, 1024, 2048), payload)
-    starts, pieces = lax.optimization_barrier((jnp.stack(sum(shared(0), [])), pieces))
-    arrived = [swap(piece, mask) for piece, mask in zip(pieces, (2, 6, 3, 7, 1))]
-    sibling = arrived[4]
-    mine = cut(starts, out_weight, (1024, 1024), payload)
-    mats = [
-        [mine[0], sibling[:, :1024], arrived[0], arrived[2]],
-        [mine[1], sibling[:, 1024:], arrived[1], arrived[3]],
-    ]
+    pieces = cut(jnp.stack(starts), out_weight, (1024,) * 4, payload)
+    starts, pieces = lax.optimization_barrier(
+        (jnp.stack(sum(shared(1), []) + sum(shared(0), [])), pieces)
+    )
+    same = [swap(piece, mask) for piece, mask in zip(pieces[:2], (2, 6))]
+    cross = [swap(piece, mask) for piece, mask in zip(pieces[2:], (3, 7))]
+    pieces = cut(starts, out_weight, (1024,) * 4, payload)
+    sibling = [swap(piece, 1) for piece in pieces[:2]]
+    here = pieces[2:]
 
     plan, row_start = pair_plan(row_counts[0], pack_of[0])
     fresh = attend_fresh(queries, new_keys, new_values, row_start)
-    plan, mats = lax.optimization_barrier((plan, mats))
-    attended = attend(plan, queries, cache, *fresh)
-
+    plan, same, sibling, here = lax.optimization_barrier((plan, same, sibling, here))
+    attended = [attend(first, plan, queries, cache, *fresh) for first in (0, PIECE)]
+    attended[0], cross = lax.optimization_barrier((attended[0], cross))
+
+    def times(rows, mat):
+        return jnp.dot(rows, mat, preferred_element_type=f32)
+
+    others = [swap(rows, 1) for rows in attended]
     near = [[swap(rows, mask) for mask in (2, 6)] for rows in attended]
-    others = [swap(rows, 1) for rows in attended]
     own = []
     got = []
     sent = []
     for rows, other, close in zip(attended, others, near):
-        close, sent = lax.optimization_barrier((close, sent))
+        local = [times(rows, here[half]) + times(other, sibling[half]) for half in range(2)]
+        close, local, sent = lax.optimization_barrier((close, local, sent))
         totals = [
-            sum(
-                jnp.dot(part, mat, preferred_element_type=f32)
-                for part, mat in zip((rows, other, arrival, swap(arrival, 1)), mats[half])
-            )
-            for half, arrival in enumerate(close)
+            local[half] + times(close[half], same[half]) + times(swap(close[half], 1), cross[half])
+            for half in range(2)
         ]
         own.append([total[:, :512] for total in totals])
         sent = [total[:, 512:].astype(bf16) for total in totals]

time: 126 us -> 126 us (level)
  waiting for transfers between devices: 51.2 us -> 37.9 us
  matrix products: 7.08 us -> 19.2 us
  Pallas kernels: 21.5 us -> 25.1 us
  local copies, waits for them, and re-layouts: 9.07 us -> 5.98 us
    ppermute x23 -> x24, waiting for transfers between devices: 51.2 us -> 29.7 us  [swap(): return lax.ppermute(value, 'tensor', [(t, t ^ mask) for t in range(count)])]
    dot_general x16, matrix products: 7.08 us -> 19.2 us  [times(): return jnp.dot(rows, mat, preferred_element_type=f32)]
    all_to_all x1, waiting for transfers between devices: 0.01 us -> 8.17 us  [on_device(): lax.all_to_all(payload, 'dp', split_axis=0, concat_axis=0, tiled=True)]
    pallas_call x1 -> x2, Pallas kernels: 6.43 us -> 8.89 us  [attend(): pl.pallas_call(functools.partial(main_kernel, first), out_shape=jax.Shape...]
    unnamed x44 -> x26, local copies, waits for them, and re-layouts: 7.15 us -> 4.85 us
    slice x1 -> x0, local copies, waits for them, and re-layouts: 1.55 us -> none  [on_device(): sibling[:, 1024:]]
    ppermute x23 -> x24, starting transfers between devices: 20.8 us -> 20.5 us  [swap(): return lax.ppermute(value, 'tensor', [(t, t ^ mask) for t in range(count)])]
  transfers between devices with their start and end apart: 24 -> 25, of which waited for: 13 -> 8; matrix products, arithmetic and copies ran while one was open for 8% -> 17% of each run, Pallas kernels for 10% -> 18%
where the time goes in v3:
time: 126 us; the launch traced here: 125 us
  waiting for transfers between devices  37.9 us (30%)
  starting transfers between devices  32.1 us (25%)
  Pallas kernels  25.1 us (20%)
  matrix products  19.2 us (15%)
  local copies, waits for them, and re-layouts  5.98 us (5%)
  other arithmetic  3.53 us (3%)
    ppermute x24, waiting for transfers between devices, swap(): return lax.ppermute(value, 'tensor', [(t, t ^ mask) for t in range(count)])  29.7 us
    ppermute x24, starting transfers between devices, swap(): return lax.ppermute(value, 'tensor', [(t, t ^ mask) for t in range(count)])  20.5 us
    dot_general x16, matrix products, times(): return jnp.dot(rows, mat, preferred_element_type=f32)  19.2 us
    all_to_all x1, starting transfers between devices, on_device(): lax.all_to_all(payload, 'dp', split_axis=0, concat_axis=0, tiled=True)  11.7 us
    pallas_call x2, Pallas kernels, attend(): pl.pallas_call(functools.partial(main_kernel, first), out_shape=jax.Shape...  8.89 us
    all_to_all x1, waiting for transfers between devices, on_device(): lax.all_to_all(payload, 'dp', split_axis=0, concat_axis=0, tiled=True)  8.17 us
    pallas_call x2, Pallas kernels, cut(): pl.pallas_call(cut_kernel, out_shape=tuple((jax.ShapeDtypeStruct((rows, w...  7.08 us
    pallas_call x1, Pallas kernels, attend_fresh(): pl.pallas_call(fresh_kernel, out_shape=(area, area), in_specs=whole(4), o...  6.16 us
  transfers between devices with their start and end apart: 25, of which 8 were waited for; matrix products, arithmetic and copies ran while one was open for 17% of the time, Pallas kernels for 18%

profile of v3, /device:TPU:2, one launch (start us, length us, event | category | flops | bytes accessed | tf_op | source)
XLA Modules:
  0.0 125.1 jit_solution(3780964698488296135)
XLA Ops:
  1.3 3.0 %shard_map.122.after = bf16[32,256,128]{2,1,0:T(8,128)(2,1)} custom-call(s32[1,32]{1,0:T(1,128)S(1)} %copy-done, bf16[32,128,128]{2,1,0:T(8,128)(2,1)} %bitcast.80, bf16[32,128,128]{2,1,0:T(8,128)(2,1)} %bitcast.81), custom_call_target="tpu_custom_call" | custom-call | flops 1048576 | bytes 4194304 | tf_op jit(solution)/shard_map/pallas_call | solution.py:225
  4.3 11.7 %all-to-all-start = ((bf16[32,256,128]{2,1,0:T(8,128)(2,1)}), bf16[32,256,128]{2,1,0:T(8,128)(2,1)}, u32[]{:S(2)}, u32[]{:S(2)}) async-start(bf16[32,256,128]{2,1,0:T(8,128)(2,1)} %shard_map.122.after), calls=%async_computation | async-start | bytes 4194304 | tf_op jit(solution)/shard_map/all_to_all | solution.py:361
  16.1 3.5 %shard_map.123 = (bf16[512,1024]{1,0:T(8,128)(2,1)}, bf16[512,1024]{1,0:T(8,128)(2,1)}, bf16[512,1024]{1,0:T(8,128)(2,1)}, bf16[512,1024]{1,0:T(8,128)(2,1)S(1)}) custom-call(s32[8]{0:T(128)S(1)} %stack.91.starts, bf16[512,8192]{1,0:T(8,128)(2,1)} %weight.3, bf16[32,256,128]{2,1,0:T(8,128)(2,1)} %shard_map.122.after), custom_call_target="tpu_custom_call" | custom-call | bytes 12582912 | tf_op jit(solution)/shard_map/pallas_call | solution.py:266
  19.8 1.7 %collective-permute-start = (bf16[512,1024]{1,0:T(8,128)(2,1)}, bf16[512,1024]{1,0:T(8,128)(2,1)S(1)}, u32[]{:S(2)}, u32[]{:S(2)}) collective-permute-start(bf16[512,1024]{1,0:T(8,128)(2,1)} %get-tuple-element.39), channel_id=1, source_target_pairs={{0,2},{1,3},{2,0},{3,1},{4,6},{5,7},{6,4},{7,5},{8,10},{9,11},{10,... | collective-permute-start | bytes 3145736 | tf_op jit(solution)/shard_map/ppermute | solution.py:352
  21.4 2.2 %collective-permute-start.1 = (bf16[512,1024]{1,0:T(8,128)(2,1)}, bf16[512,1024]{1,0:T(8,128)(2,1)}, u32[]{:S(2)}, u32[]{:S(2)}) collective-permute-start(bf16[512,1024]{1,0:T(8,128)(2,1)} %get-tuple-element.40), channel_id=1, source_target_pairs={{0,6},{1,7},{2,4},{3,5},{4,2},{5,3},{6,0},{7,1},{8,14},{9,15},{10,... | collective-permute-start | bytes 3145736 | tf_op jit(solution)/shard_map/ppermute | solution.py:352
  23.6 3.5 %shard_map.124 = (bf16[512,1024]{1,0:T(8,128)(2,1)}, bf16[512,1024]{1,0:T(8,128)(2,1)}, bf16[512,1024]{1,0:T(8,128)(2,1)S(1)}, bf16[512,1024]{1,0:T(8,128)(2,1)S(1)}) custom-call(s32[8]{0:T(128)S(1)} %stack.82.starts, bf16[512,8192]{1,0:T(8,128)(2,1)} %weight.3, bf16[32,256,128]{2,1,0:T(8,128)(2,1)} %shard_map.122.after), custom_call_target="tpu_custom_call" | custom-call | bytes 12582912 | tf_op jit(solution)/shard_map/pallas_call | solution.py:266
  28.5 17.7 %collective-permute-done = bf16[512,1024]{1,0:T(8,128)(2,1)S(1)} collective-permute-done((bf16[512,1024]{1,0:T(8,128)(2,1)}, bf16[512,1024]{1,0:T(8,128)(2,1)S(1)}, u32[]{:S(2)}, u32[]{:S(2)}) %collective-permute-start) | collective-permute-done | bytes 1048608 | tf_op jit(solution)/shard_map/ppermute | solution.py:352
  49.0 6.2 %shard_map.125 = (f32[16,128,128]{2,1,0:T(8,128)S(1)}, f32[16,128,128]{2,1,0:T(8,128)S(1)}) custom-call(bf16[512,512]{1,0:T(8,128)(2,1)S(1)} %copy-done.1, bf16[608,128]{1,0:T(8,128)(2,1)S(1)} %pad.7.fresh_k, bf16[608,128]{1,0:T(8,128)(2,1)S(1)} %pad.8.fresh_v, s32[512,128]{1,0:T(8,128)S(1)} %broadcast_in_dim.105.row_start), custom_call_target="tpu_custom_call" | custom-call | flops 2147483648 | bytes 4194304 | tf_op jit(solution)/shard_map/pallas_call | solution.py:287
  57.1 8.2 %all-to-all-done.cache_hbm = bf16[32,256,128]{2,1,0:T(8,128)(2,1)} async-done(((bf16[32,256,128]{2,1,0:T(8,128)(2,1)}), bf16[32,256,128]{2,1,0:T(8,128)(2,1)}, u32[]{:S(2)}, u32[]{:S(2)}) %all-to-all-start) | async-done | bytes 2097184 | tf_op jit(solution)/shard_map/all_to_all | solution.py:361
  66.3 4.2 %shard_map.126 = bf16[256,512]{1,0:T(8,128)(2,1)S(1)} custom-call(s32[5,48]{1,0:T(8,128)S(1)} %stack.73.plan, bf16[512,512]{1,0:T(8,128)(2,1)S(1)} %copy-done.2, bf16[32,256,128]{2,1,0:T(8,128)(2,1)} %all-to-all-done.cache_hbm, f32[16,128,128]{2,1,0:T(8,128)} %copy-done.3, f32[16,128,128]{2,1,0:T(8,128)} %copy-done.4), custom_call_target="tpu_custom_call" | custom-call | flops 2147483648 | bytes 4194304 | tf_op jit(solution)/shard_map/pallas_call | solution.py:301
  70.5 2.2 %collective-permute-done.5 = bf16[512,1024]{1,0:T(8,128)(2,1)} collective-permute-done((bf16[512,1024]{1,0:T(8,128)(2,1)S(1)}, bf16[512,1024]{1,0:T(8,128)(2,1)}, u32[]{:S(2)}, u32[]{:S(2)}) %collective-permute-start.5) | collective-permute-done | bytes 1048608 | tf_op jit(solution)/shard_map/ppermute | solution.py:352
  73.9 4.7 %shard_map.127 = bf16[256,512]{1,0:T(8,128)(2,1)S(1)} custom-call(s32[5,48]{1,0:T(8,128)S(1)} %stack.73.plan, bf16[512,512]{1,0:T(8,128)(2,1)S(1)} %copy-done.2, bf16[32,256,128]{2,1,0:T(8,128)(2,1)} %all-to-all-done.cache_hbm, f32[16,128,128]{2,1,0:T(8,128)} %copy-done.3, f32[16,128,128]{2,1,0:T(8,128)} %copy-done.4), custom_call_target="tpu_custom_call" | custom-call | flops 2147483648 | bytes 4194304 | tf_op jit(solution)/shard_map/pallas_call | solution.py:301
  78.7 2.3 %collective-permute-start.14 = (bf16[256,512]{1,0:T(8,128)(2,1)S(1)}, bf16[256,512]{1,0:T(8,128)(2,1)S(1)}, u32[]{:S(2)}, u32[]{:S(2)}) collective-permute-start(bf16[256,512]{1,0:T(8,128)(2,1)S(1)} %shard_map.127), channel_id=1, source_target_pairs={{0,6},{1,7},{2,4},{3,5},{4,2},{5,3},{6,0},{7,1},{8,14},{9,15},{10,... | collective-permute-start | bytes 786440 | tf_op jit(solution)/shard_map/ppermute | solution.py:352
  81.0 1.4 %collective-permute-start.13 = (bf16[256,512]{1,0:T(8,128)(2,1)S(1)}, bf16[256,512]{1,0:T(8,128)(2,1)S(1)}, u32[]{:S(2)}, u32[]{:S(2)}) collective-permute-start(bf16[256,512]{1,0:T(8,128)(2,1)S(1)} %shard_map.127), channel_id=1, source_target_pairs={{0,2},{1,3},{2,0},{3,1},{4,6},{5,7},{6,4},{7,5},{8,10},{9,11},{10,... | collective-permute-start | bytes 786440 | tf_op jit(solution)/shard_map/ppermute | solution.py:352
  82.4 1.7 %fusion.7 = f32[256,1024]{1,0:T(8,128)S(1)} fusion(bf16[256,512]{1,0:T(8,128)(2,1)S(1)} %collective-permute-done.8, bf16[512,1024]{1,0:T(8,128)(2,1)} %collective-permute-done.3), kind=kOutput, calls=%fused_computation.55 | convolution fusion | flops 268435456 | bytes 2359296 | tf_op jit(solution)/shard_map/dot_general | solution.py:381
  84.5 1.7 %fusion.11 = f32[256,1024]{1,0:T(8,128)S(1)} fusion(bf16[256,512]{1,0:T(8,128)(2,1)S(1)} %collective-permute-done.15, bf16[512,1024]{1,0:T(8,128)(2,1)} %collective-permute-done.3), kind=kOutput, calls=%fused_computation.59 | convolution fusion | flops 268435456 | bytes 2359296 | tf_op jit(solution)/shard_map/dot_general | solution.py:381
  86.7 1.7 %fusion.10 = f32[256,1024]{1,0:T(8,128)S(1)} fusion(bf16[256,512]{1,0:T(8,128)(2,1)S(1)} %collective-permute-done.15, bf16[512,1024]{1,0:T(8,128)(2,1)} %collective-permute-done.2), kind=kOutput, calls=%fused_computation.58 | convolution fusion | flops 268435456 | bytes 2359296 | tf_op jit(solution)/shard_map/dot_general | solution.py:381
  88.8 1.7 %fusion.6 = f32[256,1024]{1,0:T(8,128)S(1)} fusion(bf16[256,512]{1,0:T(8,128)(2,1)S(1)} %collective-permute-done.8, bf16[512,1024]{1,0:T(8,128)(2,1)} %collective-permute-done.2), kind=kOutput, calls=%fused_computation.54 | convolution fusion | flops 268435456 | bytes 2359296 | tf_op jit(solution)/shard_map/dot_general | solution.py:381
  92.1 1.7 %fusion.9 = f32[256,1024]{1,0:T(8,128)S(1)} fusion(bf16[256,512]{1,0:T(8,128)(2,1)S(1)} %collective-permute-done.7, bf16[512,1024]{1,0:T(8,128)(2,1)} %collective-permute-done.1), kind=kOutput, calls=%fused_computation.57 | convolution fusion | flops 268435456 | bytes 2359296 | tf_op jit(solution)/shard_map/dot_general | solution.py:381
  93.8 1.7 %add_add_fusion.3 = f32[256,1024]{1,0:T(8,128)S(1)} fusion(f32[256,1024]{1,0:T(8,128)S(1)} %convolution_add_fusion.3, f32[256,1024]{1,0:T(8,128)S(1)} %fusion.8, bf16[256,512]{1,0:T(8,128)(2,1)S(1)} %collective-permute-done.9, bf16[512,1024]{1,0:T(8,128)(2,1)} %collective-permute-done.4), kind=kOutput, calls=%fused_computation.10 | convolution fusion | flops 268959744 | bytes 4456448 | tf_op jit(solution)/shard_map/dot_general | solution.py:381
  96.5 1.7 %add_add_fusion.2 = f32[256,1024]{1,0:T(8,128)S(1)} fusion(f32[256,1024]{1,0:T(8,128)S(1)} %convolution_add_fusion.2, f32[256,1024]{1,0:T(8,128)S(1)} %fusion.9, bf16[256,512]{1,0:T(8,128)(2,1)S(1)} %collective-permute-done.11, bf16[512,1024]{1,0:T(8,128)(2,1)} %collective-permute-done.5), kind=kOutput, calls=%fused_computation.9 | convolution fusion | flops 268959744 | bytes 4456448 | tf_op jit(solution)/shard_map/dot_general | solution.py:381
  99.3 1.7 %fusion.13 = f32[256,1024]{1,0:T(8,128)S(1)} fusion(bf16[256,512]{1,0:T(8,128)(2,1)S(1)} %collective-permute-done.14, bf16[512,1024]{1,0:T(8,128)(2,1)} %collective-permute-done.1), kind=kOutput, calls=%fused_computation.61 | convolution fusion | flops 268435456 | bytes 2359296 | tf_op jit(solution)/shard_map/dot_general | solution.py:381
  100.9 1.7 %add_add_fusion.1 = f32[256,1024]{1,0:T(8,128)S(1)} fusion(f32[256,1024]{1,0:T(8,128)S(1)} %convolution_add_fusion.1, f32[256,1024]{1,0:T(8,128)S(1)} %fusion.12, bf16[256,512]{1,0:T(8,128)(2,1)S(1)} %collective-permute-done.16, bf16[512,1024]{1,0:T(8,128)(2,1)} %collective-permute-done.4), kind=kOutput, calls=%fused_computation.8 | convolution fusion | flops 268959744 | bytes 4456448 | tf_op jit(solution)/shard_map/dot_general | solution.py:381
  102.6 2.4 %collective-permute-start.17 = (bf16[256,512]{1,0:T(8,128)(2,1)S(1)}, bf16[256,512]{1,0:T(8,128)(2,1)S(1)}, u32[]{:S(2)}, u32[]{:S(2)}) collective-permute-start(bf16[256,512]{1,0:T(8,128)(2,1)S(1)} %slice.53), channel_id=1, source_target_pairs={{0,6},{1,7},{2,4},{3,5},{4,2},{5,3},{6,0},{7,1},{8,14},{9,15},{10,... | collective-permute-start | bytes 786440 | tf_op jit(solution)/shard_map/ppermute | solution.py:352
  105.1 1.7 %add_add_fusion = f32[256,1024]{1,0:T(8,128)S(1)} fusion(f32[256,1024]{1,0:T(8,128)S(1)} %convolution_add_fusion, f32[256,1024]{1,0:T(8,128)S(1)} %fusion.13, bf16[256,512]{1,0:T(8,128)(2,1)S(1)} %collective-permute-done.18, bf16[512,1024]{1,0:T(8,128)(2,1)} %collective-permute-done.5), kind=kOutput, calls=%fused_computation.7 | convolution fusion | flops 268959744 | bytes 4456448 | tf_op jit(solution)/shard_map/dot_general | solution.py:381
  106.8 1.3 %collective-permute-start.19 = (bf16[256,512]{1,0:T(8,128)(2,1)S(1)}, bf16[256,512]{1,0:T(8,128)(2,1)S(1)}, u32[]{:S(2)}, u32[]{:S(2)}) collective-permute-start(bf16[256,512]{1,0:T(8,128)(2,1)S(1)} %slice.52), channel_id=1, source_target_pairs={{0,2},{1,3},{2,0},{3,1},{4,6},{5,7},{6,4},{7,5},{8,10},{9,11},{10,... | collective-permute-start | bytes 786440 | tf_op jit(solution)/shard_map/ppermute | solution.py:352
  108.2 4.2 %collective-permute-done.17 = bf16[256,512]{1,0:T(8,128)(2,1)S(1)} collective-permute-done((bf16[256,512]{1,0:T(8,128)(2,1)S(1)}, bf16[256,512]{1,0:T(8,128)(2,1)S(1)}, u32[]{:S(2)}, u32[]{:S(2)}) %collective-permute-start.17) | collective-permute-done | bytes 262176 | tf_op jit(solution)/shard_map/ppermute | solution.py:352
  112.5 2.5 %collective-permute-done.19 = bf16[256,512]{1,0:T(8,128)(2,1)S(1)} collective-permute-done((bf16[256,512]{1,0:T(8,128)(2,1)S(1)}, bf16[256,512]{1,0:T(8,128)(2,1)S(1)}, u32[]{:S(2)}, u32[]{:S(2)}) %collective-permute-start.19) | collective-permute-done | bytes 262176 | tf_op jit(solution)/shard_map/ppermute | solution.py:352
  115.5 1.1 collective-permute-done.20
  118.3 3.1 %collective-permute-start.21 = (f32[512]{0:T(512)S(1)}, f32[512]{0:T(512)S(1)}, u32[]{:S(2)}, u32[]{:S(2)}) collective-permute-start(f32[512]{0:T(512)S(1)} %add.170), channel_id=1, source_target_pairs={{0,4},{1,5},{2,6},{3,7},{4,0},{5,1},{6,2},{7,3},{8,12},{9,13},{10,... | collective-permute-start | bytes 6152 | tf_op jit(solution)/shard_map/ppermute | solution.py:352
  121.5 1.9 %collective-permute-done.21 = f32[512]{0:T(512)S(1)} collective-permute-done((f32[512]{0:T(512)S(1)}, f32[512]{0:T(512)S(1)}, u32[]{:S(2)}, u32[]{:S(2)}) %collective-permute-start.21) | collective-permute-done | bytes 2080 | tf_op jit(solution)/shard_map/ppermute | solution.py:352
  123.4 1.7 %multiply_convert_fusion = (bf16[512,1024]{1,0:T(8,128)(2,1)}, bf16[512,1024]{1,0:T(8,128)(2,1)}) fusion(f32[1024]{0:T(1024)S(1)} %copy-done.10, f32[512]{0:T(512)S(1)} %add_rsqrt_fusion, f32[256,512]{1,0:T(8,128)S(1)} %slice_add_fusion, f32[256,512]{1,0:T(8,128)S(1)} %slice_add_fusion.1, f32[256,512]{1,0:T(8,128)S(1)} %slice_add_fusion.2, ...), kind=kLoop, calls=%fused_computation.1 | loop fusion | flops 4718592 | bytes 5249024 | tf_op jit(solution)/shard_map/convert_element_type | solution.py:412
  (94 shorter events, 16.8 us)
Async XLA Ops:
  4.3 61.0 %all-to-all-start = ((bf16[32,256,128]{2,1,0:T(8,128)(2,1)}), bf16[32,256,128]{2,1,0:T(8,128)(2,1)}, u32[]{:S(2)}, u32[]{:S(2)}) async-start(bf16[32,256,128]{2,1,0:T(8,128)(2,1)} %shard_map.122.after), calls=%async_computation | async-start | bytes 4194304 | tf_op jit(solution)/shard_map/all_to_all | solution.py:361
  19.7 8.4 %copy-start.8 = (bf16[512,128]{1,0:T(8,128)(2,1)S(1)}, bf16[512,128]{1,0:T(8,128)(2,1)}, u32[]{:S(2)}) copy-start(bf16[512,128]{1,0:T(8,128)(2,1)} %param.12) | copy-start | bytes 393220
  19.7 8.4 %copy-start.9 = (bf16[512,128]{1,0:T(8,128)(2,1)S(1)}, bf16[512,128]{1,0:T(8,128)(2,1)}, u32[]{:S(2)}) copy-start(bf16[512,128]{1,0:T(8,128)(2,1)} %param.13) | copy-start | bytes 393220
  19.7 8.5 %copy-start.12 = (s32[1,32]{1,0:T(1,128)S(1)}, s32[1,32]{1,0:T(1,128)}, u32[]{:S(2)}) copy-start(s32[1,32]{1,0:T(1,128)} %param.15) | copy-start | bytes 388
  19.7 26.5 %copy-start.11 = (s32[1,32]{1,0:T(1,128)S(1)}, s32[1,32]{1,0:T(1,128)}, u32[]{:S(2)}) copy-start(s32[1,32]{1,0:T(1,128)} %param.16) | copy-start | bytes 388
  19.8 26.4 %collective-permute-start = (bf16[512,1024]{1,0:T(8,128)(2,1)}, bf16[512,1024]{1,0:T(8,128)(2,1)S(1)}, u32[]{:S(2)}, u32[]{:S(2)}) collective-permute-start(bf16[512,1024]{1,0:T(8,128)(2,1)} %get-tuple-element.39), channel_id=1, source_target_pairs={{0,2},{1,3},{2,0},{3,1},{4,6},{5,7},{6,4},{7,5},{8,10},{9,11},{10,... | collective-permute-start | bytes 3145736 | tf_op jit(solution)/shard_map/ppermute | solution.py:352
  21.4 35.7 %collective-permute-start.1 = (bf16[512,1024]{1,0:T(8,128)(2,1)}, bf16[512,1024]{1,0:T(8,128)(2,1)}, u32[]{:S(2)}, u32[]{:S(2)}) collective-permute-start(bf16[512,1024]{1,0:T(8,128)(2,1)} %get-tuple-element.40), channel_id=1, source_target_pairs={{0,6},{1,7},{2,4},{3,5},{4,2},{5,3},{6,0},{7,1},{8,14},{9,15},{10,... | collective-permute-start | bytes 3145736 | tf_op jit(solution)/shard_map/ppermute | solution.py:352
  23.6 46.9 %collective-permute-start.4 = (bf16[512,1024]{1,0:T(8,128)(2,1)}, bf16[512,1024]{1,0:T(8,128)(2,1)}, u32[]{:S(2)}, u32[]{:S(2)}) collective-permute-start(bf16[512,1024]{1,0:T(8,128)(2,1)} %get-tuple-element.49), channel_id=1, source_target_pairs={{0,3},{1,2},{2,1},{3,0},{4,7},{5,6},{6,5},{7,4},{8,11},{9,10},{10,... | collective-permute-start | bytes 3145736 | tf_op jit(solution)/shard_map/ppermute | solution.py:352
  27.2 29.9 %collective-permute-start.2 = (bf16[512,1024]{1,0:T(8,128)(2,1)}, bf16[512,1024]{1,0:T(8,128)(2,1)}, u32[]{:S(2)}, u32[]{:S(2)}) collective-permute-start(bf16[512,1024]{1,0:T(8,128)(2,1)} %get-tuple-element.42), channel_id=1, source_target_pairs={{0,1},{1,0},{2,3},{3,2},{4,5},{5,4},{6,7},{7,6},{8,9},{9,8},{10,11... | collective-permute-start | bytes 3145736 | tf_op jit(solution)/shard_map/ppermute | solution.py:352
  28.0 29.1 %collective-permute-start.3 = (bf16[512,1024]{1,0:T(8,128)(2,1)}, bf16[512,1024]{1,0:T(8,128)(2,1)}, u32[]{:S(2)}, u32[]{:S(2)}) collective-permute-start(bf16[512,1024]{1,0:T(8,128)(2,1)} %get-tuple-element.43), channel_id=1, source_target_pairs={{0,1},{1,0},{2,3},{3,2},{4,5},{5,4},{6,7},{7,6},{8,9},{9,8},{10,11... | collective-permute-start | bytes 3145736 | tf_op jit(solution)/shard_map/ppermute | solution.py:352
  46.2 1.5 %copy-start.5 = (bf16[512,1024]{1,0:T(8,128)(2,1)}, bf16[512,1024]{1,0:T(8,128)(2,1)S(1)}, u32[]{:S(2)}) copy-start(bf16[512,1024]{1,0:T(8,128)(2,1)S(1)} %collective-permute-done) | copy-start | bytes 3145732
  46.2 26.5 %collective-permute-start.5 = (bf16[512,1024]{1,0:T(8,128)(2,1)S(1)}, bf16[512,1024]{1,0:T(8,128)(2,1)}, u32[]{:S(2)}, u32[]{:S(2)}) collective-permute-start(bf16[512,1024]{1,0:T(8,128)(2,1)S(1)} %get-tuple-element.50), channel_id=1, source_target_pairs={{0,7},{1,6},{2,5},{3,4},{4,3},{5,2},{6,1},{7,0},{8,15},{9,14},{10,... | collective-permute-start | bytes 3145736 | tf_op jit(solution)/shard_map/ppermute | solution.py:352
  72.7 8.3 %collective-permute-start.8 = (bf16[256,512]{1,0:T(8,128)(2,1)S(1)}, bf16[256,512]{1,0:T(8,128)(2,1)S(1)}, u32[]{:S(2)}, u32[]{:S(2)}) collective-permute-start(bf16[256,512]{1,0:T(8,128)(2,1)S(1)} %shard_map.126), channel_id=1, source_target_pairs={{0,1},{1,0},{2,3},{3,2},{4,5},{5,4},{6,7},{7,6},{8,9},{9,8},{10,11... | collective-permute-start | bytes 786440 | tf_op jit(solution)/shard_map/ppermute | solution.py:352
  72.8 18.1 %collective-permute-start.7 = (bf16[256,512]{1,0:T(8,128)(2,1)S(1)}, bf16[256,512]{1,0:T(8,128)(2,1)S(1)}, u32[]{:S(2)}, u32[]{:S(2)}) collective-permute-start(bf16[256,512]{1,0:T(8,128)(2,1)S(1)} %shard_map.126), channel_id=1, source_target_pairs={{0,6},{1,7},{2,4},{3,5},{4,2},{5,3},{6,0},{7,1},{8,14},{9,15},{10,... | collective-permute-start | bytes 786440 | tf_op jit(solution)/shard_map/ppermute | solution.py:352
  73.7 17.2 %collective-permute-start.6 = (bf16[256,512]{1,0:T(8,128)(2,1)S(1)}, bf16[256,512]{1,0:T(8,128)(2,1)S(1)}, u32[]{:S(2)}, u32[]{:S(2)}) collective-permute-start(bf16[256,512]{1,0:T(8,128)(2,1)S(1)} %shard_map.126), channel_id=1, source_target_pairs={{0,2},{1,3},{2,0},{3,1},{4,6},{5,7},{6,4},{7,5},{8,10},{9,11},{10,... | collective-permute-start | bytes 786440 | tf_op jit(solution)/shard_map/ppermute | solution.py:352
  78.6 5.9 %collective-permute-start.15 = (bf16[256,512]{1,0:T(8,128)(2,1)S(1)}, bf16[256,512]{1,0:T(8,128)(2,1)S(1)}, u32[]{:S(2)}, u32[]{:S(2)}) collective-permute-start(bf16[256,512]{1,0:T(8,128)(2,1)S(1)} %shard_map.127), channel_id=1, source_target_pairs={{0,1},{1,0},{2,3},{3,2},{4,5},{5,4},{6,7},{7,6},{8,9},{9,8},{10,11... | collective-permute-start | bytes 786440 | tf_op jit(solution)/shard_map/ppermute | solution.py:352
  78.7 19.5 %collective-permute-start.14 = (bf16[256,512]{1,0:T(8,128)(2,1)S(1)}, bf16[256,512]{1,0:T(8,128)(2,1)S(1)}, u32[]{:S(2)}, u32[]{:S(2)}) collective-permute-start(bf16[256,512]{1,0:T(8,128)(2,1)S(1)} %shard_map.127), channel_id=1, source_target_pairs={{0,6},{1,7},{2,4},{3,5},{4,2},{5,3},{6,0},{7,1},{8,14},{9,15},{10,... | collective-permute-start | bytes 786440 | tf_op jit(solution)/shard_map/ppermute | solution.py:352
  81.0 17.2 %collective-permute-start.13 = (bf16[256,512]{1,0:T(8,128)(2,1)S(1)}, bf16[256,512]{1,0:T(8,128)(2,1)S(1)}, u32[]{:S(2)}, u32[]{:S(2)}) collective-permute-start(bf16[256,512]{1,0:T(8,128)(2,1)S(1)} %shard_map.127), channel_id=1, source_target_pairs={{0,2},{1,3},{2,0},{3,1},{4,6},{5,7},{6,4},{7,5},{8,10},{9,11},{10,... | collective-permute-start | bytes 786440 | tf_op jit(solution)/shard_map/ppermute | solution.py:352
  90.9 2.9 %collective-permute-start.9 = (bf16[256,512]{1,0:T(8,128)(2,1)S(1)}, bf16[256,512]{1,0:T(8,128)(2,1)S(1)}, u32[]{:S(2)}, u32[]{:S(2)}) collective-permute-start(bf16[256,512]{1,0:T(8,128)(2,1)S(1)} %collective-permute-done.6), channel_id=1, source_target_pairs={{0,1},{1,0},{2,3},{3,2},{4,5},{5,4},{6,7},{7,6},{8,9},{9,8},{10,11... | collective-permute-start | bytes 786440 | tf_op jit(solution)/shard_map/ppermute | solution.py:352
  91.0 5.5 %collective-permute-start.11 = (bf16[256,512]{1,0:T(8,128)(2,1)S(1)}, bf16[256,512]{1,0:T(8,128)(2,1)S(1)}, u32[]{:S(2)}, u32[]{:S(2)}) collective-permute-start(bf16[256,512]{1,0:T(8,128)(2,1)S(1)} %collective-permute-done.7), channel_id=1, source_target_pairs={{0,1},{1,0},{2,3},{3,2},{4,5},{5,4},{6,7},{7,6},{8,9},{9,8},{10,11... | collective-permute-start | bytes 786440 | tf_op jit(solution)/shard_map/ppermute | solution.py:352
  95.5 12.6 %collective-permute-start.10 = (bf16[256,512]{1,0:T(8,128)(2,1)S(1)}, bf16[256,512]{1,0:T(8,128)(2,1)S(1)}, u32[]{:S(2)}, u32[]{:S(2)}) collective-permute-start(bf16[256,512]{1,0:T(8,128)(2,1)S(1)} %slice.55), channel_id=1, source_target_pairs={{0,6},{1,7},{2,4},{3,5},{4,2},{5,3},{6,0},{7,1},{8,14},{9,15},{10,... | collective-permute-start | bytes 786440 | tf_op jit(solution)/shard_map/ppermute | solution.py:352
  98.7 2.3 %collective-permute-start.16 = (bf16[256,512]{1,0:T(8,128)(2,1)S(1)}, bf16[256,512]{1,0:T(8,128)(2,1)S(1)}, u32[]{:S(2)}, u32[]{:S(2)}) collective-permute-start(bf16[256,512]{1,0:T(8,128)(2,1)S(1)} %collective-permute-done.13), channel_id=1, source_target_pairs={{0,1},{1,0},{2,3},{3,2},{4,5},{5,4},{6,7},{7,6},{8,9},{9,8},{10,11... | collective-permute-start | bytes 786440 | tf_op jit(solution)/shard_map/ppermute | solution.py:352
  98.8 9.4 %collective-permute-start.12 = (bf16[256,512]{1,0:T(8,128)(2,1)S(1)}, bf16[256,512]{1,0:T(8,128)(2,1)S(1)}, u32[]{:S(2)}, u32[]{:S(2)}) collective-permute-start(bf16[256,512]{1,0:T(8,128)(2,1)S(1)} %slice.54), channel_id=1, source_target_pairs={{0,2},{1,3},{2,0},{3,1},{4,6},{5,7},{6,4},{7,5},{8,10},{9,11},{10,... | collective-permute-start | bytes 786440 | tf_op jit(solution)/shard_map/ppermute | solution.py:352
  99.0 6.1 %collective-permute-start.18 = (bf16[256,512]{1,0:T(8,128)(2,1)S(1)}, bf16[256,512]{1,0:T(8,128)(2,1)S(1)}, u32[]{:S(2)}, u32[]{:S(2)}) collective-permute-start(bf16[256,512]{1,0:T(8,128)(2,1)S(1)} %collective-permute-done.14), channel_id=1, source_target_pairs={{0,1},{1,0},{2,3},{3,2},{4,5},{5,4},{6,7},{7,6},{8,9},{9,8},{10,11... | collective-permute-start | bytes 786440 | tf_op jit(solution)/shard_map/ppermute | solution.py:352
  102.6 9.8 %collective-permute-start.17 = (bf16[256,512]{1,0:T(8,128)(2,1)S(1)}, bf16[256,512]{1,0:T(8,128)(2,1)S(1)}, u32[]{:S(2)}, u32[]{:S(2)}) collective-permute-start(bf16[256,512]{1,0:T(8,128)(2,1)S(1)} %slice.53), channel_id=1, source_target_pairs={{0,6},{1,7},{2,4},{3,5},{4,2},{5,3},{6,0},{7,1},{8,14},{9,15},{10,... | collective-permute-start | bytes 786440 | tf_op jit(solution)/shard_map/ppermute | solution.py:352
  106.8 8.2 %collective-permute-start.19 = (bf16[256,512]{1,0:T(8,128)(2,1)S(1)}, bf16[256,512]{1,0:T(8,128)(2,1)S(1)}, u32[]{:S(2)}, u32[]{:S(2)}) collective-permute-start(bf16[256,512]{1,0:T(8,128)(2,1)S(1)} %slice.52), channel_id=1, source_target_pairs={{0,2},{1,3},{2,0},{3,1},{4,6},{5,7},{6,4},{7,5},{8,10},{9,11},{10,... | collective-permute-start | bytes 786440 | tf_op jit(solution)/shard_map/ppermute | solution.py:352
  108.1 7.0 %copy-start.7 = (bf16[512,1024]{1,0:T(8,128)(2,1)S(1)}, bf16[512,1024]{1,0:T(8,128)(2,1)}, u32[]{:S(2)}) copy-start(bf16[512,1024]{1,0:T(8,128)(2,1)} %param.14) | copy-start | bytes 3145732
  112.5 10.9 %copy-start.10 = (f32[1024]{0:T(1024)S(1)}, f32[1024]{0:T(1024)}, u32[]{:S(2)}) copy-start(f32[1024]{0:T(1024)} %param.21) | copy-start | bytes 12292
  115.5 1.2 collective-permute-start.20
  116.7 4.8 %collective-permute-start.23 = (f32[512]{0:T(512)S(1)}, f32[512]{0:T(512)S(1)}, u32[]{:S(2)}, u32[]{:S(2)}) collective-permute-start(f32[512]{0:T(512)S(1)} %add.170), channel_id=1, source_target_pairs={{0,6},{1,7},{2,4},{3,5},{4,2},{5,3},{6,0},{7,1},{8,14},{9,15},{10,... | collective-permute-start | bytes 6152 | tf_op jit(solution)/shard_map/ppermute | solution.py:352
  117.7 3.8 %collective-permute-start.22 = (f32[512]{0:T(512)S(1)}, f32[512]{0:T(512)S(1)}, u32[]{:S(2)}, u32[]{:S(2)}) collective-permute-start(f32[512]{0:T(512)S(1)} %add.170), channel_id=1, source_target_pairs={{0,2},{1,3},{2,0},{3,1},{4,6},{5,7},{6,4},{7,5},{8,10},{9,11},{10,... | collective-permute-start | bytes 6152 | tf_op jit(solution)/shard_map/ppermute | solution.py:352
  118.3 5.1 %collective-permute-start.21 = (f32[512]{0:T(512)S(1)}, f32[512]{0:T(512)S(1)}, u32[]{:S(2)}, u32[]{:S(2)}) collective-permute-start(f32[512]{0:T(512)S(1)} %add.170), channel_id=1, source_target_pairs={{0,4},{1,5},{2,6},{3,7},{4,0},{5,1},{6,2},{7,3},{8,12},{9,13},{10,... | collective-permute-start | bytes 6152 | tf_op jit(solution)/shard_map/ppermute | solution.py:352
  (6 other events, 5.9 us)

commit v4 on v3

--- a/solution.py
+++ b/solution.py
@@ -117,9 +117,23 @@
     lax.fori_loop(0, 512 // BLOCK, body, 0, unroll=2)
 
 
-def main_kernel(
-    first, plan, q, cache_hbm, mean_hbm, level_hbm, out, cache, means, levels, scores, weights, mixed, sems
-):
+def main_kernel(first, plan, starts, q, cache_hbm, mean_hbm, level_hbm, *refs):
+    cache, means, levels, scores, weights, mixed, sems, stage_sems = refs[-8:]
+    count = (len(refs) - 9) // 2
+    sources, out, staged = refs[:count], refs[count], refs[count + 1 : -8]
+    stage = []
+    for place_of, (source, target) in enumerate(zip(sources, staged)):
+        if source.shape == target.shape:
+            parts = [(source, target)]
+        elif source.shape[1] == 2 * target.shape[1]:
+            parts = [(source.at[:, pl.ds(1024 * (place_of % 2), 1024)], target)]
+        else:
+            parts = [
+                (source.at[:, pl.ds(pl.multiple_of(starts[i], 512), 512)], target.at[:, pl.ds(512 * (i % 2), 512)])
+                for i in range(len(stage), len(stage) + 2)
+            ]
+        for origin, goal in parts:
+            stage.append(pltpu.make_async_copy(origin, goal, stage_sems.at[len(stage)]))
     half = cache.shape[1] // 2
     fetch = [
         pltpu.make_async_copy(
@@ -132,6 +146,8 @@
     fetch.append(pltpu.make_async_copy(mean_hbm.at[blocks], means, sems.at[3]))
     for i in (0, 2, 3, 1):
         fetch[i].start()
+    for copy in stage:
+        copy.start()
     ones = jnp.ones((16, HD), jnp.bfloat16)
     ahead = plan[4, 0]
     if first == 0:
@@ -202,6 +218,8 @@
         base = block * BLOCK
         for h in range(GROUP):
             out[base : base + BLOCK, h * HD : (h + 1) * HD] = total[h * BLOCK : (h + 1) * BLOCK]
+    for copy in stage:
+        copy.wait()
 
 
 def whole(count):
@@ -296,16 +314,18 @@
     )(queries, jnp.pad(new_keys, front), jnp.pad(new_values, front), row_start)
 
 
-def attend(first, plan, queries, cache, fresh_mean, fresh_level):
-    area = fresh_mean.shape[1:]
+def attend(first, plan, starts, queries, cache, fresh, sources=()):
+    area = fresh[0].shape[1:]
+    rows = jax.ShapeDtypeStruct((PIECE * BLOCK, queries.shape[1]), queries.dtype)
+    staged = [pltpu.VMEM((source.shape[0], 1024), source.dtype) for source in sources]
     return pl.pallas_call(
         functools.partial(main_kernel, first),
-        out_shape=jax.ShapeDtypeStruct((PIECE * BLOCK, queries.shape[1]), queries.dtype),
+        out_shape=(rows, *staged),
         grid_spec=pltpu.PrefetchScalarGridSpec(
-            num_scalar_prefetch=1,
+            num_scalar_prefetch=2,
             grid=(),
-            in_specs=whole(1) + anywhere(3),
-            out_specs=whole(1)[0],
+            in_specs=whole(1) + anywhere(3 + len(sources)),
+            out_specs=tuple(whole(1 + len(staged))),
             scratch_shapes=[
                 pltpu.VMEM(cache.shape, cache.dtype),
                 pltpu.VMEM((PIECE, *area), jnp.float32),
@@ -314,20 +334,21 @@
                 pltpu.VMEM((PIECE + 1, *area), jnp.bfloat16),
                 pltpu.VMEM((PIECE + 1, *area), jnp.float32),
                 pltpu.SemaphoreType.DMA((4,)),
+                pltpu.SemaphoreType.DMA((len(sources) + 2,)),
             ],
         ),
-        compiler_params=pltpu.CompilerParams(vmem_limit_bytes=7 << 20),
+        compiler_params=pltpu.CompilerParams(vmem_limit_bytes=(7 + len(sources)) << 20),
         cost_estimate=pl.CostEstimate(
             flops=1 << 31, bytes_accessed=4 << 20, transcendentals=1 << 18
         ),
-    )(plan, queries, cache, *in_hbm(fresh_mean, fresh_level))
+    )(plan, starts, queries, cache, *in_hbm(*fresh), *in_hbm(*sources))
 
 
 def attention(counts, packs, queries, marked, values, new_keys, new_values):
     plan, row_start = pair_plan(counts, packs)
     fresh = attend_fresh(queries, new_keys, new_values, row_start)
     cache = jnp.concatenate([marked, values], axis=1)
-    return jnp.concatenate([attend(i, plan, queries, cache, *fresh) for i in (0, PIECE)], axis=0)
+    return jnp.concatenate([attend(i, plan, plan[0], queries, cache, fresh)[0] for i in (0, PIECE)], axis=0)
 
 
 def on_device(
@@ -362,20 +383,19 @@
 
     starts = sum([shared(mask)[half] for mask, half in ((2, 0), (6, 1), (3, 0), (7, 1))], [])
     pieces = cut(jnp.stack(starts), out_weight, (1024,) * 4, payload)
-    starts, pieces = lax.optimization_barrier(
-        (jnp.stack(sum(shared(1), []) + sum(shared(0), [])), pieces)
-    )
-    same = [swap(piece, mask) for piece, mask in zip(pieces[:2], (2, 6))]
-    cross = [swap(piece, mask) for piece, mask in zip(pieces[2:], (3, 7))]
-    pieces = cut(starts, out_weight, (1024,) * 4, payload)
-    sibling = [swap(piece, 1) for piece in pieces[:2]]
-    here = pieces[2:]
+    starts, pieces = lax.optimization_barrier((jnp.stack(sum(shared(1), [])), pieces))
+    near_mats = [swap(piece, mask) for piece, mask in zip(pieces, (2, 6, 3, 7))]
+    sibling = swap(cut(starts, out_weight, (2048,), payload)[0], 1)
 
     plan, row_start = pair_plan(row_counts[0], pack_of[0])
     fresh = attend_fresh(queries, new_keys, new_values, row_start)
-    plan, same, sibling, here = lax.optimization_barrier((plan, same, sibling, here))
-    attended = [attend(first, plan, queries, cache, *fresh) for first in (0, PIECE)]
-    attended[0], cross = lax.optimization_barrier((attended[0], cross))
+    plan, sibling, near_mats[:2] = lax.optimization_barrier((plan, sibling, near_mats[:2]))
+    starts = jnp.stack(sum(shared(0), []))
+    attended = attend(0, plan, starts, queries, cache, fresh)
+    sources = (out_weight, out_weight, sibling, sibling, *near_mats)
+    rest, *mats = attend(PIECE, plan, starts, queries, cache, fresh, sources)
+    attended = [attended[0], rest]
+    here, sibling, same, cross = (mats[i : i + 2] for i in (0, 2, 4, 6))
 
     def times(rows, mat):
         return jnp.dot(rows, mat, preferred_element_type=f32)

time: 126 us -> 114 us (0.905)
  matrix products: 19.2 us -> 7 us
  local copies, waits for them, and re-layouts: 5.98 us -> 3.66 us
  starting transfers between devices: 32.1 us -> 34.2 us
  waiting for transfers between devices: 37.9 us -> 40 us
    dot_general x16, matrix products: 19.2 us -> 7 us  [times(): return jnp.dot(rows, mat, preferred_element_type=f32)]
    all_to_all x1, waiting for transfers between devices: 8.17 us -> 12.4 us  [on_device(): lax.all_to_all(payload, 'dp', split_axis=0, concat_axis=0, tiled=True)]
    unnamed x26 -> x20, local copies, waits for them, and re-layouts: 4.85 us -> 2.62 us
    ppermute x24 -> x23, waiting for transfers between devices: 29.7 us -> 27.5 us  [swap(): return lax.ppermute(value, 'tensor', [(t, t ^ mask) for t in range(count)])]
    ppermute x24 -> x23, starting transfers between devices: 20.5 us -> 22.5 us  [swap(): return lax.ppermute(value, 'tensor', [(t, t ^ mask) for t in range(count)])]
  transfers between devices with their start and end apart: 25 -> 24, of which waited for: 8 -> 12; matrix products, arithmetic and copies ran while one was open for 17% -> 8% of each run, Pallas kernels for 18% -> 19%
where the time goes in v4:
time: 114 us
  waiting for transfers between devices  40 us (35%)
  starting transfers between devices  34.2 us (30%)
  Pallas kernels  24.2 us (21%)
  matrix products  7 us (6%)
  other arithmetic  3.69 us (3%)
  local copies, waits for them, and re-layouts  3.66 us (3%)
    ppermute x23, waiting for transfers between devices, swap(): return lax.ppermute(value, 'tensor', [(t, t ^ mask) for t in range(count)])  27.5 us
    ppermute x23, starting transfers between devices, swap(): return lax.ppermute(value, 'tensor', [(t, t ^ mask) for t in range(count)])  22.5 us
    all_to_all x1, waiting for transfers between devices, on_device(): lax.all_to_all(payload, 'dp', split_axis=0, concat_axis=0, tiled=True)  12.4 us
    all_to_all x1, starting transfers between devices, on_device(): lax.all_to_all(payload, 'dp', split_axis=0, concat_axis=0, tiled=True)  11.6 us
    pallas_call x2, Pallas kernels, attend(): pl.pallas_call(functools.partial(main_kernel, first), out_shape=(rows, *s...  7.76 us
    pallas_call x2, Pallas kernels, cut(): pl.pallas_call(cut_kernel, out_shape=tuple((jax.ShapeDtypeStruct((rows, w...  7.3 us
    dot_general x16, matrix products, times(): return jnp.dot(rows, mat, preferred_element_type=f32)  7 us
    pallas_call x1, Pallas kernels, attend_fresh(): pl.pallas_call(fresh_kernel, out_shape=(area, area), in_specs=whole(4), o...  6.17 us
  transfers between devices with their start and end apart: 24, of which 12 were waited for; matrix products, arithmetic and copies ran while one was open for 8% of the time, Pallas kernels for 19%

profile of v4, /device:TPU:2, one launch (start us, length us, event | category | flops | bytes accessed | tf_op | source)
XLA Modules:
  0.0 113.8 jit_solution(11016656174384288660)
XLA Ops:
  1.3 3.0 %shard_map.122.after = bf16[32,256,128]{2,1,0:T(8,128)(2,1)} custom-call(s32[1,32]{1,0:T(1,128)S(1)} %copy-done.3, bf16[32,128,128]{2,1,0:T(8,128)(2,1)} %bitcast.80, bf16[32,128,128]{2,1,0:T(8,128)(2,1)} %bitcast.81), custom_call_target="tpu_custom_call" | custom-call | flops 1048576 | bytes 4194304 | tf_op jit(solution)/shard_map/pallas_call | solution.py:243
  4.3 11.6 %all-to-all-start = ((bf16[32,256,128]{2,1,0:T(8,128)(2,1)}), bf16[32,256,128]{2,1,0:T(8,128)(2,1)S(1)}, u32[]{:S(2)}, u32[]{:S(2)}) async-start(bf16[32,256,128]{2,1,0:T(8,128)(2,1)} %shard_map.122.after), calls=%async_computation | async-start | bytes 4194304 | tf_op jit(solution)/shard_map/all_to_all | solution.py:382
  16.0 4.3 %shard_map.123 = (bf16[512,1024]{1,0:T(8,128)(2,1)}, bf16[512,1024]{1,0:T(8,128)(2,1)}, bf16[512,1024]{1,0:T(8,128)(2,1)}, bf16[512,1024]{1,0:T(8,128)(2,1)}) custom-call(s32[8]{0:T(128)S(1)} %stack.90.starts, bf16[512,8192]{1,0:T(8,128)(2,1)} %refs_1_.1, bf16[32,256,128]{2,1,0:T(8,128)(2,1)} %shard_map.122.after), custom_call_target="tpu_custom_call" | custom-call | bytes 12582912 | tf_op jit(solution)/shard_map/pallas_call | solution.py:284
  20.5 3.0 %shard_map.124 = bf16[512,2048]{1,0:T(8,128)(2,1)} custom-call(s32[4]{0:T(128)S(1)} %pad_add_fusion.starts, bf16[512,8192]{1,0:T(8,128)(2,1)} %refs_1_.1, bf16[32,256,128]{2,1,0:T(8,128)(2,1)} %shard_map.122.after), custom_call_target="tpu_custom_call" | custom-call | bytes 12582912 | tf_op jit(solution)/shard_map/pallas_call | solution.py:284
  23.6 1.7 %collective-permute-start.1 = (bf16[512,1024]{1,0:T(8,128)(2,1)}, bf16[512,1024]{1,0:T(8,128)(2,1)}, u32[]{:S(2)}, u32[]{:S(2)}) collective-permute-start(bf16[512,1024]{1,0:T(8,128)(2,1)} %get-tuple-element.39), channel_id=1, source_target_pairs={{0,2},{1,3},{2,0},{3,1},{4,6},{5,7},{6,4},{7,5},{8,10},{9,11},{10,... | collective-permute-start | bytes 3145736 | tf_op jit(solution)/shard_map/ppermute | solution.py:373
  25.2 2.2 %collective-permute-start.2 = (bf16[512,1024]{1,0:T(8,128)(2,1)}, bf16[512,1024]{1,0:T(8,128)(2,1)}, u32[]{:S(2)}, u32[]{:S(2)}) collective-permute-start(bf16[512,1024]{1,0:T(8,128)(2,1)} %get-tuple-element.40), channel_id=1, source_target_pairs={{0,6},{1,7},{2,4},{3,5},{4,2},{5,3},{6,0},{7,1},{8,14},{9,15},{10,... | collective-permute-start | bytes 3145736 | tf_op jit(solution)/shard_map/ppermute | solution.py:373
  27.6 0.9 collective-permute-start.6
  30.6 6.2 %shard_map.125 = (f32[16,128,128]{2,1,0:T(8,128)S(1)}, f32[16,128,128]{2,1,0:T(8,128)S(1)}) custom-call(bf16[512,512]{1,0:T(8,128)(2,1)S(1)} %copy-done.2, bf16[608,128]{1,0:T(8,128)(2,1)S(1)} %pad.7.fresh_k, bf16[608,128]{1,0:T(8,128)(2,1)S(1)} %pad.8.fresh_v, s32[512,128]{1,0:T(8,128)S(1)} %broadcast_in_dim.105.row_start), custom_call_target="tpu_custom_call" | custom-call | flops 2147483648 | bytes 4194304 | tf_op jit(solution)/shard_map/pallas_call | solution.py:305
  36.8 1.0 copy-done
  37.8 1.0 copy-done.1
  38.7 11.2 %collective-permute-done.1.refs_4_ = bf16[512,1024]{1,0:T(8,128)(2,1)} collective-permute-done((bf16[512,1024]{1,0:T(8,128)(2,1)}, bf16[512,1024]{1,0:T(8,128)(2,1)}, u32[]{:S(2)}, u32[]{:S(2)}) %collective-permute-start.1) | collective-permute-done | bytes 1048608 | tf_op jit(solution)/shard_map/ppermute | solution.py:373
  49.9 2.8 %collective-permute-done.2.refs_5_ = bf16[512,1024]{1,0:T(8,128)(2,1)} collective-permute-done((bf16[512,1024]{1,0:T(8,128)(2,1)}, bf16[512,1024]{1,0:T(8,128)(2,1)}, u32[]{:S(2)}, u32[]{:S(2)}) %collective-permute-start.2) | collective-permute-done | bytes 1048608 | tf_op jit(solution)/shard_map/ppermute | solution.py:373
  52.8 12.4 %all-to-all-done.cache_hbm = bf16[32,256,128]{2,1,0:T(8,128)(2,1)S(1)} async-done(((bf16[32,256,128]{2,1,0:T(8,128)(2,1)}), bf16[32,256,128]{2,1,0:T(8,128)(2,1)S(1)}, u32[]{:S(2)}, u32[]{:S(2)}) %all-to-all-start) | async-done | bytes 2097184 | tf_op jit(solution)/shard_map/all_to_all | solution.py:382
  65.2 3.2 %shard_map.126 = bf16[256,512]{1,0:T(8,128)(2,1)S(1)} custom-call(s32[5,48]{1,0:T(8,128)S(1)} %stack.76.plan, s32[4]{0:T(128)S(1)} %pad_add_fusion.1.starts, bf16[512,512]{1,0:T(8,128)(2,1)S(1)} %copy-done.2, bf16[32,256,128]{2,1,0:T(8,128)(2,1)S(1)} %all-to-all-done.cache_hbm, f32[16,128,128]{2,1,0:T(8,128)} %copy-done, f32[16,128,128]{2,1,0:T(8,128)} %copy-done.1), custom_call_target="tpu_custom_call" | custom-call | flops 2147483648 | bytes 4194304 | tf_op jit(solution)/shard_map/pallas_call | solution.py:321
  68.5 1.6 %collective-permute-start.3 = (bf16[256,512]{1,0:T(8,128)(2,1)S(1)}, bf16[256,512]{1,0:T(8,128)(2,1)S(1)}, u32[]{:S(2)}, u32[]{:S(2)}) collective-permute-start(bf16[256,512]{1,0:T(8,128)(2,1)S(1)} %shard_map.126), channel_id=1, source_target_pairs={{0,2},{1,3},{2,0},{3,1},{4,6},{5,7},{6,4},{7,5},{8,10},{9,11},{10,... | collective-permute-start | bytes 786440 | tf_op jit(solution)/shard_map/ppermute | solution.py:373
  70.2 2.2 %collective-permute-start.4 = (bf16[256,512]{1,0:T(8,128)(2,1)S(1)}, bf16[256,512]{1,0:T(8,128)(2,1)S(1)}, u32[]{:S(2)}, u32[]{:S(2)}) collective-permute-start(bf16[256,512]{1,0:T(8,128)(2,1)S(1)} %shard_map.126), channel_id=1, source_target_pairs={{0,6},{1,7},{2,4},{3,5},{4,2},{5,3},{6,0},{7,1},{8,14},{9,15},{10,... | collective-permute-start | bytes 786440 | tf_op jit(solution)/shard_map/ppermute | solution.py:373
  72.3 1.3 %collective-permute-done.6.refs_7_ = bf16[512,1024]{1,0:T(8,128)(2,1)} collective-permute-done((bf16[512,1024]{1,0:T(8,128)(2,1)}, bf16[512,1024]{1,0:T(8,128)(2,1)}, u32[]{:S(2)}, u32[]{:S(2)}) %collective-permute-start.6) | collective-permute-done | bytes 1048608 | tf_op jit(solution)/shard_map/ppermute | solution.py:373
  73.7 4.5 %shard_map.127 = (bf16[256,512]{1,0:T(8,128)(2,1)S(1)}, bf16[512,1024]{1,0:T(8,128)(2,1)S(1)}, bf16[512,1024]{1,0:T(8,128)(2,1)S(1)}, bf16[512,1024]{1,0:T(8,128...) custom-call(s32[5,48]{1,0:T(8,128)S(1)} %stack.76.plan, ...), custom_call_target="tpu_custom_call" | custom-call | flops 2147483648 | bytes 4194304 | tf_op jit(solution)/shard_map/pallas_call | solution.py:321
  78.2 0.9 collective-permute-start.14
  79.2 2.3 %collective-permute-start.13 = (bf16[256,512]{1,0:T(8,128)(2,1)S(1)}, bf16[256,512]{1,0:T(8,128)(2,1)S(1)}, u32[]{:S(2)}, u32[]{:S(2)}) collective-permute-start(bf16[256,512]{1,0:T(8,128)(2,1)S(1)} %get-tuple-element.61), channel_id=1, source_target_pairs={{0,6},{1,7},{2,4},{3,5},{4,2},{5,3},{6,0},{7,1},{8,14},{9,15},{10,... | collective-permute-start | bytes 786440 | tf_op jit(solution)/shard_map/ppermute | solution.py:373
  87.1 1.0 collective-permute-start.9
  91.9 2.3 %collective-permute-start.16 = (bf16[256,512]{1,0:T(8,128)(2,1)S(1)}, bf16[256,512]{1,0:T(8,128)(2,1)S(1)}, u32[]{:S(2)}, u32[]{:S(2)}) collective-permute-start(bf16[256,512]{1,0:T(8,128)(2,1)S(1)} %slice.53), channel_id=1, source_target_pairs={{0,6},{1,7},{2,4},{3,5},{4,2},{5,3},{6,0},{7,1},{8,14},{9,15},{10,... | collective-permute-start | bytes 786440 | tf_op jit(solution)/shard_map/ppermute | solution.py:373
  94.7 1.0 collective-permute-start.18
  95.6 1.9 %collective-permute-done.9 = bf16[256,512]{1,0:T(8,128)(2,1)S(1)} collective-permute-done((bf16[256,512]{1,0:T(8,128)(2,1)S(1)}, bf16[256,512]{1,0:T(8,128)(2,1)S(1)}, u32[]{:S(2)}, u32[]{:S(2)}) %collective-permute-start.9) | collective-permute-done | bytes 262176 | tf_op jit(solution)/shard_map/ppermute | solution.py:373
  97.7 4.8 %collective-permute-done.16 = bf16[256,512]{1,0:T(8,128)(2,1)S(1)} collective-permute-done((bf16[256,512]{1,0:T(8,128)(2,1)S(1)}, bf16[256,512]{1,0:T(8,128)(2,1)S(1)}, u32[]{:S(2)}, u32[]{:S(2)}) %collective-permute-start.16) | collective-permute-done | bytes 262176 | tf_op jit(solution)/shard_map/ppermute | solution.py:373
  103.4 1.1 %collective-permute-done.19 = f32[512]{0:T(512)S(1)} collective-permute-done((f32[512]{0:T(512)S(1)}, f32[512]{0:T(512)S(1)}, u32[]{:S(2)}, u32[]{:S(2)}) %collective-permute-start.19) | collective-permute-done | bytes 2080 | tf_op jit(solution)/shard_map/ppermute | solution.py:373
  104.5 2.0 %collective-permute-start.20 = (f32[512]{0:T(512)S(1)}, f32[512]{0:T(512)S(1)}, u32[]{:S(2)}, u32[]{:S(2)}) collective-permute-start(f32[512]{0:T(512)S(1)} %add.170), channel_id=1, source_target_pairs={{0,4},{1,5},{2,6},{3,7},{4,0},{5,1},{6,2},{7,3},{8,12},{9,13},{10,... | collective-permute-start | bytes 6152 | tf_op jit(solution)/shard_map/ppermute | solution.py:373
  106.5 0.9 collective-permute-start.21
  107.4 1.3 %collective-permute-start.22 = (f32[512]{0:T(512)S(1)}, f32[512]{0:T(512)S(1)}, u32[]{:S(2)}, u32[]{:S(2)}) collective-permute-start(f32[512]{0:T(512)S(1)} %add.170), channel_id=1, source_target_pairs={{0,6},{1,7},{2,4},{3,5},{4,2},{5,3},{6,0},{7,1},{8,14},{9,15},{10,... | collective-permute-start | bytes 6152 | tf_op jit(solution)/shard_map/ppermute | solution.py:373
  108.6 1.0 collective-permute-done.20
  110.1 2.1 %collective-permute-done.22 = f32[512]{0:T(512)S(1)} collective-permute-done((f32[512]{0:T(512)S(1)}, f32[512]{0:T(512)S(1)}, u32[]{:S(2)}, u32[]{:S(2)}) %collective-permute-start.22) | collective-permute-done | bytes 2080 | tf_op jit(solution)/shard_map/ppermute | solution.py:373
  112.2 1.7 %multiply_convert_fusion = (bf16[512,1024]{1,0:T(8,128)(2,1)}, bf16[512,1024]{1,0:T(8,128)(2,1)}) fusion(f32[1024]{0:T(1024)S(1)} %copy-done.7, f32[512]{0:T(512)S(1)} %add_rsqrt_fusion, f32[256,512]{1,0:T(8,128)S(1)} %slice_add_fusion, f32[256,512]{1,0:T(8,128)S(1)} %slice_add_fusion.1, f32[256,512]{1,0:T(8,128)S(1)} %slice_add_fusion.2, ...), kind=kLoop, calls=%fused_computation.1 | loop fusion | flops 4718592 | bytes 5249024 | tf_op jit(solution)/shard_map/convert_element_type | solution.py:432
  (87 shorter events, 14.6 us)
Async XLA Ops:
  4.3 60.9 %all-to-all-start = ((bf16[32,256,128]{2,1,0:T(8,128)(2,1)}), bf16[32,256,128]{2,1,0:T(8,128)(2,1)S(1)}, u32[]{:S(2)}, u32[]{:S(2)}) async-start(bf16[32,256,128]{2,1,0:T(8,128)(2,1)} %shard_map.122.after), calls=%async_computation | async-start | bytes 4194304 | tf_op jit(solution)/shard_map/all_to_all | solution.py:382
  20.4 8.0 %copy-start.9 = (s32[1,32]{1,0:T(1,128)S(1)}, s32[1,32]{1,0:T(1,128)}, u32[]{:S(2)}) copy-start(s32[1,32]{1,0:T(1,128)} %param.15) | copy-start | bytes 388
  20.4 8.3 %copy-start.5 = (bf16[512,128]{1,0:T(8,128)(2,1)S(1)}, bf16[512,128]{1,0:T(8,128)(2,1)}, u32[]{:S(2)}) copy-start(bf16[512,128]{1,0:T(8,128)(2,1)} %param.12) | copy-start | bytes 393220
  20.4 8.3 %copy-start.6 = (bf16[512,128]{1,0:T(8,128)(2,1)S(1)}, bf16[512,128]{1,0:T(8,128)(2,1)}, u32[]{:S(2)}) copy-start(bf16[512,128]{1,0:T(8,128)(2,1)} %param.13) | copy-start | bytes 393220
  20.5 8.4 %copy-start.8 = (s32[1,32]{1,0:T(1,128)S(1)}, s32[1,32]{1,0:T(1,128)}, u32[]{:S(2)}) copy-start(s32[1,32]{1,0:T(1,128)} %param.16) | copy-start | bytes 388
  20.5 10.1 %copy-start.2 = (bf16[512,512]{1,0:T(8,128)(2,1)S(1)}, bf16[512,512]{1,0:T(8,128)(2,1)}, u32[]{:S(2)}) copy-start(bf16[512,512]{1,0:T(8,128)(2,1)} %q.5) | copy-start | bytes 1572868
  23.5 29.3 %collective-permute-start = (bf16[512,2048]{1,0:T(8,128)(2,1)}, bf16[512,2048]{1,0:T(8,128)(2,1)}, u32[]{:S(2)}, u32[]{:S(2)}) collective-permute-start(bf16[512,2048]{1,0:T(8,128)(2,1)} %shard_map.124), channel_id=1, source_target_pairs={{0,1},{1,0},{2,3},{3,2},{4,5},{5,4},{6,7},{7,6},{8,9},{9,8},{10,11... | collective-permute-start | bytes 6291464 | tf_op jit(solution)/shard_map/ppermute | solution.py:373
  23.6 26.4 %collective-permute-start.1 = (bf16[512,1024]{1,0:T(8,128)(2,1)}, bf16[512,1024]{1,0:T(8,128)(2,1)}, u32[]{:S(2)}, u32[]{:S(2)}) collective-permute-start(bf16[512,1024]{1,0:T(8,128)(2,1)} %get-tuple-element.39), channel_id=1, source_target_pairs={{0,2},{1,3},{2,0},{3,1},{4,6},{5,7},{6,4},{7,5},{8,10},{9,11},{10,... | collective-permute-start | bytes 3145736 | tf_op jit(solution)/shard_map/ppermute | solution.py:373
  25.2 27.5 %collective-permute-start.2 = (bf16[512,1024]{1,0:T(8,128)(2,1)}, bf16[512,1024]{1,0:T(8,128)(2,1)}, u32[]{:S(2)}, u32[]{:S(2)}) collective-permute-start(bf16[512,1024]{1,0:T(8,128)(2,1)} %get-tuple-element.40), channel_id=1, source_target_pairs={{0,6},{1,7},{2,4},{3,5},{4,2},{5,3},{6,0},{7,1},{8,14},{9,15},{10,... | collective-permute-start | bytes 3145736 | tf_op jit(solution)/shard_map/ppermute | solution.py:373
  27.4 44.9 %collective-permute-start.5 = (bf16[512,1024]{1,0:T(8,128)(2,1)}, bf16[512,1024]{1,0:T(8,128)(2,1)}, u32[]{:S(2)}, u32[]{:S(2)}) collective-permute-start(bf16[512,1024]{1,0:T(8,128)(2,1)} %get-tuple-element.47), channel_id=1, source_target_pairs={{0,3},{1,2},{2,1},{3,0},{4,7},{5,6},{6,5},{7,4},{8,11},{9,10},{10,... | collective-permute-start | bytes 3145736 | tf_op jit(solution)/shard_map/ppermute | solution.py:373
  27.6 46.1 %collective-permute-start.6 = (bf16[512,1024]{1,0:T(8,128)(2,1)}, bf16[512,1024]{1,0:T(8,128)(2,1)}, u32[]{:S(2)}, u32[]{:S(2)}) collective-permute-start(bf16[512,1024]{1,0:T(8,128)(2,1)} %get-tuple-element.48), channel_id=1, source_target_pairs={{0,7},{1,6},{2,5},{3,4},{4,3},{5,2},{6,1},{7,0},{8,15},{9,14},{10,... | collective-permute-start | bytes 3145736 | tf_op jit(solution)/shard_map/ppermute | solution.py:373
  36.8 1.0 copy-start
  68.4 10.8 %collective-permute-start.7 = (bf16[256,512]{1,0:T(8,128)(2,1)S(1)}, bf16[256,512]{1,0:T(8,128)(2,1)S(1)}, u32[]{:S(2)}, u32[]{:S(2)}) collective-permute-start(bf16[256,512]{1,0:T(8,128)(2,1)S(1)} %shard_map.126), channel_id=1, source_target_pairs={{0,1},{1,0},{2,3},{3,2},{4,5},{5,4},{6,7},{7,6},{8,9},{9,8},{10,11... | collective-permute-start | bytes 786440 | tf_op jit(solution)/shard_map/ppermute | solution.py:373
  68.5 14.8 %collective-permute-start.3 = (bf16[256,512]{1,0:T(8,128)(2,1)S(1)}, bf16[256,512]{1,0:T(8,128)(2,1)S(1)}, u32[]{:S(2)}, u32[]{:S(2)}) collective-permute-start(bf16[256,512]{1,0:T(8,128)(2,1)S(1)} %shard_map.126), channel_id=1, source_target_pairs={{0,2},{1,3},{2,0},{3,1},{4,6},{5,7},{6,4},{7,5},{8,10},{9,11},{10,... | collective-permute-start | bytes 786440 | tf_op jit(solution)/shard_map/ppermute | solution.py:373
  70.2 13.1 %collective-permute-start.4 = (bf16[256,512]{1,0:T(8,128)(2,1)S(1)}, bf16[256,512]{1,0:T(8,128)(2,1)S(1)}, u32[]{:S(2)}, u32[]{:S(2)}) collective-permute-start(bf16[256,512]{1,0:T(8,128)(2,1)S(1)} %shard_map.126), channel_id=1, source_target_pairs={{0,6},{1,7},{2,4},{3,5},{4,2},{5,3},{6,0},{7,1},{8,14},{9,15},{10,... | collective-permute-start | bytes 786440 | tf_op jit(solution)/shard_map/ppermute | solution.py:373
  78.2 6.2 %collective-permute-start.14 = (bf16[256,512]{1,0:T(8,128)(2,1)S(1)}, bf16[256,512]{1,0:T(8,128)(2,1)S(1)}, u32[]{:S(2)}, u32[]{:S(2)}) collective-permute-start(bf16[256,512]{1,0:T(8,128)(2,1)S(1)} %get-tuple-element.61), channel_id=1, source_target_pairs={{0,1},{1,0},{2,3},{3,2},{4,5},{5,4},{6,7},{7,6},{8,9},{9,8},{10,11... | collective-permute-start | bytes 786440 | tf_op jit(solution)/shard_map/ppermute | solution.py:373
  79.1 10.3 %collective-permute-start.12 = (bf16[256,512]{1,0:T(8,128)(2,1)S(1)}, bf16[256,512]{1,0:T(8,128)(2,1)S(1)}, u32[]{:S(2)}, u32[]{:S(2)}) collective-permute-start(bf16[256,512]{1,0:T(8,128)(2,1)S(1)} %get-tuple-element.61), channel_id=1, source_target_pairs={{0,2},{1,3},{2,0},{3,1},{4,6},{5,7},{6,4},{7,5},{8,10},{9,11},{10,... | collective-permute-start | bytes 786440 | tf_op jit(solution)/shard_map/ppermute | solution.py:373
  79.2 10.2 %collective-permute-start.13 = (bf16[256,512]{1,0:T(8,128)(2,1)S(1)}, bf16[256,512]{1,0:T(8,128)(2,1)S(1)}, u32[]{:S(2)}, u32[]{:S(2)}) collective-permute-start(bf16[256,512]{1,0:T(8,128)(2,1)S(1)} %get-tuple-element.61), channel_id=1, source_target_pairs={{0,6},{1,7},{2,4},{3,5},{4,2},{5,3},{6,0},{7,1},{8,14},{9,15},{10,... | collective-permute-start | bytes 786440 | tf_op jit(solution)/shard_map/ppermute | solution.py:373
  83.3 3.3 %collective-permute-start.8 = (bf16[256,512]{1,0:T(8,128)(2,1)S(1)}, bf16[256,512]{1,0:T(8,128)(2,1)S(1)}, u32[]{:S(2)}, u32[]{:S(2)}) collective-permute-start(bf16[256,512]{1,0:T(8,128)(2,1)S(1)} %collective-permute-done.3), channel_id=1, source_target_pairs={{0,1},{1,0},{2,3},{3,2},{4,5},{5,4},{6,7},{7,6},{8,9},{9,8},{10,11... | collective-permute-start | bytes 786440 | tf_op jit(solution)/shard_map/ppermute | solution.py:373
  83.4 4.7 %collective-permute-start.10 = (bf16[256,512]{1,0:T(8,128)(2,1)S(1)}, bf16[256,512]{1,0:T(8,128)(2,1)S(1)}, u32[]{:S(2)}, u32[]{:S(2)}) collective-permute-start(bf16[256,512]{1,0:T(8,128)(2,1)S(1)} %collective-permute-done.4), channel_id=1, source_target_pairs={{0,1},{1,0},{2,3},{3,2},{4,5},{5,4},{6,7},{7,6},{8,9},{9,8},{10,11... | collective-permute-start | bytes 786440 | tf_op jit(solution)/shard_map/ppermute | solution.py:373
  87.1 10.4 %collective-permute-start.9 = (bf16[256,512]{1,0:T(8,128)(2,1)S(1)}, bf16[256,512]{1,0:T(8,128)(2,1)S(1)}, u32[]{:S(2)}, u32[]{:S(2)}) collective-permute-start(bf16[256,512]{1,0:T(8,128)(2,1)S(1)} %slice.55), channel_id=1, source_target_pairs={{0,6},{1,7},{2,4},{3,5},{4,2},{5,3},{6,0},{7,1},{8,14},{9,15},{10,... | collective-permute-start | bytes 786440 | tf_op jit(solution)/shard_map/ppermute | solution.py:373
  88.6 9.1 %collective-permute-start.11 = (bf16[256,512]{1,0:T(8,128)(2,1)S(1)}, bf16[256,512]{1,0:T(8,128)(2,1)S(1)}, u32[]{:S(2)}, u32[]{:S(2)}) collective-permute-start(bf16[256,512]{1,0:T(8,128)(2,1)S(1)} %slice.54), channel_id=1, source_target_pairs={{0,2},{1,3},{2,0},{3,1},{4,6},{5,7},{6,4},{7,5},{8,10},{9,11},{10,... | collective-permute-start | bytes 786440 | tf_op jit(solution)/shard_map/ppermute | solution.py:373
  89.8 1.6 %collective-permute-start.15 = (bf16[256,512]{1,0:T(8,128)(2,1)S(1)}, bf16[256,512]{1,0:T(8,128)(2,1)S(1)}, u32[]{:S(2)}, u32[]{:S(2)}) collective-permute-start(bf16[256,512]{1,0:T(8,128)(2,1)S(1)} %collective-permute-done.12), channel_id=1, source_target_pairs={{0,1},{1,0},{2,3},{3,2},{4,5},{5,4},{6,7},{7,6},{8,9},{9,8},{10,11... | collective-permute-start | bytes 786440 | tf_op jit(solution)/shard_map/ppermute | solution.py:373
  89.9 4.3 %collective-permute-start.17 = (bf16[256,512]{1,0:T(8,128)(2,1)S(1)}, bf16[256,512]{1,0:T(8,128)(2,1)S(1)}, u32[]{:S(2)}, u32[]{:S(2)}) collective-permute-start(bf16[256,512]{1,0:T(8,128)(2,1)S(1)} %collective-permute-done.13), channel_id=1, source_target_pairs={{0,1},{1,0},{2,3},{3,2},{4,5},{5,4},{6,7},{7,6},{8,9},{9,8},{10,11... | collective-permute-start | bytes 786440 | tf_op jit(solution)/shard_map/ppermute | solution.py:373
  91.9 10.6 %collective-permute-start.16 = (bf16[256,512]{1,0:T(8,128)(2,1)S(1)}, bf16[256,512]{1,0:T(8,128)(2,1)S(1)}, u32[]{:S(2)}, u32[]{:S(2)}) collective-permute-start(bf16[256,512]{1,0:T(8,128)(2,1)S(1)} %slice.53), channel_id=1, source_target_pairs={{0,6},{1,7},{2,4},{3,5},{4,2},{5,3},{6,0},{7,1},{8,14},{9,15},{10,... | collective-permute-start | bytes 786440 | tf_op jit(solution)/shard_map/ppermute | solution.py:373
  94.7 8.2 %collective-permute-start.18 = (bf16[256,512]{1,0:T(8,128)(2,1)S(1)}, bf16[256,512]{1,0:T(8,128)(2,1)S(1)}, u32[]{:S(2)}, u32[]{:S(2)}) collective-permute-start(bf16[256,512]{1,0:T(8,128)(2,1)S(1)} %slice.52), channel_id=1, source_target_pairs={{0,2},{1,3},{2,0},{3,1},{4,6},{5,7},{6,4},{7,5},{8,10},{9,11},{10,... | collective-permute-start | bytes 786440 | tf_op jit(solution)/shard_map/ppermute | solution.py:373
  97.6 5.3 %copy-start.4 = (bf16[512,1024]{1,0:T(8,128)(2,1)S(1)}, bf16[512,1024]{1,0:T(8,128)(2,1)}, u32[]{:S(2)}) copy-start(bf16[512,1024]{1,0:T(8,128)(2,1)} %param.14) | copy-start | bytes 3145732
  102.6 9.6 %copy-start.7 = (f32[1024]{0:T(1024)S(1)}, f32[1024]{0:T(1024)}, u32[]{:S(2)}) copy-start(f32[1024]{0:T(1024)} %param.21) | copy-start | bytes 12292
  103.3 1.2 %collective-permute-start.19 = (f32[512]{0:T(512)S(1)}, f32[512]{0:T(512)S(1)}, u32[]{:S(2)}, u32[]{:S(2)}) collective-permute-start(f32[512]{0:T(512)S(1)} %multiply_reduce_fusion), channel_id=1, source_target_pairs={{0,1},{1,0},{2,3},{3,2},{4,5},{5,4},{6,7},{7,6},{8,9},{9,8},{10,11... | collective-permute-start | bytes 6152 | tf_op jit(solution)/shard_map/ppermute | solution.py:373
  104.5 5.1 %collective-permute-start.20 = (f32[512]{0:T(512)S(1)}, f32[512]{0:T(512)S(1)}, u32[]{:S(2)}, u32[]{:S(2)}) collective-permute-start(f32[512]{0:T(512)S(1)} %add.170), channel_id=1, source_target_pairs={{0,4},{1,5},{2,6},{3,7},{4,0},{5,1},{6,2},{7,3},{8,12},{9,13},{10,... | collective-permute-start | bytes 6152 | tf_op jit(solution)/shard_map/ppermute | solution.py:373
  106.5 3.6 %collective-permute-start.21 = (f32[512]{0:T(512)S(1)}, f32[512]{0:T(512)S(1)}, u32[]{:S(2)}, u32[]{:S(2)}) collective-permute-start(f32[512]{0:T(512)S(1)} %add.170), channel_id=1, source_target_pairs={{0,2},{1,3},{2,0},{3,1},{4,6},{5,7},{6,4},{7,5},{8,10},{9,11},{10,... | collective-permute-start | bytes 6152 | tf_op jit(solution)/shard_map/ppermute | solution.py:373
  107.4 4.8 %collective-permute-start.22 = (f32[512]{0:T(512)S(1)}, f32[512]{0:T(512)S(1)}, u32[]{:S(2)}, u32[]{:S(2)}) collective-permute-start(f32[512]{0:T(512)S(1)} %add.170), channel_id=1, source_target_pairs={{0,6},{1,7},{2,4},{3,5},{4,2},{5,3},{6,0},{7,1},{8,14},{9,15},{10,... | collective-permute-start | bytes 6152 | tf_op jit(solution)/shard_map/ppermute | solution.py:373
  (2 other events, 1.6 us)

commit v5 on v4

--- a/solution.py
+++ b/solution.py
@@ -17,7 +17,7 @@
 BLOCK = 32
 FRESH = 128
 PAIRS = 48
-CHUNKS = 4
+CHUNKS = 8
 PIECE = 8
 UNROLL = 8
 LOW = -1e30
@@ -61,7 +61,7 @@
     return [ref[pl.ds(base, BLOCK), h * HD : (h + 1) * HD] for h in range(GROUP)]
 
 
-def payload_kernel(lengths, keys, values, out, held, sems):
+def payload_kernel(lengths_hbm, keys, values, out, lengths, held, sems, lengths_sem):
     packs, prefix, _ = keys.shape
     tile = packs // CHUNKS
 
@@ -75,9 +75,12 @@
         )
 
     steps = [copies(c) for c in range(CHUNKS)]
+    fetch = pltpu.make_async_copy(lengths_hbm, lengths, lengths_sem)
+    fetch.start()
     for step in steps:
         step[0].start()
         step[1].start()
+    fetch.wait()
     position = lax.broadcasted_iota(jnp.int32, keys.shape[1:], 0)
     for c, step in enumerate(steps):
         step[0].wait()
@@ -117,36 +120,42 @@
     lax.fori_loop(0, 512 // BLOCK, body, 0, unroll=2)
 
 
-def main_kernel(first, plan, starts, q, cache_hbm, mean_hbm, level_hbm, *refs):
-    cache, means, levels, scores, weights, mixed, sems, stage_sems = refs[-8:]
-    count = (len(refs) - 9) // 2
-    sources, out, staged = refs[:count], refs[count], refs[count + 1 : -8]
+def main_kernel(first, plan, starts, q, cache_in, mean_hbm, level_hbm, *refs):
+    means, levels, scores, weights, mixed, sems, stage_sems = refs[-7:]
+    refs = refs[:-7]
+    if first == 0:
+        cache, refs = refs[-1], refs[:-1]
+    else:
+        cache = cache_in
+    count = (len(refs) - 1) // 2
+    sources, out, staged = refs[:count], refs[count], refs[count + 1 :]
     stage = []
-    for place_of, (source, target) in enumerate(zip(sources, staged)):
+    for spot, (source, target) in enumerate(zip(sources, staged)):
         if source.shape == target.shape:
             parts = [(source, target)]
         elif source.shape[1] == 2 * target.shape[1]:
-            parts = [(source.at[:, pl.ds(1024 * (place_of % 2), 1024)], target)]
+            parts = [(source.at[:, pl.ds(1024 * (spot % 2), 1024)], target)]
         else:
-            parts = [
-                (source.at[:, pl.ds(pl.multiple_of(starts[i], 512), 512)], target.at[:, pl.ds(512 * (i % 2), 512)])
-                for i in range(len(stage), len(stage) + 2)
-            ]
+            parts = []
+            for i in range(2):
+                start = pl.multiple_of(starts[2 * spot + i], 512)
+                parts.append((source.at[:, pl.ds(start, 512)], target.at[:, pl.ds(512 * i, 512)]))
         for origin, goal in parts:
             stage.append(pltpu.make_async_copy(origin, goal, stage_sems.at[len(stage)]))
     half = cache.shape[1] // 2
+    blocks = pl.ds(first, PIECE)
     fetch = [
-        pltpu.make_async_copy(
-            cache_hbm.at[:, pl.ds(i * half, half)], cache.at[:, pl.ds(i * half, half)], sems.at[i]
-        )
-        for i in range(2)
+        pltpu.make_async_copy(level_hbm.at[blocks], levels, sems.at[0]),
+        pltpu.make_async_copy(mean_hbm.at[blocks], means, sems.at[1]),
     ]
-    blocks = pl.ds(first, PIECE)
-    fetch.append(pltpu.make_async_copy(level_hbm.at[blocks], levels, sems.at[2]))
-    fetch.append(pltpu.make_async_copy(mean_hbm.at[blocks], means, sems.at[3]))
-    for i in (0, 2, 3, 1):
-        fetch[i].start()
-    for copy in stage:
+    halves = []
+    if first == 0:
+        for i in range(2):
+            part = pl.ds(i * half, half)
+            halves.append(
+                pltpu.make_async_copy(cache_in.at[:, part], cache.at[:, part], sems.at[2 + i])
+            )
+    for copy in halves[:1] + fetch + halves[1:] + stage:
         copy.start()
     ones = jnp.ones((16, HD), jnp.bfloat16)
     ahead = plan[4, 0]
@@ -206,12 +215,14 @@
                 mixed[block, part] += jnp.where(mine, found[h * BLOCK : (h + 1) * BLOCK], 0.0)
         return carry
 
-    fetch[0].wait()
+    for copy in halves[:1]:
+        copy.wait()
     lax.fori_loop(lower, upper, score, 0)
-    fetch[2].wait()
-    fetch[3].wait()
+    for copy in fetch:
+        copy.wait()
     lax.fori_loop(0, PIECE, soften, 0, unroll=PIECE)
-    fetch[1].wait()
+    for copy in halves[1:]:
+        copy.wait()
     lax.fori_loop(lower, upper, mix, 0)
     for block in range(PIECE):
         total = mixed[block].astype(jnp.bfloat16)
@@ -243,19 +254,17 @@
     return pl.pallas_call(
         payload_kernel,
         out_shape=jax.ShapeDtypeStruct((packs, 2 * prefix, width), keys.dtype),
-        grid_spec=pltpu.PrefetchScalarGridSpec(
-            num_scalar_prefetch=1,
-            grid=(),
-            in_specs=far(2),
-            out_specs=far(1)[0],
-            scratch_shapes=[
-                pltpu.VMEM((packs, 2 * prefix, width), keys.dtype),
-                pltpu.SemaphoreType.DMA((3, CHUNKS)),
-            ],
-        ),
+        in_specs=far(3),
+        out_specs=far(1)[0],
+        scratch_shapes=[
+            pltpu.SMEM(lengths.shape, lengths.dtype),
+            pltpu.VMEM((packs, 2 * prefix, width), keys.dtype),
+            pltpu.SemaphoreType.DMA((3, CHUNKS)),
+            pltpu.SemaphoreType.DMA,
+        ],
         compiler_params=pltpu.CompilerParams(vmem_limit_bytes=4 << 20),
         cost_estimate=pl.CostEstimate(flops=1 << 20, bytes_accessed=4 << 20, transcendentals=0),
-    )(lengths, *in_hbm(keys, values))
+    )(*in_hbm(lengths, keys, values))
 
 
 def cut_kernel(starts, weight, after, *refs):
@@ -314,20 +323,23 @@
     )(queries, jnp.pad(new_keys, front), jnp.pad(new_values, front), row_start)
 
 
-def attend(first, plan, starts, queries, cache, fresh, sources=()):
+def attend(first, plan, starts, queries, cache, fresh, sources):
     area = fresh[0].shape[1:]
-    rows = jax.ShapeDtypeStruct((PIECE * BLOCK, queries.shape[1]), queries.dtype)
-    staged = [pltpu.VMEM((source.shape[0], 1024), source.dtype) for source in sources]
+    outs = [jax.ShapeDtypeStruct((PIECE * BLOCK, queries.shape[1]), queries.dtype)]
+    outs += [pltpu.VMEM((source.shape[0], 1024), source.dtype) for source in sources]
+    if first == 0:
+        outs.append(pltpu.VMEM(cache.shape, cache.dtype))
     return pl.pallas_call(
         functools.partial(main_kernel, first),
-        out_shape=(rows, *staged),
+        out_shape=tuple(outs),
         grid_spec=pltpu.PrefetchScalarGridSpec(
             num_scalar_prefetch=2,
             grid=(),
-            in_specs=whole(1) + anywhere(3 + len(sources)),
-            out_specs=tuple(whole(1 + len(staged))),
+            in_specs=whole(1)
+            + (anywhere(1) if first == 0 else whole(1))
+            + anywhere(2 + len(sources)),
+            out_specs=tuple(whole(len(outs))),
             scratch_shapes=[
-                pltpu.VMEM(cache.shape, cache.dtype),
                 pltpu.VMEM((PIECE, *area), jnp.float32),
                 pltpu.VMEM((PIECE, *area), jnp.float32),
                 pltpu.VMEM((PIECE + 1, *area), jnp.float32),
@@ -337,18 +349,18 @@
                 pltpu.SemaphoreType.DMA((len(sources) + 2,)),
             ],
         ),
-        compiler_params=pltpu.CompilerParams(vmem_limit_bytes=(7 + len(sources)) << 20),
+        compiler_params=pltpu.CompilerParams(vmem_limit_bytes=12 << 20),
         cost_estimate=pl.CostEstimate(
             flops=1 << 31, bytes_accessed=4 << 20, transcendentals=1 << 18
         ),
-    )(plan, starts, queries, cache, *in_hbm(*fresh), *in_hbm(*sources))
-
-
-def attention(counts, packs, queries, marked, values, new_keys, new_values):
-    plan, row_start = pair_plan(counts, packs)
-    fresh = attend_fresh(queries, new_keys, new_values, row_start)
-    cache = jnp.concatenate([marked, values], axis=1)
-    return jnp.concatenate([attend(i, plan, plan[0], queries, cache, fresh)[0] for i in (0, PIECE)], axis=0)
+    )(plan, starts, queries, cache, *in_hbm(*fresh, *sources))
+
+
+def attend_all(plan, starts, queries, cache, fresh, sources):
+    middle = len(sources) // 2
+    rows_a, *mats_a, cache = attend(0, plan, starts, queries, cache, fresh, sources[:middle])
+    rows_b, *mats_b = attend(PIECE, plan, starts, queries, cache, fresh, sources[middle:])
+    return [rows_a, rows_b], mats_a + mats_b
 
 
 def on_device(
@@ -382,19 +394,16 @@
     cache = lax.all_to_all(payload, "dp", split_axis=0, concat_axis=0, tiled=True)
 
     starts = sum([shared(mask)[half] for mask, half in ((2, 0), (6, 1), (3, 0), (7, 1))], [])
-    pieces = cut(jnp.stack(starts), out_weight, (1024,) * 4, payload)
-    starts, pieces = lax.optimization_barrier((jnp.stack(sum(shared(1), [])), pieces))
-    near_mats = [swap(piece, mask) for piece, mask in zip(pieces, (2, 6, 3, 7))]
-    sibling = swap(cut(starts, out_weight, (2048,), payload)[0], 1)
+    starts = jnp.stack(starts + sum(shared(1), []))
+    pieces = cut(starts, out_weight, (1024, 1024, 1024, 1024, 2048), payload)
+    *near_mats, sibling = [swap(piece, mask) for piece, mask in zip(pieces, (2, 6, 3, 7, 1))]
 
     plan, row_start = pair_plan(row_counts[0], pack_of[0])
     fresh = attend_fresh(queries, new_keys, new_values, row_start)
     plan, sibling, near_mats[:2] = lax.optimization_barrier((plan, sibling, near_mats[:2]))
+    sources = (out_weight, out_weight, sibling, sibling, *near_mats)
     starts = jnp.stack(sum(shared(0), []))
-    attended = attend(0, plan, starts, queries, cache, fresh)
-    sources = (out_weight, out_weight, sibling, sibling, *near_mats)
-    rest, *mats = attend(PIECE, plan, starts, queries, cache, fresh, sources)
-    attended = [attended[0], rest]
+    attended, mats = attend_all(plan, starts, queries, cache, fresh, sources)
     here, sibling, same, cross = (mats[i : i + 2] for i in (0, 2, 4, 6))
 
     def times(rows, mat):
@@ -406,10 +415,13 @@
     got = []
     sent = []
     for rows, other, close in zip(attended, others, near):
+        rows, other, sent = lax.optimization_barrier((rows, other, sent))
+        close, sent = lax.optimization_barrier((close, sent))
+        side = [swap(part, 1) for part in close]
         local = [times(rows, here[half]) + times(other, sibling[half]) for half in range(2)]
-        close, local, sent = lax.optimization_barrier((close, local, sent))
+        close, local = lax.optimization_barrier((close, local))
         totals = [
-            local[half] + times(close[half], same[half]) + times(swap(close[half], 1), cross[half])
+            local[half] + times(close[half], same[half]) + times(side[half], cross[half])
             for half in range(2)
         ]
         own.append([total[:, :512] for total in totals])

time: 114 us -> 126 us (1.11)
  waiting for transfers between devices: 40 us -> 55.9 us
  starting transfers between devices: 34.2 us -> 32 us
  Pallas kernels: 24.2 us -> 22.6 us
    ppermute x23, waiting for transfers between devices: 27.5 us -> 42.3 us  [swap(): return lax.ppermute(value, 'tensor', [(t, t ^ mask) for t in range(count)])]
    ppermute x23, starting transfers between devices: 22.5 us -> 20.4 us  [swap(): return lax.ppermute(value, 'tensor', [(t, t ^ mask) for t in range(count)])]
    pallas_call x2 -> x1, Pallas kernels: 7.3 us -> 6.12 us  [cut(): pl.pallas_call(cut_kernel, out_shape=tuple((jax.ShapeDtypeStruct((rows, w...]
    unnamed x20 -> x18, local copies, waits for them, and re-layouts: 2.62 us -> 1.98 us
  transfers between devices with their start and end apart: 24 -> 24, of which waited for: 12 -> 17; matrix products, arithmetic and copies ran while one was open for 8% -> 8% of each run, Pallas kernels for 19% -> 12%
where the time goes in v5:
time: 126 us; the launch traced here: 125 us
  waiting for transfers between devices  55.9 us (44%)
  starting transfers between devices  32 us (25%)
  Pallas kernels  22.6 us (18%)
  matrix products  7.02 us (6%)
  other arithmetic  3.61 us (3%)
  local copies, waits for them, and re-layouts  3.03 us (2%)
    ppermute x23, waiting for transfers between devices, swap(): return lax.ppermute(value, 'tensor', [(t, t ^ mask) for t in range(count)])  42.3 us
    ppermute x23, starting transfers between devices, swap(): return lax.ppermute(value, 'tensor', [(t, t ^ mask) for t in range(count)])  20.4 us
    all_to_all x1, waiting for transfers between devices, on_device(): lax.all_to_all(payload, 'dp', split_axis=0, concat_axis=0, tiled=True)  13.6 us
    all_to_all x1, starting transfers between devices, on_device(): lax.all_to_all(payload, 'dp', split_axis=0, concat_axis=0, tiled=True)  11.6 us
    pallas_call x2, Pallas kernels, attend(): pl.pallas_call(functools.partial(main_kernel, first), out_shape=tuple(out...  7.7 us
    dot_general x16, matrix products, times(): return jnp.dot(rows, mat, preferred_element_type=f32)  7.02 us
    pallas_call x1, Pallas kernels, attend_fresh(): pl.pallas_call(fresh_kernel, out_shape=(area, area), in_specs=whole(4), o...  6.16 us
    pallas_call x1, Pallas kernels, cut(): pl.pallas_call(cut_kernel, out_shape=tuple((jax.ShapeDtypeStruct((rows, w...  6.12 us
  transfers between devices with their start and end apart: 24, of which 17 were waited for; matrix products, arithmetic and copies ran while one was open for 8% of the time, Pallas kernels for 12%

profile of v5, /device:TPU:2, one launch (start us, length us, event | category | flops | bytes accessed | tf_op | source)
XLA Modules:
  0.0 125.3 jit_solution(10533576881175171692)
XLA Ops:
  0.6 2.6 %shard_map.122.after = bf16[32,256,128]{2,1,0:T(8,128)(2,1)} custom-call(s32[1,32]{1,0:T(1,128)} %lengths_hbm.1, bf16[32,128,128]{2,1,0:T(8,128)(2,1)} %bitcast.80, bf16[32,128,128]{2,1,0:T(8,128)(2,1)} %bitcast.81), custom_call_target="tpu_custom_call" | custom-call | flops 1048576 | bytes 4194304 | tf_op jit(solution)/shard_map/pallas_call | solution.py:254
  3.2 11.6 %all-to-all-start = ((bf16[32,256,128]{2,1,0:T(8,128)(2,1)}), bf16[32,256,128]{2,1,0:T(8,128)(2,1)S(1)}, u32[]{:S(2)}, u32[]{:S(2)}) async-start(bf16[32,256,128]{2,1,0:T(8,128)(2,1)} %shard_map.122.after), calls=%async_computation | async-start | bytes 4194304 | tf_op jit(solution)/shard_map/all_to_all | solution.py:394
  15.0 6.1 %shard_map.123 = (bf16[512,1024]{1,0:T(8,128)(2,1)}, bf16[512,1024]{1,0:T(8,128)(2,1)}, bf16[512,1024]{1,0:T(8,128)(2,1)}, bf16[512,1024]{1,0:T(8,128)(2,1)}, bf16[512,2048]{1,0:T(8,128)(2,1)}) custom-call(s32[12]{0:T(128)S(1)} %stack.86.starts, bf16[512,8192]{1,0:T(8,128)(2,1)} %refs_1_.1, bf16[32,256,128]{2,1,0:T(8,128)(2,1)} %shard_map.122.after), custom_call_target="tpu_custom_call" | custom-call | bytes 12582912 | tf_op jit(solution)/shard_map/pallas_call | solution.py:293
  21.3 1.7 %collective-permute-start.1 = (bf16[512,1024]{1,0:T(8,128)(2,1)}, bf16[512,1024]{1,0:T(8,128)(2,1)}, u32[]{:S(2)}, u32[]{:S(2)}) collective-permute-start(bf16[512,1024]{1,0:T(8,128)(2,1)} %get-tuple-element.41), channel_id=1, source_target_pairs={{0,2},{1,3},{2,0},{3,1},{4,6},{5,7},{6,4},{7,5},{8,10},{9,11},{10,... | collective-permute-start | bytes 3145736 | tf_op jit(solution)/shard_map/ppermute | solution.py:385
  22.9 2.2 %collective-permute-start.2 = (bf16[512,1024]{1,0:T(8,128)(2,1)}, bf16[512,1024]{1,0:T(8,128)(2,1)}, u32[]{:S(2)}, u32[]{:S(2)}) collective-permute-start(bf16[512,1024]{1,0:T(8,128)(2,1)} %get-tuple-element.42), channel_id=1, source_target_pairs={{0,6},{1,7},{2,4},{3,5},{4,2},{5,3},{6,0},{7,1},{8,14},{9,15},{10,... | collective-permute-start | bytes 3145736 | tf_op jit(solution)/shard_map/ppermute | solution.py:385
  28.3 6.2 %shard_map.124 = (f32[16,128,128]{2,1,0:T(8,128)S(1)}, f32[16,128,128]{2,1,0:T(8,128)S(1)}) custom-call(bf16[512,512]{1,0:T(8,128)(2,1)S(1)} %copy-done.2, bf16[608,128]{1,0:T(8,128)(2,1)S(1)} %pad.7.fresh_k, bf16[608,128]{1,0:T(8,128)(2,1)S(1)} %pad.8.fresh_v, s32[512,128]{1,0:T(8,128)S(1)} %broadcast_in_dim.105.row_start), custom_call_target="tpu_custom_call" | custom-call | flops 2147483648 | bytes 4194304 | tf_op jit(solution)/shard_map/pallas_call | solution.py:314
  35.5 1.0 copy-done.1
  36.4 11.2 %collective-permute-done.1.refs_0_ = bf16[512,1024]{1,0:T(8,128)(2,1)} collective-permute-done((bf16[512,1024]{1,0:T(8,128)(2,1)}, bf16[512,1024]{1,0:T(8,128)(2,1)}, u32[]{:S(2)}, u32[]{:S(2)}) %collective-permute-start.1) | collective-permute-done | bytes 1048608 | tf_op jit(solution)/shard_map/ppermute | solution.py:385
  47.6 2.8 %collective-permute-done.2.refs_1_ = bf16[512,1024]{1,0:T(8,128)(2,1)} collective-permute-done((bf16[512,1024]{1,0:T(8,128)(2,1)}, bf16[512,1024]{1,0:T(8,128)(2,1)}, u32[]{:S(2)}, u32[]{:S(2)}) %collective-permute-start.2) | collective-permute-done | bytes 1048608 | tf_op jit(solution)/shard_map/ppermute | solution.py:385
  50.5 13.6 %all-to-all-done.cache_in = bf16[32,256,128]{2,1,0:T(8,128)(2,1)S(1)} async-done(((bf16[32,256,128]{2,1,0:T(8,128)(2,1)}), bf16[32,256,128]{2,1,0:T(8,128)(2,1)S(1)}, u32[]{:S(2)}, u32[]{:S(2)}) %all-to-all-start) | async-done | bytes 2097184 | tf_op jit(solution)/shard_map/all_to_all | solution.py:394
  64.1 3.3 %shard_map.125 = (bf16[256,512]{1,0:T(8,128)(2,1)S(1)}, bf16[512,1024]{1,0:T(8,128)(2,1)S(1)}, bf16[512,1024]{1,0:T(8,128)(2,1)S(1)}, bf16[512,1024]{1,0:T(8,128...) custom-call(s32[5,48]{1,0:T(8,128)S(1)} %stack.73.plan, s32[4]{0:T(128)S(1)} %pad_add_fusion.starts, ...), custom_call_target="tpu_custom_call" | custom-call | flops 2147483648 | bytes 4194304 | tf_op jit(solution)/shard_map/pallas_call | solution.py:332
  67.4 1.8 %collective-permute-done.6.refs_2_ = bf16[512,1024]{1,0:T(8,128)(2,1)} collective-permute-done((bf16[512,1024]{1,0:T(8,128)(2,1)}, bf16[512,1024]{1,0:T(8,128)(2,1)}, u32[]{:S(2)}, u32[]{:S(2)}) %collective-permute-start.6) | collective-permute-done | bytes 1048608 | tf_op jit(solution)/shard_map/ppermute | solution.py:385
  69.2 2.2 %collective-permute-done.7.refs_3_ = bf16[512,1024]{1,0:T(8,128)(2,1)} collective-permute-done((bf16[512,1024]{1,0:T(8,128)(2,1)}, bf16[512,1024]{1,0:T(8,128)(2,1)}, u32[]{:S(2)}, u32[]{:S(2)}) %collective-permute-start.7) | collective-permute-done | bytes 1048608 | tf_op jit(solution)/shard_map/ppermute | solution.py:385
  71.3 4.4 %shard_map.126 = (bf16[256,512]{1,0:T(8,128)(2,1)S(1)}, bf16[512,1024]{1,0:T(8,128)(2,1)S(1)}, bf16[512,1024]{1,0:T(8,128)(2,1)S(1)}, bf16[512,1024]{1,0:T(8,128)(2,1)S(1)}, bf16[512,1024]{1,0:T(8,128)(2,1)S(1)}) custom-call(s32[5,48]{1,0:T(8,128)S(1)} %stack.73.plan, s32[4]{0:T(128)S(1)} %pad_add_fusion.starts, bf16[512,512]{1,0:T(8,128)(2,1)S(1)} %copy-done.2, ...), custom_call_target="tpu_custom_call" | custom-call | flops 2147483648 | bytes 4194304 | tf_op jit(solution)/shard_map/pallas_call | solution.py:332
  75.8 2.3 %collective-permute-start.13 = (bf16[256,512]{1,0:T(8,128)(2,1)S(1)}, bf16[256,512]{1,0:T(8,128)(2,1)S(1)}, u32[]{:S(2)}, u32[]{:S(2)}) collective-permute-start(bf16[256,512]{1,0:T(8,128)(2,1)S(1)} %get-tuple-element.72), channel_id=1, source_target_pairs={{0,6},{1,7},{2,4},{3,5},{4,2},{5,3},{6,0},{7,1},{8,14},{9,15},{10,... | collective-permute-start | bytes 786440 | tf_op jit(solution)/shard_map/ppermute | solution.py:385
  78.4 1.1 collective-permute-start.4
  79.4 1.1 collective-permute-start.3
  80.6 5.6 %collective-permute-done.13 = bf16[256,512]{1,0:T(8,128)(2,1)S(1)} collective-permute-done((bf16[256,512]{1,0:T(8,128)(2,1)S(1)}, bf16[256,512]{1,0:T(8,128)(2,1)S(1)}, u32[]{:S(2)}, u32[]{:S(2)}) %collective-permute-start.13) | collective-permute-done | bytes 262176 | tf_op jit(solution)/shard_map/ppermute | solution.py:385
  86.2 1.0 collective-permute-done.12
  87.7 3.8 %collective-permute-done.4 = bf16[256,512]{1,0:T(8,128)(2,1)S(1)} collective-permute-done((bf16[256,512]{1,0:T(8,128)(2,1)S(1)}, bf16[256,512]{1,0:T(8,128)(2,1)S(1)}, u32[]{:S(2)}, u32[]{:S(2)}) %collective-permute-start.4) | collective-permute-done | bytes 262176 | tf_op jit(solution)/shard_map/ppermute | solution.py:385
  100.4 1.3 %collective-permute-start.16 = (bf16[256,512]{1,0:T(8,128)(2,1)S(1)}, bf16[256,512]{1,0:T(8,128)(2,1)S(1)}, u32[]{:S(2)}, u32[]{:S(2)}) collective-permute-start(bf16[256,512]{1,0:T(8,128)(2,1)S(1)} %slice.53), channel_id=1, source_target_pairs={{0,6},{1,7},{2,4},{3,5},{4,2},{5,3},{6,0},{7,1},{8,14},{9,15},{10,... | collective-permute-start | bytes 786440 | tf_op jit(solution)/shard_map/ppermute | solution.py:385
  101.8 1.4 %collective-permute-start.11 = (bf16[256,512]{1,0:T(8,128)(2,1)S(1)}, bf16[256,512]{1,0:T(8,128)(2,1)S(1)}, u32[]{:S(2)}, u32[]{:S(2)}) collective-permute-start(bf16[256,512]{1,0:T(8,128)(2,1)S(1)} %slice.54), channel_id=1, source_target_pairs={{0,2},{1,3},{2,0},{3,1},{4,6},{5,7},{6,4},{7,5},{8,10},{9,11},{10,... | collective-permute-start | bytes 786440 | tf_op jit(solution)/shard_map/ppermute | solution.py:385
  103.2 1.7 %collective-permute-start.9 = (bf16[256,512]{1,0:T(8,128)(2,1)S(1)}, bf16[256,512]{1,0:T(8,128)(2,1)S(1)}, u32[]{:S(2)}, u32[]{:S(2)}) collective-permute-start(bf16[256,512]{1,0:T(8,128)(2,1)S(1)} %slice.55), channel_id=1, source_target_pairs={{0,6},{1,7},{2,4},{3,5},{4,2},{5,3},{6,0},{7,1},{8,14},{9,15},{10,... | collective-permute-start | bytes 786440 | tf_op jit(solution)/shard_map/ppermute | solution.py:385
  104.9 3.5 %collective-permute-done.18 = bf16[256,512]{1,0:T(8,128)(2,1)S(1)} collective-permute-done((bf16[256,512]{1,0:T(8,128)(2,1)S(1)}, bf16[256,512]{1,0:T(8,128)(2,1)S(1)}, u32[]{:S(2)}, u32[]{:S(2)}) %collective-permute-start.18) | collective-permute-done | bytes 262176 | tf_op jit(solution)/shard_map/ppermute | solution.py:385
  108.5 2.5 %collective-permute-done.16 = bf16[256,512]{1,0:T(8,128)(2,1)S(1)} collective-permute-done((bf16[256,512]{1,0:T(8,128)(2,1)S(1)}, bf16[256,512]{1,0:T(8,128)(2,1)S(1)}, u32[]{:S(2)}, u32[]{:S(2)}) %collective-permute-start.16) | collective-permute-done | bytes 262176 | tf_op jit(solution)/shard_map/ppermute | solution.py:385
  111.0 2.0 %collective-permute-done.11 = bf16[256,512]{1,0:T(8,128)(2,1)S(1)} collective-permute-done((bf16[256,512]{1,0:T(8,128)(2,1)S(1)}, bf16[256,512]{1,0:T(8,128)(2,1)S(1)}, u32[]{:S(2)}, u32[]{:S(2)}) %collective-permute-start.11) | collective-permute-done | bytes 262176 | tf_op jit(solution)/shard_map/ppermute | solution.py:385
  113.2 2.2 %collective-permute-done.9 = bf16[256,512]{1,0:T(8,128)(2,1)S(1)} collective-permute-done((bf16[256,512]{1,0:T(8,128)(2,1)S(1)}, bf16[256,512]{1,0:T(8,128)(2,1)S(1)}, u32[]{:S(2)}, u32[]{:S(2)}) %collective-permute-start.9) | collective-permute-done | bytes 262176 | tf_op jit(solution)/shard_map/ppermute | solution.py:385
  115.9 1.1 collective-permute-done.19
  117.0 1.5 %collective-permute-start.22 = (f32[512]{0:T(512)S(1)}, f32[512]{0:T(512)S(1)}, u32[]{:S(2)}, u32[]{:S(2)}) collective-permute-start(f32[512]{0:T(512)S(1)} %add.170), channel_id=1, source_target_pairs={{0,6},{1,7},{2,4},{3,5},{4,2},{5,3},{6,0},{7,1},{8,14},{9,15},{10,... | collective-permute-start | bytes 6152 | tf_op jit(solution)/shard_map/ppermute | solution.py:385
  118.5 3.2 %collective-permute-start.20 = (f32[512]{0:T(512)S(1)}, f32[512]{0:T(512)S(1)}, u32[]{:S(2)}, u32[]{:S(2)}) collective-permute-start(f32[512]{0:T(512)S(1)} %add.170), channel_id=1, source_target_pairs={{0,4},{1,5},{2,6},{3,7},{4,0},{5,1},{6,2},{7,3},{8,12},{9,13},{10,... | collective-permute-start | bytes 6152 | tf_op jit(solution)/shard_map/ppermute | solution.py:385
  122.1 1.5 %collective-permute-done.20 = f32[512]{0:T(512)S(1)} collective-permute-done((f32[512]{0:T(512)S(1)}, f32[512]{0:T(512)S(1)}, u32[]{:S(2)}, u32[]{:S(2)}) %collective-permute-start.20) | collective-permute-done | bytes 2080 | tf_op jit(solution)/shard_map/ppermute | solution.py:385
  123.6 1.7 %multiply_convert_fusion = (bf16[512,1024]{1,0:T(8,128)(2,1)}, bf16[512,1024]{1,0:T(8,128)(2,1)}) fusion(f32[1024]{0:T(1024)S(1)} %copy-done.6, f32[512]{0:T(512)S(1)} %add_rsqrt_fusion, f32[256,512]{1,0:T(8,128)S(1)} %slice_add_fusion, f32[256,512]{1,0:T(8,128)S(1)} %slice_add_fusion.1, f32[256,512]{1,0:T(8,128)S(1)} %slice_add_fusion.2, ...), kind=kLoop, calls=%fused_computation.1 | loop fusion | flops 4718592 | bytes 5249024 | tf_op jit(solution)/shard_map/convert_element_type | solution.py:444
  (83 shorter events, 15.0 us)
Async XLA Ops:
  3.2 60.9 %all-to-all-start = ((bf16[32,256,128]{2,1,0:T(8,128)(2,1)}), bf16[32,256,128]{2,1,0:T(8,128)(2,1)S(1)}, u32[]{:S(2)}, u32[]{:S(2)}) async-start(bf16[32,256,128]{2,1,0:T(8,128)(2,1)} %shard_map.122.after), calls=%async_computation | async-start | bytes 4194304 | tf_op jit(solution)/shard_map/all_to_all | solution.py:394
  15.0 11.1 %copy-start.8 = (s32[1,32]{1,0:T(1,128)S(1)}, s32[1,32]{1,0:T(1,128)}, u32[]{:S(2)}) copy-start(s32[1,32]{1,0:T(1,128)} %param.15) | copy-start | bytes 388
  15.0 11.4 %copy-start.4 = (bf16[512,128]{1,0:T(8,128)(2,1)S(1)}, bf16[512,128]{1,0:T(8,128)(2,1)}, u32[]{:S(2)}) copy-start(bf16[512,128]{1,0:T(8,128)(2,1)} %param.12) | copy-start | bytes 393220
  15.0 11.4 %copy-start.5 = (bf16[512,128]{1,0:T(8,128)(2,1)S(1)}, bf16[512,128]{1,0:T(8,128)(2,1)}, u32[]{:S(2)}) copy-start(bf16[512,128]{1,0:T(8,128)(2,1)} %param.13) | copy-start | bytes 393220
  15.0 11.5 %copy-start.7 = (s32[1,32]{1,0:T(1,128)S(1)}, s32[1,32]{1,0:T(1,128)}, u32[]{:S(2)}) copy-start(s32[1,32]{1,0:T(1,128)} %param.16) | copy-start | bytes 388
  15.0 13.3 %copy-start.2 = (bf16[512,512]{1,0:T(8,128)(2,1)S(1)}, bf16[512,512]{1,0:T(8,128)(2,1)}, u32[]{:S(2)}) copy-start(bf16[512,512]{1,0:T(8,128)(2,1)} %q.5) | copy-start | bytes 1572868
  21.2 29.3 %collective-permute-start = (bf16[512,2048]{1,0:T(8,128)(2,1)}, bf16[512,2048]{1,0:T(8,128)(2,1)}, u32[]{:S(2)}, u32[]{:S(2)}) collective-permute-start(bf16[512,2048]{1,0:T(8,128)(2,1)} %get-tuple-element.40), channel_id=1, source_target_pairs={{0,1},{1,0},{2,3},{3,2},{4,5},{5,4},{6,7},{7,6},{8,9},{9,8},{10,11... | collective-permute-start | bytes 6291464 | tf_op jit(solution)/shard_map/ppermute | solution.py:385
  21.3 26.4 %collective-permute-start.1 = (bf16[512,1024]{1,0:T(8,128)(2,1)}, bf16[512,1024]{1,0:T(8,128)(2,1)}, u32[]{:S(2)}, u32[]{:S(2)}) collective-permute-start(bf16[512,1024]{1,0:T(8,128)(2,1)} %get-tuple-element.41), channel_id=1, source_target_pairs={{0,2},{1,3},{2,0},{3,1},{4,6},{5,7},{6,4},{7,5},{8,10},{9,11},{10,... | collective-permute-start | bytes 3145736 | tf_op jit(solution)/shard_map/ppermute | solution.py:385
  22.9 27.5 %collective-permute-start.2 = (bf16[512,1024]{1,0:T(8,128)(2,1)}, bf16[512,1024]{1,0:T(8,128)(2,1)}, u32[]{:S(2)}, u32[]{:S(2)}) collective-permute-start(bf16[512,1024]{1,0:T(8,128)(2,1)} %get-tuple-element.42), channel_id=1, source_target_pairs={{0,6},{1,7},{2,4},{3,5},{4,2},{5,3},{6,0},{7,1},{8,14},{9,15},{10,... | collective-permute-start | bytes 3145736 | tf_op jit(solution)/shard_map/ppermute | solution.py:385
  25.1 44.0 %collective-permute-start.6 = (bf16[512,1024]{1,0:T(8,128)(2,1)}, bf16[512,1024]{1,0:T(8,128)(2,1)}, u32[]{:S(2)}, u32[]{:S(2)}) collective-permute-start(bf16[512,1024]{1,0:T(8,128)(2,1)} %get-tuple-element.61), channel_id=1, source_target_pairs={{0,3},{1,2},{2,1},{3,0},{4,7},{5,6},{6,5},{7,4},{8,11},{9,10},{10,... | collective-permute-start | bytes 3145736 | tf_op jit(solution)/shard_map/ppermute | solution.py:385
  25.3 46.1 %collective-permute-start.7 = (bf16[512,1024]{1,0:T(8,128)(2,1)}, bf16[512,1024]{1,0:T(8,128)(2,1)}, u32[]{:S(2)}, u32[]{:S(2)}) collective-permute-start(bf16[512,1024]{1,0:T(8,128)(2,1)} %get-tuple-element.62), channel_id=1, source_target_pairs={{0,7},{1,6},{2,5},{3,4},{4,3},{5,2},{6,1},{7,0},{8,15},{9,14},{10,... | collective-permute-start | bytes 3145736 | tf_op jit(solution)/shard_map/ppermute | solution.py:385
  34.5 1.0 copy-start
  75.8 10.4 %collective-permute-start.13 = (bf16[256,512]{1,0:T(8,128)(2,1)S(1)}, bf16[256,512]{1,0:T(8,128)(2,1)S(1)}, u32[]{:S(2)}, u32[]{:S(2)}) collective-permute-start(bf16[256,512]{1,0:T(8,128)(2,1)S(1)} %get-tuple-element.72), channel_id=1, source_target_pairs={{0,6},{1,7},{2,4},{3,5},{4,2},{5,3},{6,0},{7,1},{8,14},{9,15},{10,... | collective-permute-start | bytes 786440 | tf_op jit(solution)/shard_map/ppermute | solution.py:385
  78.0 9.1 %collective-permute-start.12 = (bf16[256,512]{1,0:T(8,128)(2,1)S(1)}, bf16[256,512]{1,0:T(8,128)(2,1)S(1)}, u32[]{:S(2)}, u32[]{:S(2)}) collective-permute-start(bf16[256,512]{1,0:T(8,128)(2,1)S(1)} %get-tuple-element.72), channel_id=1, source_target_pairs={{0,2},{1,3},{2,0},{3,1},{4,6},{5,7},{6,4},{7,5},{8,10},{9,11},{10,... | collective-permute-start | bytes 786440 | tf_op jit(solution)/shard_map/ppermute | solution.py:385
  78.0 9.1 %collective-permute-start.5 = (bf16[256,512]{1,0:T(8,128)(2,1)S(1)}, bf16[256,512]{1,0:T(8,128)(2,1)S(1)}, u32[]{:S(2)}, u32[]{:S(2)}) collective-permute-start(bf16[256,512]{1,0:T(8,128)(2,1)S(1)} %get-tuple-element.50), channel_id=1, source_target_pairs={{0,1},{1,0},{2,3},{3,2},{4,5},{5,4},{6,7},{7,6},{8,9},{9,8},{10,11... | collective-permute-start | bytes 786440 | tf_op jit(solution)/shard_map/ppermute | solution.py:385
  78.4 13.1 %collective-permute-start.4 = (bf16[256,512]{1,0:T(8,128)(2,1)S(1)}, bf16[256,512]{1,0:T(8,128)(2,1)S(1)}, u32[]{:S(2)}, u32[]{:S(2)}) collective-permute-start(bf16[256,512]{1,0:T(8,128)(2,1)S(1)} %get-tuple-element.50), channel_id=1, source_target_pairs={{0,6},{1,7},{2,4},{3,5},{4,2},{5,3},{6,0},{7,1},{8,14},{9,15},{10,... | collective-permute-start | bytes 786440 | tf_op jit(solution)/shard_map/ppermute | solution.py:385
  79.4 12.8 %collective-permute-start.3 = (bf16[256,512]{1,0:T(8,128)(2,1)S(1)}, bf16[256,512]{1,0:T(8,128)(2,1)S(1)}, u32[]{:S(2)}, u32[]{:S(2)}) collective-permute-start(bf16[256,512]{1,0:T(8,128)(2,1)S(1)} %get-tuple-element.50), channel_id=1, source_target_pairs={{0,2},{1,3},{2,0},{3,1},{4,6},{5,7},{6,4},{7,5},{8,10},{9,11},{10,... | collective-permute-start | bytes 786440 | tf_op jit(solution)/shard_map/ppermute | solution.py:385
  86.2 10.3 %collective-permute-start.14 = (bf16[256,512]{1,0:T(8,128)(2,1)S(1)}, bf16[256,512]{1,0:T(8,128)(2,1)S(1)}, u32[]{:S(2)}, u32[]{:S(2)}) collective-permute-start(bf16[256,512]{1,0:T(8,128)(2,1)S(1)} %get-tuple-element.72), channel_id=1, source_target_pairs={{0,1},{1,0},{2,3},{3,2},{4,5},{5,4},{6,7},{7,6},{8,9},{9,8},{10,11... | collective-permute-start | bytes 786440 | tf_op jit(solution)/shard_map/ppermute | solution.py:385
  87.2 12.3 %collective-permute-start.15 = (bf16[256,512]{1,0:T(8,128)(2,1)S(1)}, bf16[256,512]{1,0:T(8,128)(2,1)S(1)}, u32[]{:S(2)}, u32[]{:S(2)}) collective-permute-start(bf16[256,512]{1,0:T(8,128)(2,1)S(1)} %collective-permute-done.12), channel_id=1, source_target_pairs={{0,1},{1,0},{2,3},{3,2},{4,5},{5,4},{6,7},{7,6},{8,9},{9,8},{10,11... | collective-permute-start | bytes 786440 | tf_op jit(solution)/shard_map/ppermute | solution.py:385
  87.2 11.0 %collective-permute-start.17 = (bf16[256,512]{1,0:T(8,128)(2,1)S(1)}, bf16[256,512]{1,0:T(8,128)(2,1)S(1)}, u32[]{:S(2)}, u32[]{:S(2)}) collective-permute-start(bf16[256,512]{1,0:T(8,128)(2,1)S(1)} %collective-permute-done.13), channel_id=1, source_target_pairs={{0,1},{1,0},{2,3},{3,2},{4,5},{5,4},{6,7},{7,6},{8,9},{9,8},{10,11... | collective-permute-start | bytes 786440 | tf_op jit(solution)/shard_map/ppermute | solution.py:385
  92.2 2.3 %collective-permute-start.8 = (bf16[256,512]{1,0:T(8,128)(2,1)S(1)}, bf16[256,512]{1,0:T(8,128)(2,1)S(1)}, u32[]{:S(2)}, u32[]{:S(2)}) collective-permute-start(bf16[256,512]{1,0:T(8,128)(2,1)S(1)} %collective-permute-done.3), channel_id=1, source_target_pairs={{0,1},{1,0},{2,3},{3,2},{4,5},{5,4},{6,7},{7,6},{8,9},{9,8},{10,11... | collective-permute-start | bytes 786440 | tf_op jit(solution)/shard_map/ppermute | solution.py:385
  92.2 3.2 %collective-permute-start.10 = (bf16[256,512]{1,0:T(8,128)(2,1)S(1)}, bf16[256,512]{1,0:T(8,128)(2,1)S(1)}, u32[]{:S(2)}, u32[]{:S(2)}) collective-permute-start(bf16[256,512]{1,0:T(8,128)(2,1)S(1)} %collective-permute-done.4), channel_id=1, source_target_pairs={{0,1},{1,0},{2,3},{3,2},{4,5},{5,4},{6,7},{7,6},{8,9},{9,8},{10,11... | collective-permute-start | bytes 786440 | tf_op jit(solution)/shard_map/ppermute | solution.py:385
  99.1 9.3 %collective-permute-start.18 = (bf16[256,512]{1,0:T(8,128)(2,1)S(1)}, bf16[256,512]{1,0:T(8,128)(2,1)S(1)}, u32[]{:S(2)}, u32[]{:S(2)}) collective-permute-start(bf16[256,512]{1,0:T(8,128)(2,1)S(1)} %slice.52), channel_id=1, source_target_pairs={{0,2},{1,3},{2,0},{3,1},{4,6},{5,7},{6,4},{7,5},{8,10},{9,11},{10,... | collective-permute-start | bytes 786440 | tf_op jit(solution)/shard_map/ppermute | solution.py:385
  100.4 10.5 %collective-permute-start.16 = (bf16[256,512]{1,0:T(8,128)(2,1)S(1)}, bf16[256,512]{1,0:T(8,128)(2,1)S(1)}, u32[]{:S(2)}, u32[]{:S(2)}) collective-permute-start(bf16[256,512]{1,0:T(8,128)(2,1)S(1)} %slice.53), channel_id=1, source_target_pairs={{0,6},{1,7},{2,4},{3,5},{4,2},{5,3},{6,0},{7,1},{8,14},{9,15},{10,... | collective-permute-start | bytes 786440 | tf_op jit(solution)/shard_map/ppermute | solution.py:385
  101.8 11.3 %collective-permute-start.11 = (bf16[256,512]{1,0:T(8,128)(2,1)S(1)}, bf16[256,512]{1,0:T(8,128)(2,1)S(1)}, u32[]{:S(2)}, u32[]{:S(2)}) collective-permute-start(bf16[256,512]{1,0:T(8,128)(2,1)S(1)} %slice.54), channel_id=1, source_target_pairs={{0,2},{1,3},{2,0},{3,1},{4,6},{5,7},{6,4},{7,5},{8,10},{9,11},{10,... | collective-permute-start | bytes 786440 | tf_op jit(solution)/shard_map/ppermute | solution.py:385
  103.2 12.1 %collective-permute-start.9 = (bf16[256,512]{1,0:T(8,128)(2,1)S(1)}, bf16[256,512]{1,0:T(8,128)(2,1)S(1)}, u32[]{:S(2)}, u32[]{:S(2)}) collective-permute-start(bf16[256,512]{1,0:T(8,128)(2,1)S(1)} %slice.55), channel_id=1, source_target_pairs={{0,6},{1,7},{2,4},{3,5},{4,2},{5,3},{6,0},{7,1},{8,14},{9,15},{10,... | collective-permute-start | bytes 786440 | tf_op jit(solution)/shard_map/ppermute | solution.py:385
  108.5 6.9 %copy-start.3 = (bf16[512,1024]{1,0:T(8,128)(2,1)S(1)}, bf16[512,1024]{1,0:T(8,128)(2,1)}, u32[]{:S(2)}) copy-start(bf16[512,1024]{1,0:T(8,128)(2,1)} %param.14) | copy-start | bytes 3145732
  113.1 10.5 %copy-start.6 = (f32[1024]{0:T(1024)S(1)}, f32[1024]{0:T(1024)}, u32[]{:S(2)}) copy-start(f32[1024]{0:T(1024)} %param.21) | copy-start | bytes 12292
  115.8 1.2 collective-permute-start.19
  117.0 4.8 %collective-permute-start.22 = (f32[512]{0:T(512)S(1)}, f32[512]{0:T(512)S(1)}, u32[]{:S(2)}, u32[]{:S(2)}) collective-permute-start(f32[512]{0:T(512)S(1)} %add.170), channel_id=1, source_target_pairs={{0,6},{1,7},{2,4},{3,5},{4,2},{5,3},{6,0},{7,1},{8,14},{9,15},{10,... | collective-permute-start | bytes 6152 | tf_op jit(solution)/shard_map/ppermute | solution.py:385
  118.5 3.6 %collective-permute-start.21 = (f32[512]{0:T(512)S(1)}, f32[512]{0:T(512)S(1)}, u32[]{:S(2)}, u32[]{:S(2)}) collective-permute-start(f32[512]{0:T(512)S(1)} %add.170), channel_id=1, source_target_pairs={{0,2},{1,3},{2,0},{3,1},{4,6},{5,7},{6,4},{7,5},{8,10},{9,11},{10,... | collective-permute-start | bytes 6152 | tf_op jit(solution)/shard_map/ppermute | solution.py:385
  118.5 5.1 %collective-permute-start.20 = (f32[512]{0:T(512)S(1)}, f32[512]{0:T(512)S(1)}, u32[]{:S(2)}, u32[]{:S(2)}) collective-permute-start(f32[512]{0:T(512)S(1)} %add.170), channel_id=1, source_target_pairs={{0,4},{1,5},{2,6},{3,7},{4,0},{5,1},{6,2},{7,3},{8,12},{9,13},{10,... | collective-permute-start | bytes 6152 | tf_op jit(solution)/shard_map/ppermute | solution.py:385
  (1 other events, 1.0 us)

commit v6 on v4

--- a/solution.py
+++ b/solution.py
@@ -17,7 +17,7 @@
 BLOCK = 32
 FRESH = 128
 PAIRS = 48
-CHUNKS = 4
+CHUNKS = 8
 PIECE = 8
 UNROLL = 8
 LOW = -1e30
@@ -61,7 +61,7 @@
     return [ref[pl.ds(base, BLOCK), h * HD : (h + 1) * HD] for h in range(GROUP)]
 
 
-def payload_kernel(lengths, keys, values, out, held, sems):
+def payload_kernel(lengths_hbm, keys, values, out, lengths, held, sems, lengths_sem):
     packs, prefix, _ = keys.shape
     tile = packs // CHUNKS
 
@@ -75,9 +75,12 @@
         )
 
     steps = [copies(c) for c in range(CHUNKS)]
+    fetch = pltpu.make_async_copy(lengths_hbm, lengths, lengths_sem)
+    fetch.start()
     for step in steps:
         step[0].start()
         step[1].start()
+    fetch.wait()
     position = lax.broadcasted_iota(jnp.int32, keys.shape[1:], 0)
     for c, step in enumerate(steps):
         step[0].wait()
@@ -146,8 +149,6 @@
     fetch.append(pltpu.make_async_copy(mean_hbm.at[blocks], means, sems.at[3]))
     for i in (0, 2, 3, 1):
         fetch[i].start()
-    for copy in stage:
-        copy.start()
     ones = jnp.ones((16, HD), jnp.bfloat16)
     ahead = plan[4, 0]
     if first == 0:
@@ -207,6 +208,8 @@
         return carry
 
     fetch[0].wait()
+    for copy in stage:
+        copy.start()
     lax.fori_loop(lower, upper, score, 0)
     fetch[2].wait()
     fetch[3].wait()
@@ -243,56 +246,45 @@
     return pl.pallas_call(
         payload_kernel,
         out_shape=jax.ShapeDtypeStruct((packs, 2 * prefix, width), keys.dtype),
-        grid_spec=pltpu.PrefetchScalarGridSpec(
-            num_scalar_prefetch=1,
-            grid=(),
-            in_specs=far(2),
-            out_specs=far(1)[0],
-            scratch_shapes=[
-                pltpu.VMEM((packs, 2 * prefix, width), keys.dtype),
-                pltpu.SemaphoreType.DMA((3, CHUNKS)),
-            ],
-        ),
+        in_specs=far(3),
+        out_specs=far(1)[0],
+        scratch_shapes=[
+            pltpu.SMEM(lengths.shape, lengths.dtype),
+            pltpu.VMEM((packs, 2 * prefix, width), keys.dtype),
+            pltpu.SemaphoreType.DMA((3, CHUNKS)),
+            pltpu.SemaphoreType.DMA,
+        ],
         compiler_params=pltpu.CompilerParams(vmem_limit_bytes=4 << 20),
         cost_estimate=pl.CostEstimate(flops=1 << 20, bytes_accessed=4 << 20, transcendentals=0),
-    )(lengths, *in_hbm(keys, values))
+    )(*in_hbm(lengths, keys, values))
 
 
 def cut_kernel(starts, weight, after, *refs):
-    outs, held, sems = refs[:-2], refs[-2], refs[-1]
-    fetch, store = [], []
+    outs, sems = refs[:-1], refs[-1]
+    copies = []
     for out in outs:
         for i in range(out.shape[1] // 512):
-            slot = len(fetch)
-            start = pl.multiple_of(starts[slot], 512)
-            source = weight.at[:, pl.ds(start, 512)]
+            slot = len(copies)
+            source = weight.at[:, pl.ds(pl.multiple_of(starts[slot], 512), 512)]
             target = out.at[:, pl.ds(i * 512, 512)]
-            fetch.append(pltpu.make_async_copy(source, held.at[slot], sems.at[0, slot]))
-            store.append(pltpu.make_async_copy(held.at[slot], target, sems.at[1, slot]))
-    for copy in fetch:
+            copies.append(pltpu.make_async_copy(source, target, sems.at[slot]))
+    for copy in copies:
         copy.start()
-    for first, second in zip(fetch, store):
-        first.wait()
-        second.start()
-    for copy in store:
+    for copy in copies:
         copy.wait()
 
 
 def cut(starts, weight, widths, after):
     rows = weight.shape[0]
-    count = sum(widths) // 512
     return pl.pallas_call(
         cut_kernel,
-        out_shape=tuple(jax.ShapeDtypeStruct((rows, width), weight.dtype) for width in widths),
+        out_shape=tuple(pltpu.VMEM((rows, width), weight.dtype) for width in widths),
         grid_spec=pltpu.PrefetchScalarGridSpec(
             num_scalar_prefetch=1,
             grid=(),
             in_specs=far(1) + anywhere(1),
-            out_specs=tuple(far(len(widths))),
-            scratch_shapes=[
-                pltpu.VMEM((count, rows, 512), weight.dtype),
-                pltpu.SemaphoreType.DMA((2, count)),
-            ],
+            out_specs=tuple(whole(len(widths))),
+            scratch_shapes=[pltpu.SemaphoreType.DMA((sum(widths) // 512,))],
         ),
         compiler_params=pltpu.CompilerParams(vmem_limit_bytes=8 << 20),
         cost_estimate=pl.CostEstimate(flops=0, bytes_accessed=12 << 20, transcendentals=0),
@@ -382,10 +374,9 @@
     cache = lax.all_to_all(payload, "dp", split_axis=0, concat_axis=0, tiled=True)
 
     starts = sum([shared(mask)[half] for mask, half in ((2, 0), (6, 1), (3, 0), (7, 1))], [])
-    pieces = cut(jnp.stack(starts), out_weight, (1024,) * 4, payload)
-    starts, pieces = lax.optimization_barrier((jnp.stack(sum(shared(1), [])), pieces))
-    near_mats = [swap(piece, mask) for piece, mask in zip(pieces, (2, 6, 3, 7))]
-    sibling = swap(cut(starts, out_weight, (2048,), payload)[0], 1)
+    starts = jnp.stack(starts + sum(shared(1), []))
+    pieces = cut(starts, out_weight, (1024, 1024, 1024, 1024, 2048), payload)
+    *near_mats, sibling = [swap(piece, mask) for piece, mask in zip(pieces, (2, 6, 3, 7, 1))]
 
     plan, row_start = pair_plan(row_counts[0], pack_of[0])
     fresh = attend_fresh(queries, new_keys, new_values, row_start)

time: 114 us -> 111 us (0.974)
  Pallas kernels: 24.2 us -> 22.6 us
    all_to_all x1, waiting for transfers between devices: 12.4 us -> 13.7 us  [on_device(): lax.all_to_all(payload, 'dp', split_axis=0, concat_axis=0, tiled=True)]
    ppermute x23, waiting for transfers between devices: 27.5 us -> 26.2 us  [swap(): return lax.ppermute(value, 'tensor', [(t, t ^ mask) for t in range(count)])]
    pallas_call x2 -> x1, Pallas kernels: 7.3 us -> 6.06 us  [cut(): pl.pallas_call(cut_kernel, out_shape=tuple((pltpu.VMEM((rows, width), wei...]
    unnamed x20 -> x18, local copies, waits for them, and re-layouts: 2.62 us -> 1.98 us
  transfers between devices with their start and end apart: 24 -> 24, of which waited for: 12 -> 11; matrix products, arithmetic and copies ran while one was open for 8% -> 9% of each run, Pallas kernels for 19% -> 18%
where the time goes in v6:
time: 111 us
  waiting for transfers between devices  40 us (36%)
  starting transfers between devices  33.8 us (30%)
  Pallas kernels  22.6 us (20%)
  matrix products  7 us (6%)
  other arithmetic  3.61 us (3%)
  local copies, waits for them, and re-layouts  3.03 us (3%)
  between operations  1.15 us (1%)
    ppermute x23, waiting for transfers between devices, swap(): return lax.ppermute(value, 'tensor', [(t, t ^ mask) for t in range(count)])  26.2 us
    ppermute x23, starting transfers between devices, swap(): return lax.ppermute(value, 'tensor', [(t, t ^ mask) for t in range(count)])  22.2 us
    all_to_all x1, waiting for transfers between devices, on_device(): lax.all_to_all(payload, 'dp', split_axis=0, concat_axis=0, tiled=True)  13.7 us
    all_to_all x1, starting transfers between devices, on_device(): lax.all_to_all(payload, 'dp', split_axis=0, concat_axis=0, tiled=True)  11.6 us
    pallas_call x2, Pallas kernels, attend(): pl.pallas_call(functools.partial(main_kernel, first), out_shape=(rows, *s...  7.76 us
    dot_general x16, matrix products, times(): return jnp.dot(rows, mat, preferred_element_type=f32)  7 us
    pallas_call x1, Pallas kernels, attend_fresh(): pl.pallas_call(fresh_kernel, out_shape=(area, area), in_specs=whole(4), o...  6.17 us
    pallas_call x1, Pallas kernels, cut(): pl.pallas_call(cut_kernel, out_shape=tuple((pltpu.VMEM((rows, width), wei...  6.06 us
  transfers between devices with their start and end apart: 24, of which 11 were waited for; matrix products, arithmetic and copies ran while one was open for 9% of the time, Pallas kernels for 18%

profile of v6, /device:TPU:2, one launch (start us, length us, event | category | flops | bytes accessed | tf_op | source)
XLA Modules:
  0.0 111.1 jit_solution(17096377891221202211)
XLA Ops:
  0.6 2.6 %shard_map.122.after = bf16[32,256,128]{2,1,0:T(8,128)(2,1)} custom-call(s32[1,32]{1,0:T(1,128)} %lengths_hbm.1, bf16[32,128,128]{2,1,0:T(8,128)(2,1)} %bitcast.80, bf16[32,128,128]{2,1,0:T(8,128)(2,1)} %bitcast.81), custom_call_target="tpu_custom_call" | custom-call | flops 1048576 | bytes 4194304 | tf_op jit(solution)/shard_map/pallas_call | solution.py:246
  3.2 11.6 %all-to-all-start = ((bf16[32,256,128]{2,1,0:T(8,128)(2,1)}), bf16[32,256,128]{2,1,0:T(8,128)(2,1)S(1)}, u32[]{:S(2)}, u32[]{:S(2)}) async-start(bf16[32,256,128]{2,1,0:T(8,128)(2,1)} %shard_map.122.after), calls=%async_computation | async-start | bytes 4194304 | tf_op jit(solution)/shard_map/all_to_all | solution.py:374
  15.0 6.1 %shard_map.123 = (bf16[512,1024]{1,0:T(8,128)(2,1)}, bf16[512,1024]{1,0:T(8,128)(2,1)}, bf16[512,1024]{1,0:T(8,128)(2,1)}, bf16[512,1024]{1,0:T(8,128)(2,1)}, bf16[512,2048]{1,0:T(8,128)(2,1)}) custom-call(s32[12]{0:T(128)S(1)} %stack.86.starts, bf16[512,8192]{1,0:T(8,128)(2,1)} %refs_1_.1, bf16[32,256,128]{2,1,0:T(8,128)(2,1)} %shard_map.122.after), custom_call_target="tpu_custom_call" | custom-call | bytes 12582912 | tf_op jit(solution)/shard_map/pallas_call | solution.py:279
  21.2 1.7 %collective-permute-start.1 = (bf16[512,1024]{1,0:T(8,128)(2,1)}, bf16[512,1024]{1,0:T(8,128)(2,1)}, u32[]{:S(2)}, u32[]{:S(2)}) collective-permute-start(bf16[512,1024]{1,0:T(8,128)(2,1)} %get-tuple-element.31), channel_id=1, source_target_pairs={{0,2},{1,3},{2,0},{3,1},{4,6},{5,7},{6,4},{7,5},{8,10},{9,11},{10,... | collective-permute-start | bytes 3145736 | tf_op jit(solution)/shard_map/ppermute | solution.py:365
  22.9 2.2 %collective-permute-start.2 = (bf16[512,1024]{1,0:T(8,128)(2,1)}, bf16[512,1024]{1,0:T(8,128)(2,1)}, u32[]{:S(2)}, u32[]{:S(2)}) collective-permute-start(bf16[512,1024]{1,0:T(8,128)(2,1)} %get-tuple-element.32), channel_id=1, source_target_pairs={{0,6},{1,7},{2,4},{3,5},{4,2},{5,3},{6,0},{7,1},{8,14},{9,15},{10,... | collective-permute-start | bytes 3145736 | tf_op jit(solution)/shard_map/ppermute | solution.py:365
  25.2 0.9 collective-permute-start.6
  27.3 0.6 stack_broadcast_in_dim.3
  28.2 6.2 %shard_map.124 = (f32[16,128,128]{2,1,0:T(8,128)S(1)}, f32[16,128,128]{2,1,0:T(8,128)S(1)}) custom-call(bf16[512,512]{1,0:T(8,128)(2,1)S(1)} %copy-done.2, bf16[608,128]{1,0:T(8,128)(2,1)S(1)} %pad.7.fresh_k, bf16[608,128]{1,0:T(8,128)(2,1)S(1)} %pad.8.fresh_v, s32[512,128]{1,0:T(8,128)S(1)} %broadcast_in_dim.105.row_start), custom_call_target="tpu_custom_call" | custom-call | flops 2147483648 | bytes 4194304 | tf_op jit(solution)/shard_map/pallas_call | solution.py:297
  34.4 1.0 copy-done
  35.4 1.0 copy-done.1
  36.4 11.2 %collective-permute-done.1.refs_4_ = bf16[512,1024]{1,0:T(8,128)(2,1)} collective-permute-done((bf16[512,1024]{1,0:T(8,128)(2,1)}, bf16[512,1024]{1,0:T(8,128)(2,1)}, u32[]{:S(2)}, u32[]{:S(2)}) %collective-permute-start.1) | collective-permute-done | bytes 1048608 | tf_op jit(solution)/shard_map/ppermute | solution.py:365
  47.6 2.8 %collective-permute-done.2.refs_5_ = bf16[512,1024]{1,0:T(8,128)(2,1)} collective-permute-done((bf16[512,1024]{1,0:T(8,128)(2,1)}, bf16[512,1024]{1,0:T(8,128)(2,1)}, u32[]{:S(2)}, u32[]{:S(2)}) %collective-permute-start.2) | collective-permute-done | bytes 1048608 | tf_op jit(solution)/shard_map/ppermute | solution.py:365
  50.4 13.7 %all-to-all-done.cache_hbm = bf16[32,256,128]{2,1,0:T(8,128)(2,1)S(1)} async-done(((bf16[32,256,128]{2,1,0:T(8,128)(2,1)}), bf16[32,256,128]{2,1,0:T(8,128)(2,1)S(1)}, u32[]{:S(2)}, u32[]{:S(2)}) %all-to-all-start) | async-done | bytes 2097184 | tf_op jit(solution)/shard_map/all_to_all | solution.py:374
  64.1 3.2 %shard_map.125 = bf16[256,512]{1,0:T(8,128)(2,1)S(1)} custom-call(s32[5,48]{1,0:T(8,128)S(1)} %stack.73.plan, s32[4]{0:T(128)S(1)} %pad_add_fusion.starts, bf16[512,512]{1,0:T(8,128)(2,1)S(1)} %copy-done.2, bf16[32,256,128]{2,1,0:T(8,128)(2,1)S(1)} %all-to-all-done.cache_hbm, f32[16,128,128]{2,1,0:T(8,128)} %copy-done, f32[16,128,128]{2,1,0:T(8,128)} %copy-done.1), custom_call_target="tpu_custom_call" | custom-call | flops 2147483648 | bytes 4194304 | tf_op jit(solution)/shard_map/pallas_call | solution.py:313
  67.4 1.7 %collective-permute-start.3 = (bf16[256,512]{1,0:T(8,128)(2,1)S(1)}, bf16[256,512]{1,0:T(8,128)(2,1)S(1)}, u32[]{:S(2)}, u32[]{:S(2)}) collective-permute-start(bf16[256,512]{1,0:T(8,128)(2,1)S(1)} %shard_map.125), channel_id=1, source_target_pairs={{0,2},{1,3},{2,0},{3,1},{4,6},{5,7},{6,4},{7,5},{8,10},{9,11},{10,... | collective-permute-start | bytes 786440 | tf_op jit(solution)/shard_map/ppermute | solution.py:365
  69.1 2.2 %collective-permute-start.4 = (bf16[256,512]{1,0:T(8,128)(2,1)S(1)}, bf16[256,512]{1,0:T(8,128)(2,1)S(1)}, u32[]{:S(2)}, u32[]{:S(2)}) collective-permute-start(bf16[256,512]{1,0:T(8,128)(2,1)S(1)} %shard_map.125), channel_id=1, source_target_pairs={{0,6},{1,7},{2,4},{3,5},{4,2},{5,3},{6,0},{7,1},{8,14},{9,15},{10,... | collective-permute-start | bytes 786440 | tf_op jit(solution)/shard_map/ppermute | solution.py:365
  71.3 4.5 %shard_map.126 = (bf16[256,512]{1,0:T(8,128)(2,1)S(1)}, bf16[512,1024]{1,0:T(8,128)(2,1)S(1)}, bf16[512,1024]{1,0:T(8,128)(2,1)S(1)}, bf16[512,1024]{1,0:T(8,128...) custom-call(s32[5,48]{1,0:T(8,128)S(1)} %stack.73.plan, ...), custom_call_target="tpu_custom_call" | custom-call | flops 2147483648 | bytes 4194304 | tf_op jit(solution)/shard_map/pallas_call | solution.py:313
  75.8 0.7 collective-permute-start.14
  76.7 2.1 %collective-permute-start.13 = (bf16[256,512]{1,0:T(8,128)(2,1)S(1)}, bf16[256,512]{1,0:T(8,128)(2,1)S(1)}, u32[]{:S(2)}, u32[]{:S(2)}) collective-permute-start(bf16[256,512]{1,0:T(8,128)(2,1)S(1)} %get-tuple-element.53), channel_id=1, source_target_pairs={{0,6},{1,7},{2,4},{3,5},{4,2},{5,3},{6,0},{7,1},{8,14},{9,15},{10,... | collective-permute-start | bytes 786440 | tf_op jit(solution)/shard_map/ppermute | solution.py:365
  84.4 1.2 %collective-permute-start.9 = (bf16[256,512]{1,0:T(8,128)(2,1)S(1)}, bf16[256,512]{1,0:T(8,128)(2,1)S(1)}, u32[]{:S(2)}, u32[]{:S(2)}) collective-permute-start(bf16[256,512]{1,0:T(8,128)(2,1)S(1)} %slice.55), channel_id=1, source_target_pairs={{0,6},{1,7},{2,4},{3,5},{4,2},{5,3},{6,0},{7,1},{8,14},{9,15},{10,... | collective-permute-start | bytes 786440 | tf_op jit(solution)/shard_map/ppermute | solution.py:365
  86.1 0.7 collective-permute-start.11
  89.4 2.3 %collective-permute-start.16 = (bf16[256,512]{1,0:T(8,128)(2,1)S(1)}, bf16[256,512]{1,0:T(8,128)(2,1)S(1)}, u32[]{:S(2)}, u32[]{:S(2)}) collective-permute-start(bf16[256,512]{1,0:T(8,128)(2,1)S(1)} %slice.53), channel_id=1, source_target_pairs={{0,6},{1,7},{2,4},{3,5},{4,2},{5,3},{6,0},{7,1},{8,14},{9,15},{10,... | collective-permute-start | bytes 786440 | tf_op jit(solution)/shard_map/ppermute | solution.py:365
  92.2 0.8 collective-permute-start.18
  92.9 1.9 %collective-permute-done.9 = bf16[256,512]{1,0:T(8,128)(2,1)S(1)} collective-permute-done((bf16[256,512]{1,0:T(8,128)(2,1)S(1)}, bf16[256,512]{1,0:T(8,128)(2,1)S(1)}, u32[]{:S(2)}, u32[]{:S(2)}) %collective-permute-start.9) | collective-permute-done | bytes 262176 | tf_op jit(solution)/shard_map/ppermute | solution.py:365
  95.0 4.8 %collective-permute-done.16 = bf16[256,512]{1,0:T(8,128)(2,1)S(1)} collective-permute-done((bf16[256,512]{1,0:T(8,128)(2,1)S(1)}, bf16[256,512]{1,0:T(8,128)(2,1)S(1)}, u32[]{:S(2)}, u32[]{:S(2)}) %collective-permute-start.16) | collective-permute-done | bytes 262176 | tf_op jit(solution)/shard_map/ppermute | solution.py:365
  100.9 1.1 %collective-permute-done.19 = f32[512]{0:T(512)S(1)} collective-permute-done((f32[512]{0:T(512)S(1)}, f32[512]{0:T(512)S(1)}, u32[]{:S(2)}, u32[]{:S(2)}) %collective-permute-start.19) | collective-permute-done | bytes 2080 | tf_op jit(solution)/shard_map/ppermute | solution.py:365
  102.0 2.0 %collective-permute-start.20 = (f32[512]{0:T(512)S(1)}, f32[512]{0:T(512)S(1)}, u32[]{:S(2)}, u32[]{:S(2)}) collective-permute-start(f32[512]{0:T(512)S(1)} %add.170), channel_id=1, source_target_pairs={{0,4},{1,5},{2,6},{3,7},{4,0},{5,1},{6,2},{7,3},{8,12},{9,13},{10,... | collective-permute-start | bytes 6152 | tf_op jit(solution)/shard_map/ppermute | solution.py:365
  104.0 0.7 collective-permute-start.21
  104.7 1.4 %collective-permute-start.22 = (f32[512]{0:T(512)S(1)}, f32[512]{0:T(512)S(1)}, u32[]{:S(2)}, u32[]{:S(2)}) collective-permute-start(f32[512]{0:T(512)S(1)} %add.170), channel_id=1, source_target_pairs={{0,6},{1,7},{2,4},{3,5},{4,2},{5,3},{6,0},{7,1},{8,14},{9,15},{10,... | collective-permute-start | bytes 6152 | tf_op jit(solution)/shard_map/ppermute | solution.py:365
  106.1 1.0 collective-permute-done.20
  107.6 1.9 %collective-permute-done.22 = f32[512]{0:T(512)S(1)} collective-permute-done((f32[512]{0:T(512)S(1)}, f32[512]{0:T(512)S(1)}, u32[]{:S(2)}, u32[]{:S(2)}) %collective-permute-start.22) | collective-permute-done | bytes 2080 | tf_op jit(solution)/shard_map/ppermute | solution.py:365
  109.5 1.7 %multiply_convert_fusion = (bf16[512,1024]{1,0:T(8,128)(2,1)}, bf16[512,1024]{1,0:T(8,128)(2,1)}) fusion(f32[1024]{0:T(1024)S(1)} %copy-done.6, f32[512]{0:T(512)S(1)} %add_rsqrt_fusion, f32[256,512]{1,0:T(8,128)S(1)} %slice_add_fusion, f32[256,512]{1,0:T(8,128)S(1)} %slice_add_fusion.1, f32[256,512]{1,0:T(8,128)S(1)} %slice_add_fusion.2, ...), kind=kLoop, calls=%fused_computation.1 | loop fusion | flops 4718592 | bytes 5249024 | tf_op jit(solution)/shard_map/convert_element_type | solution.py:423
  (83 shorter events, 12.7 us)
Async XLA Ops:
  3.2 60.9 %all-to-all-start = ((bf16[32,256,128]{2,1,0:T(8,128)(2,1)}), bf16[32,256,128]{2,1,0:T(8,128)(2,1)S(1)}, u32[]{:S(2)}, u32[]{:S(2)}) async-start(bf16[32,256,128]{2,1,0:T(8,128)(2,1)} %shard_map.122.after), calls=%async_computation | async-start | bytes 4194304 | tf_op jit(solution)/shard_map/all_to_all | solution.py:374
  15.0 11.1 %copy-start.8 = (s32[1,32]{1,0:T(1,128)S(1)}, s32[1,32]{1,0:T(1,128)}, u32[]{:S(2)}) copy-start(s32[1,32]{1,0:T(1,128)} %param.15) | copy-start | bytes 388
  15.0 11.3 %copy-start.4 = (bf16[512,128]{1,0:T(8,128)(2,1)S(1)}, bf16[512,128]{1,0:T(8,128)(2,1)}, u32[]{:S(2)}) copy-start(bf16[512,128]{1,0:T(8,128)(2,1)} %param.12) | copy-start | bytes 393220
  15.0 11.4 %copy-start.5 = (bf16[512,128]{1,0:T(8,128)(2,1)S(1)}, bf16[512,128]{1,0:T(8,128)(2,1)}, u32[]{:S(2)}) copy-start(bf16[512,128]{1,0:T(8,128)(2,1)} %param.13) | copy-start | bytes 393220
  15.0 11.5 %copy-start.7 = (s32[1,32]{1,0:T(1,128)S(1)}, s32[1,32]{1,0:T(1,128)}, u32[]{:S(2)}) copy-start(s32[1,32]{1,0:T(1,128)} %param.16) | copy-start | bytes 388
  15.0 13.2 %copy-start.2 = (bf16[512,512]{1,0:T(8,128)(2,1)S(1)}, bf16[512,512]{1,0:T(8,128)(2,1)}, u32[]{:S(2)}) copy-start(bf16[512,512]{1,0:T(8,128)(2,1)} %q.5) | copy-start | bytes 1572868
  21.1 29.3 %collective-permute-start = (bf16[512,2048]{1,0:T(8,128)(2,1)}, bf16[512,2048]{1,0:T(8,128)(2,1)}, u32[]{:S(2)}, u32[]{:S(2)}) collective-permute-start(bf16[512,2048]{1,0:T(8,128)(2,1)} %get-tuple-element.30), channel_id=1, source_target_pairs={{0,1},{1,0},{2,3},{3,2},{4,5},{5,4},{6,7},{7,6},{8,9},{9,8},{10,11... | collective-permute-start | bytes 6291464 | tf_op jit(solution)/shard_map/ppermute | solution.py:365
  21.2 26.4 %collective-permute-start.1 = (bf16[512,1024]{1,0:T(8,128)(2,1)}, bf16[512,1024]{1,0:T(8,128)(2,1)}, u32[]{:S(2)}, u32[]{:S(2)}) collective-permute-start(bf16[512,1024]{1,0:T(8,128)(2,1)} %get-tuple-element.31), channel_id=1, source_target_pairs={{0,2},{1,3},{2,0},{3,1},{4,6},{5,7},{6,4},{7,5},{8,10},{9,11},{10,... | collective-permute-start | bytes 3145736 | tf_op jit(solution)/shard_map/ppermute | solution.py:365
  22.9 27.5 %collective-permute-start.2 = (bf16[512,1024]{1,0:T(8,128)(2,1)}, bf16[512,1024]{1,0:T(8,128)(2,1)}, u32[]{:S(2)}, u32[]{:S(2)}) collective-permute-start(bf16[512,1024]{1,0:T(8,128)(2,1)} %get-tuple-element.32), channel_id=1, source_target_pairs={{0,6},{1,7},{2,4},{3,5},{4,2},{5,3},{6,0},{7,1},{8,14},{9,15},{10,... | collective-permute-start | bytes 3145736 | tf_op jit(solution)/shard_map/ppermute | solution.py:365
  25.1 46.2 %collective-permute-start.5 = (bf16[512,1024]{1,0:T(8,128)(2,1)}, bf16[512,1024]{1,0:T(8,128)(2,1)}, u32[]{:S(2)}, u32[]{:S(2)}) collective-permute-start(bf16[512,1024]{1,0:T(8,128)(2,1)} %get-tuple-element.39), channel_id=1, source_target_pairs={{0,3},{1,2},{2,1},{3,0},{4,7},{5,6},{6,5},{7,4},{8,11},{9,10},{10,... | collective-permute-start | bytes 3145736 | tf_op jit(solution)/shard_map/ppermute | solution.py:365
  25.2 46.1 %collective-permute-start.6 = (bf16[512,1024]{1,0:T(8,128)(2,1)}, bf16[512,1024]{1,0:T(8,128)(2,1)}, u32[]{:S(2)}, u32[]{:S(2)}) collective-permute-start(bf16[512,1024]{1,0:T(8,128)(2,1)} %get-tuple-element.40), channel_id=1, source_target_pairs={{0,7},{1,6},{2,5},{3,4},{4,3},{5,2},{6,1},{7,0},{8,15},{9,14},{10,... | collective-permute-start | bytes 3145736 | tf_op jit(solution)/shard_map/ppermute | solution.py:365
  34.4 1.0 copy-start
  67.3 9.4 %collective-permute-start.7 = (bf16[256,512]{1,0:T(8,128)(2,1)S(1)}, bf16[256,512]{1,0:T(8,128)(2,1)S(1)}, u32[]{:S(2)}, u32[]{:S(2)}) collective-permute-start(bf16[256,512]{1,0:T(8,128)(2,1)S(1)} %shard_map.125), channel_id=1, source_target_pairs={{0,1},{1,0},{2,3},{3,2},{4,5},{5,4},{6,7},{7,6},{8,9},{9,8},{10,11... | collective-permute-start | bytes 786440 | tf_op jit(solution)/shard_map/ppermute | solution.py:365
  67.4 13.1 %collective-permute-start.3 = (bf16[256,512]{1,0:T(8,128)(2,1)S(1)}, bf16[256,512]{1,0:T(8,128)(2,1)S(1)}, u32[]{:S(2)}, u32[]{:S(2)}) collective-permute-start(bf16[256,512]{1,0:T(8,128)(2,1)S(1)} %shard_map.125), channel_id=1, source_target_pairs={{0,2},{1,3},{2,0},{3,1},{4,6},{5,7},{6,4},{7,5},{8,10},{9,11},{10,... | collective-permute-start | bytes 786440 | tf_op jit(solution)/shard_map/ppermute | solution.py:365
  69.1 11.5 %collective-permute-start.4 = (bf16[256,512]{1,0:T(8,128)(2,1)S(1)}, bf16[256,512]{1,0:T(8,128)(2,1)S(1)}, u32[]{:S(2)}, u32[]{:S(2)}) collective-permute-start(bf16[256,512]{1,0:T(8,128)(2,1)S(1)} %shard_map.125), channel_id=1, source_target_pairs={{0,6},{1,7},{2,4},{3,5},{4,2},{5,3},{6,0},{7,1},{8,14},{9,15},{10,... | collective-permute-start | bytes 786440 | tf_op jit(solution)/shard_map/ppermute | solution.py:365
  75.8 5.8 %collective-permute-start.14 = (bf16[256,512]{1,0:T(8,128)(2,1)S(1)}, bf16[256,512]{1,0:T(8,128)(2,1)S(1)}, u32[]{:S(2)}, u32[]{:S(2)}) collective-permute-start(bf16[256,512]{1,0:T(8,128)(2,1)S(1)} %get-tuple-element.53), channel_id=1, source_target_pairs={{0,1},{1,0},{2,3},{3,2},{4,5},{5,4},{6,7},{7,6},{8,9},{9,8},{10,11... | collective-permute-start | bytes 786440 | tf_op jit(solution)/shard_map/ppermute | solution.py:365
  76.5 10.3 %collective-permute-start.12 = (bf16[256,512]{1,0:T(8,128)(2,1)S(1)}, bf16[256,512]{1,0:T(8,128)(2,1)S(1)}, u32[]{:S(2)}, u32[]{:S(2)}) collective-permute-start(bf16[256,512]{1,0:T(8,128)(2,1)S(1)} %get-tuple-element.53), channel_id=1, source_target_pairs={{0,2},{1,3},{2,0},{3,1},{4,6},{5,7},{6,4},{7,5},{8,10},{9,11},{10,... | collective-permute-start | bytes 786440 | tf_op jit(solution)/shard_map/ppermute | solution.py:365
  76.7 10.1 %collective-permute-start.13 = (bf16[256,512]{1,0:T(8,128)(2,1)S(1)}, bf16[256,512]{1,0:T(8,128)(2,1)S(1)}, u32[]{:S(2)}, u32[]{:S(2)}) collective-permute-start(bf16[256,512]{1,0:T(8,128)(2,1)S(1)} %get-tuple-element.53), channel_id=1, source_target_pairs={{0,6},{1,7},{2,4},{3,5},{4,2},{5,3},{6,0},{7,1},{8,14},{9,15},{10,... | collective-permute-start | bytes 786440 | tf_op jit(solution)/shard_map/ppermute | solution.py:365
  80.6 3.3 %collective-permute-start.8 = (bf16[256,512]{1,0:T(8,128)(2,1)S(1)}, bf16[256,512]{1,0:T(8,128)(2,1)S(1)}, u32[]{:S(2)}, u32[]{:S(2)}) collective-permute-start(bf16[256,512]{1,0:T(8,128)(2,1)S(1)} %collective-permute-done.3), channel_id=1, source_target_pairs={{0,1},{1,0},{2,3},{3,2},{4,5},{5,4},{6,7},{7,6},{8,9},{9,8},{10,11... | collective-permute-start | bytes 786440 | tf_op jit(solution)/shard_map/ppermute | solution.py:365
  80.7 4.9 %collective-permute-start.10 = (bf16[256,512]{1,0:T(8,128)(2,1)S(1)}, bf16[256,512]{1,0:T(8,128)(2,1)S(1)}, u32[]{:S(2)}, u32[]{:S(2)}) collective-permute-start(bf16[256,512]{1,0:T(8,128)(2,1)S(1)} %collective-permute-done.4), channel_id=1, source_target_pairs={{0,1},{1,0},{2,3},{3,2},{4,5},{5,4},{6,7},{7,6},{8,9},{9,8},{10,11... | collective-permute-start | bytes 786440 | tf_op jit(solution)/shard_map/ppermute | solution.py:365
  84.4 10.4 %collective-permute-start.9 = (bf16[256,512]{1,0:T(8,128)(2,1)S(1)}, bf16[256,512]{1,0:T(8,128)(2,1)S(1)}, u32[]{:S(2)}, u32[]{:S(2)}) collective-permute-start(bf16[256,512]{1,0:T(8,128)(2,1)S(1)} %slice.55), channel_id=1, source_target_pairs={{0,6},{1,7},{2,4},{3,5},{4,2},{5,3},{6,0},{7,1},{8,14},{9,15},{10,... | collective-permute-start | bytes 786440 | tf_op jit(solution)/shard_map/ppermute | solution.py:365
  86.1 8.8 %collective-permute-start.11 = (bf16[256,512]{1,0:T(8,128)(2,1)S(1)}, bf16[256,512]{1,0:T(8,128)(2,1)S(1)}, u32[]{:S(2)}, u32[]{:S(2)}) collective-permute-start(bf16[256,512]{1,0:T(8,128)(2,1)S(1)} %slice.54), channel_id=1, source_target_pairs={{0,2},{1,3},{2,0},{3,1},{4,6},{5,7},{6,4},{7,5},{8,10},{9,11},{10,... | collective-permute-start | bytes 786440 | tf_op jit(solution)/shard_map/ppermute | solution.py:365
  87.3 1.6 %collective-permute-start.15 = (bf16[256,512]{1,0:T(8,128)(2,1)S(1)}, bf16[256,512]{1,0:T(8,128)(2,1)S(1)}, u32[]{:S(2)}, u32[]{:S(2)}) collective-permute-start(bf16[256,512]{1,0:T(8,128)(2,1)S(1)} %collective-permute-done.12), channel_id=1, source_target_pairs={{0,1},{1,0},{2,3},{3,2},{4,5},{5,4},{6,7},{7,6},{8,9},{9,8},{10,11... | collective-permute-start | bytes 786440 | tf_op jit(solution)/shard_map/ppermute | solution.py:365
  87.4 4.3 %collective-permute-start.17 = (bf16[256,512]{1,0:T(8,128)(2,1)S(1)}, bf16[256,512]{1,0:T(8,128)(2,1)S(1)}, u32[]{:S(2)}, u32[]{:S(2)}) collective-permute-start(bf16[256,512]{1,0:T(8,128)(2,1)S(1)} %collective-permute-done.13), channel_id=1, source_target_pairs={{0,1},{1,0},{2,3},{3,2},{4,5},{5,4},{6,7},{7,6},{8,9},{9,8},{10,11... | collective-permute-start | bytes 786440 | tf_op jit(solution)/shard_map/ppermute | solution.py:365
  89.4 10.4 %collective-permute-start.16 = (bf16[256,512]{1,0:T(8,128)(2,1)S(1)}, bf16[256,512]{1,0:T(8,128)(2,1)S(1)}, u32[]{:S(2)}, u32[]{:S(2)}) collective-permute-start(bf16[256,512]{1,0:T(8,128)(2,1)S(1)} %slice.53), channel_id=1, source_target_pairs={{0,6},{1,7},{2,4},{3,5},{4,2},{5,3},{6,0},{7,1},{8,14},{9,15},{10,... | collective-permute-start | bytes 786440 | tf_op jit(solution)/shard_map/ppermute | solution.py:365
  92.2 8.2 %collective-permute-start.18 = (bf16[256,512]{1,0:T(8,128)(2,1)S(1)}, bf16[256,512]{1,0:T(8,128)(2,1)S(1)}, u32[]{:S(2)}, u32[]{:S(2)}) collective-permute-start(bf16[256,512]{1,0:T(8,128)(2,1)S(1)} %slice.52), channel_id=1, source_target_pairs={{0,2},{1,3},{2,0},{3,1},{4,6},{5,7},{6,4},{7,5},{8,10},{9,11},{10,... | collective-permute-start | bytes 786440 | tf_op jit(solution)/shard_map/ppermute | solution.py:365
  94.9 5.5 %copy-start.3 = (bf16[512,1024]{1,0:T(8,128)(2,1)S(1)}, bf16[512,1024]{1,0:T(8,128)(2,1)}, u32[]{:S(2)}) copy-start(bf16[512,1024]{1,0:T(8,128)(2,1)} %param.14) | copy-start | bytes 3145732
  99.9 9.6 %copy-start.6 = (f32[1024]{0:T(1024)S(1)}, f32[1024]{0:T(1024)}, u32[]{:S(2)}) copy-start(f32[1024]{0:T(1024)} %param.21) | copy-start | bytes 12292
  100.8 1.2 %collective-permute-start.19 = (f32[512]{0:T(512)S(1)}, f32[512]{0:T(512)S(1)}, u32[]{:S(2)}, u32[]{:S(2)}) collective-permute-start(f32[512]{0:T(512)S(1)} %multiply_reduce_fusion), channel_id=1, source_target_pairs={{0,1},{1,0},{2,3},{3,2},{4,5},{5,4},{6,7},{7,6},{8,9},{9,8},{10,11... | collective-permute-start | bytes 6152 | tf_op jit(solution)/shard_map/ppermute | solution.py:365
  102.0 5.1 %collective-permute-start.20 = (f32[512]{0:T(512)S(1)}, f32[512]{0:T(512)S(1)}, u32[]{:S(2)}, u32[]{:S(2)}) collective-permute-start(f32[512]{0:T(512)S(1)} %add.170), channel_id=1, source_target_pairs={{0,4},{1,5},{2,6},{3,7},{4,0},{5,1},{6,2},{7,3},{8,12},{9,13},{10,... | collective-permute-start | bytes 6152 | tf_op jit(solution)/shard_map/ppermute | solution.py:365
  104.0 3.6 %collective-permute-start.21 = (f32[512]{0:T(512)S(1)}, f32[512]{0:T(512)S(1)}, u32[]{:S(2)}, u32[]{:S(2)}) collective-permute-start(f32[512]{0:T(512)S(1)} %add.170), channel_id=1, source_target_pairs={{0,2},{1,3},{2,0},{3,1},{4,6},{5,7},{6,4},{7,5},{8,10},{9,11},{10,... | collective-permute-start | bytes 6152 | tf_op jit(solution)/shard_map/ppermute | solution.py:365
  104.7 4.8 %collective-permute-start.22 = (f32[512]{0:T(512)S(1)}, f32[512]{0:T(512)S(1)}, u32[]{:S(2)}, u32[]{:S(2)}) collective-permute-start(f32[512]{0:T(512)S(1)} %add.170), channel_id=1, source_target_pairs={{0,6},{1,7},{2,4},{3,5},{4,2},{5,3},{6,0},{7,1},{8,14},{9,15},{10,... | collective-permute-start | bytes 6152 | tf_op jit(solution)/shard_map/ppermute | solution.py:365
  (1 other events, 1.0 us)

commit v7 on v6

--- a/solution.py
+++ b/solution.py
@@ -120,10 +120,10 @@
     lax.fori_loop(0, 512 // BLOCK, body, 0, unroll=2)
 
 
-def main_kernel(first, plan, starts, q, cache_hbm, mean_hbm, level_hbm, *refs):
-    cache, means, levels, scores, weights, mixed, sems, stage_sems = refs[-8:]
-    count = (len(refs) - 9) // 2
-    sources, out, staged = refs[:count], refs[count], refs[count + 1 : -8]
+def main_kernel(first, plan, starts, q, cache, mean_hbm, level_hbm, *refs):
+    means, levels, scores, weights, mixed, sems, stage_sems = refs[-7:]
+    count = (len(refs) - 8) // 2
+    sources, out, staged = refs[:count], refs[count], refs[count + 1 : -7]
     stage = []
     for place_of, (source, target) in enumerate(zip(sources, staged)):
         if source.shape == target.shape:
@@ -138,17 +138,13 @@
         for origin, goal in parts:
             stage.append(pltpu.make_async_copy(origin, goal, stage_sems.at[len(stage)]))
     half = cache.shape[1] // 2
+    blocks = pl.ds(first, PIECE)
     fetch = [
-        pltpu.make_async_copy(
-            cache_hbm.at[:, pl.ds(i * half, half)], cache.at[:, pl.ds(i * half, half)], sems.at[i]
-        )
-        for i in range(2)
+        pltpu.make_async_copy(level_hbm.at[blocks], levels, sems.at[0]),
+        pltpu.make_async_copy(mean_hbm.at[blocks], means, sems.at[1]),
     ]
-    blocks = pl.ds(first, PIECE)
-    fetch.append(pltpu.make_async_copy(level_hbm.at[blocks], levels, sems.at[2]))
-    fetch.append(pltpu.make_async_copy(mean_hbm.at[blocks], means, sems.at[3]))
-    for i in (0, 2, 3, 1):
-        fetch[i].start()
+    for copy in fetch + stage:
+        copy.start()
     ones = jnp.ones((16, HD), jnp.bfloat16)
     ahead = plan[4, 0]
     if first == 0:
@@ -207,14 +203,10 @@
                 mixed[block, part] += jnp.where(mine, found[h * BLOCK : (h + 1) * BLOCK], 0.0)
         return carry
 
-    fetch[0].wait()
-    for copy in stage:
-        copy.start()
     lax.fori_loop(lower, upper, score, 0)
-    fetch[2].wait()
-    fetch[3].wait()
+    for copy in fetch:
+        copy.wait()
     lax.fori_loop(0, PIECE, soften, 0, unroll=PIECE)
-    fetch[1].wait()
     lax.fori_loop(lower, upper, mix, 0)
     for block in range(PIECE):
         total = mixed[block].astype(jnp.bfloat16)
@@ -316,31 +308,23 @@
         grid_spec=pltpu.PrefetchScalarGridSpec(
             num_scalar_prefetch=2,
             grid=(),
-            in_specs=whole(1) + anywhere(3 + len(sources)),
+            in_specs=whole(2) + anywhere(2 + len(sources)),
             out_specs=tuple(whole(1 + len(staged))),
             scratch_shapes=[
-                pltpu.VMEM(cache.shape, cache.dtype),
                 pltpu.VMEM((PIECE, *area), jnp.float32),
                 pltpu.VMEM((PIECE, *area), jnp.float32),
                 pltpu.VMEM((PIECE + 1, *area), jnp.float32),
                 pltpu.VMEM((PIECE + 1, *area), jnp.bfloat16),
                 pltpu.VMEM((PIECE + 1, *area), jnp.float32),
-                pltpu.SemaphoreType.DMA((4,)),
+                pltpu.SemaphoreType.DMA((2,)),
                 pltpu.SemaphoreType.DMA((len(sources) + 2,)),
             ],
         ),
-        compiler_params=pltpu.CompilerParams(vmem_limit_bytes=(7 + len(sources)) << 20),
+        compiler_params=pltpu.CompilerParams(vmem_limit_bytes=12 << 20),
         cost_estimate=pl.CostEstimate(
             flops=1 << 31, bytes_accessed=4 << 20, transcendentals=1 << 18
         ),
-    )(plan, starts, queries, cache, *in_hbm(*fresh), *in_hbm(*sources))
-
-
-def attention(counts, packs, queries, marked, values, new_keys, new_values):
-    plan, row_start = pair_plan(counts, packs)
-    fresh = attend_fresh(queries, new_keys, new_values, row_start)
-    cache = jnp.concatenate([marked, values], axis=1)
-    return jnp.concatenate([attend(i, plan, plan[0], queries, cache, fresh)[0] for i in (0, PIECE)], axis=0)
+    )(plan, starts, queries, cache, *in_hbm(*fresh, *sources))
 
 
 def on_device(
@@ -372,6 +356,7 @@
 
     payload = make_payload(prefix_lengths, cache_keys[0], cache_values[0])
     cache = lax.all_to_all(payload, "dp", split_axis=0, concat_axis=0, tiled=True)
+    cache = pltpu.with_memory_space_constraint(cache, pltpu.VMEM)
 
     starts = sum([shared(mask)[half] for mask, half in ((2, 0), (6, 1), (3, 0), (7, 1))], [])
     starts = jnp.stack(starts + sum(shared(1), []))
@@ -382,10 +367,10 @@
     fresh = attend_fresh(queries, new_keys, new_values, row_start)
     plan, sibling, near_mats[:2] = lax.optimization_barrier((plan, sibling, near_mats[:2]))
     starts = jnp.stack(sum(shared(0), []))
-    attended = attend(0, plan, starts, queries, cache, fresh)
+    rows = attend(0, plan, starts, queries, cache, fresh)[0]
     sources = (out_weight, out_weight, sibling, sibling, *near_mats)
     rest, *mats = attend(PIECE, plan, starts, queries, cache, fresh, sources)
-    attended = [attended[0], rest]
+    attended = [rows, rest]
     here, sibling, same, cross = (mats[i : i + 2] for i in (0, 2, 4, 6))
 
     def times(rows, mat):

time: 111 us -> 113 us (1.018)
  Pallas kernels: 22.6 us -> 23.9 us
    pallas_call x2, Pallas kernels: 7.76 us -> 9.05 us  [attend(): pl.pallas_call(functools.partial(main_kernel, first), out_shape=(rows, *s...]
  transfers between devices with their start and end apart: 24 -> 24, of which waited for: 11 -> 11; matrix products, arithmetic and copies ran while one was open for 9% -> 9% of each run, Pallas kernels for 18% -> 19%
where the time goes in v7:
time: 113 us; the launch traced here: 112 us
  waiting for transfers between devices  40 us (35%)
  starting transfers between devices  33.4 us (30%)
  Pallas kernels  23.9 us (21%)
  matrix products  6.99 us (6%)
  other arithmetic  3.62 us (3%)
  local copies, waits for them, and re-layouts  3.03 us (3%)
  between operations  1.15 us (1%)
    ppermute x23, waiting for transfers between devices, swap(): return lax.ppermute(value, 'tensor', [(t, t ^ mask) for t in range(count)])  26.2 us
    ppermute x23, starting transfers between devices, swap(): return lax.ppermute(value, 'tensor', [(t, t ^ mask) for t in range(count)])  21.8 us
    all_to_all x1, waiting for transfers between devices, on_device(): lax.all_to_all(payload, 'dp', split_axis=0, concat_axis=0, tiled=True)  13.7 us
    all_to_all x1, starting transfers between devices, on_device(): lax.all_to_all(payload, 'dp', split_axis=0, concat_axis=0, tiled=True)  11.6 us
    pallas_call x2, Pallas kernels, attend(): pl.pallas_call(functools.partial(main_kernel, first), out_shape=(rows, *s...  9.05 us
    dot_general x16, matrix products, times(): return jnp.dot(rows, mat, preferred_element_type=f32)  6.99 us
    pallas_call x1, Pallas kernels, attend_fresh(): pl.pallas_call(fresh_kernel, out_shape=(area, area), in_specs=whole(4), o...  6.17 us
    pallas_call x1, Pallas kernels, cut(): pl.pallas_call(cut_kernel, out_shape=tuple((pltpu.VMEM((rows, width), wei...  6.06 us
  transfers between devices with their start and end apart: 24, of which 11 were waited for; matrix products, arithmetic and copies ran while one was open for 9% of the time, Pallas kernels for 19%

profile of v7, /device:TPU:2, one launch (start us, length us, event | category | flops | bytes accessed | tf_op | source)
XLA Modules:
  0.0 112.0 jit_solution(13081199415584846660)
XLA Ops:
  0.6 2.6 %shard_map.122.after = bf16[32,256,128]{2,1,0:T(8,128)(2,1)} custom-call(s32[1,32]{1,0:T(1,128)} %lengths_hbm.1, bf16[32,128,128]{2,1,0:T(8,128)(2,1)} %bitcast.80, bf16[32,128,128]{2,1,0:T(8,128)(2,1)} %bitcast.81), custom_call_target="tpu_custom_call" | custom-call | flops 1048576 | bytes 4194304 | tf_op jit(solution)/shard_map/pallas_call | solution.py:238
  3.2 11.6 %all-to-all-start = ((bf16[32,256,128]{2,1,0:T(8,128)(2,1)}), bf16[32,256,128]{2,1,0:T(8,128)(2,1)S(1)}, u32[]{:S(2)}, u32[]{:S(2)}) async-start(bf16[32,256,128]{2,1,0:T(8,128)(2,1)} %shard_map.122.after), calls=%async_computation | async-start | bytes 4194304 | tf_op jit(solution)/shard_map/all_to_all | solution.py:358
  15.0 6.1 %shard_map.123 = (bf16[512,1024]{1,0:T(8,128)(2,1)}, bf16[512,1024]{1,0:T(8,128)(2,1)}, bf16[512,1024]{1,0:T(8,128)(2,1)}, bf16[512,1024]{1,0:T(8,128)(2,1)}, bf16[512,2048]{1,0:T(8,128)(2,1)}) custom-call(s32[12]{0:T(128)S(1)} %stack.86.starts, bf16[512,8192]{1,0:T(8,128)(2,1)} %refs_1_.1, bf16[32,256,128]{2,1,0:T(8,128)(2,1)} %shard_map.122.after), custom_call_target="tpu_custom_call" | custom-call | bytes 12582912 | tf_op jit(solution)/shard_map/pallas_call | solution.py:271
  21.2 1.7 %collective-permute-start.1 = (bf16[512,1024]{1,0:T(8,128)(2,1)}, bf16[512,1024]{1,0:T(8,128)(2,1)}, u32[]{:S(2)}, u32[]{:S(2)}) collective-permute-start(bf16[512,1024]{1,0:T(8,128)(2,1)} %get-tuple-element.31), channel_id=1, source_target_pairs={{0,2},{1,3},{2,0},{3,1},{4,6},{5,7},{6,4},{7,5},{8,10},{9,11},{10,... | collective-permute-start | bytes 3145736 | tf_op jit(solution)/shard_map/ppermute | solution.py:349
  22.9 2.2 %collective-permute-start.2 = (bf16[512,1024]{1,0:T(8,128)(2,1)}, bf16[512,1024]{1,0:T(8,128)(2,1)}, u32[]{:S(2)}, u32[]{:S(2)}) collective-permute-start(bf16[512,1024]{1,0:T(8,128)(2,1)} %get-tuple-element.32), channel_id=1, source_target_pairs={{0,6},{1,7},{2,4},{3,5},{4,2},{5,3},{6,0},{7,1},{8,14},{9,15},{10,... | collective-permute-start | bytes 3145736 | tf_op jit(solution)/shard_map/ppermute | solution.py:349
  25.2 0.9 collective-permute-start.6
  26.6 0.6 fusion.2
  27.3 0.6 stack_broadcast_in_dim.3
  28.2 6.2 %shard_map.124 = (f32[16,128,128]{2,1,0:T(8,128)S(1)}, f32[16,128,128]{2,1,0:T(8,128)S(1)}) custom-call(bf16[512,512]{1,0:T(8,128)(2,1)S(1)} %copy-done.2, bf16[608,128]{1,0:T(8,128)(2,1)S(1)} %pad.7.fresh_k, bf16[608,128]{1,0:T(8,128)(2,1)S(1)} %pad.8.fresh_v, s32[512,128]{1,0:T(8,128)S(1)} %broadcast_in_dim.105.row_start), custom_call_target="tpu_custom_call" | custom-call | flops 2147483648 | bytes 4194304 | tf_op jit(solution)/shard_map/pallas_call | solution.py:289
  34.4 1.0 copy-done
  35.4 1.0 copy-done.1
  36.4 11.2 %collective-permute-done.1.refs_4_ = bf16[512,1024]{1,0:T(8,128)(2,1)} collective-permute-done((bf16[512,1024]{1,0:T(8,128)(2,1)}, bf16[512,1024]{1,0:T(8,128)(2,1)}, u32[]{:S(2)}, u32[]{:S(2)}) %collective-permute-start.1) | collective-permute-done | bytes 1048608 | tf_op jit(solution)/shard_map/ppermute | solution.py:349
  47.6 2.8 %collective-permute-done.2.refs_5_ = bf16[512,1024]{1,0:T(8,128)(2,1)} collective-permute-done((bf16[512,1024]{1,0:T(8,128)(2,1)}, bf16[512,1024]{1,0:T(8,128)(2,1)}, u32[]{:S(2)}, u32[]{:S(2)}) %collective-permute-start.2) | collective-permute-done | bytes 1048608 | tf_op jit(solution)/shard_map/ppermute | solution.py:349
  50.4 13.7 %all-to-all-done.cache = bf16[32,256,128]{2,1,0:T(8,128)(2,1)S(1)} async-done(((bf16[32,256,128]{2,1,0:T(8,128)(2,1)}), bf16[32,256,128]{2,1,0:T(8,128)(2,1)S(1)}, u32[]{:S(2)}, u32[]{:S(2)}) %all-to-all-start) | async-done | bytes 2097184 | tf_op jit(solution)/shard_map/all_to_all | solution.py:358
  64.1 3.5 %shard_map.125 = bf16[256,512]{1,0:T(8,128)(2,1)S(1)} custom-call(s32[5,48]{1,0:T(8,128)S(1)} %stack.73.plan, s32[4]{0:T(128)S(1)} %pad_add_fusion.starts, bf16[512,512]{1,0:T(8,128)(2,1)S(1)} %copy-done.2, bf16[32,256,128]{2,1,0:T(8,128)(2,1)S(1)} %all-to-all-done.cache, f32[16,128,128]{2,1,0:T(8,128)} %copy-done, f32[16,128,128]{2,1,0:T(8,128)} %copy-done.1), custom_call_target="tpu_custom_call" | custom-call | flops 2147483648 | bytes 4194304 | tf_op jit(solution)/shard_map/pallas_call | solution.py:305
  67.8 1.7 %collective-permute-start.3 = (bf16[256,512]{1,0:T(8,128)(2,1)S(1)}, bf16[256,512]{1,0:T(8,128)(2,1)S(1)}, u32[]{:S(2)}, u32[]{:S(2)}) collective-permute-start(bf16[256,512]{1,0:T(8,128)(2,1)S(1)} %shard_map.125), channel_id=1, source_target_pairs={{0,2},{1,3},{2,0},{3,1},{4,6},{5,7},{6,4},{7,5},{8,10},{9,11},{10,... | collective-permute-start | bytes 786440 | tf_op jit(solution)/shard_map/ppermute | solution.py:349
  69.4 2.2 %collective-permute-start.4 = (bf16[256,512]{1,0:T(8,128)(2,1)S(1)}, bf16[256,512]{1,0:T(8,128)(2,1)S(1)}, u32[]{:S(2)}, u32[]{:S(2)}) collective-permute-start(bf16[256,512]{1,0:T(8,128)(2,1)S(1)} %shard_map.125), channel_id=1, source_target_pairs={{0,6},{1,7},{2,4},{3,5},{4,2},{5,3},{6,0},{7,1},{8,14},{9,15},{10,... | collective-permute-start | bytes 786440 | tf_op jit(solution)/shard_map/ppermute | solution.py:349
  71.6 5.5 %shard_map.126 = (bf16[256,512]{1,0:T(8,128)(2,1)S(1)}, bf16[512,1024]{1,0:T(8,128)(2,1)S(1)}, bf16[512,1024]{1,0:T(8,128)(2,1)S(1)}, bf16[512,1024]{1,0:T(8,128...) custom-call(s32[5,48]{1,0:T(8,128)S(1)} %stack.73.plan, ...), custom_call_target="tpu_custom_call" | custom-call | flops 2147483648 | bytes 4194304 | tf_op jit(solution)/shard_map/pallas_call | solution.py:305
  78.0 1.7 %collective-permute-start.13 = (bf16[256,512]{1,0:T(8,128)(2,1)S(1)}, bf16[256,512]{1,0:T(8,128)(2,1)S(1)}, u32[]{:S(2)}, u32[]{:S(2)}) collective-permute-start(bf16[256,512]{1,0:T(8,128)(2,1)S(1)} %get-tuple-element.53), channel_id=1, source_target_pairs={{0,6},{1,7},{2,4},{3,5},{4,2},{5,3},{6,0},{7,1},{8,14},{9,15},{10,... | collective-permute-start | bytes 786440 | tf_op jit(solution)/shard_map/ppermute | solution.py:349
  85.3 1.6 %collective-permute-start.9 = (bf16[256,512]{1,0:T(8,128)(2,1)S(1)}, bf16[256,512]{1,0:T(8,128)(2,1)S(1)}, u32[]{:S(2)}, u32[]{:S(2)}) collective-permute-start(bf16[256,512]{1,0:T(8,128)(2,1)S(1)} %slice.55), channel_id=1, source_target_pairs={{0,6},{1,7},{2,4},{3,5},{4,2},{5,3},{6,0},{7,1},{8,14},{9,15},{10,... | collective-permute-start | bytes 786440 | tf_op jit(solution)/shard_map/ppermute | solution.py:349
  89.2 0.6 collective-permute-done.15
  90.3 2.3 %collective-permute-start.16 = (bf16[256,512]{1,0:T(8,128)(2,1)S(1)}, bf16[256,512]{1,0:T(8,128)(2,1)S(1)}, u32[]{:S(2)}, u32[]{:S(2)}) collective-permute-start(bf16[256,512]{1,0:T(8,128)(2,1)S(1)} %slice.53), channel_id=1, source_target_pairs={{0,6},{1,7},{2,4},{3,5},{4,2},{5,3},{6,0},{7,1},{8,14},{9,15},{10,... | collective-permute-start | bytes 786440 | tf_op jit(solution)/shard_map/ppermute | solution.py:349
  93.0 0.8 collective-permute-start.18
  93.8 1.9 %collective-permute-done.9 = bf16[256,512]{1,0:T(8,128)(2,1)S(1)} collective-permute-done((bf16[256,512]{1,0:T(8,128)(2,1)S(1)}, bf16[256,512]{1,0:T(8,128)(2,1)S(1)}, u32[]{:S(2)}, u32[]{:S(2)}) %collective-permute-start.9) | collective-permute-done | bytes 262176 | tf_op jit(solution)/shard_map/ppermute | solution.py:349
  95.9 4.8 %collective-permute-done.16 = bf16[256,512]{1,0:T(8,128)(2,1)S(1)} collective-permute-done((bf16[256,512]{1,0:T(8,128)(2,1)S(1)}, bf16[256,512]{1,0:T(8,128)(2,1)S(1)}, u32[]{:S(2)}, u32[]{:S(2)}) %collective-permute-start.16) | collective-permute-done | bytes 262176 | tf_op jit(solution)/shard_map/ppermute | solution.py:349
  101.8 1.1 %collective-permute-done.19 = f32[512]{0:T(512)S(1)} collective-permute-done((f32[512]{0:T(512)S(1)}, f32[512]{0:T(512)S(1)}, u32[]{:S(2)}, u32[]{:S(2)}) %collective-permute-start.19) | collective-permute-done | bytes 2080 | tf_op jit(solution)/shard_map/ppermute | solution.py:349
  103.0 1.9 %collective-permute-start.20 = (f32[512]{0:T(512)S(1)}, f32[512]{0:T(512)S(1)}, u32[]{:S(2)}, u32[]{:S(2)}) collective-permute-start(f32[512]{0:T(512)S(1)} %add.170), channel_id=1, source_target_pairs={{0,4},{1,5},{2,6},{3,7},{4,0},{5,1},{6,2},{7,3},{8,12},{9,13},{10,... | collective-permute-start | bytes 6152 | tf_op jit(solution)/shard_map/ppermute | solution.py:349
  104.9 0.7 collective-permute-start.21
  105.5 1.5 %collective-permute-start.22 = (f32[512]{0:T(512)S(1)}, f32[512]{0:T(512)S(1)}, u32[]{:S(2)}, u32[]{:S(2)}) collective-permute-start(f32[512]{0:T(512)S(1)} %add.170), channel_id=1, source_target_pairs={{0,6},{1,7},{2,4},{3,5},{4,2},{5,3},{6,0},{7,1},{8,14},{9,15},{10,... | collective-permute-start | bytes 6152 | tf_op jit(solution)/shard_map/ppermute | solution.py:349
  107.1 1.0 collective-permute-done.20
  108.4 1.9 %collective-permute-done.22 = f32[512]{0:T(512)S(1)} collective-permute-done((f32[512]{0:T(512)S(1)}, f32[512]{0:T(512)S(1)}, u32[]{:S(2)}, u32[]{:S(2)}) %collective-permute-start.22) | collective-permute-done | bytes 2080 | tf_op jit(solution)/shard_map/ppermute | solution.py:349
  110.3 1.7 %multiply_convert_fusion = (bf16[512,1024]{1,0:T(8,128)(2,1)}, bf16[512,1024]{1,0:T(8,128)(2,1)}) fusion(f32[1024]{0:T(1024)S(1)} %copy-done.6, f32[512]{0:T(512)S(1)} %add_rsqrt_fusion, f32[256,512]{1,0:T(8,128)S(1)} %slice_add_fusion, f32[256,512]{1,0:T(8,128)S(1)} %slice_add_fusion.1, f32[256,512]{1,0:T(8,128)S(1)} %slice_add_fusion.2, ...), kind=kLoop, calls=%fused_computation.1 | loop fusion | flops 4718592 | bytes 5249024 | tf_op jit(solution)/shard_map/convert_element_type | solution.py:408
  (83 shorter events, 12.5 us)
Async XLA Ops:
  3.2 60.9 %all-to-all-start = ((bf16[32,256,128]{2,1,0:T(8,128)(2,1)}), bf16[32,256,128]{2,1,0:T(8,128)(2,1)S(1)}, u32[]{:S(2)}, u32[]{:S(2)}) async-start(bf16[32,256,128]{2,1,0:T(8,128)(2,1)} %shard_map.122.after), calls=%async_computation | async-start | bytes 4194304 | tf_op jit(solution)/shard_map/all_to_all | solution.py:358
  15.0 11.1 %copy-start.8 = (s32[1,32]{1,0:T(1,128)S(1)}, s32[1,32]{1,0:T(1,128)}, u32[]{:S(2)}) copy-start(s32[1,32]{1,0:T(1,128)} %param.15) | copy-start | bytes 388
  15.0 11.3 %copy-start.4 = (bf16[512,128]{1,0:T(8,128)(2,1)S(1)}, bf16[512,128]{1,0:T(8,128)(2,1)}, u32[]{:S(2)}) copy-start(bf16[512,128]{1,0:T(8,128)(2,1)} %param.12) | copy-start | bytes 393220
  15.0 11.4 %copy-start.5 = (bf16[512,128]{1,0:T(8,128)(2,1)S(1)}, bf16[512,128]{1,0:T(8,128)(2,1)}, u32[]{:S(2)}) copy-start(bf16[512,128]{1,0:T(8,128)(2,1)} %param.13) | copy-start | bytes 393220
  15.0 11.5 %copy-start.7 = (s32[1,32]{1,0:T(1,128)S(1)}, s32[1,32]{1,0:T(1,128)}, u32[]{:S(2)}) copy-start(s32[1,32]{1,0:T(1,128)} %param.16) | copy-start | bytes 388
  15.0 13.2 %copy-start.2 = (bf16[512,512]{1,0:T(8,128)(2,1)S(1)}, bf16[512,512]{1,0:T(8,128)(2,1)}, u32[]{:S(2)}) copy-start(bf16[512,512]{1,0:T(8,128)(2,1)} %q.5) | copy-start | bytes 1572868
  21.1 29.3 %collective-permute-start = (bf16[512,2048]{1,0:T(8,128)(2,1)}, bf16[512,2048]{1,0:T(8,128)(2,1)}, u32[]{:S(2)}, u32[]{:S(2)}) collective-permute-start(bf16[512,2048]{1,0:T(8,128)(2,1)} %get-tuple-element.30), channel_id=1, source_target_pairs={{0,1},{1,0},{2,3},{3,2},{4,5},{5,4},{6,7},{7,6},{8,9},{9,8},{10,11... | collective-permute-start | bytes 6291464 | tf_op jit(solution)/shard_map/ppermute | solution.py:349
  21.2 26.4 %collective-permute-start.1 = (bf16[512,1024]{1,0:T(8,128)(2,1)}, bf16[512,1024]{1,0:T(8,128)(2,1)}, u32[]{:S(2)}, u32[]{:S(2)}) collective-permute-start(bf16[512,1024]{1,0:T(8,128)(2,1)} %get-tuple-element.31), channel_id=1, source_target_pairs={{0,2},{1,3},{2,0},{3,1},{4,6},{5,7},{6,4},{7,5},{8,10},{9,11},{10,... | collective-permute-start | bytes 3145736 | tf_op jit(solution)/shard_map/ppermute | solution.py:349
  22.9 27.5 %collective-permute-start.2 = (bf16[512,1024]{1,0:T(8,128)(2,1)}, bf16[512,1024]{1,0:T(8,128)(2,1)}, u32[]{:S(2)}, u32[]{:S(2)}) collective-permute-start(bf16[512,1024]{1,0:T(8,128)(2,1)} %get-tuple-element.32), channel_id=1, source_target_pairs={{0,6},{1,7},{2,4},{3,5},{4,2},{5,3},{6,0},{7,1},{8,14},{9,15},{10,... | collective-permute-start | bytes 3145736 | tf_op jit(solution)/shard_map/ppermute | solution.py:349
  25.1 46.5 %collective-permute-start.5 = (bf16[512,1024]{1,0:T(8,128)(2,1)}, bf16[512,1024]{1,0:T(8,128)(2,1)}, u32[]{:S(2)}, u32[]{:S(2)}) collective-permute-start(bf16[512,1024]{1,0:T(8,128)(2,1)} %get-tuple-element.39), channel_id=1, source_target_pairs={{0,3},{1,2},{2,1},{3,0},{4,7},{5,6},{6,5},{7,4},{8,11},{9,10},{10,... | collective-permute-start | bytes 3145736 | tf_op jit(solution)/shard_map/ppermute | solution.py:349
  25.2 46.4 %collective-permute-start.6 = (bf16[512,1024]{1,0:T(8,128)(2,1)}, bf16[512,1024]{1,0:T(8,128)(2,1)}, u32[]{:S(2)}, u32[]{:S(2)}) collective-permute-start(bf16[512,1024]{1,0:T(8,128)(2,1)} %get-tuple-element.40), channel_id=1, source_target_pairs={{0,7},{1,6},{2,5},{3,4},{4,3},{5,2},{6,1},{7,0},{8,15},{9,14},{10,... | collective-permute-start | bytes 3145736 | tf_op jit(solution)/shard_map/ppermute | solution.py:349
  34.4 1.0 copy-start
  67.7 10.3 %collective-permute-start.7 = (bf16[256,512]{1,0:T(8,128)(2,1)S(1)}, bf16[256,512]{1,0:T(8,128)(2,1)S(1)}, u32[]{:S(2)}, u32[]{:S(2)}) collective-permute-start(bf16[256,512]{1,0:T(8,128)(2,1)S(1)} %shard_map.125), channel_id=1, source_target_pairs={{0,1},{1,0},{2,3},{3,2},{4,5},{5,4},{6,7},{7,6},{8,9},{9,8},{10,11... | collective-permute-start | bytes 786440 | tf_op jit(solution)/shard_map/ppermute | solution.py:349
  67.8 13.7 %collective-permute-start.3 = (bf16[256,512]{1,0:T(8,128)(2,1)S(1)}, bf16[256,512]{1,0:T(8,128)(2,1)S(1)}, u32[]{:S(2)}, u32[]{:S(2)}) collective-permute-start(bf16[256,512]{1,0:T(8,128)(2,1)S(1)} %shard_map.125), channel_id=1, source_target_pairs={{0,2},{1,3},{2,0},{3,1},{4,6},{5,7},{6,4},{7,5},{8,10},{9,11},{10,... | collective-permute-start | bytes 786440 | tf_op jit(solution)/shard_map/ppermute | solution.py:349
  69.4 12.1 %collective-permute-start.4 = (bf16[256,512]{1,0:T(8,128)(2,1)S(1)}, bf16[256,512]{1,0:T(8,128)(2,1)S(1)}, u32[]{:S(2)}, u32[]{:S(2)}) collective-permute-start(bf16[256,512]{1,0:T(8,128)(2,1)S(1)} %shard_map.125), channel_id=1, source_target_pairs={{0,6},{1,7},{2,4},{3,5},{4,2},{5,3},{6,0},{7,1},{8,14},{9,15},{10,... | collective-permute-start | bytes 786440 | tf_op jit(solution)/shard_map/ppermute | solution.py:349
  77.1 5.4 %collective-permute-start.14 = (bf16[256,512]{1,0:T(8,128)(2,1)S(1)}, bf16[256,512]{1,0:T(8,128)(2,1)S(1)}, u32[]{:S(2)}, u32[]{:S(2)}) collective-permute-start(bf16[256,512]{1,0:T(8,128)(2,1)S(1)} %get-tuple-element.53), channel_id=1, source_target_pairs={{0,1},{1,0},{2,3},{3,2},{4,5},{5,4},{6,7},{7,6},{8,9},{9,8},{10,11... | collective-permute-start | bytes 786440 | tf_op jit(solution)/shard_map/ppermute | solution.py:349
  77.4 10.3 %collective-permute-start.12 = (bf16[256,512]{1,0:T(8,128)(2,1)S(1)}, bf16[256,512]{1,0:T(8,128)(2,1)S(1)}, u32[]{:S(2)}, u32[]{:S(2)}) collective-permute-start(bf16[256,512]{1,0:T(8,128)(2,1)S(1)} %get-tuple-element.53), channel_id=1, source_target_pairs={{0,2},{1,3},{2,0},{3,1},{4,6},{5,7},{6,4},{7,5},{8,10},{9,11},{10,... | collective-permute-start | bytes 786440 | tf_op jit(solution)/shard_map/ppermute | solution.py:349
  78.0 9.8 %collective-permute-start.13 = (bf16[256,512]{1,0:T(8,128)(2,1)S(1)}, bf16[256,512]{1,0:T(8,128)(2,1)S(1)}, u32[]{:S(2)}, u32[]{:S(2)}) collective-permute-start(bf16[256,512]{1,0:T(8,128)(2,1)S(1)} %get-tuple-element.53), channel_id=1, source_target_pairs={{0,6},{1,7},{2,4},{3,5},{4,2},{5,3},{6,0},{7,1},{8,14},{9,15},{10,... | collective-permute-start | bytes 786440 | tf_op jit(solution)/shard_map/ppermute | solution.py:349
  81.5 3.3 %collective-permute-start.8 = (bf16[256,512]{1,0:T(8,128)(2,1)S(1)}, bf16[256,512]{1,0:T(8,128)(2,1)S(1)}, u32[]{:S(2)}, u32[]{:S(2)}) collective-permute-start(bf16[256,512]{1,0:T(8,128)(2,1)S(1)} %collective-permute-done.3), channel_id=1, source_target_pairs={{0,1},{1,0},{2,3},{3,2},{4,5},{5,4},{6,7},{7,6},{8,9},{9,8},{10,11... | collective-permute-start | bytes 786440 | tf_op jit(solution)/shard_map/ppermute | solution.py:349
  81.6 5.3 %collective-permute-start.10 = (bf16[256,512]{1,0:T(8,128)(2,1)S(1)}, bf16[256,512]{1,0:T(8,128)(2,1)S(1)}, u32[]{:S(2)}, u32[]{:S(2)}) collective-permute-start(bf16[256,512]{1,0:T(8,128)(2,1)S(1)} %collective-permute-done.4), channel_id=1, source_target_pairs={{0,1},{1,0},{2,3},{3,2},{4,5},{5,4},{6,7},{7,6},{8,9},{9,8},{10,11... | collective-permute-start | bytes 786440 | tf_op jit(solution)/shard_map/ppermute | solution.py:349
  85.3 10.4 %collective-permute-start.9 = (bf16[256,512]{1,0:T(8,128)(2,1)S(1)}, bf16[256,512]{1,0:T(8,128)(2,1)S(1)}, u32[]{:S(2)}, u32[]{:S(2)}) collective-permute-start(bf16[256,512]{1,0:T(8,128)(2,1)S(1)} %slice.55), channel_id=1, source_target_pairs={{0,6},{1,7},{2,4},{3,5},{4,2},{5,3},{6,0},{7,1},{8,14},{9,15},{10,... | collective-permute-start | bytes 786440 | tf_op jit(solution)/shard_map/ppermute | solution.py:349
  87.3 8.4 %collective-permute-start.11 = (bf16[256,512]{1,0:T(8,128)(2,1)S(1)}, bf16[256,512]{1,0:T(8,128)(2,1)S(1)}, u32[]{:S(2)}, u32[]{:S(2)}) collective-permute-start(bf16[256,512]{1,0:T(8,128)(2,1)S(1)} %slice.54), channel_id=1, source_target_pairs={{0,2},{1,3},{2,0},{3,1},{4,6},{5,7},{6,4},{7,5},{8,10},{9,11},{10,... | collective-permute-start | bytes 786440 | tf_op jit(solution)/shard_map/ppermute | solution.py:349
  88.2 1.6 %collective-permute-start.15 = (bf16[256,512]{1,0:T(8,128)(2,1)S(1)}, bf16[256,512]{1,0:T(8,128)(2,1)S(1)}, u32[]{:S(2)}, u32[]{:S(2)}) collective-permute-start(bf16[256,512]{1,0:T(8,128)(2,1)S(1)} %collective-permute-done.12), channel_id=1, source_target_pairs={{0,1},{1,0},{2,3},{3,2},{4,5},{5,4},{6,7},{7,6},{8,9},{9,8},{10,11... | collective-permute-start | bytes 786440 | tf_op jit(solution)/shard_map/ppermute | solution.py:349
  88.3 4.3 %collective-permute-start.17 = (bf16[256,512]{1,0:T(8,128)(2,1)S(1)}, bf16[256,512]{1,0:T(8,128)(2,1)S(1)}, u32[]{:S(2)}, u32[]{:S(2)}) collective-permute-start(bf16[256,512]{1,0:T(8,128)(2,1)S(1)} %collective-permute-done.13), channel_id=1, source_target_pairs={{0,1},{1,0},{2,3},{3,2},{4,5},{5,4},{6,7},{7,6},{8,9},{9,8},{10,11... | collective-permute-start | bytes 786440 | tf_op jit(solution)/shard_map/ppermute | solution.py:349
  90.3 10.4 %collective-permute-start.16 = (bf16[256,512]{1,0:T(8,128)(2,1)S(1)}, bf16[256,512]{1,0:T(8,128)(2,1)S(1)}, u32[]{:S(2)}, u32[]{:S(2)}) collective-permute-start(bf16[256,512]{1,0:T(8,128)(2,1)S(1)} %slice.53), channel_id=1, source_target_pairs={{0,6},{1,7},{2,4},{3,5},{4,2},{5,3},{6,0},{7,1},{8,14},{9,15},{10,... | collective-permute-start | bytes 786440 | tf_op jit(solution)/shard_map/ppermute | solution.py:349
  93.0 8.2 %collective-permute-start.18 = (bf16[256,512]{1,0:T(8,128)(2,1)S(1)}, bf16[256,512]{1,0:T(8,128)(2,1)S(1)}, u32[]{:S(2)}, u32[]{:S(2)}) collective-permute-start(bf16[256,512]{1,0:T(8,128)(2,1)S(1)} %slice.52), channel_id=1, source_target_pairs={{0,2},{1,3},{2,0},{3,1},{4,6},{5,7},{6,4},{7,5},{8,10},{9,11},{10,... | collective-permute-start | bytes 786440 | tf_op jit(solution)/shard_map/ppermute | solution.py:349
  95.8 5.6 %copy-start.3 = (bf16[512,1024]{1,0:T(8,128)(2,1)S(1)}, bf16[512,1024]{1,0:T(8,128)(2,1)}, u32[]{:S(2)}) copy-start(bf16[512,1024]{1,0:T(8,128)(2,1)} %param.14) | copy-start | bytes 3145732
  100.7 9.6 %copy-start.6 = (f32[1024]{0:T(1024)S(1)}, f32[1024]{0:T(1024)}, u32[]{:S(2)}) copy-start(f32[1024]{0:T(1024)} %param.21) | copy-start | bytes 12292
  101.7 1.2 %collective-permute-start.19 = (f32[512]{0:T(512)S(1)}, f32[512]{0:T(512)S(1)}, u32[]{:S(2)}, u32[]{:S(2)}) collective-permute-start(f32[512]{0:T(512)S(1)} %multiply_reduce_fusion), channel_id=1, source_target_pairs={{0,1},{1,0},{2,3},{3,2},{4,5},{5,4},{6,7},{7,6},{8,9},{9,8},{10,11... | collective-permute-start | bytes 6152 | tf_op jit(solution)/shard_map/ppermute | solution.py:349
  103.0 5.1 %collective-permute-start.20 = (f32[512]{0:T(512)S(1)}, f32[512]{0:T(512)S(1)}, u32[]{:S(2)}, u32[]{:S(2)}) collective-permute-start(f32[512]{0:T(512)S(1)} %add.170), channel_id=1, source_target_pairs={{0,4},{1,5},{2,6},{3,7},{4,0},{5,1},{6,2},{7,3},{8,12},{9,13},{10,... | collective-permute-start | bytes 6152 | tf_op jit(solution)/shard_map/ppermute | solution.py:349
  104.9 3.6 %collective-permute-start.21 = (f32[512]{0:T(512)S(1)}, f32[512]{0:T(512)S(1)}, u32[]{:S(2)}, u32[]{:S(2)}) collective-permute-start(f32[512]{0:T(512)S(1)} %add.170), channel_id=1, source_target_pairs={{0,2},{1,3},{2,0},{3,1},{4,6},{5,7},{6,4},{7,5},{8,10},{9,11},{10,... | collective-permute-start | bytes 6152 | tf_op jit(solution)/shard_map/ppermute | solution.py:349
  105.5 4.8 %collective-permute-start.22 = (f32[512]{0:T(512)S(1)}, f32[512]{0:T(512)S(1)}, u32[]{:S(2)}, u32[]{:S(2)}) collective-permute-start(f32[512]{0:T(512)S(1)} %add.170), channel_id=1, source_target_pairs={{0,6},{1,7},{2,4},{3,5},{4,2},{5,3},{6,0},{7,1},{8,14},{9,15},{10,... | collective-permute-start | bytes 6152 | tf_op jit(solution)/shard_map/ppermute | solution.py:349
  (1 other events, 1.0 us)

commit v8 on v6

--- a/solution.py
+++ b/solution.py
@@ -122,21 +122,14 @@
 
 def main_kernel(first, plan, starts, q, cache_hbm, mean_hbm, level_hbm, *refs):
     cache, means, levels, scores, weights, mixed, sems, stage_sems = refs[-8:]
-    count = (len(refs) - 9) // 2
-    sources, out, staged = refs[:count], refs[count], refs[count + 1 : -8]
     stage = []
-    for place_of, (source, target) in enumerate(zip(sources, staged)):
-        if source.shape == target.shape:
-            parts = [(source, target)]
-        elif source.shape[1] == 2 * target.shape[1]:
-            parts = [(source.at[:, pl.ds(1024 * (place_of % 2), 1024)], target)]
-        else:
-            parts = [
-                (source.at[:, pl.ds(pl.multiple_of(starts[i], 512), 512)], target.at[:, pl.ds(512 * (i % 2), 512)])
-                for i in range(len(stage), len(stage) + 2)
-            ]
-        for origin, goal in parts:
-            stage.append(pltpu.make_async_copy(origin, goal, stage_sems.at[len(stage)]))
+    if len(refs) > 9:
+        own = [refs[16 + i % 2].at[pl.ds(512 * (i // 2), 512)] for i in range(8)]
+        stage = staging(1, starts, refs[:6], refs[8:16], stage_sems.at[0])
+        stage += staging(0, starts, refs[:6], own, stage_sems.at[1])
+        out = refs[7]
+    else:
+        out = refs[0]
     half = cache.shape[1] // 2
     fetch = [
         pltpu.make_async_copy(
@@ -263,10 +256,10 @@
     outs, sems = refs[:-1], refs[-1]
     copies = []
     for out in outs:
-        for i in range(out.shape[1] // 512):
+        for i in range(out.shape[0] // 512):
             slot = len(copies)
             source = weight.at[:, pl.ds(pl.multiple_of(starts[slot], 512), 512)]
-            target = out.at[:, pl.ds(i * 512, 512)]
+            target = out.at[pl.ds(i * 512, 512)]
             copies.append(pltpu.make_async_copy(source, target, sems.at[slot]))
     for copy in copies:
         copy.start()
@@ -274,21 +267,35 @@
         copy.wait()
 
 
-def cut(starts, weight, widths, after):
-    rows = weight.shape[0]
+def cut(starts, weight, heights, after):
     return pl.pallas_call(
         cut_kernel,
-        out_shape=tuple(pltpu.VMEM((rows, width), weight.dtype) for width in widths),
+        out_shape=tuple(pltpu.VMEM((height, 512), weight.dtype) for height in heights),
         grid_spec=pltpu.PrefetchScalarGridSpec(
             num_scalar_prefetch=1,
             grid=(),
             in_specs=far(1) + anywhere(1),
-            out_specs=tuple(whole(len(widths))),
-            scratch_shapes=[pltpu.SemaphoreType.DMA((sum(widths) // 512,))],
+            out_specs=tuple(whole(len(heights))),
+            scratch_shapes=[pltpu.SemaphoreType.DMA((sum(heights) // 512,))],
         ),
         compiler_params=pltpu.CompilerParams(vmem_limit_bytes=8 << 20),
         cost_estimate=pl.CostEstimate(flops=0, bytes_accessed=12 << 20, transcendentals=0),
     )(starts, *in_hbm(weight), after)
+
+
+def staging(part, starts, sources, targets, sems):
+    weight, sibling, *near = sources
+    blocks = []
+    for half in range(2):
+        start = pl.multiple_of(starts[2 * half + part], 512)
+        blocks.append(weight.at[:, pl.ds(start, 512)])
+    for half in range(2):
+        blocks.append(sibling.at[pl.ds(1024 * half + 512 * part, 512)])
+    blocks += [block.at[pl.ds(512 * part, 512)] for block in near]
+    return [
+        pltpu.make_async_copy(block, target, sems.at[i])
+        for i, (block, target) in enumerate(zip(blocks, targets))
+    ]
 
 
 def attend_fresh(queries, new_keys, new_values, row_start):
@@ -306,17 +313,20 @@
     )(queries, jnp.pad(new_keys, front), jnp.pad(new_values, front), row_start)
 
 
-def attend(first, plan, starts, queries, cache, fresh, sources=()):
+def attend(first, plan, starts, queries, cache, fresh, sources=(), after=()):
     area = fresh[0].shape[1:]
     rows = jax.ShapeDtypeStruct((PIECE * BLOCK, queries.shape[1]), queries.dtype)
-    staged = [pltpu.VMEM((source.shape[0], 1024), source.dtype) for source in sources]
+    staged = []
+    if sources:
+        staged = [pltpu.VMEM((512, 512), queries.dtype)] * 8
+        staged += [pltpu.VMEM((2048, 512), queries.dtype)] * 2
     return pl.pallas_call(
         functools.partial(main_kernel, first),
         out_shape=(rows, *staged),
         grid_spec=pltpu.PrefetchScalarGridSpec(
             num_scalar_prefetch=2,
             grid=(),
-            in_specs=whole(1) + anywhere(3 + len(sources)),
+            in_specs=whole(1) + anywhere(3 + len(sources) + len(after)),
             out_specs=tuple(whole(1 + len(staged))),
             scratch_shapes=[
                 pltpu.VMEM(cache.shape, cache.dtype),
@@ -326,21 +336,14 @@
                 pltpu.VMEM((PIECE + 1, *area), jnp.bfloat16),
                 pltpu.VMEM((PIECE + 1, *area), jnp.float32),
                 pltpu.SemaphoreType.DMA((4,)),
-                pltpu.SemaphoreType.DMA((len(sources) + 2,)),
+                pltpu.SemaphoreType.DMA((2, 8)),
             ],
         ),
-        compiler_params=pltpu.CompilerParams(vmem_limit_bytes=(7 + len(sources)) << 20),
+        compiler_params=pltpu.CompilerParams(vmem_limit_bytes=(16 if sources else 7) << 20),
         cost_estimate=pl.CostEstimate(
             flops=1 << 31, bytes_accessed=4 << 20, transcendentals=1 << 18
         ),
-    )(plan, starts, queries, cache, *in_hbm(*fresh), *in_hbm(*sources))
-
-
-def attention(counts, packs, queries, marked, values, new_keys, new_values):
-    plan, row_start = pair_plan(counts, packs)
-    fresh = attend_fresh(queries, new_keys, new_values, row_start)
-    cache = jnp.concatenate([marked, values], axis=1)
-    return jnp.concatenate([attend(i, plan, plan[0], queries, cache, fresh)[0] for i in (0, PIECE)], axis=0)
+    )(plan, starts, queries, cache, *in_hbm(*fresh), *in_hbm(*sources), *after)
 
 
 def on_device(
@@ -382,37 +385,48 @@
     fresh = attend_fresh(queries, new_keys, new_values, row_start)
     plan, sibling, near_mats[:2] = lax.optimization_barrier((plan, sibling, near_mats[:2]))
     starts = jnp.stack(sum(shared(0), []))
-    attended = attend(0, plan, starts, queries, cache, fresh)
-    sources = (out_weight, out_weight, sibling, sibling, *near_mats)
-    rest, *mats = attend(PIECE, plan, starts, queries, cache, fresh, sources)
-    attended = [attended[0], rest]
-    here, sibling, same, cross = (mats[i : i + 2] for i in (0, 2, 4, 6))
+    first = attend(0, plan, starts, queries, cache, fresh)[0]
+    sources = (out_weight, sibling, *near_mats)
+    others_a = swap(first, 1)
+    second, *mats, own_0, own_1 = attend(PIECE, plan, starts, queries, cache, fresh, sources, (others_a,))
+    attended = [first, second]
 
     def times(rows, mat):
         return jnp.dot(rows, mat, preferred_element_type=f32)
 
-    others = [swap(rows, 1) for rows in attended]
+    others = [others_a, swap(second, 1)]
     near = [[swap(rows, mask) for mask in (2, 6)] for rows in attended]
-    own = []
+    inputs = []
     got = []
     sent = []
     for rows, other, close in zip(attended, others, near):
-        local = [times(rows, here[half]) + times(other, sibling[half]) for half in range(2)]
+        local = [times(rows, mats[half]) + times(other, mats[2 + half]) for half in range(2)]
         close, local, sent = lax.optimization_barrier((close, local, sent))
-        totals = [
-            local[half] + times(close[half], same[half]) + times(swap(close[half], 1), cross[half])
+        side = [swap(part, 1) for part in close]
+        sent = [
+            local[half] + times(close[half], mats[4 + half]) + times(side[half], mats[6 + half])
             for half in range(2)
         ]
-        own.append([total[:, :512] for total in totals])
-        sent = [total[:, 512:].astype(bf16) for total in totals]
+        sent = [total.astype(bf16) for total in sent]
+        sent, side = lax.optimization_barrier((sent, side))
         got.append([swap(part, mask) for part, mask in zip(sent, (6, 2))])
-
+        inputs.append([[rows, other, close[half], side[half]] for half in range(2)])
+
+    got[0], inputs = lax.optimization_barrier((got[0], inputs))
+    own = [
+        times(
+            jnp.concatenate([jnp.concatenate(halves[half], axis=1) for halves in inputs], axis=0),
+            mat,
+        )
+        for half, mat in enumerate((own_0, own_1))
+    ]
+    own = lax.optimization_barrier(own)
     delta = jnp.concatenate(
         [
-            jnp.concatenate([a + b.astype(f32) for a, b in zip(*pair)], axis=1)
-            for pair in zip(own, got)
+            own[half] + jnp.concatenate([pair[half] for pair in got], axis=0).astype(f32)
+            for half in range(2)
         ],
-        axis=0,
+        axis=1,
     )
     summed = hidden.astype(f32) + delta
     residual_out = summed.astype(bf16)

time: 111 us -> 114 us (1.027); the launches traced: 111 us -> 113 us
  waiting for transfers between devices: 40 us -> 42.4 us
    ppermute x23, waiting for transfers between devices: 26.2 us -> 28.7 us  [swap(): return lax.ppermute(value, 'tensor', [(t, t ^ mask) for t in range(count)])]
    dot_general x16 -> x18, matrix products: 7 us -> 7.24 us  [times(): return jnp.dot(rows, mat, preferred_element_type=f32)]
  transfers between devices with their start and end apart: 24 -> 24, of which waited for: 11 -> 15; matrix products, arithmetic and copies ran while one was open for 9% -> 8% of each run, Pallas kernels for 18% -> 18%
where the time goes in v8:
time: 114 us; the launch traced here: 113 us
  waiting for transfers between devices  42.4 us (37%)
  starting transfers between devices  33 us (29%)
  Pallas kernels  22.7 us (20%)
  matrix products  7.24 us (6%)
  other arithmetic  3.64 us (3%)
  local copies, waits for them, and re-layouts  2.89 us (3%)
    ppermute x23, waiting for transfers between devices, swap(): return lax.ppermute(value, 'tensor', [(t, t ^ mask) for t in range(count)])  28.7 us
    ppermute x23, starting transfers between devices, swap(): return lax.ppermute(value, 'tensor', [(t, t ^ mask) for t in range(count)])  21.3 us
    all_to_all x1, waiting for transfers between devices, on_device(): lax.all_to_all(payload, 'dp', split_axis=0, concat_axis=0, tiled=True)  13.7 us
    all_to_all x1, starting transfers between devices, on_device(): lax.all_to_all(payload, 'dp', split_axis=0, concat_axis=0, tiled=True)  11.6 us
    pallas_call x2, Pallas kernels, attend(): pl.pallas_call(functools.partial(main_kernel, first), out_shape=(rows, *s...  7.9 us
    dot_general x18, matrix products, times(): return jnp.dot(rows, mat, preferred_element_type=f32)  7.24 us
    pallas_call x1, Pallas kernels, attend_fresh(): pl.pallas_call(fresh_kernel, out_shape=(area, area), in_specs=whole(4), o...  6.17 us
    pallas_call x1, Pallas kernels, cut(): pl.pallas_call(cut_kernel, out_shape=tuple((pltpu.VMEM((height, 512), wei...  6.06 us
  transfers between devices with their start and end apart: 24, of which 15 were waited for; matrix products, arithmetic and copies ran while one was open for 8% of the time, Pallas kernels for 18%

profile of v8, /device:TPU:2, one launch (start us, length us, event | category | flops | bytes accessed | tf_op | source)
XLA Modules:
  0.0 112.9 jit_solution(4033528115678352393)
XLA Ops:
  0.6 2.6 %shard_map.122.after = bf16[32,256,128]{2,1,0:T(8,128)(2,1)} custom-call(s32[1,32]{1,0:T(1,128)} %lengths_hbm.1, bf16[32,128,128]{2,1,0:T(8,128)(2,1)} %bitcast.82, bf16[32,128,128]{2,1,0:T(8,128)(2,1)} %bitcast.83), custom_call_target="tpu_custom_call" | custom-call | flops 1048576 | bytes 4194304 | tf_op jit(solution)/shard_map/pallas_call | solution.py:239
  3.2 11.6 %all-to-all-start = ((bf16[32,256,128]{2,1,0:T(8,128)(2,1)}), bf16[32,256,128]{2,1,0:T(8,128)(2,1)S(1)}, u32[]{:S(2)}, u32[]{:S(2)}) async-start(bf16[32,256,128]{2,1,0:T(8,128)(2,1)} %shard_map.122.after), calls=%async_computation | async-start | bytes 4194304 | tf_op jit(solution)/shard_map/all_to_all | solution.py:377
  15.0 6.1 %shard_map.123 = (bf16[1024,512]{1,0:T(8,128)(2,1)}, bf16[1024,512]{1,0:T(8,128)(2,1)}, bf16[1024,512]{1,0:T(8,128)(2,1)}, bf16[1024,512]{1,0:T(8,128)(2,1)}, bf16[2048,512]{1,0:T(8,128)(2,1)}) custom-call(s32[12]{0:T(128)S(1)} %stack.86.starts, bf16[512,8192]{1,0:T(8,128)(2,1)} %refs_0_.1, bf16[32,256,128]{2,1,0:T(8,128)(2,1)} %shard_map.122.after), custom_call_target="tpu_custom_call" | custom-call | bytes 12582912 | tf_op jit(solution)/shard_map/pallas_call | solution.py:271
  21.2 1.7 %collective-permute-start.1 = (bf16[1024,512]{1,0:T(8,128)(2,1)}, bf16[1024,512]{1,0:T(8,128)(2,1)}, u32[]{:S(2)}, u32[]{:S(2)}) collective-permute-start(bf16[1024,512]{1,0:T(8,128)(2,1)} %get-tuple-element.61), channel_id=1, source_target_pairs={{0,2},{1,3},{2,0},{3,1},{4,6},{5,7},{6,4},{7,5},{8,10},{9,11},{10,... | collective-permute-start | bytes 3145736 | tf_op jit(solution)/shard_map/ppermute | solution.py:368
  22.9 2.2 %collective-permute-start.2 = (bf16[1024,512]{1,0:T(8,128)(2,1)}, bf16[1024,512]{1,0:T(8,128)(2,1)}, u32[]{:S(2)}, u32[]{:S(2)}) collective-permute-start(bf16[1024,512]{1,0:T(8,128)(2,1)} %get-tuple-element.62), channel_id=1, source_target_pairs={{0,6},{1,7},{2,4},{3,5},{4,2},{5,3},{6,0},{7,1},{8,14},{9,15},{10,... | collective-permute-start | bytes 3145736 | tf_op jit(solution)/shard_map/ppermute | solution.py:368
  25.2 0.9 collective-permute-start.6
  27.2 0.6 stack_broadcast_in_dim.3
  28.2 6.2 %shard_map.124 = (f32[16,128,128]{2,1,0:T(8,128)S(1)}, f32[16,128,128]{2,1,0:T(8,128)S(1)}) custom-call(bf16[512,512]{1,0:T(8,128)(2,1)S(1)} %copy-done.2, bf16[608,128]{1,0:T(8,128)(2,1)S(1)} %pad.7.fresh_k, bf16[608,128]{1,0:T(8,128)(2,1)S(1)} %pad.8.fresh_v, s32[512,128]{1,0:T(8,128)S(1)} %broadcast_in_dim.105.row_start), custom_call_target="tpu_custom_call" | custom-call | flops 2147483648 | bytes 4194304 | tf_op jit(solution)/shard_map/pallas_call | solution.py:304
  34.4 1.0 copy-done
  35.4 1.0 copy-done.1
  36.4 11.2 %collective-permute-done.1.refs_2_ = bf16[1024,512]{1,0:T(8,128)(2,1)} collective-permute-done((bf16[1024,512]{1,0:T(8,128)(2,1)}, bf16[1024,512]{1,0:T(8,128)(2,1)}, u32[]{:S(2)}, u32[]{:S(2)}) %collective-permute-start.1) | collective-permute-done | bytes 1048608 | tf_op jit(solution)/shard_map/ppermute | solution.py:368
  47.6 2.8 %collective-permute-done.2.refs_3_ = bf16[1024,512]{1,0:T(8,128)(2,1)} collective-permute-done((bf16[1024,512]{1,0:T(8,128)(2,1)}, bf16[1024,512]{1,0:T(8,128)(2,1)}, u32[]{:S(2)}, u32[]{:S(2)}) %collective-permute-start.2) | collective-permute-done | bytes 1048608 | tf_op jit(solution)/shard_map/ppermute | solution.py:368
  50.4 13.7 %all-to-all-done.cache_hbm = bf16[32,256,128]{2,1,0:T(8,128)(2,1)S(1)} async-done(((bf16[32,256,128]{2,1,0:T(8,128)(2,1)}), bf16[32,256,128]{2,1,0:T(8,128)(2,1)S(1)}, u32[]{:S(2)}, u32[]{:S(2)}) %all-to-all-start) | async-done | bytes 2097184 | tf_op jit(solution)/shard_map/all_to_all | solution.py:377
  64.1 3.3 %shard_map.125 = bf16[256,512]{1,0:T(8,128)(2,1)S(1)} custom-call(s32[5,48]{1,0:T(8,128)S(1)} %stack.73.plan, s32[4]{0:T(128)S(1)} %pad_add_fusion.starts, bf16[512,512]{1,0:T(8,128)(2,1)S(1)} %copy-done.2, bf16[32,256,128]{2,1,0:T(8,128)(2,1)S(1)} %all-to-all-done.cache_hbm, f32[16,128,128]{2,1,0:T(8,128)} %copy-done, f32[16,128,128]{2,1,0:T(8,128)} %copy-done.1), custom_call_target="tpu_custom_call" | custom-call | flops 2147483648 | bytes 4194304 | tf_op jit(solution)/shard_map/pallas_call | solution.py:323
  67.6 3.1 %collective-permute-start.4 = (bf16[256,512]{1,0:T(8,128)(2,1)S(1)}, bf16[256,512]{1,0:T(8,128)(2,1)S(1)}, u32[]{:S(2)}, u32[]{:S(2)}) collective-permute-start(bf16[256,512]{1,0:T(8,128)(2,1)S(1)} %shard_map.125), channel_id=1, source_target_pairs={{0,6},{1,7},{2,4},{3,5},{4,2},{5,3},{6,0},{7,1},{8,14},{9,15},{10,... | collective-permute-start | bytes 786440 | tf_op jit(solution)/shard_map/ppermute | solution.py:368
  71.3 4.6 %shard_map.126 = (bf16[256,512]{1,0:T(8,128)(2,1)S(1)}, bf16[512,512]{1,0:T(8,128)(2,1)S(1)}, bf16[512,512]{1,0:T(8,128)(2,1)S(1)}, bf16[512,512]{1,0:T(8,128)(2...) custom-call(s32[5,48]{1,0:T(8,128)S(1)} %stack.73.plan, ...), custom_call_target="tpu_custom_call" | custom-call | flops 2147483648 | bytes 4194304 | tf_op jit(solution)/shard_map/pallas_call | solution.py:323
  75.9 2.3 %collective-permute-start.14 = (bf16[256,512]{1,0:T(8,128)(2,1)S(1)}, bf16[256,512]{1,0:T(8,128)(2,1)S(1)}, u32[]{:S(2)}, u32[]{:S(2)}) collective-permute-start(bf16[256,512]{1,0:T(8,128)(2,1)S(1)} %get-tuple-element.107), channel_id=1, source_target_pairs={{0,6},{1,7},{2,4},{3,5},{4,2},{5,3},{6,0},{7,1},{8,14},{9,15},{10,... | collective-permute-start | bytes 786440 | tf_op jit(solution)/shard_map/ppermute | solution.py:368
  82.9 3.1 %collective-permute-done.14 = bf16[256,512]{1,0:T(8,128)(2,1)S(1)} collective-permute-done((bf16[256,512]{1,0:T(8,128)(2,1)S(1)}, bf16[256,512]{1,0:T(8,128)(2,1)S(1)}, u32[]{:S(2)}, u32[]{:S(2)}) %collective-permute-start.14) | collective-permute-done | bytes 262176 | tf_op jit(solution)/shard_map/ppermute | solution.py:368
  86.0 0.7 collective-permute-done.13
  87.0 1.6 %collective-permute-start.10 = (bf16[256,512]{1,0:T(8,128)(2,1)S(1)}, bf16[256,512]{1,0:T(8,128)(2,1)S(1)}, u32[]{:S(2)}, u32[]{:S(2)}) collective-permute-start(bf16[256,512]{1,0:T(8,128)(2,1)S(1)} %add_convert_fusion.3), channel_id=1, source_target_pairs={{0,6},{1,7},{2,4},{3,5},{4,2},{5,3},{6,0},{7,1},{8,14},{9,15},{10,... | collective-permute-start | bytes 786440 | tf_op jit(solution)/shard_map/ppermute | solution.py:368
  89.4 0.7 collective-permute-done.16
  90.4 1.8 %collective-permute-start.17 = (bf16[256,512]{1,0:T(8,128)(2,1)S(1)}, bf16[256,512]{1,0:T(8,128)(2,1)S(1)}, u32[]{:S(2)}, u32[]{:S(2)}) collective-permute-start(bf16[256,512]{1,0:T(8,128)(2,1)S(1)} %add_convert_fusion.1), channel_id=1, source_target_pairs={{0,6},{1,7},{2,4},{3,5},{4,2},{5,3},{6,0},{7,1},{8,14},{9,15},{10,... | collective-permute-start | bytes 786440 | tf_op jit(solution)/shard_map/ppermute | solution.py:368
  92.2 1.4 %collective-permute-start.18 = (bf16[256,512]{1,0:T(8,128)(2,1)S(1)}, bf16[256,512]{1,0:T(8,128)(2,1)S(1)}, u32[]{:S(2)}, u32[]{:S(2)}) collective-permute-start(bf16[256,512]{1,0:T(8,128)(2,1)S(1)} %add_convert_fusion), channel_id=1, source_target_pairs={{0,2},{1,3},{2,0},{3,1},{4,6},{5,7},{6,4},{7,5},{8,10},{9,11},{10,... | collective-permute-start | bytes 786440 | tf_op jit(solution)/shard_map/ppermute | solution.py:368
  93.7 3.7 %collective-permute-done.10 = bf16[256,512]{1,0:T(8,128)(2,1)S(1)} collective-permute-done((bf16[256,512]{1,0:T(8,128)(2,1)S(1)}, bf16[256,512]{1,0:T(8,128)(2,1)S(1)}, u32[]{:S(2)}, u32[]{:S(2)}) %collective-permute-start.10) | collective-permute-done | bytes 262176 | tf_op jit(solution)/shard_map/ppermute | solution.py:368
  97.7 1.2 %fusion.16 = f32[512,512]{1,0:T(8,128)S(1)} fusion(bf16[2048,512]{1,0:T(8,128)(2,1)S(1)} %get-tuple-element.111, bf16[256,512]{1,0:T(8,128)(2,1)S(1)} %collective-permute-done.16, bf16[256,512]{1,0:T(8,128)(2,1)S(1)} %collective-permute-done.14, bf16[256,512]{1,0:T(8,128)(2,1)S(1)} %collective-permute-done.12, bf16[256,512]{1,0:T(8,128)(2,1)S(1)} %get-tuple-element.107, ...), kind=kOutput, calls=%fused_computation.16 | convolution fusion | flops 1090519040 | bytes 5242880 | tf_op jit(solution)/shard_map/dot_general | solution.py:395
  98.9 1.2 %fusion = f32[512,512]{1,0:T(8,128)S(1)} fusion(bf16[2048,512]{1,0:T(8,128)(2,1)S(1)} %get-tuple-element.102, bf16[256,512]{1,0:T(8,128)(2,1)S(1)} %collective-permute-done.15, bf16[256,512]{1,0:T(8,128)(2,1)S(1)} %collective-permute-done.13, bf16[256,512]{1,0:T(8,128)(2,1)S(1)} %collective-permute-done.12, bf16[256,512]{1,0:T(8,128)(2,1)S(1)} %get-tuple-element.107, ...), kind=kOutput, calls=%fused_computation | convolution fusion | flops 1090519040 | bytes 5242880 | tf_op jit(solution)/shard_map/dot_general | solution.py:395
  100.2 2.4 %collective-permute-done.17 = bf16[256,512]{1,0:T(8,128)(2,1)S(1)} collective-permute-done((bf16[256,512]{1,0:T(8,128)(2,1)S(1)}, bf16[256,512]{1,0:T(8,128)(2,1)S(1)}, u32[]{:S(2)}, u32[]{:S(2)}) %collective-permute-start.17) | collective-permute-done | bytes 262176 | tf_op jit(solution)/shard_map/ppermute | solution.py:368
  103.5 1.1 %collective-permute-done.19 = f32[512]{0:T(512)S(1)} collective-permute-done((f32[512]{0:T(512)S(1)}, f32[512]{0:T(512)S(1)}, u32[]{:S(2)}, u32[]{:S(2)}) %collective-permute-start.19) | collective-permute-done | bytes 2080 | tf_op jit(solution)/shard_map/ppermute | solution.py:368
  104.6 1.5 %collective-permute-start.22 = (f32[512]{0:T(512)S(1)}, f32[512]{0:T(512)S(1)}, u32[]{:S(2)}, u32[]{:S(2)}) collective-permute-start(f32[512]{0:T(512)S(1)} %add.162), channel_id=1, source_target_pairs={{0,6},{1,7},{2,4},{3,5},{4,2},{5,3},{6,0},{7,1},{8,14},{9,15},{10,... | collective-permute-start | bytes 6152 | tf_op jit(solution)/shard_map/ppermute | solution.py:368
  106.2 3.1 %collective-permute-start.20 = (f32[512]{0:T(512)S(1)}, f32[512]{0:T(512)S(1)}, u32[]{:S(2)}, u32[]{:S(2)}) collective-permute-start(f32[512]{0:T(512)S(1)} %add.162), channel_id=1, source_target_pairs={{0,4},{1,5},{2,6},{3,7},{4,0},{5,1},{6,2},{7,3},{8,12},{9,13},{10,... | collective-permute-start | bytes 6152 | tf_op jit(solution)/shard_map/ppermute | solution.py:368
  109.7 1.5 %collective-permute-done.20 = f32[512]{0:T(512)S(1)} collective-permute-done((f32[512]{0:T(512)S(1)}, f32[512]{0:T(512)S(1)}, u32[]{:S(2)}, u32[]{:S(2)}) %collective-permute-start.20) | collective-permute-done | bytes 2080 | tf_op jit(solution)/shard_map/ppermute | solution.py:368
  111.3 1.7 %multiply_convert_fusion = (bf16[512,1024]{1,0:T(8,128)(2,1)}, bf16[512,1024]{1,0:T(8,128)(2,1)}) fusion(f32[1024]{0:T(1024)S(1)} %copy-done.6, f32[512]{0:T(512)S(1)} %add_rsqrt_fusion, f32[512,512]{1,0:T(8,128)S(1)} %convert_add_fusion, f32[512,512]{1,0:T(8,128)S(1)} %convert_add_fusion.1, bf16[512,1024]{1,0:T(8,128)(2,1)S(1)} %copy-done.3), kind=kLoop, calls=%fused_computation.33 | loop fusion | flops 3670016 | bytes 5249024 | tf_op jit(solution)/shard_map/convert_element_type | solution.py:437
  (79 shorter events, 10.1 us)
Async XLA Ops:
  3.2 60.9 %all-to-all-start = ((bf16[32,256,128]{2,1,0:T(8,128)(2,1)}), bf16[32,256,128]{2,1,0:T(8,128)(2,1)S(1)}, u32[]{:S(2)}, u32[]{:S(2)}) async-start(bf16[32,256,128]{2,1,0:T(8,128)(2,1)} %shard_map.122.after), calls=%async_computation | async-start | bytes 4194304 | tf_op jit(solution)/shard_map/all_to_all | solution.py:377
  15.0 11.1 %copy-start.8 = (s32[1,32]{1,0:T(1,128)S(1)}, s32[1,32]{1,0:T(1,128)}, u32[]{:S(2)}) copy-start(s32[1,32]{1,0:T(1,128)} %param.15) | copy-start | bytes 388
  15.0 11.3 %copy-start.7 = (s32[1,32]{1,0:T(1,128)S(1)}, s32[1,32]{1,0:T(1,128)}, u32[]{:S(2)}) copy-start(s32[1,32]{1,0:T(1,128)} %param.16) | copy-start | bytes 388
  15.0 11.5 %copy-start.4 = (bf16[512,128]{1,0:T(8,128)(2,1)S(1)}, bf16[512,128]{1,0:T(8,128)(2,1)}, u32[]{:S(2)}) copy-start(bf16[512,128]{1,0:T(8,128)(2,1)} %param.12) | copy-start | bytes 393220
  15.0 11.6 %copy-start.5 = (bf16[512,128]{1,0:T(8,128)(2,1)S(1)}, bf16[512,128]{1,0:T(8,128)(2,1)}, u32[]{:S(2)}) copy-start(bf16[512,128]{1,0:T(8,128)(2,1)} %param.13) | copy-start | bytes 393220
  15.0 13.2 %copy-start.2 = (bf16[512,512]{1,0:T(8,128)(2,1)S(1)}, bf16[512,512]{1,0:T(8,128)(2,1)}, u32[]{:S(2)}) copy-start(bf16[512,512]{1,0:T(8,128)(2,1)} %q.5) | copy-start | bytes 1572868
  21.1 29.3 %collective-permute-start = (bf16[2048,512]{1,0:T(8,128)(2,1)}, bf16[2048,512]{1,0:T(8,128)(2,1)}, u32[]{:S(2)}, u32[]{:S(2)}) collective-permute-start(bf16[2048,512]{1,0:T(8,128)(2,1)} %get-tuple-element.60), channel_id=1, source_target_pairs={{0,1},{1,0},{2,3},{3,2},{4,5},{5,4},{6,7},{7,6},{8,9},{9,8},{10,11... | collective-permute-start | bytes 6291464 | tf_op jit(solution)/shard_map/ppermute | solution.py:368
  21.2 26.4 %collective-permute-start.1 = (bf16[1024,512]{1,0:T(8,128)(2,1)}, bf16[1024,512]{1,0:T(8,128)(2,1)}, u32[]{:S(2)}, u32[]{:S(2)}) collective-permute-start(bf16[1024,512]{1,0:T(8,128)(2,1)} %get-tuple-element.61), channel_id=1, source_target_pairs={{0,2},{1,3},{2,0},{3,1},{4,6},{5,7},{6,4},{7,5},{8,10},{9,11},{10,... | collective-permute-start | bytes 3145736 | tf_op jit(solution)/shard_map/ppermute | solution.py:368
  22.9 27.5 %collective-permute-start.2 = (bf16[1024,512]{1,0:T(8,128)(2,1)}, bf16[1024,512]{1,0:T(8,128)(2,1)}, u32[]{:S(2)}, u32[]{:S(2)}) collective-permute-start(bf16[1024,512]{1,0:T(8,128)(2,1)} %get-tuple-element.62), channel_id=1, source_target_pairs={{0,6},{1,7},{2,4},{3,5},{4,2},{5,3},{6,0},{7,1},{8,14},{9,15},{10,... | collective-permute-start | bytes 3145736 | tf_op jit(solution)/shard_map/ppermute | solution.py:368
  25.1 45.8 %collective-permute-start.5 = (bf16[1024,512]{1,0:T(8,128)(2,1)}, bf16[1024,512]{1,0:T(8,128)(2,1)}, u32[]{:S(2)}, u32[]{:S(2)}) collective-permute-start(bf16[1024,512]{1,0:T(8,128)(2,1)} %get-tuple-element.69), channel_id=1, source_target_pairs={{0,3},{1,2},{2,1},{3,0},{4,7},{5,6},{6,5},{7,4},{8,11},{9,10},{10,... | collective-permute-start | bytes 3145736 | tf_op jit(solution)/shard_map/ppermute | solution.py:368
  25.2 46.1 %collective-permute-start.6 = (bf16[1024,512]{1,0:T(8,128)(2,1)}, bf16[1024,512]{1,0:T(8,128)(2,1)}, u32[]{:S(2)}, u32[]{:S(2)}) collective-permute-start(bf16[1024,512]{1,0:T(8,128)(2,1)} %get-tuple-element.70), channel_id=1, source_target_pairs={{0,7},{1,6},{2,5},{3,4},{4,3},{5,2},{6,1},{7,0},{8,15},{9,14},{10,... | collective-permute-start | bytes 3145736 | tf_op jit(solution)/shard_map/ppermute | solution.py:368
  34.4 1.0 copy-start
  67.5 3.8 %collective-permute-start.7 = (bf16[256,512]{1,0:T(8,128)(2,1)S(1)}, bf16[256,512]{1,0:T(8,128)(2,1)S(1)}, u32[]{:S(2)}, u32[]{:S(2)}) collective-permute-start(bf16[256,512]{1,0:T(8,128)(2,1)S(1)} %shard_map.125), channel_id=1, source_target_pairs={{0,1},{1,0},{2,3},{3,2},{4,5},{5,4},{6,7},{7,6},{8,9},{9,8},{10,11... | collective-permute-start | bytes 786440 | tf_op jit(solution)/shard_map/ppermute | solution.py:368
  67.6 12.1 %collective-permute-start.4 = (bf16[256,512]{1,0:T(8,128)(2,1)S(1)}, bf16[256,512]{1,0:T(8,128)(2,1)S(1)}, u32[]{:S(2)}, u32[]{:S(2)}) collective-permute-start(bf16[256,512]{1,0:T(8,128)(2,1)S(1)} %shard_map.125), channel_id=1, source_target_pairs={{0,6},{1,7},{2,4},{3,5},{4,2},{5,3},{6,0},{7,1},{8,14},{9,15},{10,... | collective-permute-start | bytes 786440 | tf_op jit(solution)/shard_map/ppermute | solution.py:368
  70.7 9.0 %collective-permute-start.3 = (bf16[256,512]{1,0:T(8,128)(2,1)S(1)}, bf16[256,512]{1,0:T(8,128)(2,1)S(1)}, u32[]{:S(2)}, u32[]{:S(2)}) collective-permute-start(bf16[256,512]{1,0:T(8,128)(2,1)S(1)} %shard_map.125), channel_id=1, source_target_pairs={{0,2},{1,3},{2,0},{3,1},{4,6},{5,7},{6,4},{7,5},{8,10},{9,11},{10,... | collective-permute-start | bytes 786440 | tf_op jit(solution)/shard_map/ppermute | solution.py:368
  75.9 10.1 %collective-permute-start.14 = (bf16[256,512]{1,0:T(8,128)(2,1)S(1)}, bf16[256,512]{1,0:T(8,128)(2,1)S(1)}, u32[]{:S(2)}, u32[]{:S(2)}) collective-permute-start(bf16[256,512]{1,0:T(8,128)(2,1)S(1)} %get-tuple-element.107), channel_id=1, source_target_pairs={{0,6},{1,7},{2,4},{3,5},{4,2},{5,3},{6,0},{7,1},{8,14},{9,15},{10,... | collective-permute-start | bytes 786440 | tf_op jit(solution)/shard_map/ppermute | solution.py:368
  78.1 8.5 %collective-permute-start.13 = (bf16[256,512]{1,0:T(8,128)(2,1)S(1)}, bf16[256,512]{1,0:T(8,128)(2,1)S(1)}, u32[]{:S(2)}, u32[]{:S(2)}) collective-permute-start(bf16[256,512]{1,0:T(8,128)(2,1)S(1)} %get-tuple-element.107), channel_id=1, source_target_pairs={{0,2},{1,3},{2,0},{3,1},{4,6},{5,7},{6,4},{7,5},{8,10},{9,11},{10,... | collective-permute-start | bytes 786440 | tf_op jit(solution)/shard_map/ppermute | solution.py:368
  78.1 2.8 %collective-permute-start.12 = (bf16[256,512]{1,0:T(8,128)(2,1)S(1)}, bf16[256,512]{1,0:T(8,128)(2,1)S(1)}, u32[]{:S(2)}, u32[]{:S(2)}) collective-permute-start(bf16[256,512]{1,0:T(8,128)(2,1)S(1)} %get-tuple-element.107), channel_id=1, source_target_pairs={{0,1},{1,0},{2,3},{3,2},{4,5},{5,4},{6,7},{7,6},{8,9},{9,8},{10,11... | collective-permute-start | bytes 786440 | tf_op jit(solution)/shard_map/ppermute | solution.py:368
  79.7 1.6 %collective-permute-start.8 = (bf16[256,512]{1,0:T(8,128)(2,1)S(1)}, bf16[256,512]{1,0:T(8,128)(2,1)S(1)}, u32[]{:S(2)}, u32[]{:S(2)}) collective-permute-start(bf16[256,512]{1,0:T(8,128)(2,1)S(1)} %collective-permute-done.3), channel_id=1, source_target_pairs={{0,1},{1,0},{2,3},{3,2},{4,5},{5,4},{6,7},{7,6},{8,9},{9,8},{10,11... | collective-permute-start | bytes 786440 | tf_op jit(solution)/shard_map/ppermute | solution.py:368
  80.0 2.0 %collective-permute-start.9 = (bf16[256,512]{1,0:T(8,128)(2,1)S(1)}, bf16[256,512]{1,0:T(8,128)(2,1)S(1)}, u32[]{:S(2)}, u32[]{:S(2)}) collective-permute-start(bf16[256,512]{1,0:T(8,128)(2,1)S(1)} %collective-permute-done.4), channel_id=1, source_target_pairs={{0,1},{1,0},{2,3},{3,2},{4,5},{5,4},{6,7},{7,6},{8,9},{9,8},{10,11... | collective-permute-start | bytes 786440 | tf_op jit(solution)/shard_map/ppermute | solution.py:368
  86.7 2.4 %collective-permute-start.15 = (bf16[256,512]{1,0:T(8,128)(2,1)S(1)}, bf16[256,512]{1,0:T(8,128)(2,1)S(1)}, u32[]{:S(2)}, u32[]{:S(2)}) collective-permute-start(bf16[256,512]{1,0:T(8,128)(2,1)S(1)} %collective-permute-done.13), channel_id=1, source_target_pairs={{0,1},{1,0},{2,3},{3,2},{4,5},{5,4},{6,7},{7,6},{8,9},{9,8},{10,11... | collective-permute-start | bytes 786440 | tf_op jit(solution)/shard_map/ppermute | solution.py:368
  87.0 10.4 %collective-permute-start.10 = (bf16[256,512]{1,0:T(8,128)(2,1)S(1)}, bf16[256,512]{1,0:T(8,128)(2,1)S(1)}, u32[]{:S(2)}, u32[]{:S(2)}) collective-permute-start(bf16[256,512]{1,0:T(8,128)(2,1)S(1)} %add_convert_fusion.3), channel_id=1, source_target_pairs={{0,6},{1,7},{2,4},{3,5},{4,2},{5,3},{6,0},{7,1},{8,14},{9,15},{10,... | collective-permute-start | bytes 786440 | tf_op jit(solution)/shard_map/ppermute | solution.py:368
  88.6 9.1 %collective-permute-start.11 = (bf16[256,512]{1,0:T(8,128)(2,1)S(1)}, bf16[256,512]{1,0:T(8,128)(2,1)S(1)}, u32[]{:S(2)}, u32[]{:S(2)}) collective-permute-start(bf16[256,512]{1,0:T(8,128)(2,1)S(1)} %add_convert_fusion.2), channel_id=1, source_target_pairs={{0,2},{1,3},{2,0},{3,1},{4,6},{5,7},{6,4},{7,5},{8,10},{9,11},{10,... | collective-permute-start | bytes 786440 | tf_op jit(solution)/shard_map/ppermute | solution.py:368
  88.6 1.5 %collective-permute-start.16 = (bf16[256,512]{1,0:T(8,128)(2,1)S(1)}, bf16[256,512]{1,0:T(8,128)(2,1)S(1)}, u32[]{:S(2)}, u32[]{:S(2)}) collective-permute-start(bf16[256,512]{1,0:T(8,128)(2,1)S(1)} %collective-permute-done.14), channel_id=1, source_target_pairs={{0,1},{1,0},{2,3},{3,2},{4,5},{5,4},{6,7},{7,6},{8,9},{9,8},{10,11... | collective-permute-start | bytes 786440 | tf_op jit(solution)/shard_map/ppermute | solution.py:368
  90.4 12.2 %collective-permute-start.17 = (bf16[256,512]{1,0:T(8,128)(2,1)S(1)}, bf16[256,512]{1,0:T(8,128)(2,1)S(1)}, u32[]{:S(2)}, u32[]{:S(2)}) collective-permute-start(bf16[256,512]{1,0:T(8,128)(2,1)S(1)} %add_convert_fusion.1), channel_id=1, source_target_pairs={{0,6},{1,7},{2,4},{3,5},{4,2},{5,3},{6,0},{7,1},{8,14},{9,15},{10,... | collective-permute-start | bytes 786440 | tf_op jit(solution)/shard_map/ppermute | solution.py:368
  92.2 10.6 %collective-permute-start.18 = (bf16[256,512]{1,0:T(8,128)(2,1)S(1)}, bf16[256,512]{1,0:T(8,128)(2,1)S(1)}, u32[]{:S(2)}, u32[]{:S(2)}) collective-permute-start(bf16[256,512]{1,0:T(8,128)(2,1)S(1)} %add_convert_fusion), channel_id=1, source_target_pairs={{0,2},{1,3},{2,0},{3,1},{4,6},{5,7},{6,4},{7,5},{8,10},{9,11},{10,... | collective-permute-start | bytes 786440 | tf_op jit(solution)/shard_map/ppermute | solution.py:368
  100.2 2.8 %copy-start.3 = (bf16[512,1024]{1,0:T(8,128)(2,1)S(1)}, bf16[512,1024]{1,0:T(8,128)(2,1)}, u32[]{:S(2)}) copy-start(bf16[512,1024]{1,0:T(8,128)(2,1)} %param.14) | copy-start | bytes 3145732
  103.0 8.3 %copy-start.6 = (f32[1024]{0:T(1024)S(1)}, f32[1024]{0:T(1024)}, u32[]{:S(2)}) copy-start(f32[1024]{0:T(1024)} %param.21) | copy-start | bytes 12292
  103.4 1.2 %collective-permute-start.19 = (f32[512]{0:T(512)S(1)}, f32[512]{0:T(512)S(1)}, u32[]{:S(2)}, u32[]{:S(2)}) collective-permute-start(f32[512]{0:T(512)S(1)} %multiply_reduce_fusion), channel_id=1, source_target_pairs={{0,1},{1,0},{2,3},{3,2},{4,5},{5,4},{6,7},{7,6},{8,9},{9,8},{10,11... | collective-permute-start | bytes 6152 | tf_op jit(solution)/shard_map/ppermute | solution.py:368
  104.6 4.8 %collective-permute-start.22 = (f32[512]{0:T(512)S(1)}, f32[512]{0:T(512)S(1)}, u32[]{:S(2)}, u32[]{:S(2)}) collective-permute-start(f32[512]{0:T(512)S(1)} %add.162), channel_id=1, source_target_pairs={{0,6},{1,7},{2,4},{3,5},{4,2},{5,3},{6,0},{7,1},{8,14},{9,15},{10,... | collective-permute-start | bytes 6152 | tf_op jit(solution)/shard_map/ppermute | solution.py:368
  106.1 3.6 %collective-permute-start.21 = (f32[512]{0:T(512)S(1)}, f32[512]{0:T(512)S(1)}, u32[]{:S(2)}, u32[]{:S(2)}) collective-permute-start(f32[512]{0:T(512)S(1)} %add.162), channel_id=1, source_target_pairs={{0,2},{1,3},{2,0},{3,1},{4,6},{5,7},{6,4},{7,5},{8,10},{9,11},{10,... | collective-permute-start | bytes 6152 | tf_op jit(solution)/shard_map/ppermute | solution.py:368
  106.2 5.1 %collective-permute-start.20 = (f32[512]{0:T(512)S(1)}, f32[512]{0:T(512)S(1)}, u32[]{:S(2)}, u32[]{:S(2)}) collective-permute-start(f32[512]{0:T(512)S(1)} %add.162), channel_id=1, source_target_pairs={{0,4},{1,5},{2,6},{3,7},{4,0},{5,1},{6,2},{7,3},{8,12},{9,13},{10,... | collective-permute-start | bytes 6152 | tf_op jit(solution)/shard_map/ppermute | solution.py:368
  (1 other events, 1.0 us)

commit v9 on v8

--- a/solution.py
+++ b/solution.py
@@ -400,33 +400,32 @@
     got = []
     sent = []
     for rows, other, close in zip(attended, others, near):
+        if sent:
+            sent, inputs[0] = lax.optimization_barrier((sent, inputs[0]))
+            got.append([swap(part, mask) for part, mask in zip(sent, (6, 2))])
         local = [times(rows, mats[half]) + times(other, mats[2 + half]) for half in range(2)]
-        close, local, sent = lax.optimization_barrier((close, local, sent))
+        local = lax.optimization_barrier(local)
         side = [swap(part, 1) for part in close]
         sent = [
             local[half] + times(close[half], mats[4 + half]) + times(side[half], mats[6 + half])
             for half in range(2)
         ]
         sent = [total.astype(bf16) for total in sent]
-        sent, side = lax.optimization_barrier((sent, side))
-        got.append([swap(part, mask) for part, mask in zip(sent, (6, 2))])
         inputs.append([[rows, other, close[half], side[half]] for half in range(2)])
-
-    got[0], inputs = lax.optimization_barrier((got[0], inputs))
+    sent, inputs[1] = lax.optimization_barrier((sent, inputs[1]))
+    got.append([swap(part, mask) for part, mask in zip(sent, (6, 2))])
+
     own = [
-        times(
-            jnp.concatenate([jnp.concatenate(halves[half], axis=1) for halves in inputs], axis=0),
-            mat,
-        )
-        for half, mat in enumerate((own_0, own_1))
+        [times(jnp.concatenate(parts, axis=1), mat) for parts, mat in zip(halves, (own_0, own_1))]
+        for halves in inputs
     ]
-    own = lax.optimization_barrier(own)
+    own = [[lax.optimization_barrier(part) for part in halves] for halves in own]
     delta = jnp.concatenate(
         [
-            own[half] + jnp.concatenate([pair[half] for pair in got], axis=0).astype(f32)
-            for half in range(2)
+            jnp.concatenate([mine + part.astype(f32) for mine, part in zip(*pair)], axis=1)
+            for pair in zip(own, got)
         ],
-        axis=1,
+        axis=0,
     )
     summed = hidden.astype(f32) + delta
     residual_out = summed.astype(bf16)

time: 114 us -> 111 us (0.974); the launches traced: 113 us -> 111 us
  waiting for transfers between devices: 42.4 us -> 39.7 us
    ppermute x23, waiting for transfers between devices: 28.7 us -> 26 us  [swap(): return lax.ppermute(value, 'tensor', [(t, t ^ mask) for t in range(count)])]
    dot_general x18 -> x20, matrix products: 7.24 us -> 7.58 us  [times(): return jnp.dot(rows, mat, preferred_element_type=f32)]
  transfers between devices with their start and end apart: 24 -> 24, of which waited for: 15 -> 12; matrix products, arithmetic and copies ran while one was open for 8% -> 9% of each run, Pallas kernels for 18% -> 19%
where the time goes in v9:
time: 111 us
  waiting for transfers between devices  39.7 us (36%)
  starting transfers between devices  33.1 us (30%)
  Pallas kernels  23.2 us (21%)
  matrix products  7.58 us (7%)
  other arithmetic  3.58 us (3%)
  local copies, waits for them, and re-layouts  2.89 us (3%)
  between operations  1.13 us (1%)
    ppermute x23, waiting for transfers between devices, swap(): return lax.ppermute(value, 'tensor', [(t, t ^ mask) for t in range(count)])  26 us
    ppermute x23, starting transfers between devices, swap(): return lax.ppermute(value, 'tensor', [(t, t ^ mask) for t in range(count)])  21.5 us
    all_to_all x1, waiting for transfers between devices, on_device(): lax.all_to_all(payload, 'dp', split_axis=0, concat_axis=0, tiled=True)  13.7 us
    all_to_all x1, starting transfers between devices, on_device(): lax.all_to_all(payload, 'dp', split_axis=0, concat_axis=0, tiled=True)  11.6 us
    pallas_call x2, Pallas kernels, attend(): pl.pallas_call(functools.partial(main_kernel, first), out_shape=(rows, *s...  8.38 us
    dot_general x20, matrix products, times(): return jnp.dot(rows, mat, preferred_element_type=f32)  7.58 us
    pallas_call x1, Pallas kernels, attend_fresh(): pl.pallas_call(fresh_kernel, out_shape=(area, area), in_specs=whole(4), o...  6.16 us
    pallas_call x1, Pallas kernels, cut(): pl.pallas_call(cut_kernel, out_shape=tuple((pltpu.VMEM((height, 512), wei...  6.06 us
  transfers between devices with their start and end apart: 24, of which 12 were waited for; matrix products, arithmetic and copies ran while one was open for 9% of the time, Pallas kernels for 19%

profile of v9, /device:TPU:2, one launch (start us, length us, event | category | flops | bytes accessed | tf_op | source)
XLA Modules:
  0.0 111.3 jit_solution(2594179678373838696)
XLA Ops:
  0.6 2.6 %shard_map.122.after = bf16[32,256,128]{2,1,0:T(8,128)(2,1)} custom-call(s32[1,32]{1,0:T(1,128)} %lengths_hbm.1, bf16[32,128,128]{2,1,0:T(8,128)(2,1)} %bitcast.84, bf16[32,128,128]{2,1,0:T(8,128)(2,1)} %bitcast.85), custom_call_target="tpu_custom_call" | custom-call | flops 1048576 | bytes 4194304 | tf_op jit(solution)/shard_map/pallas_call | solution.py:239
  3.2 11.6 %all-to-all-start = ((bf16[32,256,128]{2,1,0:T(8,128)(2,1)}), bf16[32,256,128]{2,1,0:T(8,128)(2,1)S(1)}, u32[]{:S(2)}, u32[]{:S(2)}) async-start(bf16[32,256,128]{2,1,0:T(8,128)(2,1)} %shard_map.122.after), calls=%async_computation | async-start | bytes 4194304 | tf_op jit(solution)/shard_map/all_to_all | solution.py:377
  15.0 6.1 %shard_map.123 = (bf16[1024,512]{1,0:T(8,128)(2,1)}, bf16[1024,512]{1,0:T(8,128)(2,1)}, bf16[1024,512]{1,0:T(8,128)(2,1)}, bf16[1024,512]{1,0:T(8,128)(2,1)}, bf16[2048,512]{1,0:T(8,128)(2,1)}) custom-call(s32[12]{0:T(128)S(1)} %stack.86.starts, bf16[512,8192]{1,0:T(8,128)(2,1)} %refs_0_.1, bf16[32,256,128]{2,1,0:T(8,128)(2,1)} %shard_map.122.after), custom_call_target="tpu_custom_call" | custom-call | bytes 12582912 | tf_op jit(solution)/shard_map/pallas_call | solution.py:271
  21.2 1.7 %collective-permute-start.1 = (bf16[1024,512]{1,0:T(8,128)(2,1)}, bf16[1024,512]{1,0:T(8,128)(2,1)}, u32[]{:S(2)}, u32[]{:S(2)}) collective-permute-start(bf16[1024,512]{1,0:T(8,128)(2,1)} %get-tuple-element.49), channel_id=1, source_target_pairs={{0,2},{1,3},{2,0},{3,1},{4,6},{5,7},{6,4},{7,5},{8,10},{9,11},{10,... | collective-permute-start | bytes 3145736 | tf_op jit(solution)/shard_map/ppermute | solution.py:368
  22.9 2.2 %collective-permute-start.2 = (bf16[1024,512]{1,0:T(8,128)(2,1)}, bf16[1024,512]{1,0:T(8,128)(2,1)}, u32[]{:S(2)}, u32[]{:S(2)}) collective-permute-start(bf16[1024,512]{1,0:T(8,128)(2,1)} %get-tuple-element.50), channel_id=1, source_target_pairs={{0,6},{1,7},{2,4},{3,5},{4,2},{5,3},{6,0},{7,1},{8,14},{9,15},{10,... | collective-permute-start | bytes 3145736 | tf_op jit(solution)/shard_map/ppermute | solution.py:368
  25.2 0.9 collective-permute-start.4
  28.2 6.2 %shard_map.124 = (f32[16,128,128]{2,1,0:T(8,128)S(1)}, f32[16,128,128]{2,1,0:T(8,128)S(1)}) custom-call(bf16[512,512]{1,0:T(8,128)(2,1)S(1)} %copy-done.2, bf16[608,128]{1,0:T(8,128)(2,1)S(1)} %pad.7.fresh_k, bf16[608,128]{1,0:T(8,128)(2,1)S(1)} %pad.8.fresh_v, s32[512,128]{1,0:T(8,128)S(1)} %broadcast_in_dim.105.row_start), custom_call_target="tpu_custom_call" | custom-call | flops 2147483648 | bytes 4194304 | tf_op jit(solution)/shard_map/pallas_call | solution.py:304
  34.4 1.0 copy-done
  35.4 1.0 copy-done.1
  36.4 11.2 %collective-permute-done.1.refs_2_ = bf16[1024,512]{1,0:T(8,128)(2,1)} collective-permute-done((bf16[1024,512]{1,0:T(8,128)(2,1)}, bf16[1024,512]{1,0:T(8,128)(2,1)}, u32[]{:S(2)}, u32[]{:S(2)}) %collective-permute-start.1) | collective-permute-done | bytes 1048608 | tf_op jit(solution)/shard_map/ppermute | solution.py:368
  47.6 2.8 %collective-permute-done.2.refs_3_ = bf16[1024,512]{1,0:T(8,128)(2,1)} collective-permute-done((bf16[1024,512]{1,0:T(8,128)(2,1)}, bf16[1024,512]{1,0:T(8,128)(2,1)}, u32[]{:S(2)}, u32[]{:S(2)}) %collective-permute-start.2) | collective-permute-done | bytes 1048608 | tf_op jit(solution)/shard_map/ppermute | solution.py:368
  50.4 13.7 %all-to-all-done.cache_hbm = bf16[32,256,128]{2,1,0:T(8,128)(2,1)S(1)} async-done(((bf16[32,256,128]{2,1,0:T(8,128)(2,1)}), bf16[32,256,128]{2,1,0:T(8,128)(2,1)S(1)}, u32[]{:S(2)}, u32[]{:S(2)}) %all-to-all-start) | async-done | bytes 2097184 | tf_op jit(solution)/shard_map/all_to_all | solution.py:377
  64.1 3.8 %shard_map.125 = bf16[256,512]{1,0:T(8,128)(2,1)S(1)} custom-call(s32[5,48]{1,0:T(8,128)S(1)} %stack.73.plan, s32[4]{0:T(128)S(1)} %pad_add_fusion.starts, bf16[512,512]{1,0:T(8,128)(2,1)S(1)} %copy-done.2, bf16[32,256,128]{2,1,0:T(8,128)(2,1)S(1)} %all-to-all-done.cache_hbm, f32[16,128,128]{2,1,0:T(8,128)} %copy-done, f32[16,128,128]{2,1,0:T(8,128)} %copy-done.1), custom_call_target="tpu_custom_call" | custom-call | flops 2147483648 | bytes 4194304 | tf_op jit(solution)/shard_map/pallas_call | solution.py:323
  68.0 3.1 %collective-permute-start.8 = (bf16[256,512]{1,0:T(8,128)(2,1)S(1)}, bf16[256,512]{1,0:T(8,128)(2,1)S(1)}, u32[]{:S(2)}, u32[]{:S(2)}) collective-permute-start(bf16[256,512]{1,0:T(8,128)(2,1)S(1)} %shard_map.125), channel_id=1, source_target_pairs={{0,6},{1,7},{2,4},{3,5},{4,2},{5,3},{6,0},{7,1},{8,14},{9,15},{10,... | collective-permute-start | bytes 786440 | tf_op jit(solution)/shard_map/ppermute | solution.py:368
  71.3 4.6 %shard_map.126 = (bf16[256,512]{1,0:T(8,128)(2,1)S(1)}, bf16[512,512]{1,0:T(8,128)(2,1)S(1)}, bf16[512,512]{1,0:T(8,128)(2,1)S(1)}, bf16[512,512]{1,0:T(8,128)(2...) custom-call(s32[5,48]{1,0:T(8,128)S(1)} %stack.73.plan, ...), custom_call_target="tpu_custom_call" | custom-call | flops 2147483648 | bytes 4194304 | tf_op jit(solution)/shard_map/pallas_call | solution.py:323
  75.9 0.7 collective-permute-start.12
  76.6 2.2 %collective-permute-start.15 = (bf16[256,512]{1,0:T(8,128)(2,1)S(1)}, bf16[256,512]{1,0:T(8,128)(2,1)S(1)}, u32[]{:S(2)}, u32[]{:S(2)}) collective-permute-start(bf16[256,512]{1,0:T(8,128)(2,1)S(1)} %get-tuple-element.84), channel_id=1, source_target_pairs={{0,6},{1,7},{2,4},{3,5},{4,2},{5,3},{6,0},{7,1},{8,14},{9,15},{10,... | collective-permute-start | bytes 786440 | tf_op jit(solution)/shard_map/ppermute | solution.py:368
  82.3 0.7 fusion.4
  83.0 1.9 %collective-permute-start.10 = (bf16[256,512]{1,0:T(8,128)(2,1)S(1)}, bf16[256,512]{1,0:T(8,128)(2,1)S(1)}, u32[]{:S(2)}, u32[]{:S(2)}) collective-permute-start(bf16[256,512]{1,0:T(8,128)(2,1)S(1)} %fusion), channel_id=1, source_target_pairs={{0,6},{1,7},{2,4},{3,5},{4,2},{5,3},{6,0},{7,1},{8,14},{9,15},{10,... | collective-permute-start | bytes 786440 | tf_op jit(solution)/shard_map/ppermute | solution.py:368
  84.9 0.7 fusion.12
  85.6 0.7 collective-permute-start.11
  90.1 2.3 %collective-permute-start.17 = (bf16[256,512]{1,0:T(8,128)(2,1)S(1)}, bf16[256,512]{1,0:T(8,128)(2,1)S(1)}, u32[]{:S(2)}, u32[]{:S(2)}) collective-permute-start(bf16[256,512]{1,0:T(8,128)(2,1)S(1)} %fusion.2), channel_id=1, source_target_pairs={{0,6},{1,7},{2,4},{3,5},{4,2},{5,3},{6,0},{7,1},{8,14},{9,15},{10,... | collective-permute-start | bytes 786440 | tf_op jit(solution)/shard_map/ppermute | solution.py:368
  92.3 0.7 fusion.20
  93.0 0.7 fusion.28
  93.9 6.0 %collective-permute-done.17 = bf16[256,512]{1,0:T(8,128)(2,1)S(1)} collective-permute-done((bf16[256,512]{1,0:T(8,128)(2,1)S(1)}, bf16[256,512]{1,0:T(8,128)(2,1)S(1)}, u32[]{:S(2)}, u32[]{:S(2)}) %collective-permute-start.17) | collective-permute-done | bytes 262176 | tf_op jit(solution)/shard_map/ppermute | solution.py:368
  101.2 1.1 %collective-permute-done.19 = f32[512]{0:T(512)S(1)} collective-permute-done((f32[512]{0:T(512)S(1)}, f32[512]{0:T(512)S(1)}, u32[]{:S(2)}, u32[]{:S(2)}) %collective-permute-start.19) | collective-permute-done | bytes 2080 | tf_op jit(solution)/shard_map/ppermute | solution.py:368
  102.3 1.3 %collective-permute-start.20 = (f32[512]{0:T(512)S(1)}, f32[512]{0:T(512)S(1)}, u32[]{:S(2)}, u32[]{:S(2)}) collective-permute-start(f32[512]{0:T(512)S(1)} %add.170), channel_id=1, source_target_pairs={{0,4},{1,5},{2,6},{3,7},{4,0},{5,1},{6,2},{7,3},{8,12},{9,13},{10,... | collective-permute-start | bytes 6152 | tf_op jit(solution)/shard_map/ppermute | solution.py:368
  103.6 1.2 %collective-permute-start.21 = (f32[512]{0:T(512)S(1)}, f32[512]{0:T(512)S(1)}, u32[]{:S(2)}, u32[]{:S(2)}) collective-permute-start(f32[512]{0:T(512)S(1)} %add.170), channel_id=1, source_target_pairs={{0,2},{1,3},{2,0},{3,1},{4,6},{5,7},{6,4},{7,5},{8,10},{9,11},{10,... | collective-permute-start | bytes 6152 | tf_op jit(solution)/shard_map/ppermute | solution.py:368
  104.8 1.6 %collective-permute-start.22 = (f32[512]{0:T(512)S(1)}, f32[512]{0:T(512)S(1)}, u32[]{:S(2)}, u32[]{:S(2)}) collective-permute-start(f32[512]{0:T(512)S(1)} %add.170), channel_id=1, source_target_pairs={{0,6},{1,7},{2,4},{3,5},{4,2},{5,3},{6,0},{7,1},{8,14},{9,15},{10,... | collective-permute-start | bytes 6152 | tf_op jit(solution)/shard_map/ppermute | solution.py:368
  106.4 1.0 collective-permute-done.20
  107.4 2.2 %collective-permute-done.22 = f32[512]{0:T(512)S(1)} collective-permute-done((f32[512]{0:T(512)S(1)}, f32[512]{0:T(512)S(1)}, u32[]{:S(2)}, u32[]{:S(2)}) %collective-permute-start.22) | collective-permute-done | bytes 2080 | tf_op jit(solution)/shard_map/ppermute | solution.py:368
  109.6 1.7 %multiply_convert_fusion = (bf16[512,1024]{1,0:T(8,128)(2,1)}, bf16[512,1024]{1,0:T(8,128)(2,1)}) fusion(f32[1024]{0:T(1024)S(1)} %copy-done.6, f32[512]{0:T(512)S(1)} %add_rsqrt_fusion, f32[256,512]{1,0:T(8,128)S(1)} %convert_add_fusion, f32[256,512]{1,0:T(8,128)S(1)} %convert_add_fusion.1, f32[256,512]{1,0:T(8,128)S(1)} %convert_add_fusion.2, ...), kind=kLoop, calls=%fused_computation.1 | loop fusion | flops 4718592 | bytes 5249024 | tf_op jit(solution)/shard_map/convert_element_type | solution.py:436
  (83 shorter events, 11.2 us)
Async XLA Ops:
  3.2 60.9 %all-to-all-start = ((bf16[32,256,128]{2,1,0:T(8,128)(2,1)}), bf16[32,256,128]{2,1,0:T(8,128)(2,1)S(1)}, u32[]{:S(2)}, u32[]{:S(2)}) async-start(bf16[32,256,128]{2,1,0:T(8,128)(2,1)} %shard_map.122.after), calls=%async_computation | async-start | bytes 4194304 | tf_op jit(solution)/shard_map/all_to_all | solution.py:377
  15.0 11.1 %copy-start.8 = (s32[1,32]{1,0:T(1,128)S(1)}, s32[1,32]{1,0:T(1,128)}, u32[]{:S(2)}) copy-start(s32[1,32]{1,0:T(1,128)} %param.15) | copy-start | bytes 388
  15.0 11.3 %copy-start.7 = (s32[1,32]{1,0:T(1,128)S(1)}, s32[1,32]{1,0:T(1,128)}, u32[]{:S(2)}) copy-start(s32[1,32]{1,0:T(1,128)} %param.16) | copy-start | bytes 388
  15.0 11.5 %copy-start.4 = (bf16[512,128]{1,0:T(8,128)(2,1)S(1)}, bf16[512,128]{1,0:T(8,128)(2,1)}, u32[]{:S(2)}) copy-start(bf16[512,128]{1,0:T(8,128)(2,1)} %param.12) | copy-start | bytes 393220
  15.0 11.6 %copy-start.5 = (bf16[512,128]{1,0:T(8,128)(2,1)S(1)}, bf16[512,128]{1,0:T(8,128)(2,1)}, u32[]{:S(2)}) copy-start(bf16[512,128]{1,0:T(8,128)(2,1)} %param.13) | copy-start | bytes 393220
  15.0 13.2 %copy-start.2 = (bf16[512,512]{1,0:T(8,128)(2,1)S(1)}, bf16[512,512]{1,0:T(8,128)(2,1)}, u32[]{:S(2)}) copy-start(bf16[512,512]{1,0:T(8,128)(2,1)} %q.5) | copy-start | bytes 1572868
  21.1 29.3 %collective-permute-start = (bf16[2048,512]{1,0:T(8,128)(2,1)}, bf16[2048,512]{1,0:T(8,128)(2,1)}, u32[]{:S(2)}, u32[]{:S(2)}) collective-permute-start(bf16[2048,512]{1,0:T(8,128)(2,1)} %get-tuple-element.48), channel_id=1, source_target_pairs={{0,1},{1,0},{2,3},{3,2},{4,5},{5,4},{6,7},{7,6},{8,9},{9,8},{10,11... | collective-permute-start | bytes 6291464 | tf_op jit(solution)/shard_map/ppermute | solution.py:368
  21.2 26.4 %collective-permute-start.1 = (bf16[1024,512]{1,0:T(8,128)(2,1)}, bf16[1024,512]{1,0:T(8,128)(2,1)}, u32[]{:S(2)}, u32[]{:S(2)}) collective-permute-start(bf16[1024,512]{1,0:T(8,128)(2,1)} %get-tuple-element.49), channel_id=1, source_target_pairs={{0,2},{1,3},{2,0},{3,1},{4,6},{5,7},{6,4},{7,5},{8,10},{9,11},{10,... | collective-permute-start | bytes 3145736 | tf_op jit(solution)/shard_map/ppermute | solution.py:368
  22.9 27.5 %collective-permute-start.2 = (bf16[1024,512]{1,0:T(8,128)(2,1)}, bf16[1024,512]{1,0:T(8,128)(2,1)}, u32[]{:S(2)}, u32[]{:S(2)}) collective-permute-start(bf16[1024,512]{1,0:T(8,128)(2,1)} %get-tuple-element.50), channel_id=1, source_target_pairs={{0,6},{1,7},{2,4},{3,5},{4,2},{5,3},{6,0},{7,1},{8,14},{9,15},{10,... | collective-permute-start | bytes 3145736 | tf_op jit(solution)/shard_map/ppermute | solution.py:368
  25.1 46.2 %collective-permute-start.3 = (bf16[1024,512]{1,0:T(8,128)(2,1)}, bf16[1024,512]{1,0:T(8,128)(2,1)}, u32[]{:S(2)}, u32[]{:S(2)}) collective-permute-start(bf16[1024,512]{1,0:T(8,128)(2,1)} %get-tuple-element.57), channel_id=1, source_target_pairs={{0,3},{1,2},{2,1},{3,0},{4,7},{5,6},{6,5},{7,4},{8,11},{9,10},{10,... | collective-permute-start | bytes 3145736 | tf_op jit(solution)/shard_map/ppermute | solution.py:368
  25.2 46.1 %collective-permute-start.4 = (bf16[1024,512]{1,0:T(8,128)(2,1)}, bf16[1024,512]{1,0:T(8,128)(2,1)}, u32[]{:S(2)}, u32[]{:S(2)}) collective-permute-start(bf16[1024,512]{1,0:T(8,128)(2,1)} %get-tuple-element.58), channel_id=1, source_target_pairs={{0,7},{1,6},{2,5},{3,4},{4,3},{5,2},{6,1},{7,0},{8,15},{9,14},{10,... | collective-permute-start | bytes 3145736 | tf_op jit(solution)/shard_map/ppermute | solution.py:368
  34.4 1.0 copy-start
  67.9 3.3 %collective-permute-start.5 = (bf16[256,512]{1,0:T(8,128)(2,1)S(1)}, bf16[256,512]{1,0:T(8,128)(2,1)S(1)}, u32[]{:S(2)}, u32[]{:S(2)}) collective-permute-start(bf16[256,512]{1,0:T(8,128)(2,1)S(1)} %shard_map.125), channel_id=1, source_target_pairs={{0,1},{1,0},{2,3},{3,2},{4,5},{5,4},{6,7},{7,6},{8,9},{9,8},{10,11... | collective-permute-start | bytes 786440 | tf_op jit(solution)/shard_map/ppermute | solution.py:368
  68.0 11.9 %collective-permute-start.8 = (bf16[256,512]{1,0:T(8,128)(2,1)S(1)}, bf16[256,512]{1,0:T(8,128)(2,1)S(1)}, u32[]{:S(2)}, u32[]{:S(2)}) collective-permute-start(bf16[256,512]{1,0:T(8,128)(2,1)S(1)} %shard_map.125), channel_id=1, source_target_pairs={{0,6},{1,7},{2,4},{3,5},{4,2},{5,3},{6,0},{7,1},{8,14},{9,15},{10,... | collective-permute-start | bytes 786440 | tf_op jit(solution)/shard_map/ppermute | solution.py:368
  71.1 9.0 %collective-permute-start.6 = (bf16[256,512]{1,0:T(8,128)(2,1)S(1)}, bf16[256,512]{1,0:T(8,128)(2,1)S(1)}, u32[]{:S(2)}, u32[]{:S(2)}) collective-permute-start(bf16[256,512]{1,0:T(8,128)(2,1)S(1)} %shard_map.125), channel_id=1, source_target_pairs={{0,2},{1,3},{2,0},{3,1},{4,6},{5,7},{6,4},{7,5},{8,10},{9,11},{10,... | collective-permute-start | bytes 786440 | tf_op jit(solution)/shard_map/ppermute | solution.py:368
  75.9 10.5 %collective-permute-start.12 = (bf16[256,512]{1,0:T(8,128)(2,1)S(1)}, bf16[256,512]{1,0:T(8,128)(2,1)S(1)}, u32[]{:S(2)}, u32[]{:S(2)}) collective-permute-start(bf16[256,512]{1,0:T(8,128)(2,1)S(1)} %get-tuple-element.84), channel_id=1, source_target_pairs={{0,1},{1,0},{2,3},{3,2},{4,5},{5,4},{6,7},{7,6},{8,9},{9,8},{10,11... | collective-permute-start | bytes 786440 | tf_op jit(solution)/shard_map/ppermute | solution.py:368
  76.6 11.0 %collective-permute-start.15 = (bf16[256,512]{1,0:T(8,128)(2,1)S(1)}, bf16[256,512]{1,0:T(8,128)(2,1)S(1)}, u32[]{:S(2)}, u32[]{:S(2)}) collective-permute-start(bf16[256,512]{1,0:T(8,128)(2,1)S(1)} %get-tuple-element.84), channel_id=1, source_target_pairs={{0,6},{1,7},{2,4},{3,5},{4,2},{5,3},{6,0},{7,1},{8,14},{9,15},{10,... | collective-permute-start | bytes 786440 | tf_op jit(solution)/shard_map/ppermute | solution.py:368
  78.7 9.3 %collective-permute-start.13 = (bf16[256,512]{1,0:T(8,128)(2,1)S(1)}, bf16[256,512]{1,0:T(8,128)(2,1)S(1)}, u32[]{:S(2)}, u32[]{:S(2)}) collective-permute-start(bf16[256,512]{1,0:T(8,128)(2,1)S(1)} %get-tuple-element.84), channel_id=1, source_target_pairs={{0,2},{1,3},{2,0},{3,1},{4,6},{5,7},{6,4},{7,5},{8,10},{9,11},{10,... | collective-permute-start | bytes 786440 | tf_op jit(solution)/shard_map/ppermute | solution.py:368
  80.0 1.6 %collective-permute-start.9 = (bf16[256,512]{1,0:T(8,128)(2,1)S(1)}, bf16[256,512]{1,0:T(8,128)(2,1)S(1)}, u32[]{:S(2)}, u32[]{:S(2)}) collective-permute-start(bf16[256,512]{1,0:T(8,128)(2,1)S(1)} %collective-permute-done.8), channel_id=1, source_target_pairs={{0,1},{1,0},{2,3},{3,2},{4,5},{5,4},{6,7},{7,6},{8,9},{9,8},{10,11... | collective-permute-start | bytes 786440 | tf_op jit(solution)/shard_map/ppermute | solution.py:368
  80.1 1.9 %collective-permute-start.7 = (bf16[256,512]{1,0:T(8,128)(2,1)S(1)}, bf16[256,512]{1,0:T(8,128)(2,1)S(1)}, u32[]{:S(2)}, u32[]{:S(2)}) collective-permute-start(bf16[256,512]{1,0:T(8,128)(2,1)S(1)} %collective-permute-done.6), channel_id=1, source_target_pairs={{0,1},{1,0},{2,3},{3,2},{4,5},{5,4},{6,7},{7,6},{8,9},{9,8},{10,11... | collective-permute-start | bytes 786440 | tf_op jit(solution)/shard_map/ppermute | solution.py:368
  83.0 10.8 %collective-permute-start.10 = (bf16[256,512]{1,0:T(8,128)(2,1)S(1)}, bf16[256,512]{1,0:T(8,128)(2,1)S(1)}, u32[]{:S(2)}, u32[]{:S(2)}) collective-permute-start(bf16[256,512]{1,0:T(8,128)(2,1)S(1)} %fusion), channel_id=1, source_target_pairs={{0,6},{1,7},{2,4},{3,5},{4,2},{5,3},{6,0},{7,1},{8,14},{9,15},{10,... | collective-permute-start | bytes 786440 | tf_op jit(solution)/shard_map/ppermute | solution.py:368
  85.6 8.3 %collective-permute-start.11 = (bf16[256,512]{1,0:T(8,128)(2,1)S(1)}, bf16[256,512]{1,0:T(8,128)(2,1)S(1)}, u32[]{:S(2)}, u32[]{:S(2)}) collective-permute-start(bf16[256,512]{1,0:T(8,128)(2,1)S(1)} %fusion.1), channel_id=1, source_target_pairs={{0,2},{1,3},{2,0},{3,1},{4,6},{5,7},{6,4},{7,5},{8,10},{9,11},{10,... | collective-permute-start | bytes 786440 | tf_op jit(solution)/shard_map/ppermute | solution.py:368
  87.6 1.6 %collective-permute-start.16 = (bf16[256,512]{1,0:T(8,128)(2,1)S(1)}, bf16[256,512]{1,0:T(8,128)(2,1)S(1)}, u32[]{:S(2)}, u32[]{:S(2)}) collective-permute-start(bf16[256,512]{1,0:T(8,128)(2,1)S(1)} %collective-permute-done.15), channel_id=1, source_target_pairs={{0,1},{1,0},{2,3},{3,2},{4,5},{5,4},{6,7},{7,6},{8,9},{9,8},{10,11... | collective-permute-start | bytes 786440 | tf_op jit(solution)/shard_map/ppermute | solution.py:368
  88.0 1.7 %collective-permute-start.14 = (bf16[256,512]{1,0:T(8,128)(2,1)S(1)}, bf16[256,512]{1,0:T(8,128)(2,1)S(1)}, u32[]{:S(2)}, u32[]{:S(2)}) collective-permute-start(bf16[256,512]{1,0:T(8,128)(2,1)S(1)} %collective-permute-done.13), channel_id=1, source_target_pairs={{0,1},{1,0},{2,3},{3,2},{4,5},{5,4},{6,7},{7,6},{8,9},{9,8},{10,11... | collective-permute-start | bytes 786440 | tf_op jit(solution)/shard_map/ppermute | solution.py:368
  90.1 9.9 %collective-permute-start.17 = (bf16[256,512]{1,0:T(8,128)(2,1)S(1)}, bf16[256,512]{1,0:T(8,128)(2,1)S(1)}, u32[]{:S(2)}, u32[]{:S(2)}) collective-permute-start(bf16[256,512]{1,0:T(8,128)(2,1)S(1)} %fusion.2), channel_id=1, source_target_pairs={{0,6},{1,7},{2,4},{3,5},{4,2},{5,3},{6,0},{7,1},{8,14},{9,15},{10,... | collective-permute-start | bytes 786440 | tf_op jit(solution)/shard_map/ppermute | solution.py:368
  92.3 8.3 %collective-permute-start.18 = (bf16[256,512]{1,0:T(8,128)(2,1)S(1)}, bf16[256,512]{1,0:T(8,128)(2,1)S(1)}, u32[]{:S(2)}, u32[]{:S(2)}) collective-permute-start(bf16[256,512]{1,0:T(8,128)(2,1)S(1)} %fusion.3), channel_id=1, source_target_pairs={{0,2},{1,3},{2,0},{3,1},{4,6},{5,7},{6,4},{7,5},{8,10},{9,11},{10,... | collective-permute-start | bytes 786440 | tf_op jit(solution)/shard_map/ppermute | solution.py:368
  93.8 6.9 %copy-start.3 = (bf16[512,1024]{1,0:T(8,128)(2,1)S(1)}, bf16[512,1024]{1,0:T(8,128)(2,1)}, u32[]{:S(2)}) copy-start(bf16[512,1024]{1,0:T(8,128)(2,1)} %param.14) | copy-start | bytes 3145732
  100.0 9.6 %copy-start.6 = (f32[1024]{0:T(1024)S(1)}, f32[1024]{0:T(1024)}, u32[]{:S(2)}) copy-start(f32[1024]{0:T(1024)} %param.21) | copy-start | bytes 12292
  101.1 1.2 %collective-permute-start.19 = (f32[512]{0:T(512)S(1)}, f32[512]{0:T(512)S(1)}, u32[]{:S(2)}, u32[]{:S(2)}) collective-permute-start(f32[512]{0:T(512)S(1)} %multiply_reduce_fusion), channel_id=1, source_target_pairs={{0,1},{1,0},{2,3},{3,2},{4,5},{5,4},{6,7},{7,6},{8,9},{9,8},{10,11... | collective-permute-start | bytes 6152 | tf_op jit(solution)/shard_map/ppermute | solution.py:368
  102.3 5.1 %collective-permute-start.20 = (f32[512]{0:T(512)S(1)}, f32[512]{0:T(512)S(1)}, u32[]{:S(2)}, u32[]{:S(2)}) collective-permute-start(f32[512]{0:T(512)S(1)} %add.170), channel_id=1, source_target_pairs={{0,4},{1,5},{2,6},{3,7},{4,0},{5,1},{6,2},{7,3},{8,12},{9,13},{10,... | collective-permute-start | bytes 6152 | tf_op jit(solution)/shard_map/ppermute | solution.py:368
  103.6 3.8 %collective-permute-start.21 = (f32[512]{0:T(512)S(1)}, f32[512]{0:T(512)S(1)}, u32[]{:S(2)}, u32[]{:S(2)}) collective-permute-start(f32[512]{0:T(512)S(1)} %add.170), channel_id=1, source_target_pairs={{0,2},{1,3},{2,0},{3,1},{4,6},{5,7},{6,4},{7,5},{8,10},{9,11},{10,... | collective-permute-start | bytes 6152 | tf_op jit(solution)/shard_map/ppermute | solution.py:368
  104.8 4.8 %collective-permute-start.22 = (f32[512]{0:T(512)S(1)}, f32[512]{0:T(512)S(1)}, u32[]{:S(2)}, u32[]{:S(2)}) collective-permute-start(f32[512]{0:T(512)S(1)} %add.170), channel_id=1, source_target_pairs={{0,6},{1,7},{2,4},{3,5},{4,2},{5,3},{6,0},{7,1},{8,14},{9,15},{10,... | collective-permute-start | bytes 6152 | tf_op jit(solution)/shard_map/ppermute | solution.py:368
  (1 other events, 1.0 us)

commit v10 on v9

--- a/solution.py
+++ b/solution.py
@@ -122,14 +122,11 @@
 
 def main_kernel(first, plan, starts, q, cache_hbm, mean_hbm, level_hbm, *refs):
     cache, means, levels, scores, weights, mixed, sems, stage_sems = refs[-8:]
-    stage = []
-    if len(refs) > 9:
-        own = [refs[16 + i % 2].at[pl.ds(512 * (i // 2), 512)] for i in range(8)]
-        stage = staging(1, starts, refs[:6], refs[8:16], stage_sems.at[0])
-        stage += staging(0, starts, refs[:6], own, stage_sems.at[1])
-        out = refs[7]
-    else:
-        out = refs[0]
+    count, waits = (2, 0) if first == 0 else (4, 1)
+    out, *targets = refs[count + waits : -8]
+    own = [targets[4 + i % 2].at[pl.ds(512 * (i // 2), 512)] for i in range(4)]
+    stage = staging(1, starts, refs[:count], targets[:4], stage_sems.at[0])
+    stage += staging(0, starts, refs[:count], own, stage_sems.at[1])
     half = cache.shape[1] // 2
     fetch = [
         pltpu.make_async_copy(
@@ -284,14 +281,16 @@
 
 
 def staging(part, starts, sources, targets, sems):
-    weight, sibling, *near = sources
-    blocks = []
-    for half in range(2):
-        start = pl.multiple_of(starts[2 * half + part], 512)
-        blocks.append(weight.at[:, pl.ds(start, 512)])
-    for half in range(2):
-        blocks.append(sibling.at[pl.ds(1024 * half + 512 * part, 512)])
-    blocks += [block.at[pl.ds(512 * part, 512)] for block in near]
+    if len(sources) == 2:
+        weight, sibling = sources
+        blocks = []
+        for half in range(2):
+            start = pl.multiple_of(starts[2 * half + part], 512)
+            blocks.append(weight.at[:, pl.ds(start, 512)])
+        for half in range(2):
+            blocks.append(sibling.at[pl.ds(1024 * half + 512 * part, 512)])
+    else:
+        blocks = [block.at[pl.ds(512 * part, 512)] for block in sources]
     return [
         pltpu.make_async_copy(block, target, sems.at[i])
         for i, (block, target) in enumerate(zip(blocks, targets))
@@ -313,13 +312,11 @@
     )(queries, jnp.pad(new_keys, front), jnp.pad(new_values, front), row_start)
 
 
-def attend(first, plan, starts, queries, cache, fresh, sources=(), after=()):
+def attend(first, plan, starts, queries, cache, fresh, sources, after=()):
     area = fresh[0].shape[1:]
     rows = jax.ShapeDtypeStruct((PIECE * BLOCK, queries.shape[1]), queries.dtype)
-    staged = []
-    if sources:
-        staged = [pltpu.VMEM((512, 512), queries.dtype)] * 8
-        staged += [pltpu.VMEM((2048, 512), queries.dtype)] * 2
+    staged = [pltpu.VMEM((512, 512), queries.dtype)] * 4
+    staged += [pltpu.VMEM((1024, 512), queries.dtype)] * 2
     return pl.pallas_call(
         functools.partial(main_kernel, first),
         out_shape=(rows, *staged),
@@ -336,10 +333,10 @@
                 pltpu.VMEM((PIECE + 1, *area), jnp.bfloat16),
                 pltpu.VMEM((PIECE + 1, *area), jnp.float32),
                 pltpu.SemaphoreType.DMA((4,)),
-                pltpu.SemaphoreType.DMA((2, 8)),
+                pltpu.SemaphoreType.DMA((2, 4)),
             ],
         ),
-        compiler_params=pltpu.CompilerParams(vmem_limit_bytes=(16 if sources else 7) << 20),
+        compiler_params=pltpu.CompilerParams(vmem_limit_bytes=12 << 20),
         cost_estimate=pl.CostEstimate(
             flops=1 << 31, bytes_accessed=4 << 20, transcendentals=1 << 18
         ),
@@ -385,10 +382,13 @@
     fresh = attend_fresh(queries, new_keys, new_values, row_start)
     plan, sibling, near_mats[:2] = lax.optimization_barrier((plan, sibling, near_mats[:2]))
     starts = jnp.stack(sum(shared(0), []))
-    first = attend(0, plan, starts, queries, cache, fresh)[0]
-    sources = (out_weight, sibling, *near_mats)
+    first, *mats, own_0, own_1 = attend(
+        0, plan, starts, queries, cache, fresh, (out_weight, sibling)
+    )
     others_a = swap(first, 1)
-    second, *mats, own_0, own_1 = attend(PIECE, plan, starts, queries, cache, fresh, sources, (others_a,))
+    second, *rest = attend(PIECE, plan, starts, queries, cache, fresh, near_mats, (others_a,))
+    mats += rest[:4]
+    own_mats = ((own_0, rest[4]), (own_1, rest[5]))
     attended = [first, second]
 
     def times(rows, mat):
@@ -416,7 +416,11 @@
     got.append([swap(part, mask) for part, mask in zip(sent, (6, 2))])
 
     own = [
-        [times(jnp.concatenate(parts, axis=1), mat) for parts, mat in zip(halves, (own_0, own_1))]
+        [
+            times(jnp.concatenate(parts[:2], axis=1), mat[0])
+            + times(jnp.concatenate(parts[2:], axis=1), mat[1])
+            for parts, mat in zip(halves, own_mats)
+        ]
         for halves in inputs
     ]
     own = [[lax.optimization_barrier(part) for part in halves] for halves in own]

time: 111 us -> 112 us (level)
  local copies, waits for them, and re-layouts: 2.89 us -> 5.79 us
  waiting for transfers between devices: 39.7 us -> 37.4 us
  Pallas kernels: 23.2 us -> 21.1 us
  starting transfers between devices: 33.1 us -> 34.9 us
    unnamed x18 -> x22, local copies, waits for them, and re-layouts: 1.98 us -> 4.87 us
    ppermute x23, starting transfers between devices: 21.5 us -> 23.2 us  [swap(): return lax.ppermute(value, 'tensor', [(t, t ^ mask) for t in range(count)])]
    all_to_all x1, waiting for transfers between devices: 13.7 us -> 12.2 us  [on_device(): lax.all_to_all(payload, 'dp', split_axis=0, concat_axis=0, tiled=True)]
    pallas_call x2, Pallas kernels: 8.38 us -> 7.05 us  [attend(): pl.pallas_call(functools.partial(main_kernel, first), out_shape=(rows, *s...]
    dot_general x20 -> x24, matrix products: 7.58 us -> 8.21 us  [times(): return jnp.dot(rows, mat, preferred_element_type=f32)]
  transfers between devices with their start and end apart: 24 -> 24, of which waited for: 12 -> 12; matrix products, arithmetic and copies ran while one was open for 9% -> 9% of each run, Pallas kernels for 19% -> 17%
where the time goes in v10:
time: 112 us
  waiting for transfers between devices  37.4 us (33%)
  starting transfers between devices  34.9 us (31%)
  Pallas kernels  21.1 us (19%)
  matrix products  8.21 us (7%)
  local copies, waits for them, and re-layouts  5.79 us (5%)
  other arithmetic  3.59 us (3%)
  between operations  1.16 us (1%)
    ppermute x23, waiting for transfers between devices, swap(): return lax.ppermute(value, 'tensor', [(t, t ^ mask) for t in range(count)])  25.2 us
    ppermute x23, starting transfers between devices, swap(): return lax.ppermute(value, 'tensor', [(t, t ^ mask) for t in range(count)])  23.2 us
    all_to_all x1, waiting for transfers between devices, on_device(): lax.all_to_all(payload, 'dp', split_axis=0, concat_axis=0, tiled=True)  12.2 us
    all_to_all x1, starting transfers between devices, on_device(): lax.all_to_all(payload, 'dp', split_axis=0, concat_axis=0, tiled=True)  11.6 us
    dot_general x24, matrix products, times(): return jnp.dot(rows, mat, preferred_element_type=f32)  8.21 us
    pallas_call x2, Pallas kernels, attend(): pl.pallas_call(functools.partial(main_kernel, first), out_shape=(rows, *s...  7.05 us
    pallas_call x1, Pallas kernels, attend_fresh(): pl.pallas_call(fresh_kernel, out_shape=(area, area), in_specs=whole(4), o...  6.16 us
    pallas_call x1, Pallas kernels, cut(): pl.pallas_call(cut_kernel, out_shape=tuple((pltpu.VMEM((height, 512), wei...  6.03 us
  transfers between devices with their start and end apart: 24, of which 12 were waited for; matrix products, arithmetic and copies ran while one was open for 9% of the time, Pallas kernels for 17%

profile of v10, /device:TPU:2, one launch (start us, length us, event | category | flops | bytes accessed | tf_op | source)
XLA Modules:
  0.0 112.1 jit_solution(10060445886366482738)
XLA Ops:
  0.6 1.8 %shard_map.122.after = bf16[32,256,128]{2,1,0:T(8,128)(2,1)S(1)} custom-call(s32[1,32]{1,0:T(1,128)} %lengths_hbm.1, bf16[32,128,128]{2,1,0:T(8,128)(2,1)} %bitcast.88, bf16[32,128,128]{2,1,0:T(8,128)(2,1)} %bitcast.89), custom_call_target="tpu_custom_call" | custom-call | flops 1048576 | bytes 4194304 | tf_op jit(solution)/shard_map/pallas_call | solution.py:236
  2.5 1.3 %copy-done = bf16[32,256,128]{2,1,0:T(8,128)(2,1)} copy-done((bf16[32,256,128]{2,1,0:T(8,128)(2,1)}, bf16[32,256,128]{2,1,0:T(8,128)(2,1)S(1)}, u32[]{:S(2)}) %copy-start) | copy-done | bytes 2097176
  3.8 11.6 %all-to-all-start = ((bf16[32,256,128]{2,1,0:T(8,128)(2,1)}), bf16[32,256,128]{2,1,0:T(8,128)(2,1)S(1)}, u32[]{:S(2)}, u32[]{:S(2)}) async-start(bf16[32,256,128]{2,1,0:T(8,128)(2,1)} %copy-done), calls=%async_computation | async-start | bytes 4194304 | tf_op jit(solution)/shard_map/all_to_all | solution.py:374
  15.6 1.6 %copy-done.1 = bf16[32,256,128]{2,1,0:T(8,128)(2,1)S(1)} copy-done((bf16[32,256,128]{2,1,0:T(8,128)(2,1)S(1)}, bf16[32,256,128]{2,1,0:T(8,128)(2,1)}, u32[]{:S(2)}) %copy-start.1) | copy-done | bytes 2097176
  17.2 6.0 %shard_map.123 = (bf16[1024,512]{1,0:T(8,128)(2,1)}, bf16[1024,512]{1,0:T(8,128)(2,1)}, bf16[1024,512]{1,0:T(8,128)(2,1)}, bf16[1024,512]{1,0:T(8,128)(2,1)}, bf16[2048,512]{1,0:T(8,128)(2,1)}) custom-call(s32[12]{0:T(128)S(1)} %stack.86.starts, bf16[512,8192]{1,0:T(8,128)(2,1)} %refs_0_.1, bf16[32,256,128]{2,1,0:T(8,128)(2,1)S(1)} %copy-done.1), custom_call_target="tpu_custom_call" | custom-call | bytes 12582912 | tf_op jit(solution)/shard_map/pallas_call | solution.py:268
  23.3 1.7 %collective-permute-start.1 = (bf16[1024,512]{1,0:T(8,128)(2,1)}, bf16[1024,512]{1,0:T(8,128)(2,1)}, u32[]{:S(2)}, u32[]{:S(2)}) collective-permute-start(bf16[1024,512]{1,0:T(8,128)(2,1)} %get-tuple-element.52), channel_id=1, source_target_pairs={{0,2},{1,3},{2,0},{3,1},{4,6},{5,7},{6,4},{7,5},{8,10},{9,11},{10,... | collective-permute-start | bytes 3145736 | tf_op jit(solution)/shard_map/ppermute | solution.py:365
  25.0 2.2 %collective-permute-start.2 = (bf16[1024,512]{1,0:T(8,128)(2,1)}, bf16[1024,512]{1,0:T(8,128)(2,1)}, u32[]{:S(2)}, u32[]{:S(2)}) collective-permute-start(bf16[1024,512]{1,0:T(8,128)(2,1)} %get-tuple-element.53), channel_id=1, source_target_pairs={{0,6},{1,7},{2,4},{3,5},{4,2},{5,3},{6,0},{7,1},{8,14},{9,15},{10,... | collective-permute-start | bytes 3145736 | tf_op jit(solution)/shard_map/ppermute | solution.py:365
  27.3 0.9 collective-permute-start.6
  30.3 6.2 %shard_map.124 = (f32[16,128,128]{2,1,0:T(8,128)S(1)}, f32[16,128,128]{2,1,0:T(8,128)S(1)}) custom-call(bf16[512,512]{1,0:T(8,128)(2,1)S(1)} %copy-done.4, bf16[608,128]{1,0:T(8,128)(2,1)S(1)} %pad.7.fresh_k, bf16[608,128]{1,0:T(8,128)(2,1)S(1)} %pad.8.fresh_v, s32[512,128]{1,0:T(8,128)S(1)} %broadcast_in_dim.105.row_start), custom_call_target="tpu_custom_call" | custom-call | flops 2147483648 | bytes 4194304 | tf_op jit(solution)/shard_map/pallas_call | solution.py:303
  36.5 1.0 copy-done.2
  37.5 1.0 copy-done.3
  38.5 11.2 %collective-permute-done.1.refs_0_ = bf16[1024,512]{1,0:T(8,128)(2,1)} collective-permute-done((bf16[1024,512]{1,0:T(8,128)(2,1)}, bf16[1024,512]{1,0:T(8,128)(2,1)}, u32[]{:S(2)}, u32[]{:S(2)}) %collective-permute-start.1) | collective-permute-done | bytes 1048608 | tf_op jit(solution)/shard_map/ppermute | solution.py:365
  49.7 2.8 %collective-permute-done.2.refs_1_ = bf16[1024,512]{1,0:T(8,128)(2,1)} collective-permute-done((bf16[1024,512]{1,0:T(8,128)(2,1)}, bf16[1024,512]{1,0:T(8,128)(2,1)}, u32[]{:S(2)}, u32[]{:S(2)}) %collective-permute-start.2) | collective-permute-done | bytes 1048608 | tf_op jit(solution)/shard_map/ppermute | solution.py:365
  52.5 12.2 %all-to-all-done.cache_hbm = bf16[32,256,128]{2,1,0:T(8,128)(2,1)S(1)} async-done(((bf16[32,256,128]{2,1,0:T(8,128)(2,1)}), bf16[32,256,128]{2,1,0:T(8,128)(2,1)S(1)}, u32[]{:S(2)}, u32[]{:S(2)}) %all-to-all-start) | async-done | bytes 2097184 | tf_op jit(solution)/shard_map/all_to_all | solution.py:374
  64.7 3.3 %shard_map.125 = (bf16[256,512]{1,0:T(8,128)(2,1)S(1)}, bf16[512,512]{1,0:T(8,128)(2,1)S(1)}, bf16[512,512]{1,0:T(8,128)(2,1)S(1)}, bf16[512,512]{1,0:T(8,128)(2...) custom-call(s32[5,48]{1,0:T(8,128)S(1)} %stack.73.plan, ...), custom_call_target="tpu_custom_call" | custom-call | flops 2147483648 | bytes 4194304 | tf_op jit(solution)/shard_map/pallas_call | solution.py:320
  68.1 1.7 %collective-permute-start.4 = (bf16[256,512]{1,0:T(8,128)(2,1)S(1)}, bf16[256,512]{1,0:T(8,128)(2,1)S(1)}, u32[]{:S(2)}, u32[]{:S(2)}) collective-permute-start(bf16[256,512]{1,0:T(8,128)(2,1)S(1)} %get-tuple-element.73), channel_id=1, source_target_pairs={{0,2},{1,3},{2,0},{3,1},{4,6},{5,7},{6,4},{7,5},{8,10},{9,11},{10,... | collective-permute-start | bytes 786440 | tf_op jit(solution)/shard_map/ppermute | solution.py:365
  69.7 2.2 %collective-permute-start.8 = (bf16[256,512]{1,0:T(8,128)(2,1)S(1)}, bf16[256,512]{1,0:T(8,128)(2,1)S(1)}, u32[]{:S(2)}, u32[]{:S(2)}) collective-permute-start(bf16[256,512]{1,0:T(8,128)(2,1)S(1)} %get-tuple-element.73), channel_id=1, source_target_pairs={{0,6},{1,7},{2,4},{3,5},{4,2},{5,3},{6,0},{7,1},{8,14},{9,15},{10,... | collective-permute-start | bytes 786440 | tf_op jit(solution)/shard_map/ppermute | solution.py:365
  72.5 0.9 collective-permute-done.6.refs_3_
  73.4 3.8 %shard_map.126 = (bf16[256,512]{1,0:T(8,128)(2,1)S(1)}, bf16[512,512]{1,0:T(8,128)(2,1)S(1)}, bf16[512,512]{1,0:T(8,128)(2,1)S(1)}, bf16[512,512]{1,0:T(8,128)(2...) custom-call(s32[5,48]{1,0:T(8,128)S(1)} %stack.73.plan, ...), custom_call_target="tpu_custom_call" | custom-call | flops 2147483648 | bytes 4194304 | tf_op jit(solution)/shard_map/pallas_call | solution.py:320
  77.2 1.0 collective-permute-start.12
  78.3 2.4 %collective-permute-start.15 = (bf16[256,512]{1,0:T(8,128)(2,1)S(1)}, bf16[256,512]{1,0:T(8,128)(2,1)S(1)}, u32[]{:S(2)}, u32[]{:S(2)}) collective-permute-start(bf16[256,512]{1,0:T(8,128)(2,1)S(1)} %get-tuple-element.90), channel_id=1, source_target_pairs={{0,6},{1,7},{2,4},{3,5},{4,2},{5,3},{6,0},{7,1},{8,14},{9,15},{10,... | collective-permute-start | bytes 786440 | tf_op jit(solution)/shard_map/ppermute | solution.py:365
  85.2 1.2 %collective-permute-start.11 = (bf16[256,512]{1,0:T(8,128)(2,1)S(1)}, bf16[256,512]{1,0:T(8,128)(2,1)S(1)}, u32[]{:S(2)}, u32[]{:S(2)}) collective-permute-start(bf16[256,512]{1,0:T(8,128)(2,1)S(1)} %fusion.1), channel_id=1, source_target_pairs={{0,2},{1,3},{2,0},{3,1},{4,6},{5,7},{6,4},{7,5},{8,10},{9,11},{10,... | collective-permute-start | bytes 786440 | tf_op jit(solution)/shard_map/ppermute | solution.py:365
  87.3 1.1 %collective-permute-start.10 = (bf16[256,512]{1,0:T(8,128)(2,1)S(1)}, bf16[256,512]{1,0:T(8,128)(2,1)S(1)}, u32[]{:S(2)}, u32[]{:S(2)}) collective-permute-start(bf16[256,512]{1,0:T(8,128)(2,1)S(1)} %fusion), channel_id=1, source_target_pairs={{0,6},{1,7},{2,4},{3,5},{4,2},{5,3},{6,0},{7,1},{8,14},{9,15},{10,... | collective-permute-start | bytes 786440 | tf_op jit(solution)/shard_map/ppermute | solution.py:365
  91.0 2.3 %collective-permute-start.17 = (bf16[256,512]{1,0:T(8,128)(2,1)S(1)}, bf16[256,512]{1,0:T(8,128)(2,1)S(1)}, u32[]{:S(2)}, u32[]{:S(2)}) collective-permute-start(bf16[256,512]{1,0:T(8,128)(2,1)S(1)} %fusion.2), channel_id=1, source_target_pairs={{0,6},{1,7},{2,4},{3,5},{4,2},{5,3},{6,0},{7,1},{8,14},{9,15},{10,... | collective-permute-start | bytes 786440 | tf_op jit(solution)/shard_map/ppermute | solution.py:365
  95.3 2.5 %collective-permute-done.10 = bf16[256,512]{1,0:T(8,128)(2,1)S(1)} collective-permute-done((bf16[256,512]{1,0:T(8,128)(2,1)S(1)}, bf16[256,512]{1,0:T(8,128)(2,1)S(1)}, u32[]{:S(2)}, u32[]{:S(2)}) %collective-permute-start.10) | collective-permute-done | bytes 262176 | tf_op jit(solution)/shard_map/ppermute | solution.py:365
  97.9 1.7 %collective-permute-done.18 = bf16[256,512]{1,0:T(8,128)(2,1)S(1)} collective-permute-done((bf16[256,512]{1,0:T(8,128)(2,1)S(1)}, bf16[256,512]{1,0:T(8,128)(2,1)S(1)}, u32[]{:S(2)}, u32[]{:S(2)}) %collective-permute-start.18) | collective-permute-done | bytes 262176 | tf_op jit(solution)/shard_map/ppermute | solution.py:365
  99.6 2.8 %collective-permute-done.17 = bf16[256,512]{1,0:T(8,128)(2,1)S(1)} collective-permute-done((bf16[256,512]{1,0:T(8,128)(2,1)S(1)}, bf16[256,512]{1,0:T(8,128)(2,1)S(1)}, u32[]{:S(2)}, u32[]{:S(2)}) %collective-permute-start.17) | collective-permute-done | bytes 262176 | tf_op jit(solution)/shard_map/ppermute | solution.py:365
  103.0 1.1 %collective-permute-done.19 = f32[512]{0:T(512)S(1)} collective-permute-done((f32[512]{0:T(512)S(1)}, f32[512]{0:T(512)S(1)}, u32[]{:S(2)}, u32[]{:S(2)}) %collective-permute-start.19) | collective-permute-done | bytes 2080 | tf_op jit(solution)/shard_map/ppermute | solution.py:365
  104.1 1.1 collective-permute-start.22
  105.2 3.6 %collective-permute-start.20 = (f32[512]{0:T(512)S(1)}, f32[512]{0:T(512)S(1)}, u32[]{:S(2)}, u32[]{:S(2)}) collective-permute-start(f32[512]{0:T(512)S(1)} %add.186), channel_id=1, source_target_pairs={{0,4},{1,5},{2,6},{3,7},{4,0},{5,1},{6,2},{7,3},{8,12},{9,13},{10,... | collective-permute-start | bytes 6152 | tf_op jit(solution)/shard_map/ppermute | solution.py:365
  108.9 1.5 %collective-permute-done.20 = f32[512]{0:T(512)S(1)} collective-permute-done((f32[512]{0:T(512)S(1)}, f32[512]{0:T(512)S(1)}, u32[]{:S(2)}, u32[]{:S(2)}) %collective-permute-start.20) | collective-permute-done | bytes 2080 | tf_op jit(solution)/shard_map/ppermute | solution.py:365
  110.4 1.7 %multiply_convert_fusion = (bf16[512,1024]{1,0:T(8,128)(2,1)}, bf16[512,1024]{1,0:T(8,128)(2,1)}) fusion(f32[1024]{0:T(1024)S(1)} %copy-done.8, f32[512]{0:T(512)S(1)} %add_rsqrt_fusion, f32[256,512]{1,0:T(8,128)S(1)} %convert_add_fusion, f32[256,512]{1,0:T(8,128)S(1)} %convert_add_fusion.1, f32[256,512]{1,0:T(8,128)S(1)} %convert_add_fusion.2, ...), kind=kLoop, calls=%fused_computation.1 | loop fusion | flops 4718592 | bytes 5249024 | tf_op jit(solution)/shard_map/convert_element_type | solution.py:440
  (91 shorter events, 13.6 us)
Async XLA Ops:
  3.8 60.9 %all-to-all-start = ((bf16[32,256,128]{2,1,0:T(8,128)(2,1)}), bf16[32,256,128]{2,1,0:T(8,128)(2,1)S(1)}, u32[]{:S(2)}, u32[]{:S(2)}) async-start(bf16[32,256,128]{2,1,0:T(8,128)(2,1)} %copy-done), calls=%async_computation | async-start | bytes 4194304 | tf_op jit(solution)/shard_map/all_to_all | solution.py:374
  15.6 1.6 %copy-start.1 = (bf16[32,256,128]{2,1,0:T(8,128)(2,1)S(1)}, bf16[32,256,128]{2,1,0:T(8,128)(2,1)}, u32[]{:S(2)}) copy-start(bf16[32,256,128]{2,1,0:T(8,128)(2,1)} %copy-done) | copy-start | bytes 6291460
  17.1 11.0 %copy-start.10 = (s32[1,32]{1,0:T(1,128)S(1)}, s32[1,32]{1,0:T(1,128)}, u32[]{:S(2)}) copy-start(s32[1,32]{1,0:T(1,128)} %param.15) | copy-start | bytes 388
  17.2 11.4 %copy-start.9 = (s32[1,32]{1,0:T(1,128)S(1)}, s32[1,32]{1,0:T(1,128)}, u32[]{:S(2)}) copy-start(s32[1,32]{1,0:T(1,128)} %param.16) | copy-start | bytes 388
  17.2 12.2 %copy-start.6 = (bf16[512,128]{1,0:T(8,128)(2,1)S(1)}, bf16[512,128]{1,0:T(8,128)(2,1)}, u32[]{:S(2)}) copy-start(bf16[512,128]{1,0:T(8,128)(2,1)} %param.12) | copy-start | bytes 393220
  17.2 12.2 %copy-start.7 = (bf16[512,128]{1,0:T(8,128)(2,1)S(1)}, bf16[512,128]{1,0:T(8,128)(2,1)}, u32[]{:S(2)}) copy-start(bf16[512,128]{1,0:T(8,128)(2,1)} %param.13) | copy-start | bytes 393220
  17.2 13.2 %copy-start.4 = (bf16[512,512]{1,0:T(8,128)(2,1)S(1)}, bf16[512,512]{1,0:T(8,128)(2,1)}, u32[]{:S(2)}) copy-start(bf16[512,512]{1,0:T(8,128)(2,1)} %q.5) | copy-start | bytes 1572868
  23.2 29.3 %collective-permute-start = (bf16[2048,512]{1,0:T(8,128)(2,1)}, bf16[2048,512]{1,0:T(8,128)(2,1)}, u32[]{:S(2)}, u32[]{:S(2)}) collective-permute-start(bf16[2048,512]{1,0:T(8,128)(2,1)} %get-tuple-element.51), channel_id=1, source_target_pairs={{0,1},{1,0},{2,3},{3,2},{4,5},{5,4},{6,7},{7,6},{8,9},{9,8},{10,11... | collective-permute-start | bytes 6291464 | tf_op jit(solution)/shard_map/ppermute | solution.py:365
  23.3 26.4 %collective-permute-start.1 = (bf16[1024,512]{1,0:T(8,128)(2,1)}, bf16[1024,512]{1,0:T(8,128)(2,1)}, u32[]{:S(2)}, u32[]{:S(2)}) collective-permute-start(bf16[1024,512]{1,0:T(8,128)(2,1)} %get-tuple-element.52), channel_id=1, source_target_pairs={{0,2},{1,3},{2,0},{3,1},{4,6},{5,7},{6,4},{7,5},{8,10},{9,11},{10,... | collective-permute-start | bytes 3145736 | tf_op jit(solution)/shard_map/ppermute | solution.py:365
  25.0 27.5 %collective-permute-start.2 = (bf16[1024,512]{1,0:T(8,128)(2,1)}, bf16[1024,512]{1,0:T(8,128)(2,1)}, u32[]{:S(2)}, u32[]{:S(2)}) collective-permute-start(bf16[1024,512]{1,0:T(8,128)(2,1)} %get-tuple-element.53), channel_id=1, source_target_pairs={{0,6},{1,7},{2,4},{3,5},{4,2},{5,3},{6,0},{7,1},{8,14},{9,15},{10,... | collective-permute-start | bytes 3145736 | tf_op jit(solution)/shard_map/ppermute | solution.py:365
  27.2 45.4 %collective-permute-start.5 = (bf16[1024,512]{1,0:T(8,128)(2,1)}, bf16[1024,512]{1,0:T(8,128)(2,1)}, u32[]{:S(2)}, u32[]{:S(2)}) collective-permute-start(bf16[1024,512]{1,0:T(8,128)(2,1)} %get-tuple-element.66), channel_id=1, source_target_pairs={{0,3},{1,2},{2,1},{3,0},{4,7},{5,6},{6,5},{7,4},{8,11},{9,10},{10,... | collective-permute-start | bytes 3145736 | tf_op jit(solution)/shard_map/ppermute | solution.py:365
  27.3 46.1 %collective-permute-start.6 = (bf16[1024,512]{1,0:T(8,128)(2,1)}, bf16[1024,512]{1,0:T(8,128)(2,1)}, u32[]{:S(2)}, u32[]{:S(2)}) collective-permute-start(bf16[1024,512]{1,0:T(8,128)(2,1)} %get-tuple-element.67), channel_id=1, source_target_pairs={{0,7},{1,6},{2,5},{3,4},{4,3},{5,2},{6,1},{7,0},{8,15},{9,14},{10,... | collective-permute-start | bytes 3145736 | tf_op jit(solution)/shard_map/ppermute | solution.py:365
  68.0 5.4 %collective-permute-start.3 = (bf16[256,512]{1,0:T(8,128)(2,1)S(1)}, bf16[256,512]{1,0:T(8,128)(2,1)S(1)}, u32[]{:S(2)}, u32[]{:S(2)}) collective-permute-start(bf16[256,512]{1,0:T(8,128)(2,1)S(1)} %get-tuple-element.73), channel_id=1, source_target_pairs={{0,1},{1,0},{2,3},{3,2},{4,5},{5,4},{6,7},{7,6},{8,9},{9,8},{10,11... | collective-permute-start | bytes 786440 | tf_op jit(solution)/shard_map/ppermute | solution.py:365
  68.1 13.2 %collective-permute-start.4 = (bf16[256,512]{1,0:T(8,128)(2,1)S(1)}, bf16[256,512]{1,0:T(8,128)(2,1)S(1)}, u32[]{:S(2)}, u32[]{:S(2)}) collective-permute-start(bf16[256,512]{1,0:T(8,128)(2,1)S(1)} %get-tuple-element.73), channel_id=1, source_target_pairs={{0,2},{1,3},{2,0},{3,1},{4,6},{5,7},{6,4},{7,5},{8,10},{9,11},{10,... | collective-permute-start | bytes 786440 | tf_op jit(solution)/shard_map/ppermute | solution.py:365
  69.7 11.6 %collective-permute-start.8 = (bf16[256,512]{1,0:T(8,128)(2,1)S(1)}, bf16[256,512]{1,0:T(8,128)(2,1)S(1)}, u32[]{:S(2)}, u32[]{:S(2)}) collective-permute-start(bf16[256,512]{1,0:T(8,128)(2,1)S(1)} %get-tuple-element.73), channel_id=1, source_target_pairs={{0,6},{1,7},{2,4},{3,5},{4,2},{5,3},{6,0},{7,1},{8,14},{9,15},{10,... | collective-permute-start | bytes 786440 | tf_op jit(solution)/shard_map/ppermute | solution.py:365
  77.2 5.3 %collective-permute-start.12 = (bf16[256,512]{1,0:T(8,128)(2,1)S(1)}, bf16[256,512]{1,0:T(8,128)(2,1)S(1)}, u32[]{:S(2)}, u32[]{:S(2)}) collective-permute-start(bf16[256,512]{1,0:T(8,128)(2,1)S(1)} %get-tuple-element.90), channel_id=1, source_target_pairs={{0,1},{1,0},{2,3},{3,2},{4,5},{5,4},{6,7},{7,6},{8,9},{9,8},{10,11... | collective-permute-start | bytes 786440 | tf_op jit(solution)/shard_map/ppermute | solution.py:365
  78.2 10.3 %collective-permute-start.13 = (bf16[256,512]{1,0:T(8,128)(2,1)S(1)}, bf16[256,512]{1,0:T(8,128)(2,1)S(1)}, u32[]{:S(2)}, u32[]{:S(2)}) collective-permute-start(bf16[256,512]{1,0:T(8,128)(2,1)S(1)} %get-tuple-element.90), channel_id=1, source_target_pairs={{0,2},{1,3},{2,0},{3,1},{4,6},{5,7},{6,4},{7,5},{8,10},{9,11},{10,... | collective-permute-start | bytes 786440 | tf_op jit(solution)/shard_map/ppermute | solution.py:365
  78.3 10.5 %collective-permute-start.15 = (bf16[256,512]{1,0:T(8,128)(2,1)S(1)}, bf16[256,512]{1,0:T(8,128)(2,1)S(1)}, u32[]{:S(2)}, u32[]{:S(2)}) collective-permute-start(bf16[256,512]{1,0:T(8,128)(2,1)S(1)} %get-tuple-element.90), channel_id=1, source_target_pairs={{0,6},{1,7},{2,4},{3,5},{4,2},{5,3},{6,0},{7,1},{8,14},{9,15},{10,... | collective-permute-start | bytes 786440 | tf_op jit(solution)/shard_map/ppermute | solution.py:365
  81.3 2.4 %collective-permute-start.7 = (bf16[256,512]{1,0:T(8,128)(2,1)S(1)}, bf16[256,512]{1,0:T(8,128)(2,1)S(1)}, u32[]{:S(2)}, u32[]{:S(2)}) collective-permute-start(bf16[256,512]{1,0:T(8,128)(2,1)S(1)} %collective-permute-done.4), channel_id=1, source_target_pairs={{0,1},{1,0},{2,3},{3,2},{4,5},{5,4},{6,7},{7,6},{8,9},{9,8},{10,11... | collective-permute-start | bytes 786440 | tf_op jit(solution)/shard_map/ppermute | solution.py:365
  81.4 2.6 %collective-permute-start.9 = (bf16[256,512]{1,0:T(8,128)(2,1)S(1)}, bf16[256,512]{1,0:T(8,128)(2,1)S(1)}, u32[]{:S(2)}, u32[]{:S(2)}) collective-permute-start(bf16[256,512]{1,0:T(8,128)(2,1)S(1)} %collective-permute-done.8), channel_id=1, source_target_pairs={{0,1},{1,0},{2,3},{3,2},{4,5},{5,4},{6,7},{7,6},{8,9},{9,8},{10,11... | collective-permute-start | bytes 786440 | tf_op jit(solution)/shard_map/ppermute | solution.py:365
  85.2 9.9 %collective-permute-start.11 = (bf16[256,512]{1,0:T(8,128)(2,1)S(1)}, bf16[256,512]{1,0:T(8,128)(2,1)S(1)}, u32[]{:S(2)}, u32[]{:S(2)}) collective-permute-start(bf16[256,512]{1,0:T(8,128)(2,1)S(1)} %fusion.1), channel_id=1, source_target_pairs={{0,2},{1,3},{2,0},{3,1},{4,6},{5,7},{6,4},{7,5},{8,10},{9,11},{10,... | collective-permute-start | bytes 786440 | tf_op jit(solution)/shard_map/ppermute | solution.py:365
  87.3 10.5 %collective-permute-start.10 = (bf16[256,512]{1,0:T(8,128)(2,1)S(1)}, bf16[256,512]{1,0:T(8,128)(2,1)S(1)}, u32[]{:S(2)}, u32[]{:S(2)}) collective-permute-start(bf16[256,512]{1,0:T(8,128)(2,1)S(1)} %fusion), channel_id=1, source_target_pairs={{0,6},{1,7},{2,4},{3,5},{4,2},{5,3},{6,0},{7,1},{8,14},{9,15},{10,... | collective-permute-start | bytes 786440 | tf_op jit(solution)/shard_map/ppermute | solution.py:365
  88.5 1.5 %collective-permute-start.14 = (bf16[256,512]{1,0:T(8,128)(2,1)S(1)}, bf16[256,512]{1,0:T(8,128)(2,1)S(1)}, u32[]{:S(2)}, u32[]{:S(2)}) collective-permute-start(bf16[256,512]{1,0:T(8,128)(2,1)S(1)} %collective-permute-done.13), channel_id=1, source_target_pairs={{0,1},{1,0},{2,3},{3,2},{4,5},{5,4},{6,7},{7,6},{8,9},{9,8},{10,11... | collective-permute-start | bytes 786440 | tf_op jit(solution)/shard_map/ppermute | solution.py:365
  88.8 1.8 %collective-permute-start.16 = (bf16[256,512]{1,0:T(8,128)(2,1)S(1)}, bf16[256,512]{1,0:T(8,128)(2,1)S(1)}, u32[]{:S(2)}, u32[]{:S(2)}) collective-permute-start(bf16[256,512]{1,0:T(8,128)(2,1)S(1)} %collective-permute-done.15), channel_id=1, source_target_pairs={{0,1},{1,0},{2,3},{3,2},{4,5},{5,4},{6,7},{7,6},{8,9},{9,8},{10,11... | collective-permute-start | bytes 786440 | tf_op jit(solution)/shard_map/ppermute | solution.py:365
  90.9 8.7 %collective-permute-start.18 = (bf16[256,512]{1,0:T(8,128)(2,1)S(1)}, bf16[256,512]{1,0:T(8,128)(2,1)S(1)}, u32[]{:S(2)}, u32[]{:S(2)}) collective-permute-start(bf16[256,512]{1,0:T(8,128)(2,1)S(1)} %fusion.3), channel_id=1, source_target_pairs={{0,2},{1,3},{2,0},{3,1},{4,6},{5,7},{6,4},{7,5},{8,10},{9,11},{10,... | collective-permute-start | bytes 786440 | tf_op jit(solution)/shard_map/ppermute | solution.py:365
  91.0 11.4 %collective-permute-start.17 = (bf16[256,512]{1,0:T(8,128)(2,1)S(1)}, bf16[256,512]{1,0:T(8,128)(2,1)S(1)}, u32[]{:S(2)}, u32[]{:S(2)}) collective-permute-start(bf16[256,512]{1,0:T(8,128)(2,1)S(1)} %fusion.2), channel_id=1, source_target_pairs={{0,6},{1,7},{2,4},{3,5},{4,2},{5,3},{6,0},{7,1},{8,14},{9,15},{10,... | collective-permute-start | bytes 786440 | tf_op jit(solution)/shard_map/ppermute | solution.py:365
  95.2 7.3 %copy-start.5 = (bf16[512,1024]{1,0:T(8,128)(2,1)S(1)}, bf16[512,1024]{1,0:T(8,128)(2,1)}, u32[]{:S(2)}) copy-start(bf16[512,1024]{1,0:T(8,128)(2,1)} %param.14) | copy-start | bytes 3145732
  99.6 10.8 %copy-start.8 = (f32[1024]{0:T(1024)S(1)}, f32[1024]{0:T(1024)}, u32[]{:S(2)}) copy-start(f32[1024]{0:T(1024)} %param.21) | copy-start | bytes 12292
  102.9 1.2 %collective-permute-start.19 = (f32[512]{0:T(512)S(1)}, f32[512]{0:T(512)S(1)}, u32[]{:S(2)}, u32[]{:S(2)}) collective-permute-start(f32[512]{0:T(512)S(1)} %multiply_reduce_fusion), channel_id=1, source_target_pairs={{0,1},{1,0},{2,3},{3,2},{4,5},{5,4},{6,7},{7,6},{8,9},{9,8},{10,11... | collective-permute-start | bytes 6152 | tf_op jit(solution)/shard_map/ppermute | solution.py:365
  104.1 4.8 %collective-permute-start.22 = (f32[512]{0:T(512)S(1)}, f32[512]{0:T(512)S(1)}, u32[]{:S(2)}, u32[]{:S(2)}) collective-permute-start(f32[512]{0:T(512)S(1)} %add.186), channel_id=1, source_target_pairs={{0,6},{1,7},{2,4},{3,5},{4,2},{5,3},{6,0},{7,1},{8,14},{9,15},{10,... | collective-permute-start | bytes 6152 | tf_op jit(solution)/shard_map/ppermute | solution.py:365
  105.2 3.7 %collective-permute-start.21 = (f32[512]{0:T(512)S(1)}, f32[512]{0:T(512)S(1)}, u32[]{:S(2)}, u32[]{:S(2)}) collective-permute-start(f32[512]{0:T(512)S(1)} %add.186), channel_id=1, source_target_pairs={{0,2},{1,3},{2,0},{3,1},{4,6},{5,7},{6,4},{7,5},{8,10},{9,11},{10,... | collective-permute-start | bytes 6152 | tf_op jit(solution)/shard_map/ppermute | solution.py:365
  105.2 5.2 %collective-permute-start.20 = (f32[512]{0:T(512)S(1)}, f32[512]{0:T(512)S(1)}, u32[]{:S(2)}, u32[]{:S(2)}) collective-permute-start(f32[512]{0:T(512)S(1)} %add.186), channel_id=1, source_target_pairs={{0,4},{1,5},{2,6},{3,7},{4,0},{5,1},{6,2},{7,3},{8,12},{9,13},{10,... | collective-permute-start | bytes 6152 | tf_op jit(solution)/shard_map/ppermute | solution.py:365
  (3 other events, 3.3 us)

commit v11 on v6

--- a/solution.py
+++ b/solution.py
@@ -417,8 +417,7 @@
     summed = hidden.astype(f32) + delta
     residual_out = summed.astype(bf16)
     squares = jnp.sum(summed * summed, axis=1)
-    squares = squares + swap(squares, 1)
-    squares = squares + swap(squares, 4) + swap(squares, 2) + swap(squares, 6)
+    squares = squares + sum(swap(squares, mask) for mask in (4, 5, 2, 3, 6, 7, 1))
     mean_square = squares / D
     normed = (summed * lax.rsqrt(mean_square + 1e-06)[:, None] * norm_gain[None, :]).astype(bf16)
     return (residual_out, normed)

time: 111 us -> 114 us (1.027)
  starting transfers between devices: 33.8 us -> 38.1 us
  waiting for transfers between devices: 40 us -> 38.1 us
    ppermute x23 -> x26, starting transfers between devices: 22.2 us -> 26.4 us  [swap(): return lax.ppermute(value, 'tensor', [(t, t ^ mask) for t in range(count)])]
    ppermute x23 -> x26, waiting for transfers between devices: 26.2 us -> 24.4 us  [swap(): return lax.ppermute(value, 'tensor', [(t, t ^ mask) for t in range(count)])]
  transfers between devices with their start and end apart: 24 -> 27, of which waited for: 11 -> 9; matrix products, arithmetic and copies ran while one was open for 9% -> 8% of each run, Pallas kernels for 18% -> 18%
where the time goes in v11:
time: 114 us
  starting transfers between devices  38.1 us (33%)
  waiting for transfers between devices  38.1 us (33%)
  Pallas kernels  22.6 us (20%)
  matrix products  7 us (6%)
  other arithmetic  3.6 us (3%)
  local copies, waits for them, and re-layouts  3.03 us (3%)
  between operations  1.15 us (1%)
    ppermute x26, starting transfers between devices, swap(): return lax.ppermute(value, 'tensor', [(t, t ^ mask) for t in range(count)])  26.4 us
    ppermute x26, waiting for transfers between devices, swap(): return lax.ppermute(value, 'tensor', [(t, t ^ mask) for t in range(count)])  24.4 us
    all_to_all x1, waiting for transfers between devices, on_device(): lax.all_to_all(payload, 'dp', split_axis=0, concat_axis=0, tiled=True)  13.7 us
    all_to_all x1, starting transfers between devices, on_device(): lax.all_to_all(payload, 'dp', split_axis=0, concat_axis=0, tiled=True)  11.6 us
    pallas_call x2, Pallas kernels, attend(): pl.pallas_call(functools.partial(main_kernel, first), out_shape=(rows, *s...  7.76 us
    dot_general x16, matrix products, times(): return jnp.dot(rows, mat, preferred_element_type=f32)  7 us
    pallas_call x1, Pallas kernels, attend_fresh(): pl.pallas_call(fresh_kernel, out_shape=(area, area), in_specs=whole(4), o...  6.16 us
    pallas_call x1, Pallas kernels, cut(): pl.pallas_call(cut_kernel, out_shape=tuple((pltpu.VMEM((rows, width), wei...  6.06 us
  transfers between devices with their start and end apart: 27, of which 9 were waited for; matrix products, arithmetic and copies ran while one was open for 8% of the time, Pallas kernels for 18%

profile of v11, /device:TPU:2, one launch (start us, length us, event | category | flops | bytes accessed | tf_op | source)
XLA Modules:
  0.0 113.6 jit_solution(5420098196649602792)
XLA Ops:
  0.6 2.6 %shard_map.122.after = bf16[32,256,128]{2,1,0:T(8,128)(2,1)} custom-call(s32[1,32]{1,0:T(1,128)} %lengths_hbm.1, bf16[32,128,128]{2,1,0:T(8,128)(2,1)} %bitcast.80, bf16[32,128,128]{2,1,0:T(8,128)(2,1)} %bitcast.81), custom_call_target="tpu_custom_call" | custom-call | flops 1048576 | bytes 4194304 | tf_op jit(solution)/shard_map/pallas_call | solution.py:246
  3.2 11.6 %all-to-all-start = ((bf16[32,256,128]{2,1,0:T(8,128)(2,1)}), bf16[32,256,128]{2,1,0:T(8,128)(2,1)S(1)}, u32[]{:S(2)}, u32[]{:S(2)}) async-start(bf16[32,256,128]{2,1,0:T(8,128)(2,1)} %shard_map.122.after), calls=%async_computation | async-start | bytes 4194304 | tf_op jit(solution)/shard_map/all_to_all | solution.py:374
  15.0 6.1 %shard_map.123 = (bf16[512,1024]{1,0:T(8,128)(2,1)}, bf16[512,1024]{1,0:T(8,128)(2,1)}, bf16[512,1024]{1,0:T(8,128)(2,1)}, bf16[512,1024]{1,0:T(8,128)(2,1)}, bf16[512,2048]{1,0:T(8,128)(2,1)}) custom-call(s32[12]{0:T(128)S(1)} %stack.86.starts, bf16[512,8192]{1,0:T(8,128)(2,1)} %refs_1_.1, bf16[32,256,128]{2,1,0:T(8,128)(2,1)} %shard_map.122.after), custom_call_target="tpu_custom_call" | custom-call | bytes 12582912 | tf_op jit(solution)/shard_map/pallas_call | solution.py:279
  21.2 1.7 %collective-permute-start.1 = (bf16[512,1024]{1,0:T(8,128)(2,1)}, bf16[512,1024]{1,0:T(8,128)(2,1)}, u32[]{:S(2)}, u32[]{:S(2)}) collective-permute-start(bf16[512,1024]{1,0:T(8,128)(2,1)} %get-tuple-element.31), channel_id=1, source_target_pairs={{0,2},{1,3},{2,0},{3,1},{4,6},{5,7},{6,4},{7,5},{8,10},{9,11},{10,... | collective-permute-start | bytes 3145736 | tf_op jit(solution)/shard_map/ppermute | solution.py:365
  22.9 2.2 %collective-permute-start.2 = (bf16[512,1024]{1,0:T(8,128)(2,1)}, bf16[512,1024]{1,0:T(8,128)(2,1)}, u32[]{:S(2)}, u32[]{:S(2)}) collective-permute-start(bf16[512,1024]{1,0:T(8,128)(2,1)} %get-tuple-element.32), channel_id=1, source_target_pairs={{0,6},{1,7},{2,4},{3,5},{4,2},{5,3},{6,0},{7,1},{8,14},{9,15},{10,... | collective-permute-start | bytes 3145736 | tf_op jit(solution)/shard_map/ppermute | solution.py:365
  25.2 0.9 collective-permute-start.6
  28.2 6.2 %shard_map.124 = (f32[16,128,128]{2,1,0:T(8,128)S(1)}, f32[16,128,128]{2,1,0:T(8,128)S(1)}) custom-call(bf16[512,512]{1,0:T(8,128)(2,1)S(1)} %copy-done.2, bf16[608,128]{1,0:T(8,128)(2,1)S(1)} %pad.7.fresh_k, bf16[608,128]{1,0:T(8,128)(2,1)S(1)} %pad.8.fresh_v, s32[512,128]{1,0:T(8,128)S(1)} %broadcast_in_dim.105.row_start), custom_call_target="tpu_custom_call" | custom-call | flops 2147483648 | bytes 4194304 | tf_op jit(solution)/shard_map/pallas_call | solution.py:297
  34.4 1.0 copy-done
  35.4 1.0 copy-done.1
  36.3 11.2 %collective-permute-done.1.refs_4_ = bf16[512,1024]{1,0:T(8,128)(2,1)} collective-permute-done((bf16[512,1024]{1,0:T(8,128)(2,1)}, bf16[512,1024]{1,0:T(8,128)(2,1)}, u32[]{:S(2)}, u32[]{:S(2)}) %collective-permute-start.1) | collective-permute-done | bytes 1048608 | tf_op jit(solution)/shard_map/ppermute | solution.py:365
  47.6 2.8 %collective-permute-done.2.refs_5_ = bf16[512,1024]{1,0:T(8,128)(2,1)} collective-permute-done((bf16[512,1024]{1,0:T(8,128)(2,1)}, bf16[512,1024]{1,0:T(8,128)(2,1)}, u32[]{:S(2)}, u32[]{:S(2)}) %collective-permute-start.2) | collective-permute-done | bytes 1048608 | tf_op jit(solution)/shard_map/ppermute | solution.py:365
  50.4 13.7 %all-to-all-done.cache_hbm = bf16[32,256,128]{2,1,0:T(8,128)(2,1)S(1)} async-done(((bf16[32,256,128]{2,1,0:T(8,128)(2,1)}), bf16[32,256,128]{2,1,0:T(8,128)(2,1)S(1)}, u32[]{:S(2)}, u32[]{:S(2)}) %all-to-all-start) | async-done | bytes 2097184 | tf_op jit(solution)/shard_map/all_to_all | solution.py:374
  64.1 3.2 %shard_map.125 = bf16[256,512]{1,0:T(8,128)(2,1)S(1)} custom-call(s32[5,48]{1,0:T(8,128)S(1)} %stack.73.plan, s32[4]{0:T(128)S(1)} %pad_add_fusion.starts, bf16[512,512]{1,0:T(8,128)(2,1)S(1)} %copy-done.2, bf16[32,256,128]{2,1,0:T(8,128)(2,1)S(1)} %all-to-all-done.cache_hbm, f32[16,128,128]{2,1,0:T(8,128)} %copy-done, f32[16,128,128]{2,1,0:T(8,128)} %copy-done.1), custom_call_target="tpu_custom_call" | custom-call | flops 2147483648 | bytes 4194304 | tf_op jit(solution)/shard_map/pallas_call | solution.py:313
  67.4 1.7 %collective-permute-start.3 = (bf16[256,512]{1,0:T(8,128)(2,1)S(1)}, bf16[256,512]{1,0:T(8,128)(2,1)S(1)}, u32[]{:S(2)}, u32[]{:S(2)}) collective-permute-start(bf16[256,512]{1,0:T(8,128)(2,1)S(1)} %shard_map.125), channel_id=1, source_target_pairs={{0,2},{1,3},{2,0},{3,1},{4,6},{5,7},{6,4},{7,5},{8,10},{9,11},{10,... | collective-permute-start | bytes 786440 | tf_op jit(solution)/shard_map/ppermute | solution.py:365
  69.1 2.2 %collective-permute-start.4 = (bf16[256,512]{1,0:T(8,128)(2,1)S(1)}, bf16[256,512]{1,0:T(8,128)(2,1)S(1)}, u32[]{:S(2)}, u32[]{:S(2)}) collective-permute-start(bf16[256,512]{1,0:T(8,128)(2,1)S(1)} %shard_map.125), channel_id=1, source_target_pairs={{0,6},{1,7},{2,4},{3,5},{4,2},{5,3},{6,0},{7,1},{8,14},{9,15},{10,... | collective-permute-start | bytes 786440 | tf_op jit(solution)/shard_map/ppermute | solution.py:365
  71.3 4.5 %shard_map.126 = (bf16[256,512]{1,0:T(8,128)(2,1)S(1)}, bf16[512,1024]{1,0:T(8,128)(2,1)S(1)}, bf16[512,1024]{1,0:T(8,128)(2,1)S(1)}, bf16[512,1024]{1,0:T(8,128...) custom-call(s32[5,48]{1,0:T(8,128)S(1)} %stack.73.plan, ...), custom_call_target="tpu_custom_call" | custom-call | flops 2147483648 | bytes 4194304 | tf_op jit(solution)/shard_map/pallas_call | solution.py:313
  75.8 0.7 collective-permute-start.14
  76.7 2.1 %collective-permute-start.13 = (bf16[256,512]{1,0:T(8,128)(2,1)S(1)}, bf16[256,512]{1,0:T(8,128)(2,1)S(1)}, u32[]{:S(2)}, u32[]{:S(2)}) collective-permute-start(bf16[256,512]{1,0:T(8,128)(2,1)S(1)} %get-tuple-element.53), channel_id=1, source_target_pairs={{0,6},{1,7},{2,4},{3,5},{4,2},{5,3},{6,0},{7,1},{8,14},{9,15},{10,... | collective-permute-start | bytes 786440 | tf_op jit(solution)/shard_map/ppermute | solution.py:365
  84.4 1.2 %collective-permute-start.9 = (bf16[256,512]{1,0:T(8,128)(2,1)S(1)}, bf16[256,512]{1,0:T(8,128)(2,1)S(1)}, u32[]{:S(2)}, u32[]{:S(2)}) collective-permute-start(bf16[256,512]{1,0:T(8,128)(2,1)S(1)} %slice.55), channel_id=1, source_target_pairs={{0,6},{1,7},{2,4},{3,5},{4,2},{5,3},{6,0},{7,1},{8,14},{9,15},{10,... | collective-permute-start | bytes 786440 | tf_op jit(solution)/shard_map/ppermute | solution.py:365
  86.1 0.7 collective-permute-start.11
  89.4 2.3 %collective-permute-start.16 = (bf16[256,512]{1,0:T(8,128)(2,1)S(1)}, bf16[256,512]{1,0:T(8,128)(2,1)S(1)}, u32[]{:S(2)}, u32[]{:S(2)}) collective-permute-start(bf16[256,512]{1,0:T(8,128)(2,1)S(1)} %slice.53), channel_id=1, source_target_pairs={{0,6},{1,7},{2,4},{3,5},{4,2},{5,3},{6,0},{7,1},{8,14},{9,15},{10,... | collective-permute-start | bytes 786440 | tf_op jit(solution)/shard_map/ppermute | solution.py:365
  92.2 0.8 collective-permute-start.18
  92.9 1.9 %collective-permute-done.9 = bf16[256,512]{1,0:T(8,128)(2,1)S(1)} collective-permute-done((bf16[256,512]{1,0:T(8,128)(2,1)S(1)}, bf16[256,512]{1,0:T(8,128)(2,1)S(1)}, u32[]{:S(2)}, u32[]{:S(2)}) %collective-permute-start.9) | collective-permute-done | bytes 262176 | tf_op jit(solution)/shard_map/ppermute | solution.py:365
  95.0 4.8 %collective-permute-done.16 = bf16[256,512]{1,0:T(8,128)(2,1)S(1)} collective-permute-done((bf16[256,512]{1,0:T(8,128)(2,1)S(1)}, bf16[256,512]{1,0:T(8,128)(2,1)S(1)}, u32[]{:S(2)}, u32[]{:S(2)}) %collective-permute-start.16) | collective-permute-done | bytes 262176 | tf_op jit(solution)/shard_map/ppermute | solution.py:365
  100.7 2.1 %collective-permute-start.19 = (f32[512]{0:T(512)S(1)}, f32[512]{0:T(512)S(1)}, u32[]{:S(2)}, u32[]{:S(2)}) collective-permute-start(f32[512]{0:T(512)S(1)} %multiply_reduce_fusion), channel_id=1, source_target_pairs={{0,4},{1,5},{2,6},{3,7},{4,0},{5,1},{6,2},{7,3},{8,12},{9,13},{10,... | collective-permute-start | bytes 6152 | tf_op jit(solution)/shard_map/ppermute | solution.py:365
  102.8 0.7 collective-permute-start.21
  103.5 2.3 %collective-permute-start.22 = (f32[512]{0:T(512)S(1)}, f32[512]{0:T(512)S(1)}, u32[]{:S(2)}, u32[]{:S(2)}) collective-permute-start(f32[512]{0:T(512)S(1)} %multiply_reduce_fusion), channel_id=1, source_target_pairs={{0,3},{1,2},{2,1},{3,0},{4,7},{5,6},{6,5},{7,4},{8,11},{9,10},{10,... | collective-permute-start | bytes 6152 | tf_op jit(solution)/shard_map/ppermute | solution.py:365
  105.8 1.8 %collective-permute-start.23 = (f32[512]{0:T(512)S(1)}, f32[512]{0:T(512)S(1)}, u32[]{:S(2)}, u32[]{:S(2)}) collective-permute-start(f32[512]{0:T(512)S(1)} %multiply_reduce_fusion), channel_id=1, source_target_pairs={{0,6},{1,7},{2,4},{3,5},{4,2},{5,3},{6,0},{7,1},{8,14},{9,15},{10,... | collective-permute-start | bytes 6152 | tf_op jit(solution)/shard_map/ppermute | solution.py:365
  107.6 1.6 %collective-permute-start.25 = (f32[512]{0:T(512)S(1)}, f32[512]{0:T(512)S(1)}, u32[]{:S(2)}, u32[]{:S(2)}) collective-permute-start(f32[512]{0:T(512)S(1)} %multiply_reduce_fusion), channel_id=1, source_target_pairs={{0,1},{1,0},{2,3},{3,2},{4,5},{5,4},{6,7},{7,6},{8,9},{9,8},{10,11... | collective-permute-start | bytes 6152 | tf_op jit(solution)/shard_map/ppermute | solution.py:365
  109.2 1.4 %collective-permute-done.23 = f32[512]{0:T(512)S(1)} collective-permute-done((f32[512]{0:T(512)S(1)}, f32[512]{0:T(512)S(1)}, u32[]{:S(2)}, u32[]{:S(2)}) %collective-permute-start.23) | collective-permute-done | bytes 2080 | tf_op jit(solution)/shard_map/ppermute | solution.py:365
  110.6 1.2 %collective-permute-done.24 = f32[512]{0:T(512)S(1)} collective-permute-done((f32[512]{0:T(512)S(1)}, f32[512]{0:T(512)S(1)}, u32[]{:S(2)}, u32[]{:S(2)}) %collective-permute-start.24) | collective-permute-done | bytes 2080 | tf_op jit(solution)/shard_map/ppermute | solution.py:365
  111.9 1.7 %multiply_convert_fusion = (bf16[512,1024]{1,0:T(8,128)(2,1)}, bf16[512,1024]{1,0:T(8,128)(2,1)}) fusion(f32[1024]{0:T(1024)S(1)} %copy-done.6, f32[512]{0:T(512)S(1)} %add_rsqrt_fusion, f32[256,512]{1,0:T(8,128)S(1)} %slice_add_fusion, f32[256,512]{1,0:T(8,128)S(1)} %slice_add_fusion.1, f32[256,512]{1,0:T(8,128)S(1)} %slice_add_fusion.2, ...), kind=kLoop, calls=%fused_computation.1 | loop fusion | flops 4718592 | bytes 5249024 | tf_op jit(solution)/shard_map/convert_element_type | solution.py:422
  (88 shorter events, 12.8 us)
Async XLA Ops:
  3.2 60.9 %all-to-all-start = ((bf16[32,256,128]{2,1,0:T(8,128)(2,1)}), bf16[32,256,128]{2,1,0:T(8,128)(2,1)S(1)}, u32[]{:S(2)}, u32[]{:S(2)}) async-start(bf16[32,256,128]{2,1,0:T(8,128)(2,1)} %shard_map.122.after), calls=%async_computation | async-start | bytes 4194304 | tf_op jit(solution)/shard_map/all_to_all | solution.py:374
  15.0 11.3 %copy-start.4 = (bf16[512,128]{1,0:T(8,128)(2,1)S(1)}, bf16[512,128]{1,0:T(8,128)(2,1)}, u32[]{:S(2)}) copy-start(bf16[512,128]{1,0:T(8,128)(2,1)} %param.12) | copy-start | bytes 393220
  15.0 11.4 %copy-start.5 = (bf16[512,128]{1,0:T(8,128)(2,1)S(1)}, bf16[512,128]{1,0:T(8,128)(2,1)}, u32[]{:S(2)}) copy-start(bf16[512,128]{1,0:T(8,128)(2,1)} %param.13) | copy-start | bytes 393220
  15.0 11.5 %copy-start.7 = (s32[1,32]{1,0:T(1,128)S(1)}, s32[1,32]{1,0:T(1,128)}, u32[]{:S(2)}) copy-start(s32[1,32]{1,0:T(1,128)} %param.16) | copy-start | bytes 388
  15.0 13.2 %copy-start.2 = (bf16[512,512]{1,0:T(8,128)(2,1)S(1)}, bf16[512,512]{1,0:T(8,128)(2,1)}, u32[]{:S(2)}) copy-start(bf16[512,512]{1,0:T(8,128)(2,1)} %q.5) | copy-start | bytes 1572868
  21.1 29.3 %collective-permute-start = (bf16[512,2048]{1,0:T(8,128)(2,1)}, bf16[512,2048]{1,0:T(8,128)(2,1)}, u32[]{:S(2)}, u32[]{:S(2)}) collective-permute-start(bf16[512,2048]{1,0:T(8,128)(2,1)} %get-tuple-element.30), channel_id=1, source_target_pairs={{0,1},{1,0},{2,3},{3,2},{4,5},{5,4},{6,7},{7,6},{8,9},{9,8},{10,11... | collective-permute-start | bytes 6291464 | tf_op jit(solution)/shard_map/ppermute | solution.py:365
  21.2 26.4 %collective-permute-start.1 = (bf16[512,1024]{1,0:T(8,128)(2,1)}, bf16[512,1024]{1,0:T(8,128)(2,1)}, u32[]{:S(2)}, u32[]{:S(2)}) collective-permute-start(bf16[512,1024]{1,0:T(8,128)(2,1)} %get-tuple-element.31), channel_id=1, source_target_pairs={{0,2},{1,3},{2,0},{3,1},{4,6},{5,7},{6,4},{7,5},{8,10},{9,11},{10,... | collective-permute-start | bytes 3145736 | tf_op jit(solution)/shard_map/ppermute | solution.py:365
  22.9 27.5 %collective-permute-start.2 = (bf16[512,1024]{1,0:T(8,128)(2,1)}, bf16[512,1024]{1,0:T(8,128)(2,1)}, u32[]{:S(2)}, u32[]{:S(2)}) collective-permute-start(bf16[512,1024]{1,0:T(8,128)(2,1)} %get-tuple-element.32), channel_id=1, source_target_pairs={{0,6},{1,7},{2,4},{3,5},{4,2},{5,3},{6,0},{7,1},{8,14},{9,15},{10,... | collective-permute-start | bytes 3145736 | tf_op jit(solution)/shard_map/ppermute | solution.py:365
  25.0 46.2 %collective-permute-start.5 = (bf16[512,1024]{1,0:T(8,128)(2,1)}, bf16[512,1024]{1,0:T(8,128)(2,1)}, u32[]{:S(2)}, u32[]{:S(2)}) collective-permute-start(bf16[512,1024]{1,0:T(8,128)(2,1)} %get-tuple-element.39), channel_id=1, source_target_pairs={{0,3},{1,2},{2,1},{3,0},{4,7},{5,6},{6,5},{7,4},{8,11},{9,10},{10,... | collective-permute-start | bytes 3145736 | tf_op jit(solution)/shard_map/ppermute | solution.py:365
  25.2 46.1 %collective-permute-start.6 = (bf16[512,1024]{1,0:T(8,128)(2,1)}, bf16[512,1024]{1,0:T(8,128)(2,1)}, u32[]{:S(2)}, u32[]{:S(2)}) collective-permute-start(bf16[512,1024]{1,0:T(8,128)(2,1)} %get-tuple-element.40), channel_id=1, source_target_pairs={{0,7},{1,6},{2,5},{3,4},{4,3},{5,2},{6,1},{7,0},{8,15},{9,14},{10,... | collective-permute-start | bytes 3145736 | tf_op jit(solution)/shard_map/ppermute | solution.py:365
  67.3 9.4 %collective-permute-start.7 = (bf16[256,512]{1,0:T(8,128)(2,1)S(1)}, bf16[256,512]{1,0:T(8,128)(2,1)S(1)}, u32[]{:S(2)}, u32[]{:S(2)}) collective-permute-start(bf16[256,512]{1,0:T(8,128)(2,1)S(1)} %shard_map.125), channel_id=1, source_target_pairs={{0,1},{1,0},{2,3},{3,2},{4,5},{5,4},{6,7},{7,6},{8,9},{9,8},{10,11... | collective-permute-start | bytes 786440 | tf_op jit(solution)/shard_map/ppermute | solution.py:365
  67.4 13.1 %collective-permute-start.3 = (bf16[256,512]{1,0:T(8,128)(2,1)S(1)}, bf16[256,512]{1,0:T(8,128)(2,1)S(1)}, u32[]{:S(2)}, u32[]{:S(2)}) collective-permute-start(bf16[256,512]{1,0:T(8,128)(2,1)S(1)} %shard_map.125), channel_id=1, source_target_pairs={{0,2},{1,3},{2,0},{3,1},{4,6},{5,7},{6,4},{7,5},{8,10},{9,11},{10,... | collective-permute-start | bytes 786440 | tf_op jit(solution)/shard_map/ppermute | solution.py:365
  69.1 11.5 %collective-permute-start.4 = (bf16[256,512]{1,0:T(8,128)(2,1)S(1)}, bf16[256,512]{1,0:T(8,128)(2,1)S(1)}, u32[]{:S(2)}, u32[]{:S(2)}) collective-permute-start(bf16[256,512]{1,0:T(8,128)(2,1)S(1)} %shard_map.125), channel_id=1, source_target_pairs={{0,6},{1,7},{2,4},{3,5},{4,2},{5,3},{6,0},{7,1},{8,14},{9,15},{10,... | collective-permute-start | bytes 786440 | tf_op jit(solution)/shard_map/ppermute | solution.py:365
  75.8 5.8 %collective-permute-start.14 = (bf16[256,512]{1,0:T(8,128)(2,1)S(1)}, bf16[256,512]{1,0:T(8,128)(2,1)S(1)}, u32[]{:S(2)}, u32[]{:S(2)}) collective-permute-start(bf16[256,512]{1,0:T(8,128)(2,1)S(1)} %get-tuple-element.53), channel_id=1, source_target_pairs={{0,1},{1,0},{2,3},{3,2},{4,5},{5,4},{6,7},{7,6},{8,9},{9,8},{10,11... | collective-permute-start | bytes 786440 | tf_op jit(solution)/shard_map/ppermute | solution.py:365
  76.5 10.3 %collective-permute-start.12 = (bf16[256,512]{1,0:T(8,128)(2,1)S(1)}, bf16[256,512]{1,0:T(8,128)(2,1)S(1)}, u32[]{:S(2)}, u32[]{:S(2)}) collective-permute-start(bf16[256,512]{1,0:T(8,128)(2,1)S(1)} %get-tuple-element.53), channel_id=1, source_target_pairs={{0,2},{1,3},{2,0},{3,1},{4,6},{5,7},{6,4},{7,5},{8,10},{9,11},{10,... | collective-permute-start | bytes 786440 | tf_op jit(solution)/shard_map/ppermute | solution.py:365
  76.7 10.1 %collective-permute-start.13 = (bf16[256,512]{1,0:T(8,128)(2,1)S(1)}, bf16[256,512]{1,0:T(8,128)(2,1)S(1)}, u32[]{:S(2)}, u32[]{:S(2)}) collective-permute-start(bf16[256,512]{1,0:T(8,128)(2,1)S(1)} %get-tuple-element.53), channel_id=1, source_target_pairs={{0,6},{1,7},{2,4},{3,5},{4,2},{5,3},{6,0},{7,1},{8,14},{9,15},{10,... | collective-permute-start | bytes 786440 | tf_op jit(solution)/shard_map/ppermute | solution.py:365
  80.6 3.3 %collective-permute-start.8 = (bf16[256,512]{1,0:T(8,128)(2,1)S(1)}, bf16[256,512]{1,0:T(8,128)(2,1)S(1)}, u32[]{:S(2)}, u32[]{:S(2)}) collective-permute-start(bf16[256,512]{1,0:T(8,128)(2,1)S(1)} %collective-permute-done.3), channel_id=1, source_target_pairs={{0,1},{1,0},{2,3},{3,2},{4,5},{5,4},{6,7},{7,6},{8,9},{9,8},{10,11... | collective-permute-start | bytes 786440 | tf_op jit(solution)/shard_map/ppermute | solution.py:365
  80.7 4.9 %collective-permute-start.10 = (bf16[256,512]{1,0:T(8,128)(2,1)S(1)}, bf16[256,512]{1,0:T(8,128)(2,1)S(1)}, u32[]{:S(2)}, u32[]{:S(2)}) collective-permute-start(bf16[256,512]{1,0:T(8,128)(2,1)S(1)} %collective-permute-done.4), channel_id=1, source_target_pairs={{0,1},{1,0},{2,3},{3,2},{4,5},{5,4},{6,7},{7,6},{8,9},{9,8},{10,11... | collective-permute-start | bytes 786440 | tf_op jit(solution)/shard_map/ppermute | solution.py:365
  84.4 10.4 %collective-permute-start.9 = (bf16[256,512]{1,0:T(8,128)(2,1)S(1)}, bf16[256,512]{1,0:T(8,128)(2,1)S(1)}, u32[]{:S(2)}, u32[]{:S(2)}) collective-permute-start(bf16[256,512]{1,0:T(8,128)(2,1)S(1)} %slice.55), channel_id=1, source_target_pairs={{0,6},{1,7},{2,4},{3,5},{4,2},{5,3},{6,0},{7,1},{8,14},{9,15},{10,... | collective-permute-start | bytes 786440 | tf_op jit(solution)/shard_map/ppermute | solution.py:365
  86.1 8.8 %collective-permute-start.11 = (bf16[256,512]{1,0:T(8,128)(2,1)S(1)}, bf16[256,512]{1,0:T(8,128)(2,1)S(1)}, u32[]{:S(2)}, u32[]{:S(2)}) collective-permute-start(bf16[256,512]{1,0:T(8,128)(2,1)S(1)} %slice.54), channel_id=1, source_target_pairs={{0,2},{1,3},{2,0},{3,1},{4,6},{5,7},{6,4},{7,5},{8,10},{9,11},{10,... | collective-permute-start | bytes 786440 | tf_op jit(solution)/shard_map/ppermute | solution.py:365
  87.3 1.6 %collective-permute-start.15 = (bf16[256,512]{1,0:T(8,128)(2,1)S(1)}, bf16[256,512]{1,0:T(8,128)(2,1)S(1)}, u32[]{:S(2)}, u32[]{:S(2)}) collective-permute-start(bf16[256,512]{1,0:T(8,128)(2,1)S(1)} %collective-permute-done.12), channel_id=1, source_target_pairs={{0,1},{1,0},{2,3},{3,2},{4,5},{5,4},{6,7},{7,6},{8,9},{9,8},{10,11... | collective-permute-start | bytes 786440 | tf_op jit(solution)/shard_map/ppermute | solution.py:365
  87.4 4.3 %collective-permute-start.17 = (bf16[256,512]{1,0:T(8,128)(2,1)S(1)}, bf16[256,512]{1,0:T(8,128)(2,1)S(1)}, u32[]{:S(2)}, u32[]{:S(2)}) collective-permute-start(bf16[256,512]{1,0:T(8,128)(2,1)S(1)} %collective-permute-done.13), channel_id=1, source_target_pairs={{0,1},{1,0},{2,3},{3,2},{4,5},{5,4},{6,7},{7,6},{8,9},{9,8},{10,11... | collective-permute-start | bytes 786440 | tf_op jit(solution)/shard_map/ppermute | solution.py:365
  89.4 10.4 %collective-permute-start.16 = (bf16[256,512]{1,0:T(8,128)(2,1)S(1)}, bf16[256,512]{1,0:T(8,128)(2,1)S(1)}, u32[]{:S(2)}, u32[]{:S(2)}) collective-permute-start(bf16[256,512]{1,0:T(8,128)(2,1)S(1)} %slice.53), channel_id=1, source_target_pairs={{0,6},{1,7},{2,4},{3,5},{4,2},{5,3},{6,0},{7,1},{8,14},{9,15},{10,... | collective-permute-start | bytes 786440 | tf_op jit(solution)/shard_map/ppermute | solution.py:365
  92.2 8.2 %collective-permute-start.18 = (bf16[256,512]{1,0:T(8,128)(2,1)S(1)}, bf16[256,512]{1,0:T(8,128)(2,1)S(1)}, u32[]{:S(2)}, u32[]{:S(2)}) collective-permute-start(bf16[256,512]{1,0:T(8,128)(2,1)S(1)} %slice.52), channel_id=1, source_target_pairs={{0,2},{1,3},{2,0},{3,1},{4,6},{5,7},{6,4},{7,5},{8,10},{9,11},{10,... | collective-permute-start | bytes 786440 | tf_op jit(solution)/shard_map/ppermute | solution.py:365
  99.9 12.0 %copy-start.6 = (f32[1024]{0:T(1024)S(1)}, f32[1024]{0:T(1024)}, u32[]{:S(2)}) copy-start(f32[1024]{0:T(1024)} %param.21) | copy-start | bytes 12292
  100.7 6.9 %collective-permute-start.19 = (f32[512]{0:T(512)S(1)}, f32[512]{0:T(512)S(1)}, u32[]{:S(2)}, u32[]{:S(2)}) collective-permute-start(f32[512]{0:T(512)S(1)} %multiply_reduce_fusion), channel_id=1, source_target_pairs={{0,4},{1,5},{2,6},{3,7},{4,0},{5,1},{6,2},{7,3},{8,12},{9,13},{10,... | collective-permute-start | bytes 6152 | tf_op jit(solution)/shard_map/ppermute | solution.py:365
  102.8 4.8 %collective-permute-start.20 = (f32[512]{0:T(512)S(1)}, f32[512]{0:T(512)S(1)}, u32[]{:S(2)}, u32[]{:S(2)}) collective-permute-start(f32[512]{0:T(512)S(1)} %multiply_reduce_fusion), channel_id=1, source_target_pairs={{0,5},{1,4},{2,7},{3,6},{4,1},{5,0},{6,3},{7,2},{8,13},{9,12},{10,... | collective-permute-start | bytes 6152 | tf_op jit(solution)/shard_map/ppermute | solution.py:365
  102.8 6.4 %collective-permute-start.21 = (f32[512]{0:T(512)S(1)}, f32[512]{0:T(512)S(1)}, u32[]{:S(2)}, u32[]{:S(2)}) collective-permute-start(f32[512]{0:T(512)S(1)} %multiply_reduce_fusion), channel_id=1, source_target_pairs={{0,2},{1,3},{2,0},{3,1},{4,6},{5,7},{6,4},{7,5},{8,10},{9,11},{10,... | collective-permute-start | bytes 6152 | tf_op jit(solution)/shard_map/ppermute | solution.py:365
  103.5 5.7 %collective-permute-start.22 = (f32[512]{0:T(512)S(1)}, f32[512]{0:T(512)S(1)}, u32[]{:S(2)}, u32[]{:S(2)}) collective-permute-start(f32[512]{0:T(512)S(1)} %multiply_reduce_fusion), channel_id=1, source_target_pairs={{0,3},{1,2},{2,1},{3,0},{4,7},{5,6},{6,5},{7,4},{8,11},{9,10},{10,... | collective-permute-start | bytes 6152 | tf_op jit(solution)/shard_map/ppermute | solution.py:365
  105.8 4.8 %collective-permute-start.23 = (f32[512]{0:T(512)S(1)}, f32[512]{0:T(512)S(1)}, u32[]{:S(2)}, u32[]{:S(2)}) collective-permute-start(f32[512]{0:T(512)S(1)} %multiply_reduce_fusion), channel_id=1, source_target_pairs={{0,6},{1,7},{2,4},{3,5},{4,2},{5,3},{6,0},{7,1},{8,14},{9,15},{10,... | collective-permute-start | bytes 6152 | tf_op jit(solution)/shard_map/ppermute | solution.py:365
  107.6 4.2 %collective-permute-start.24 = (f32[512]{0:T(512)S(1)}, f32[512]{0:T(512)S(1)}, u32[]{:S(2)}, u32[]{:S(2)}) collective-permute-start(f32[512]{0:T(512)S(1)} %multiply_reduce_fusion), channel_id=1, source_target_pairs={{0,7},{1,6},{2,5},{3,4},{4,3},{5,2},{6,1},{7,0},{8,15},{9,14},{10,... | collective-permute-start | bytes 6152 | tf_op jit(solution)/shard_map/ppermute | solution.py:365
  107.6 4.2 %collective-permute-start.25 = (f32[512]{0:T(512)S(1)}, f32[512]{0:T(512)S(1)}, u32[]{:S(2)}, u32[]{:S(2)}) collective-permute-start(f32[512]{0:T(512)S(1)} %multiply_reduce_fusion), channel_id=1, source_target_pairs={{0,1},{1,0},{2,3},{3,2},{4,5},{5,4},{6,7},{7,6},{8,9},{9,8},{10,11... | collective-permute-start | bytes 6152 | tf_op jit(solution)/shard_map/ppermute | solution.py:365
  (4 other events, 18.5 us)
